TPU v7x, 32 devices: a whole 2x2x4 slice. The times are simulated.
32 devices in a mesh: dp: 8 (over z, core), expert: 4 (over y, x).
Axes of the slice: x: 2, y: 2, z: 4, core: 2. Of those that a mesh axis runs over, the one named last changes fastest.
Arguments:
- tokens: bfloat16 [4096, 2048], P(('dp', 'expert')), may hold values from -6 to 6
- cotangent: bfloat16 [4096, 2048], P(('dp', 'expert')), may hold values from -6 to 6
- expert_ids: int32 [4096, 2], P(('dp', 'expert')), may hold values from 0 to 3, all different within a row; in each aligned block of 128 rows (0 to 127, 128 to 255, ...) at most 80 rows name the same one
- gate_weights: float32 [4096, 2], P(('dp', 'expert')), may hold values from 0.1 to 1
- partner: int32 [4], replicated, may hold values from 0 to 3, as said below
- w_gate: bfloat16 [4, 2048, 768], P('expert'), may hold values from -0.125 to 0.125
- w_up: bfloat16 [4, 2048, 768], P('expert'), may hold values from -0.125 to 0.125
- w_down: bfloat16 [4, 768, 2048], P('expert'), may hold values from -0.21875 to 0.21875
Outputs:
- mixed_out: bfloat16 [4096, 2048], P(('dp', 'expert'))
- token_grad: bfloat16 [4096, 2048], P(('dp', 'expert'))
- gate_grad: float32 [4096, 2], P(('dp', 'expert'))
- slot_grad_gate: float32 [4, 2048, 768], P('expert', 'dp')
- slot_grad_up: float32 [4, 2048, 768], P('expert', 'dp')
- slot_grad_down: float32 [4, 768, 2048], P('expert', None, 'dp')
Inputs may be any that keep to these rules, and one draw needn't show every extreme that they name: `expert_ids`: each row names 2 different experts. Among the 128 rows of one device no expert is named by more than 80 rows, and in every draw some device names some expert exactly 80 times. partner[partner[i]] = i and partner[i] != i for every slot i.
All inputs are finite; a program needn't handle non-finite values.
Results may differ from a plain program's by a relative error of at most 0.015.
Values may be sent and summed in bfloat16 or wider, within the bound.
No kernel may reach another device: no remote copies, remote signals or barrier semaphores. Data moves between devices by JAX's collectives and lax.ppermute only.
A program may use at most 128 MiB of HBM per device.

v0:
```python
import jax
import jax.numpy as jnp
from jax import lax
from jax.sharding import PartitionSpec as P


def as_sent(shard):

    def short(part):
        return part.astype(jnp.bfloat16) if part.dtype == jnp.float32 else part

    return jax.tree.map(short, shard)


def contract_rows(left_mat, right_mat):
    return lax.dot_general(
        left_mat, right_mat, (((0,), (0,)), ((), ())), preferred_element_type=jnp.float32
    )


def contract_cols(left_mat, right_mat):
    return lax.dot_general(
        left_mat, right_mat, (((1,), (1,)), ((), ())), preferred_element_type=jnp.float32
    )


def pick_from(stacked, source):
    return lax.dynamic_index_in_dim(stacked, source, 0, keepdims=False)


def shards(tokens, cotangent, expert_ids, gate_weights, partner, w_gate, w_up, w_down):
    groups = lax.axis_size("expert")
    my_group = lax.axis_index("expert")
    tok_count, model_width = tokens.shape
    top_count = expert_ids.shape[1]
    capacity = min(tok_count, 5 * tok_count * top_count // (4 * groups))
    buffer_rows = groups * capacity
    group_ids = jnp.arange(groups, dtype=jnp.int32)
    my_mate = pick_from(partner, my_group)
    flat_ids = expert_ids.reshape(-1)
    one_hot = (flat_ids[:, None] == group_ids[None, :]).astype(jnp.int32)
    earlier = jnp.cumsum(one_hot, axis=0) - one_hot
    slot_index = flat_ids * capacity + jnp.sum(earlier * one_hot, axis=1)
    place_mat = (slot_index[None, :] == jnp.arange(buffer_rows, dtype=jnp.int32)[:, None]).astype(
        jnp.bfloat16
    )
    gate_mat, up_mat, down_mat = (w_gate[0], w_up[0], w_down[0])
    repeated = jnp.repeat(tokens, top_count, axis=0)
    outgoing_rows = jnp.dot(place_mat, repeated, preferred_element_type=jnp.float32).astype(
        jnp.bfloat16
    )
    expert_in = lax.all_to_all(
        outgoing_rows.reshape(groups, capacity, model_width),
        "expert",
        split_axis=0,
        concat_axis=0,
        tiled=True,
    ).reshape(buffer_rows, model_width)
    gate_pre = jnp.dot(expert_in, gate_mat, preferred_element_type=jnp.float32)
    up_pre = jnp.dot(expert_in, up_mat, preferred_element_type=jnp.float32)
    sigmoid_gate = jax.nn.sigmoid(gate_pre)
    hidden = (gate_pre * sigmoid_gate * up_pre).astype(jnp.bfloat16)
    expert_out = jnp.dot(hidden, down_mat, preferred_element_type=jnp.float32).astype(jnp.bfloat16)
    returned = lax.all_to_all(
        expert_out.reshape(groups, capacity, model_width),
        "expert",
        split_axis=0,
        concat_axis=0,
        tiled=True,
    ).reshape(buffer_rows, model_width)
    per_assign = (
        jnp.take(returned, slot_index, axis=0)
        .astype(jnp.float32)
        .reshape(tok_count, top_count, model_width)
    )
    mixed_out = jnp.sum(gate_weights[:, :, None] * per_assign, axis=1).astype(jnp.bfloat16)
    cot_float = cotangent.astype(jnp.float32)
    gate_grad = jnp.sum(cot_float[:, None, :] * per_assign, axis=2)
    scaled = (
        (gate_weights[:, :, None] * cot_float[:, None, :])
        .astype(jnp.bfloat16)
        .reshape(-1, model_width)
    )
    outgoing_grads = jnp.dot(place_mat, scaled, preferred_element_type=jnp.float32).astype(
        jnp.bfloat16
    )
    grads_in = lax.all_to_all(
        outgoing_grads.reshape(groups, capacity, model_width),
        "expert",
        split_axis=0,
        concat_axis=0,
        tiled=True,
    ).reshape(buffer_rows, model_width)
    hidden_grad = contract_cols(grads_in, down_mat)
    gate_grad_pre = (
        hidden_grad * up_pre * sigmoid_gate * (1.0 + gate_pre * (1.0 - sigmoid_gate))
    ).astype(jnp.bfloat16)
    up_grad_pre = (hidden_grad * gate_pre * sigmoid_gate).astype(jnp.bfloat16)
    row_grad = (contract_cols(gate_grad_pre, gate_mat) + contract_cols(up_grad_pre, up_mat)).astype(
        jnp.bfloat16
    )
    returned_grads = lax.all_to_all(
        row_grad.reshape(groups, capacity, model_width),
        "expert",
        split_axis=0,
        concat_axis=0,
        tiled=True,
    ).reshape(buffer_rows, model_width)
    grad_rows = (
        jnp.take(returned_grads, slot_index, axis=0)
        .astype(jnp.float32)
        .reshape(tok_count, top_count, model_width)
    )
    token_grad = jnp.sum(grad_rows, axis=1).astype(jnp.bfloat16)
    partial_gate = contract_rows(expert_in, gate_grad_pre)
    partial_up = contract_rows(expert_in, up_grad_pre)
    partial_down = contract_rows(hidden, grads_in)
    sum_gate, sum_up, sum_down = (
        lax.psum_scatter(
            partial_gate.astype(jnp.bfloat16), "dp", scatter_dimension=0, tiled=True
        ).astype(jnp.float32),
        lax.psum_scatter(
            partial_up.astype(jnp.bfloat16), "dp", scatter_dimension=0, tiled=True
        ).astype(jnp.float32),
        lax.psum_scatter(
            partial_down.astype(jnp.bfloat16), "dp", scatter_dimension=1, tiled=True
        ).astype(jnp.float32),
    )
    is_mate = (partner == my_group)[:, None, None]
    outgoing = tuple(
        (
            jnp.where(is_mate, own_sum[None], jnp.zeros_like(own_sum)[None])
            for own_sum in (sum_gate, sum_up, sum_down)
        )
    )
    incoming = jax.tree.map(
        lambda part, own: part.astype(own.dtype),
        lax.all_to_all(as_sent(outgoing), "expert", split_axis=0, concat_axis=0, tiled=True),
        outgoing,
    )
    sum_gate, sum_up, sum_down = tuple(
        (pick_from(block_piece, my_mate) for block_piece in incoming)
    )
    return (mixed_out, token_grad, gate_grad, sum_gate[None], sum_up[None], sum_down[None])


def solution(mesh):
    in_specs = (
        P(("dp", "expert"), None),
        P(("dp", "expert"), None),
        P(("dp", "expert"), None),
        P(("dp", "expert"), None),
        P(),
        P("expert", None, None),
        P("expert", None, None),
        P("expert", None, None),
    )
    out_specs = (
        P(("dp", "expert"), None),
        P(("dp", "expert"), None),
        P(("dp", "expert"), None),
        P("expert", "dp", None),
        P("expert", "dp", None),
        P("expert", None, "dp"),
    )
    return jax.shard_map(shards, mesh=mesh, in_specs=in_specs, out_specs=out_specs, check_vma=False)
```

profile of v0, /device:TPU:0, one launch (start us, length us, event | category | flops | bytes accessed | tf_op | source)
XLA Modules:
  0.0 267.2 jit_solution(18066903013742447506)
XLA Ops:
  7.2 0.9 copy.18
  8.4 1.2 reduce-window.6
  10.1 2.7 %broadcast_in_dim.85 = bf16[128,2,2048]{2,1,0:T(2,128)(2,1)} broadcast(bf16[128,2048]{1,0:T(8,128)(2,1)} %param.10), dimensions={0,2} | broadcast | bytes 1572864 | tf_op jit(solution)/shard_map/broadcast_in_dim | solution.py:48
  12.8 2.2 reshape.94
  15.0 2.8 %convolution_convert_fusion.4 = bf16[320,2048]{1,0:T(8,128)(2,1)} fusion(bf16[256,2048]{1,0:T(8,128)(2,1)} %reshape.94, s32[256]{0:T(256)S(1)} %get-tuple-element.14), kind=kOutput, calls=%fused_computation.24 | convolution fusion | flops 336281600 | bytes 2360320 | tf_op jit(solution)/shard_map/dot_general | solution.py:49
  17.8 5.2 %all-to-all-start = ((bf16[4,80,2048]{2,1,0:T(8,128)(2,1)}), bf16[4,80,2048]{2,1,0:T(8,128)(2,1)}, u32[]{:S(2)}, u32[]{:S(2)}) async-start(bf16[4,80,2048]{2,1,0:T(8,128)(2,1)} %bitcast.65), calls=%async_computation | async-start | bytes 2621440 | tf_op jit(solution)/shard_map/all_to_all | solution.py:52
  23.3 3.5 %mul.79 = f32[128,2,2048]{2,1,0:T(2,128)} broadcast(bf16[128,2048]{1,0:T(8,128)(2,1)} %param.11), dimensions={0,2} | broadcast | bytes 2621440 | tf_op jit(solution)/shard_map/mul | solution.py:80
  26.7 3.6 %mul.80 = f32[256,2048]{1,0:T(8,128)} reshape(f32[128,2,2048]{2,1,0:T(2,128)} %mul.79) | data formatting | bytes 4194304 | tf_op jit(solution)/shard_map/mul | solution.py:80
  30.4 3.2 %convolution_convert_fusion.3 = bf16[320,2048]{1,0:T(8,128)(2,1)} fusion(f32[256,2048]{1,0:T(8,128)} %mul.80, f32[256]{0:T(256)S(1)} %mul.77, s32[256]{0:T(256)S(1)} %get-tuple-element.14), kind=kOutput, calls=%fused_computation.23 | convolution fusion | flops 337330176 | bytes 3409920 | tf_op jit(solution)/shard_map/dot_general | solution.py:84
  33.6 6.5 %all-to-all-done = bf16[4,80,2048]{2,1,0:T(8,128)(2,1)} async-done(((bf16[4,80,2048]{2,1,0:T(8,128)(2,1)}), bf16[4,80,2048]{2,1,0:T(8,128)(2,1)}, u32[]{:S(2)}, u32[]{:S(2)}) %all-to-all-start) | async-done | bytes 1310752 | tf_op jit(solution)/shard_map/all_to_all | solution.py:52
  40.1 4.3 %all-to-all-start.2 = ((bf16[4,80,2048]{2,1,0:T(8,128)(2,1)}), bf16[4,80,2048]{2,1,0:T(8,128)(2,1)}, u32[]{:S(2)}, u32[]{:S(2)}) async-start(bf16[4,80,2048]{2,1,0:T(8,128)(2,1)} %bitcast.64), calls=%async_computation.2 | async-start | bytes 2621440 | tf_op jit(solution)/shard_map/all_to_all | solution.py:87
  44.5 4.4 %fusion.6 = f32[320,768]{1,0:T(8,128)} fusion(bf16[320,2048]{1,0:T(8,128)(2,1)} %bitcast.3, bf16[1,2048,768]{2,1,0:T(8,128)(2,1)} %param.16), kind=kOutput, calls=%fused_computation.11 | convolution fusion | flops 1006632960 | bytes 5439488 | tf_op jit(solution)/shard_map/dot_general | solution.py:60
  48.9 11.8 %all-to-all-done.2 = bf16[4,80,2048]{2,1,0:T(8,128)(2,1)} async-done(((bf16[4,80,2048]{2,1,0:T(8,128)(2,1)}), bf16[4,80,2048]{2,1,0:T(8,128)(2,1)}, u32[]{:S(2)}, u32[]{:S(2)}) %all-to-all-start.2) | async-done | bytes 1310752 | tf_op jit(solution)/shard_map/all_to_all | solution.py:87
  60.7 3.6 %fusion = f32[320,768]{1,0:T(8,128)S(1)} fusion(bf16[320,2048]{1,0:T(8,128)(2,1)} %bitcast.10, bf16[1,768,2048]{2,1,0:T(8,128)(2,1)} %param.17), kind=kOutput, calls=%fused_computation.5 | convolution fusion | flops 1006632960 | bytes 5439488 | tf_op jit(solution)/shard_map/dot_general | solution.py:22
  64.3 3.8 %multiply_convert_fusion.3 = (bf16[320,768]{1,0:T(8,128)(2,1)}, bf16[320,768]{1,0:T(8,128)(2,1)S(1)}, bf16[320,768]{1,0:T(8,128)(2,1)}) fusion(f32[320,768]{1,0:T(8,128)S(1)} %fusion, f32[320,768]{1,0:T(8,128)S(1)} %copy-done.3, bf16[320,2048]{1,0:T(8,128)(2,1)} %bitcast.3, bf16[1,2048,768]{2,1,0:T(8,128)(2,1)S(1)} %copy-done), kind=kOutput, calls=%fused_computation.32 | convolution fusion | flops 1010565120 | bytes 7897088 | tf_op jit(solution)/shard_map/dot_general | solution.py:59
  68.1 0.8 copy-done.5
  68.8 4.9 %convolution_convert_fusion = bf16[768,2048]{1,0:T(8,128)(2,1)} fusion(bf16[320,768]{1,0:T(8,128)(2,1)S(1)} %get-tuple-element.16, bf16[320,2048]{1,0:T(8,128)(2,1)} %bitcast.10), kind=kOutput, calls=%fused_computation.2 | convolution fusion | flops 1008205824 | bytes 4947968 | tf_op jit(solution)/shard_map/dot_general | solution.py:16
  73.8 4.9 %convolution_convert_fusion.2 = bf16[2048,768]{1,0:T(8,128)(2,1)} fusion(bf16[320,2048]{1,0:T(8,128)(2,1)} %bitcast.3, bf16[320,768]{1,0:T(8,128)(2,1)} %get-tuple-element.15), kind=kOutput, calls=%fused_computation.4 | convolution fusion | flops 1008205824 | bytes 4947968 | tf_op jit(solution)/shard_map/dot_general | solution.py:16
  78.9 5.2 %convolution_convert_fusion.1 = bf16[2048,768]{1,0:T(8,128)(2,1)} fusion(bf16[320,2048]{1,0:T(8,128)(2,1)} %bitcast.3, bf16[320,768]{1,0:T(8,128)(2,1)} %get-tuple-element.17), kind=kOutput, calls=%fused_computation.3 | convolution fusion | flops 1008205824 | bytes 4947968 | tf_op jit(solution)/shard_map/dot_general | solution.py:16
  84.1 4.3 %fusion.18 = bf16[320,2048]{1,0:T(8,128)(2,1)} fusion(bf16[320,768]{1,0:T(8,128)(2,1)} %copy-done.5, bf16[1,768,2048]{2,1,0:T(8,128)(2,1)} %param.17), kind=kOutput, calls=%fused_computation.22 | convolution fusion | flops 1007288320 | bytes 4947968 | tf_op jit(solution)/shard_map/dot_general | solution.py:63
  88.4 4.3 %all-to-all-start.1 = ((bf16[4,80,2048]{2,1,0:T(8,128)(2,1)}), bf16[4,80,2048]{2,1,0:T(8,128)(2,1)}, u32[]{:S(2)}, u32[]{:S(2)}) async-start(bf16[4,80,2048]{2,1,0:T(8,128)(2,1)} %bitcast.67), calls=%async_computation.1 | async-start | bytes 2621440 | tf_op jit(solution)/shard_map/all_to_all | solution.py:64
  92.8 3.3 %fusion.4 = f32[320,2048]{1,0:T(8,128)S(1)} fusion(bf16[320,768]{1,0:T(8,128)(2,1)} %get-tuple-element.17, bf16[1,2048,768]{2,1,0:T(8,128)(2,1)} %param.16), kind=kOutput, calls=%fused_computation.9 | convolution fusion | flops 1006632960 | bytes 6258688 | tf_op jit(solution)/shard_map/dot_general | solution.py:22
  96.1 2.3 fusion.15
  98.4 10.1 %all-to-all-done.1 = bf16[4,80,2048]{2,1,0:T(8,128)(2,1)} async-done(((bf16[4,80,2048]{2,1,0:T(8,128)(2,1)}), bf16[4,80,2048]{2,1,0:T(8,128)(2,1)}, u32[]{:S(2)}, u32[]{:S(2)}) %all-to-all-start.1) | async-done | bytes 1310752 | tf_op jit(solution)/shard_map/all_to_all | solution.py:64
  108.5 4.3 %all-to-all-start.3 = ((bf16[4,80,2048]{2,1,0:T(8,128)(2,1)}), bf16[4,80,2048]{2,1,0:T(8,128)(2,1)}, u32[]{:S(2)}, u32[]{:S(2)}) async-start(bf16[4,80,2048]{2,1,0:T(8,128)(2,1)} %bitcast.66), calls=%async_computation.3 | async-start | bytes 2621440 | tf_op jit(solution)/shard_map/all_to_all | solution.py:102
  112.9 1.6 reduce-scatter.8.cloned.1.call-done
  114.5 2.5 select_convert_fusion
  117.1 11.8 %all-to-all-done.3 = bf16[4,80,2048]{2,1,0:T(8,128)(2,1)} async-done(((bf16[4,80,2048]{2,1,0:T(8,128)(2,1)}), bf16[4,80,2048]{2,1,0:T(8,128)(2,1)}, u32[]{:S(2)}, u32[]{:S(2)}) %all-to-all-start.3) | async-done | bytes 1310752 | tf_op jit(solution)/shard_map/all_to_all | solution.py:102
  128.8 4.3 %all-to-all-start.6 = ((bf16[4,768,256]{2,1,0:T(8,128)(2,1)}), bf16[4,768,256]{2,1,0:T(8,128)(2,1)}, u32[]{:S(2)}, u32[]{:S(2)}) async-start(bf16[4,768,256]{2,1,0:T(8,128)(2,1)} %select_convert_fusion), calls=%async_computation.9 | async-start | bytes 3145728 | tf_op jit(solution)/shard_map/all_to_all | solution.py:138
  133.2 23.1 %reduce-scatter.4.cloned.1.call-done = bf16[256,768]{1,0:T(8,128)(2,1)} async-done(((bf16[2048,768]{1,0:T(8,128)(2,1)}), bf16[256,768]{1,0:T(8,128)(2,1)}) %reduce-scatter.4.cloned.1.call-update) | async-done | bytes 393232 | tf_op jit(solution)/shard_map/reduce_scatter | solution.py:119
  156.3 41.8 %reduce-scatter.6.cloned.1.call-done = bf16[256,768]{1,0:T(8,128)(2,1)} async-done(((bf16[2048,768]{1,0:T(8,128)(2,1)}), bf16[256,768]{1,0:T(8,128)(2,1)}) %reduce-scatter.6.cloned.1.call-update) | async-done | bytes 393232 | tf_op jit(solution)/shard_map/reduce_scatter | solution.py:122
  198.0 3.4 %select_convert_fusion.1 = (bf16[4,256,768]{2,1,0:T(8,128)(2,1)}, bf16[4,256,768]{2,1,0:T(8,128)(2,1)}) fusion(bf16[256,768]{1,0:T(8,128)(2,1)} %reduce-scatter.6.cloned.1.call-done, pred[4]{0:T(512)(128)(4,1)S(1)} %broadcast_compare_fusion, bf16[256,768]{1,0:T(8,128)(2,1)} %reduce-scatter.4.cloned.1.call-done), kind=kLoop, calls=%fused_computation.18 | loop fusion | flops 1572864 | bytes 3932164 | tf_op jit(solution)/shard_map/convert_element_type | solution.py:10
  201.4 4.4 %all-to-all-start.5 = ((bf16[4,256,768]{2,1,0:T(8,128)(2,1)}), bf16[4,256,768]{2,1,0:T(8,128)(2,1)}, u32[]{:S(2)}, u32[]{:S(2)}) async-start(bf16[4,256,768]{2,1,0:T(8,128)(2,1)} %get-tuple-element.18), calls=%async_computation.7 | async-start | bytes 3145728 | tf_op jit(solution)/shard_map/all_to_all | solution.py:138
  205.8 0.6 dynamic_slice.15
  208.4 4.9 %gather_fusion = bf16[256,2048]{1,0:T(8,128)(2,1)} fusion(bf16[320,2048]{1,0:T(8,128)(2,1)} %bitcast.8, s32[1024]{0:T(1024)S(1)} %pad_clamp_fusion), kind=kCustom, calls=%fused_computation.clone | custom fusion | bytes 2098176 | tf_op jit(solution)/shard_map/jit(_take)/gather | solution.py:72
  213.2 9.6 %all-to-all-done.5 = bf16[4,256,768]{2,1,0:T(8,128)(2,1)} async-done(((bf16[4,256,768]{2,1,0:T(8,128)(2,1)}), bf16[4,256,768]{2,1,0:T(8,128)(2,1)}, u32[]{:S(2)}, u32[]{:S(2)}) %all-to-all-start.5) | async-done | bytes 1572896 | tf_op jit(solution)/shard_map/all_to_all | solution.py:138
  222.8 4.6 %all-to-all-start.4 = ((bf16[4,256,768]{2,1,0:T(8,128)(2,1)}), bf16[4,256,768]{2,1,0:T(8,128)(2,1)}, u32[]{:S(2)}, u32[]{:S(2)}) async-start(bf16[4,256,768]{2,1,0:T(8,128)(2,1)} %get-tuple-element.19), calls=%async_computation.5 | async-start | bytes 3145728 | tf_op jit(solution)/shard_map/all_to_all | solution.py:138
  227.4 2.3 multiply_reduce_fusion
  229.8 0.6 copy.23
  230.5 4.8 %gather_fusion.1 = bf16[256,2048]{1,0:T(8,128)(2,1)} fusion(bf16[320,2048]{1,0:T(8,128)(2,1)} %bitcast.12, s32[1024]{0:T(1024)S(1)} %pad_clamp_fusion), kind=kCustom, calls=%fused_computation.1.clone | custom fusion | bytes 2098176 | tf_op jit(solution)/shard_map/jit(_take)/gather | solution.py:110
  235.3 3.5 %broadcast_select_fusion = (bf16[256,2048]{1,0:T(8,128)(2,1)}, f32[256,2048]{1,0:T(8,128)}) fusion(bf16[256,2048]{1,0:T(8,128)(2,1)} %gather_fusion.1, pred[256]{0:T(512)(128)(4,1)S(1)} %get-tuple-element.13, bf16[256,2048]{1,0:T(8,128)(2,1)} %gather_fusion), kind=kLoop, calls=%fused_computation.30 | loop fusion | flops 1572864 | bytes 5243136 | tf_op jit(solution)/shard_map/jit(_take)/select_n | solution.py:110
  238.8 2.5 reshape.104
  241.3 3.5 %reshape.99 = f32[128,2,2048]{2,1,0:T(2,128)} reshape(f32[256,2048]{1,0:T(8,128)} %get-tuple-element.21) | data formatting | bytes 4194304 | tf_op jit(solution)/shard_map/reshape | solution.py:74
  244.8 4.6 %reduce.1 = bf16[128,2048]{1,0:T(8,128)(2,1)} reduce(bf16[128,2,2048]{2,1,0:T(2,128)(2,1)} %reshape.104, bf16[]{:T(256)} %constant.46), dimensions={1}, to_apply=%region_4.6.clone | reduce | flops 262144 | bytes 1572866 | tf_op jit(solution)/shard_map/reduce_sum | solution.py:114
  249.3 5.6 %multiply_reduce_fusion.1 = bf16[128,2048]{1,0:T(8,128)(2,1)} fusion(f32[128,2,2048]{2,1,0:T(2,128)} %reshape.99, f32[128,2]{1,0:T(8,128)S(1)} %copy.17), kind=kLoop, calls=%fused_computation.27 | loop fusion | flops 786432 | bytes 2622464 | tf_op jit(solution)/shard_map/reduce_sum | solution.py:76
  254.9 1.9 dynamic-slice_convert_fusion
  256.8 1.9 dynamic-slice_convert_fusion.1
  258.8 1.9 dynamic-slice_convert_fusion.2
  (36 shorter events, 1.5 us)
Async XLA Ops:
  7.2 57.1 %copy-start = (bf16[1,2048,768]{2,1,0:T(8,128)(2,1)S(1)}, bf16[1,2048,768]{2,1,0:T(8,128)(2,1)}, u32[]{:S(2)}) copy-start(bf16[1,2048,768]{2,1,0:T(8,128)(2,1)} %param.15) | copy-start | bytes 9437188
  15.0 8.0 %copy-start.1 = (f32[128,2]{0,1:T(2,128)S(1)}, f32[128,2]{0,1:T(2,128)}, u32[]{:S(2)}) copy-start(f32[128,2]{0,1:T(2,128)} %param.13) | copy-start | bytes 3076
  17.8 22.3 %all-to-all-start = ((bf16[4,80,2048]{2,1,0:T(8,128)(2,1)}), bf16[4,80,2048]{2,1,0:T(8,128)(2,1)}, u32[]{:S(2)}, u32[]{:S(2)}) async-start(bf16[4,80,2048]{2,1,0:T(8,128)(2,1)} %bitcast.65), calls=%async_computation | async-start | bytes 2621440 | tf_op jit(solution)/shard_map/all_to_all | solution.py:52
  40.1 20.5 %all-to-all-start.2 = ((bf16[4,80,2048]{2,1,0:T(8,128)(2,1)}), bf16[4,80,2048]{2,1,0:T(8,128)(2,1)}, u32[]{:S(2)}, u32[]{:S(2)}) async-start(bf16[4,80,2048]{2,1,0:T(8,128)(2,1)} %bitcast.64), calls=%async_computation.2 | async-start | bytes 2621440 | tf_op jit(solution)/shard_map/all_to_all | solution.py:87
  44.5 70.1 %reduce-scatter.8.cloned.1.call-start = ((), (), s32[]{:S(2)}) async-start(), calls=%async_computation.12 | async-start | bytes 3538944 | tf_op jit(solution)/shard_map/reduce_scatter | solution.py:125
  60.7 3.6 %copy-start.3 = (f32[320,768]{1,0:T(8,128)S(1)}, f32[320,768]{1,0:T(8,128)}, u32[]{:S(2)}) copy-start(f32[320,768]{1,0:T(8,128)} %fusion.6) | copy-start | bytes 2949124
  68.1 0.8 copy-start.5
  73.7 82.5 %reduce-scatter.4.cloned.1.call-start = ((), (), s32[]{:S(2)}) async-start(), calls=%async_computation.10 | async-start | bytes 3538944 | tf_op jit(solution)/shard_map/reduce_scatter | solution.py:119
  78.7 119.3 %reduce-scatter.6.cloned.1.call-start = ((), (), s32[]{:S(2)}) async-start(), calls=%async_computation.11 | async-start | bytes 3538944 | tf_op jit(solution)/shard_map/reduce_scatter | solution.py:122
  88.4 20.1 %all-to-all-start.1 = ((bf16[4,80,2048]{2,1,0:T(8,128)(2,1)}), bf16[4,80,2048]{2,1,0:T(8,128)(2,1)}, u32[]{:S(2)}, u32[]{:S(2)}) async-start(bf16[4,80,2048]{2,1,0:T(8,128)(2,1)} %bitcast.67), calls=%async_computation.1 | async-start | bytes 2621440 | tf_op jit(solution)/shard_map/all_to_all | solution.py:64
  92.8 3.4 %copy-start.4 = (bf16[320,768]{1,0:T(8,128)(2,1)S(1)}, bf16[320,768]{1,0:T(8,128)(2,1)}, u32[]{:S(2)}) copy-start(bf16[320,768]{1,0:T(8,128)(2,1)} %get-tuple-element.15) | copy-start | bytes 1474564
  98.4 14.5 %copy-start.2 = (s32[4]{0:T(128)S(1)}, s32[4]{0:T(128)}, u32[]{:S(2)}) copy-start(s32[4]{0:T(128)} %param.14) | copy-start | bytes 52
  108.5 20.3 %all-to-all-start.3 = ((bf16[4,80,2048]{2,1,0:T(8,128)(2,1)}), bf16[4,80,2048]{2,1,0:T(8,128)(2,1)}, u32[]{:S(2)}, u32[]{:S(2)}) async-start(bf16[4,80,2048]{2,1,0:T(8,128)(2,1)} %bitcast.66), calls=%async_computation.3 | async-start | bytes 2621440 | tf_op jit(solution)/shard_map/all_to_all | solution.py:102
  128.8 72.6 %all-to-all-start.6 = ((bf16[4,768,256]{2,1,0:T(8,128)(2,1)}), bf16[4,768,256]{2,1,0:T(8,128)(2,1)}, u32[]{:S(2)}, u32[]{:S(2)}) async-start(bf16[4,768,256]{2,1,0:T(8,128)(2,1)} %select_convert_fusion), calls=%async_computation.9 | async-start | bytes 3145728 | tf_op jit(solution)/shard_map/all_to_all | solution.py:138
  201.4 21.4 %all-to-all-start.5 = ((bf16[4,256,768]{2,1,0:T(8,128)(2,1)}), bf16[4,256,768]{2,1,0:T(8,128)(2,1)}, u32[]{:S(2)}, u32[]{:S(2)}) async-start(bf16[4,256,768]{2,1,0:T(8,128)(2,1)} %get-tuple-element.18), calls=%async_computation.7 | async-start | bytes 3145728 | tf_op jit(solution)/shard_map/all_to_all | solution.py:138
  222.8 36.0 %all-to-all-start.4 = ((bf16[4,256,768]{2,1,0:T(8,128)(2,1)}), bf16[4,256,768]{2,1,0:T(8,128)(2,1)}, u32[]{:S(2)}, u32[]{:S(2)}) async-start(bf16[4,256,768]{2,1,0:T(8,128)(2,1)} %get-tuple-element.19), calls=%async_computation.5 | async-start | bytes 3145728 | tf_op jit(solution)/shard_map/all_to_all | solution.py:138
Sparse Core Ops, SparseCore 0:
  73.8 40.6 reduce-scatter.7
  116.8 39.4 reduce-scatter.3
  158.6 39.4 reduce-scatter.5
where the time goes:
time: 269 us; the launch traced here: 267 us
  waiting for transfers between devices  116 us (43%)
  matrix products  42.7 us (16%)
  starting transfers between devices  31.7 us (12%)
  local copies, waits for them, and re-layouts  31.6 us (12%)
  other arithmetic  29 us (11%)
  between operations  15.9 us (6%)
    reduce_scatter x1, waiting for transfers between devices, shards(): lax.psum_scatter(partial_up.astype(jnp.bfloat16), 'dp', scatter_dimension...  41.8 us
    reduce_scatter x1, waiting for transfers between devices, shards(): lax.psum_scatter(partial_gate.astype(jnp.bfloat16), 'dp', scatter_dimensi...  23.1 us
    dot_general x3, matrix products, contract_rows(): lax.dot_general(left_mat, right_mat, (((0,), (0,)), ((), ())), preferred_...  14.9 us
    all_to_all x3, starting transfers between devices, shards(): lax.all_to_all(as_sent(outgoing), 'expert', split_axis=0, concat_axis=0,...  13.3 us
    all_to_all x1, waiting for transfers between devices, shards(): lax.all_to_all(row_grad.reshape(groups, capacity, model_width), 'expert',...  11.8 us
    all_to_all x1, waiting for transfers between devices, shards(): lax.all_to_all(outgoing_grads.reshape(groups, capacity, model_width), 'ex...  11.8 us
    all_to_all x1, waiting for transfers between devices, shards(): lax.all_to_all(expert_out.reshape(groups, capacity, model_width), 'expert...  10.1 us
    all_to_all x3, waiting for transfers between devices, shards(): lax.all_to_all(as_sent(outgoing), 'expert', split_axis=0, concat_axis=0,...  9.62 us
  transfers between devices with their start and end apart: 10, of which 8 were waited for; matrix products, arithmetic and copies ran while one was open for 29% of the time, Pallas kernels for 0%

commit v1 on v0

v1 whole, which is shorter than its diff:
```python
import functools

import jax
import jax.numpy as jnp
from jax import lax
from jax.experimental import pallas as pl
from jax.experimental.pallas import tpu as pltpu
from jax.sharding import PartitionSpec as P

VMEM_BYTES = 48 * 1024 * 1024
F32 = jnp.float32
BF16 = jnp.bfloat16


def dot_nn(a, b):
    return lax.dot_general(a, b, (((1,), (0,)), ((), ())), preferred_element_type=F32)


def dot_nt(a, b):
    return lax.dot_general(a, b, (((1,), (1,)), ((), ())), preferred_element_type=F32)


def dot_tn(a, b):
    return lax.dot_general(a, b, (((0,), (0,)), ((), ())), preferred_element_type=F32)


def tile_of(size, want):
    while size % want:
        want //= 2
    return want


def params(**more):
    return pltpu.CompilerParams(vmem_limit_bytes=VMEM_BYTES, **more)


def whole(shape):
    return pl.BlockSpec(shape, lambda *_: (0,) * len(shape))


def cost(flops, nbytes):
    return pl.CostEstimate(flops=int(flops), bytes_accessed=int(nbytes), transcendentals=0)


def slots_of(ids, cap, me):
    rows, top = ids.shape
    block = jnp.bitwise_xor(ids, me)
    lane = lax.broadcasted_iota(jnp.int32, (rows, 128), 1)
    named = [(block[:, k : k + 1] == lane).astype(F32) for k in range(top)]
    strict = lax.broadcasted_iota(jnp.int32, (rows, rows), 0) > lax.broadcasted_iota(
        jnp.int32, (rows, rows), 1
    )
    before = dot_nn(strict.astype(BF16), sum(named).astype(BF16))
    slots = []
    for k in range(top):
        pos = jnp.sum(before * named[k], axis=1, keepdims=True).astype(jnp.int32)
        slots.append(block[:, k : k + 1] * cap + pos)
        before = before + named[k]
    return slots


def places_of(slots, total):
    rows = slots[0].shape[0]
    lane = lax.broadcasted_iota(jnp.int32, (rows, total), 1)
    return [(slot == lane).astype(BF16) for slot in slots]


def place_tokens(cap, me_ref, ids_ref, tok_ref, *outs):
    picks = places_of(slots_of(ids_ref[...], cap, me_ref[0]), cap * len(outs))
    rows = dot_tn(sum(picks), tok_ref[...])
    for b, out in enumerate(outs):
        out[...] = rows[b * cap : (b + 1) * cap].astype(BF16)


def place_grads(cap, me_ref, ids_ref, gates_ref, cot_ref, *outs):
    picks = places_of(slots_of(ids_ref[...], cap, me_ref[0]), cap * len(outs))
    cot = cot_ref[...].astype(F32)
    gates = gates_ref[...]
    rows = sum(
        dot_tn(pick, (gates[:, k : k + 1] * cot).astype(BF16)) for k, pick in enumerate(picks)
    )
    for b, out in enumerate(outs):
        out[...] = rows[b * cap : (b + 1) * cap].astype(BF16)


def forward(cap, groups, *refs):
    blocks, (gate_ref, up_ref), (x_ref, pre_ref, act_ref) = refs[:groups], refs[groups:-3], refs[-3:]

    @pl.when(pl.program_id(0) == 0)
    def _():
        x_ref[...] = jnp.concatenate([block[...] for block in blocks], axis=0)

    x = x_ref[...]
    gate_pre = dot_nn(x, gate_ref[0])
    up_pre = dot_nn(x, up_ref[0])
    pre_ref[0] = gate_pre
    pre_ref[1] = up_pre
    act_ref[...] = (gate_pre * jax.nn.sigmoid(gate_pre) * up_pre).astype(BF16)


def backward(cap, groups, *refs):
    blocks, (down_ref, pre_ref), (c_ref, grad_ref) = refs[:groups], refs[groups:-2], refs[-2:]

    @pl.when(pl.program_id(0) == 0)
    def _():
        c_ref[...] = jnp.concatenate([block[...] for block in blocks], axis=0)

    hidden_grad = dot_nt(c_ref[...], down_ref[0])
    gate_pre, up_pre = pre_ref[0], pre_ref[1]
    s = jax.nn.sigmoid(gate_pre)
    grad_ref[0] = (hidden_grad * up_pre * s * (1.0 + gate_pre * (1.0 - s))).astype(BF16)
    grad_ref[1] = (hidden_grad * gate_pre * s).astype(BF16)


def expert_rows(cap, act_ref, down_ref, *outs):
    rows = dot_nn(act_ref[...], down_ref[0])
    for b, out in enumerate(outs):
        out[...] = rows[b * cap : (b + 1) * cap].astype(BF16)


def input_rows(cap, grad_ref, gate_ref, up_ref, *outs):
    rows = dot_nt(grad_ref[0], gate_ref[0]) + dot_nt(grad_ref[1], up_ref[0])
    for b, out in enumerate(outs):
        out[...] = rows[b * cap : (b + 1) * cap].astype(BF16)


def both(own_ref, other_ref, *at):
    if at:
        return jnp.concatenate([own_ref[at[0]], other_ref[at[0]]], axis=0)
    return jnp.concatenate([own_ref[...], other_ref[...]], axis=0)


def down_share(core_ref, act_own, act_other, c_own, c_other, out_ref, turned):
    @pl.when(pl.program_id(0) == 0)
    def _():
        turned[...] = both(act_own, act_other).T

    out_ref[0] = dot_nn(turned[...], both(c_own, c_other)).astype(BF16)


def gate_up_share(core_ref, x_own, x_other, g_own, g_other, gate_ref, up_ref):
    turned = both(x_own, x_other).T
    gate_ref[0] = dot_nn(turned, both(g_own, g_other, 0)).astype(BF16)
    up_ref[0] = dot_nn(turned, both(g_own, g_other, 1)).astype(BF16)


def combine(cap, groups, me_ref, ids_ref, gates_ref, cot_ref, *refs):
    outs, grads = refs[:groups], refs[groups : 2 * groups]
    mixed_ref, token_ref, dots_ref = refs[2 * groups :]
    picks = places_of(slots_of(ids_ref[...], cap, me_ref[0]), cap * groups)
    gates = gates_ref[...]
    width = mixed_ref.shape[1]
    tile = tile_of(width, 512)
    dots = [0.0] * len(picks)
    for start in range(0, width, tile):
        cols = slice(start, start + tile)
        rows = jnp.concatenate([ref[:, cols] for ref in outs], axis=0)
        cot = cot_ref[:, cols].astype(F32)
        mixed = 0.0
        for k, pick in enumerate(picks):
            picked = dot_nn(pick, rows)
            mixed = mixed + gates[:, k : k + 1] * picked
            dots[k] = dots[k] + jnp.sum(cot * picked, axis=1, keepdims=True)
        mixed_ref[:, cols] = mixed.astype(BF16)
        rows = jnp.concatenate([ref[:, cols] for ref in grads], axis=0)
        token_ref[:, cols] = dot_nn(sum(picks), rows).astype(BF16)
    dots_ref[...] = jnp.concatenate(dots, axis=1)


def share_kernels(core, chips, cols, act, act_other, c_rows, c_other, x_rows, x_other, grads, grads_other):
    total, width = x_rows.shape
    ff = act.shape[1]
    core_arr = core.astype(jnp.int32).reshape(1)

    def mine(z, core_ref):
        return (0, 2 * z + core_ref[0])

    down_q = pl.pallas_call(
        down_share,
        out_shape=jax.ShapeDtypeStruct((chips, ff, cols), BF16),
        grid_spec=pltpu.PrefetchScalarGridSpec(
            num_scalar_prefetch=1,
            grid=(chips,),
            in_specs=[whole((total, ff))] * 2 + [pl.BlockSpec((total, cols), mine)] * 2,
            out_specs=pl.BlockSpec((1, ff, cols), lambda z, _: (z, 0, 0)),
            scratch_shapes=[pltpu.VMEM((ff, 2 * total), BF16)],
        ),
        compiler_params=params(),
        cost_estimate=cost(2 * total * width * ff, 7e6),
        name="down_share",
    )(core_arr, act, act_other, c_rows, c_other)
    gate_q, up_q = pl.pallas_call(
        gate_up_share,
        out_shape=[jax.ShapeDtypeStruct((chips, cols, ff), BF16)] * 2,
        grid_spec=pltpu.PrefetchScalarGridSpec(
            num_scalar_prefetch=1,
            grid=(chips,),
            in_specs=[pl.BlockSpec((total, cols), mine)] * 2 + [whole((2, total, ff))] * 2,
            out_specs=[pl.BlockSpec((1, cols, ff), lambda z, _: (z, 0, 0))] * 2,
        ),
        compiler_params=params(),
        cost_estimate=cost(4 * total * width * ff, 9e6),
        name="gate_up_share",
    )(core_arr, x_rows, x_other, grads, grads_other)
    return down_q, gate_q, up_q


def share_dots(core, chips, cols, act, act_other, c_rows, c_other, x_rows, x_other, grads, grads_other):
    def mine(own, other):
        rows = jnp.concatenate([own, other], axis=0).reshape(-1, chips, 2, cols)
        return lax.dynamic_index_in_dim(rows, core, 2, keepdims=False)

    def dot(left, right, spec):
        return jnp.einsum(spec, left, right, preferred_element_type=F32).astype(BF16)

    acts = jnp.concatenate([act, act_other], axis=0)
    both_grads = jnp.concatenate([grads, grads_other], axis=1)
    x = mine(x_rows, x_other)
    return (
        dot(acts, mine(c_rows, c_other), "rf,rzc->zfc"),
        dot(x, both_grads[0], "rzc,rf->zcf"),
        dot(x, both_grads[1], "rzc,rf->zcf"),
    )


def line_sums(shares, chips, chip):
    up = [[(2 * i + c, 2 * i + 2 + c) for i in range(min(s, chips - 1)) for c in (0, 1)] for s in range(1, chips)]
    down = [[(2 * (chips - 1) - a + 2 * (a % 2), 2 * (chips - 1) - b + 2 * (b % 2)) for a, b in step] for step in up]

    def share_at(share, index):
        return lax.dynamic_index_in_dim(share, jnp.clip(index, 0, chips - 1), 0, keepdims=False)

    def add(part, own):
        return (part.astype(F32) + own.astype(F32)).astype(BF16)

    state = [[None, None] for _ in shares]
    for s in range(1, chips):
        for n, share in enumerate(shares):
            for side, index in ((0, chips - s + chip), (1, chip - chips + s)):
                message = share_at(share, index)
                if state[n][side] is not None:
                    message = add(state[n][side], message)
                state[n][side] = lax.ppermute(message, "dp", (up, down)[side][s - 1])
    totals = []
    for n, share in enumerate(shares):
        own = share_at(share, chip).astype(F32)
        for side in state[n]:
            if side is not None:
                own = own + side.astype(F32)
        totals.append(own.astype(BF16))
    return totals


def relocated(total, partner, me, groups):
    if groups == 4:
        turn = jnp.bitwise_xor(lax.dynamic_index_in_dim(partner, me, 0, keepdims=False), me)
        first = lax.ppermute(total, "expert", [(i, i ^ 1) for i in range(groups)])
        second = lax.ppermute(
            jnp.where(turn == 3, first, total), "expert", [(i, i ^ 2) for i in range(groups)]
        )
        return jnp.where(turn == 1, first, second).astype(F32)[None]
    is_mate = (partner == me)[:, None, None]
    parts = jnp.where(is_mate, total[None], jnp.zeros_like(total)[None])
    parts = lax.all_to_all(parts, "expert", split_axis=0, concat_axis=0, tiled=True)
    mate = lax.dynamic_index_in_dim(partner, me, 0, keepdims=False)
    return lax.dynamic_index_in_dim(parts, mate, 0, keepdims=True).astype(F32)


def shards(tokens, cotangent, expert_ids, gate_weights, partner, w_gate, w_up, w_down):
    groups = lax.axis_size("expert")
    replicas = lax.axis_size("dp")
    me = lax.axis_index("expert")
    replica = lax.axis_index("dp")
    chips, chip, core = replicas // 2, replica // 2, replica % 2
    count, width = tokens.shape
    top = expert_ids.shape[1]
    ff = w_gate.shape[2]
    cap = min(count, 5 * count * top // (4 * groups))
    total = groups * cap
    cols = width // replicas
    me_arr = me.astype(jnp.int32).reshape(1)
    smem = pl.BlockSpec(memory_space=pltpu.SMEM)
    vmem = pl.BlockSpec(memory_space=pltpu.VMEM)
    block_shape = jax.ShapeDtypeStruct((cap, width), BF16)

    def exchange(blocks):
        return [blocks[0]] + [
            lax.ppermute(blocks[b], "expert", [(i, i ^ b) for i in range(groups)])
            for b in range(1, groups)
        ]

    def swap(part):
        return lax.ppermute(part, "dp", [(i, i ^ 1) for i in range(replicas)])

    x_blocks = pl.pallas_call(
        functools.partial(place_tokens, cap),
        out_shape=[block_shape] * groups,
        in_specs=[smem, vmem, vmem],
        out_specs=[vmem] * groups,
        compiler_params=params(),
        name="place_tokens",
    )(me_arr, expert_ids, tokens)
    c_blocks = pl.pallas_call(
        functools.partial(place_grads, cap),
        out_shape=[block_shape] * groups,
        in_specs=[smem, vmem, vmem, vmem],
        out_specs=[vmem] * groups,
        compiler_params=params(),
        name="place_grads",
    )(me_arr, expert_ids, gate_weights, cotangent)
    x_blocks = exchange(x_blocks)
    *c_blocks, x_blocks = lax.optimization_barrier((*c_blocks, x_blocks))
    c_blocks = exchange(c_blocks)

    tile = tile_of(ff, 256)
    x_rows, pre, act = pl.pallas_call(
        functools.partial(forward, cap, groups),
        out_shape=[
            jax.ShapeDtypeStruct((total, width), BF16),
            jax.ShapeDtypeStruct((2, total, ff), F32),
            jax.ShapeDtypeStruct((total, ff), BF16),
        ],
        grid=(ff // tile,),
        in_specs=[whole((cap, width))] * groups
        + [pl.BlockSpec((1, width, tile), lambda j: (0, 0, j))] * 2,
        out_specs=[
            whole((total, width)),
            pl.BlockSpec((2, total, tile), lambda j: (0, 0, j)),
            pl.BlockSpec((total, tile), lambda j: (0, j)),
        ],
        compiler_params=params(),
        cost_estimate=cost(4 * total * width * ff, 10e6),
        name="forward",
    )(*x_blocks, w_gate, w_up)

    c_rows, grads = pl.pallas_call(
        functools.partial(backward, cap, groups),
        out_shape=[
            jax.ShapeDtypeStruct((total, width), BF16),
            jax.ShapeDtypeStruct((2, total, ff), BF16),
        ],
        grid=(ff // tile,),
        in_specs=[whole((cap, width))] * groups
        + [
            pl.BlockSpec((1, tile, width), lambda j: (0, j, 0)),
            pl.BlockSpec((2, total, tile), lambda j: (0, 0, j)),
        ],
        out_specs=[
            whole((total, width)),
            pl.BlockSpec((2, total, tile), lambda j: (0, 0, j)),
        ],
        compiler_params=params(),
        cost_estimate=cost(2 * total * width * ff, 10e6),
        name="backward",
    )(*c_blocks, w_down, pre)

    act_other, c_other, x_other, grads_other = swap(act), swap(c_rows), swap(x_rows), swap(grads)

    if cols % 128 == 0:
        down_q, gate_q, up_q = share_kernels(
            core, chips, cols, act, act_other, c_rows, c_other, x_rows, x_other, grads, grads_other
        )
    else:
        down_q, gate_q, up_q = share_dots(
            core, chips, cols, act, act_other, c_rows, c_other, x_rows, x_other, grads, grads_other
        )

    wide = tile_of(width, 512)
    out_blocks = pl.pallas_call(
        functools.partial(expert_rows, cap),
        out_shape=[block_shape] * groups,
        grid=(width // wide,),
        in_specs=[whole((total, ff)), pl.BlockSpec((1, ff, wide), lambda j: (0, 0, j))],
        out_specs=[pl.BlockSpec((cap, wide), lambda j: (0, j))] * groups,
        compiler_params=params(),
        cost_estimate=cost(2 * total * width * ff, 5e6),
        name="expert_rows",
    )(act, w_down)
    grad_blocks = pl.pallas_call(
        functools.partial(input_rows, cap),
        out_shape=[block_shape] * groups,
        grid=(width // wide,),
        in_specs=[whole((2, total, ff))] + [pl.BlockSpec((1, wide, ff), lambda j: (0, j, 0))] * 2,
        out_specs=[pl.BlockSpec((cap, wide), lambda j: (0, j))] * groups,
        compiler_params=params(),
        cost_estimate=cost(4 * total * width * ff, 9e6),
        name="input_rows",
    )(grads, w_gate, w_up)
    out_blocks = exchange(out_blocks)
    grad_blocks = exchange(grad_blocks)

    sums = line_sums([down_q, gate_q, up_q], chips, chip)
    slot_down, slot_gate, slot_up = [relocated(part, partner, me, groups) for part in sums]

    mixed_out, token_grad, gate_grad = pl.pallas_call(
        functools.partial(combine, cap, groups),
        out_shape=[
            jax.ShapeDtypeStruct((count, width), BF16),
            jax.ShapeDtypeStruct((count, width), BF16),
            jax.ShapeDtypeStruct((count, top), F32),
        ],
        in_specs=[smem] + [vmem] * (3 + 2 * groups),
        out_specs=[vmem] * 3,
        compiler_params=params(),
        cost_estimate=cost(6 * total * width * count, 6e6),
        name="combine",
    )(me_arr, expert_ids, gate_weights, cotangent, *out_blocks, *grad_blocks)
    return mixed_out, token_grad, gate_grad, slot_gate, slot_up, slot_down


def solution(mesh):
    rows = P(("dp", "expert"), None)
    in_specs = (
        rows,
        rows,
        rows,
        rows,
        P(),
        P("expert", None, None),
        P("expert", None, None),
        P("expert", None, None),
    )
    out_specs = (
        rows,
        rows,
        rows,
        P("expert", "dp", None),
        P("expert", "dp", None),
        P("expert", None, "dp"),
    )
    return jax.shard_map(shards, mesh=mesh, in_specs=in_specs, out_specs=out_specs, check_vma=False)
```

time: 269 us -> 194 us (0.72)
  matrix products: 42.7 us -> 0 us
  waiting for transfers between devices: 116 us -> 73.4 us
  starting transfers between devices: 31.7 us -> 64.1 us
  Pallas kernels: 0 us -> 31.4 us
  other arithmetic: 29 us -> 5.66 us
  local copies, waits for them, and re-layouts: 31.6 us -> 16.2 us
  between operations: 15.9 us -> 1.85 us
    ppermute x0 -> x40, waiting for transfers between devices: none -> 73.4 us  [the longest x12 28.4 us: exchange(): lax.ppermute(blocks[b], 'expert', [(i, i ^ b) for i in range(groups)])]
    reduce_scatter x3 -> x0, waiting for transfers between devices: 66.5 us -> none  [the longest x1 41.8 us: shards(): lax.psum_scatter(partial_up.astype(jnp.bfloat16), 'dp', scatter_dimension...]
    ppermute x0 -> x40, starting transfers between devices: none -> 64.1 us  [the longest x18 41.9 us: line_sums(): state[n][side] = lax.ppermute(message, 'dp', (up, down)[side][s - 1])]
    all_to_all x7 -> x0, waiting for transfers between devices: 49.8 us -> none  [the longest x1 11.8 us: shards(): lax.all_to_all(row_grad.reshape(groups, capacity, model_width), 'expert',...]
    dot_general x11 -> x0, matrix products: 42.7 us -> none  [the longest x3 14.9 us: contract_rows(): lax.dot_general(left_mat, right_mat, (((0,), (0,)), ((), ())), preferred_...]
    pallas_call x0 -> x9, Pallas kernels: none -> 31.4 us  [the longest x1 5.34 us: share_kernels(): pl.pallas_call(gate_up_share, out_shape=[jax.ShapeDtypeStruct((chips, col...]
    all_to_all x7 -> x0, starting transfers between devices: 31.4 us -> none  [the longest x3 13.3 us: shards(): lax.all_to_all(as_sent(outgoing), 'expert', split_axis=0, concat_axis=0,...]
    reduce_sum x4 -> x0, other arithmetic: 12.5 us -> none  [the longest x1 5.59 us: shards(): jnp.sum(gate_weights[:, :, None] * per_assign, axis=1).astype(jnp.bfloat16)]
  transfers between devices with their start and end apart: 10 -> 40, of which waited for: 8 -> 17; matrix products, arithmetic and copies ran while one was open for 29% -> 5% of each run, Pallas kernels for 0% -> 16%
where the time goes in v1:
time: 194 us; the launch traced here: 193 us
  waiting for transfers between devices  73.4 us (38%)
  starting transfers between devices  64.1 us (33%)
  Pallas kernels  31.4 us (16%)
  local copies, waits for them, and re-layouts  16.2 us (8%)
  other arithmetic  5.66 us (3%)
    ppermute x18, starting transfers between devices, line_sums(): state[n][side] = lax.ppermute(message, 'dp', (up, down)[side][s - 1])  41.9 us
    ppermute x12, waiting for transfers between devices, exchange(): lax.ppermute(blocks[b], 'expert', [(i, i ^ b) for i in range(groups)])  28.4 us
    ppermute x18, waiting for transfers between devices, line_sums(): state[n][side] = lax.ppermute(message, 'dp', (up, down)[side][s - 1])  23.7 us
    ppermute x12, starting transfers between devices, exchange(): lax.ppermute(blocks[b], 'expert', [(i, i ^ b) for i in range(groups)])  13.8 us
    unnamed x51, local copies, waits for them, and re-layouts  13.3 us
    ppermute x3, waiting for transfers between devices, relocated(): lax.ppermute(jnp.where(turn == 3, first, total), 'expert', [(i, i ^ 2) fo...  13.1 us
    ppermute x3, waiting for transfers between devices, relocated(): first = lax.ppermute(total, 'expert', [(i, i ^ 1) for i in range(groups)])  8.29 us
    pallas_call x1, Pallas kernels, share_kernels(): pl.pallas_call(gate_up_share, out_shape=[jax.ShapeDtypeStruct((chips, col...  5.34 us
  transfers between devices with their start and end apart: 40, of which 17 were waited for; matrix products, arithmetic and copies ran while one was open for 5% of the time, Pallas kernels for 16%

profile of v1, /device:TPU:0, one launch (start us, length us, event | category | flops | bytes accessed | tf_op | source)
XLA Modules:
  0.0 192.7 jit_solution(14551586681903988226)
XLA Ops:
  3.4 3.0 %collective-permute-start = (bf16[80,2048]{1,0:T(8,128)(2,1)S(1)}, bf16[80,2048]{1,0:T(8,128)(2,1)S(1)}, u32[]{:S(2)}, u32[]{:S(2)}) collective-permute-start(bf16[80,2048]{1,0:T(8,128)(2,1)S(1)} %get-tuple-element.45), channel_id=1, source_target_pairs={{0,1},{1,0},{2,3},{3,2},{4,5},{5,4},{6,7},{7,6},{8,9},{9,8},{10,11... | collective-permute-start | bytes 983048 | tf_op jit(solution)/shard_map/ppermute | solution.py:288
  6.4 1.5 collective-permute-start.1
  9.8 1.3 place_grads.1
  11.1 3.9 %collective-permute-done.refs_1_ = bf16[80,2048]{1,0:T(8,128)(2,1)S(1)} collective-permute-done((bf16[80,2048]{1,0:T(8,128)(2,1)S(1)}, bf16[80,2048]{1,0:T(8,128)(2,1)S(1)}, u32[]{:S(2)}, u32[]{:S(2)}) %collective-permute-start) | collective-permute-done | bytes 327712 | tf_op jit(solution)/shard_map/ppermute | solution.py:288
  15.0 7.6 %collective-permute-done.1.refs_2_ = bf16[80,2048]{1,0:T(8,128)(2,1)S(1)} collective-permute-done((bf16[80,2048]{1,0:T(8,128)(2,1)S(1)}, bf16[80,2048]{1,0:T(8,128)(2,1)S(1)}, u32[]{:S(2)}, u32[]{:S(2)}) %collective-permute-start.1) | collective-permute-done | bytes 327712 | tf_op jit(solution)/shard_map/ppermute | solution.py:288
  24.7 1.4 collective-permute-start.8
  26.1 5.0 %forward.1 = (bf16[320,2048]{1,0:T(8,128)(2,1)S(1)}, f32[2,320,768]{2,1,0:T(8,128)S(1)}, bf16[320,768]{1,0:T(8,128)(2,1)S(1)}) custom-call(bf16[80,2048]{1,0:T(8,128)(2,1)S(1)} %get-tuple-element.48.refs_0_, bf16[80,2048]{1,0:T(8,128)(2,1)S(1)} %collective-permute-done.refs_1_, bf16[80,2048]{1,0:T(8,128)(2,1)S(1)} %collective-permute-done.1.refs_2_, ...), custom_call_target="tpu_custom_call" | custom-call | flops 2013265920 | bytes 10000000 | tf_op jit(solution)/shard_map/forward/pallas_call | solution.py:316
  31.2 2.0 %collective-permute-done.6.refs_1_ = bf16[80,2048]{1,0:T(8,128)(2,1)S(1)} collective-permute-done((bf16[80,2048]{1,0:T(8,128)(2,1)S(1)}, bf16[80,2048]{1,0:T(8,128)(2,1)S(1)}, u32[]{:S(2)}, u32[]{:S(2)}) %collective-permute-start.6) | collective-permute-done | bytes 327712 | tf_op jit(solution)/shard_map/ppermute | solution.py:288
  33.3 5.9 %collective-permute-done.7.refs_2_ = bf16[80,2048]{1,0:T(8,128)(2,1)S(1)} collective-permute-done((bf16[80,2048]{1,0:T(8,128)(2,1)S(1)}, bf16[80,2048]{1,0:T(8,128)(2,1)S(1)}, u32[]{:S(2)}, u32[]{:S(2)}) %collective-permute-start.7) | collective-permute-done | bytes 327712 | tf_op jit(solution)/shard_map/ppermute | solution.py:288
  39.2 3.9 %backward.1 = (bf16[320,2048]{1,0:T(8,128)(2,1)S(1)}, bf16[2,320,768]{2,1,0:T(8,128)(2,1)S(1)}) custom-call(bf16[80,2048]{1,0:T(8,128)(2,1)S(1)} %get-tuple-element.57.refs_0_, bf16[80,2048]{1,0:T(8,128)(2,1)S(1)} %collective-permute-done.6.refs_1_, bf16[80,2048]{1,0:T(8,128)(2,1)S(1)} %collective-permute-done.7.refs_2_, ...), custom_call_target="tpu_custom_call" | custom-call | flops 1006632960 | bytes 10000000 | tf_op jit(solution)/shard_map/backward/pallas_call | solution.py:336
  43.7 2.1 %expert_rows.1 = (bf16[80,2048]{1,0:T(8,128)(2,1)S(1)}, bf16[80,2048]{1,0:T(8,128)(2,1)S(1)}, bf16[80,2048]{1,0:T(8,128)(2,1)S(1)}, bf16[80,2048]{1,0:T(8,128)(2,1)S(1)}) custom-call(bf16[320,768]{1,0:T(8,128)(2,1)S(1)} %get-tuple-element.52.act_ref.act_own, bf16[1,768,2048]{2,1,0:T(8,128)(2,1)S(1)} %copy-done), custom_call_target="tpu_custom_call" | custom-call | flops 1006632960 | bytes 5000000 | tf_op jit(solution)/shard_map/expert_rows/pallas_call | solution.py:369
  48.2 8.0 %collective-permute-done.3.refs_1_ = bf16[80,2048]{1,0:T(8,128)(2,1)S(1)} collective-permute-done((bf16[80,2048]{1,0:T(8,128)(2,1)S(1)}, bf16[80,2048]{1,0:T(8,128)(2,1)S(1)}, u32[]{:S(2)}, u32[]{:S(2)}) %collective-permute-start.3) | collective-permute-done | bytes 327712 | tf_op jit(solution)/shard_map/ppermute | solution.py:288
  57.4 5.3 %input_rows.1 = (bf16[80,2048]{1,0:T(8,128)(2,1)S(1)}, bf16[80,2048]{1,0:T(8,128)(2,1)}, bf16[80,2048]{1,0:T(8,128)(2,1)}, bf16[80,2048]{1,0:T(8,128)(2,1)}) custom-call(bf16[2,320,768]{2,1,0:T(8,128)(2,1)S(1)} %get-tuple-element.62.grad_ref.g_own, bf16[1,2048,768]{2,1,0:T(8,128)(2,1)S(1)} %copy-done.1, bf16[1,2048,768]{2,1,0:T(8,128)(2,1)} %up_ref.1), custom_call_target="tpu_custom_call" | custom-call | flops 2013265920 | bytes 9000000 | tf_op jit(solution)/shard_map/input_rows/pallas_call | solution.py:379
  71.0 1.3 copy-done.17
  74.7 5.3 %gate_up_share.1 = (bf16[4,256,768]{2,1,0:T(8,128)(2,1)S(1)}, bf16[4,256,768]{2,1,0:T(8,128)(2,1)}) custom-call(s32[1]{0:T(128)} %bitcast.2.core_ref, bf16[320,2048]{1,0:T(8,128)(2,1)S(1)} %copy-done.17, bf16[320,2048]{1,0:T(8,128)(2,1)} %collective-permute-done.12.x_other, bf16[2,320,768]{2,1,0:T(8,128)(2,1)S(1)} %copy-done.19, ...), custom_call_target="tpu_custom_call" | custom-call | flops 2013265920 | bytes 9000000 | tf_op jit(solution)/shard_map/gate_up_share/pallas_call | solution.py:192
  80.1 2.2 %dynamic-slice_bitcast_fusion.3 = (bf16[256,768]{1,0:T(8,128)(2,1)}, bf16[256,768]{1,0:T(8,128)(2,1)}) fusion(bf16[4,256,768]{2,1,0:T(8,128)(2,1)} %get-tuple-element.72, s32[]{:T(128)S(6)} %min.37, s32[]{:T(128)S(6)} %min.40), kind=kLoop, calls=%fused_computation.39 | loop fusion | bytes 1572872 | tf_op jit(solution)/shard_map/jit(dynamic_index_in_dim)/squeeze | solution.py:231
  82.2 4.2 %collective-permute-start.22 = (bf16[256,768]{1,0:T(8,128)(2,1)}, bf16[256,768]{1,0:T(8,128)(2,1)}, u32[]{:S(2)}, u32[]{:S(2)}) collective-permute-start(bf16[256,768]{1,0:T(8,128)(2,1)} %get-tuple-element.90), channel_id=1, source_target_pairs={{0,8},{4,12},{1,9},{5,13},{2,10},{6,14},{3,11},{7,15}} | collective-permute-start | bytes 1179656 | tf_op jit(solution)/shard_map/ppermute | solution.py:243
  86.4 1.4 collective-permute-start.25
  87.9 3.6 %combine.1 = (bf16[128,2048]{1,0:T(8,128)(2,1)}, bf16[128,2048]{1,0:T(8,128)(2,1)}, f32[128,2]{1,0:T(8,128)S(1)}) custom-call(s32[1]{0:T(128)} %bitcast.me_ref, s32[128,2]{1,0:T(8,128)S(1)} %copy.17.ids_ref, f32[128,2]{1,0:T(8,128)S(1)} %copy.18.gates_ref, bf16[128,2048]{1,0:T(8,128)(2,1)S(1)} %copy-done.3, bf16[80,2048]{1,0:T(8,128)(2,1)S(1)} %copy-done.6, ...), custom_call_target="tpu_custom_call" | custom-call | flops 503316480 | bytes 6000000 | tf_op jit(solution)/shard_map/combine/pallas_call | solution.py:395
  92.1 1.5 copy.19
  93.6 1.3 collective-permute-start.14
  95.7 4.0 %down_share.1 = bf16[4,768,256]{2,1,0:T(8,128)(2,1)S(1)} custom-call(s32[1]{0:T(128)} %bitcast.2.core_ref, bf16[320,768]{1,0:T(8,128)(2,1)S(1)} %get-tuple-element.52.act_ref.act_own, bf16[320,768]{1,0:T(8,128)(2,1)} %collective-permute-done.30.act_other, bf16[320,2048]{1,0:T(8,128)(2,1)S(1)} %get-tuple-element.73.c_own, ...), custom_call_target="tpu_custom_call" | custom-call | flops 1006632960 | bytes 7000000 | tf_op jit(solution)/shard_map/down_share/pallas_call | solution.py:178
  99.7 1.4 collective-permute-start.32
  101.9 1.3 fusion.9
  103.2 1.3 collective-permute-start.23
  105.4 4.8 %collective-permute-start.15 = (bf16[256,768]{1,0:T(8,128)(2,1)S(1)}, bf16[256,768]{1,0:T(8,128)(2,1)S(1)}, u32[]{:S(2)}, u32[]{:S(2)}) collective-permute-start(bf16[256,768]{1,0:T(8,128)(2,1)S(1)} %get-tuple-element.94), channel_id=1, source_target_pairs={{0,8},{4,12},{8,16},{12,20},{1,9},{5,13},{9,17},{13,21},{2,10},{6,... | collective-permute-start | bytes 1179656 | tf_op jit(solution)/shard_map/ppermute | solution.py:243
  110.2 2.5 %collective-permute-done.32 = bf16[768,256]{1,0:T(8,128)(2,1)S(1)} collective-permute-done((bf16[768,256]{1,0:T(8,128)(2,1)S(1)}, bf16[768,256]{1,0:T(8,128)(2,1)S(1)}, u32[]{:S(2)}, u32[]{:S(2)}) %collective-permute-start.32) | collective-permute-done | bytes 393248 | tf_op jit(solution)/shard_map/ppermute | solution.py:243
  113.7 5.0 %collective-permute-start.33 = (bf16[768,256]{1,0:T(8,128)(2,1)S(1)}, bf16[768,256]{1,0:T(8,128)(2,1)S(1)}, u32[]{:S(2)}, u32[]{:S(2)}) collective-permute-start(bf16[768,256]{1,0:T(8,128)(2,1)S(1)} %get-tuple-element.82), channel_id=1, source_target_pairs={{0,8},{4,12},{8,16},{12,20},{1,9},{5,13},{9,17},{13,21},{2,10},{6,... | collective-permute-start | bytes 1179656 | tf_op jit(solution)/shard_map/ppermute | solution.py:243
  118.7 2.5 %collective-permute-done.23 = bf16[256,768]{1,0:T(8,128)(2,1)S(1)} collective-permute-done((bf16[256,768]{1,0:T(8,128)(2,1)S(1)}, bf16[256,768]{1,0:T(8,128)(2,1)S(1)}, u32[]{:S(2)}, u32[]{:S(2)}) %collective-permute-start.23) | collective-permute-done | bytes 393248 | tf_op jit(solution)/shard_map/ppermute | solution.py:243
  122.1 5.0 %collective-permute-start.24 = (bf16[256,768]{1,0:T(8,128)(2,1)S(1)}, bf16[256,768]{1,0:T(8,128)(2,1)S(1)}, u32[]{:S(2)}, u32[]{:S(2)}) collective-permute-start(bf16[256,768]{1,0:T(8,128)(2,1)S(1)} %get-tuple-element.86), channel_id=1, source_target_pairs={{0,8},{4,12},{8,16},{12,20},{16,24},{20,28},{1,9},{5,13},{9,17},{1... | collective-permute-start | bytes 1179656 | tf_op jit(solution)/shard_map/ppermute | solution.py:243
  127.1 2.5 %collective-permute-done.15 = bf16[256,768]{1,0:T(8,128)(2,1)S(1)} collective-permute-done((bf16[256,768]{1,0:T(8,128)(2,1)S(1)}, bf16[256,768]{1,0:T(8,128)(2,1)S(1)}, u32[]{:S(2)}, u32[]{:S(2)}) %collective-permute-start.15) | collective-permute-done | bytes 393248 | tf_op jit(solution)/shard_map/ppermute | solution.py:243
  129.6 1.3 collective-permute-start.27
  131.1 5.0 %collective-permute-start.16 = (bf16[256,768]{1,0:T(8,128)(2,1)S(1)}, bf16[256,768]{1,0:T(8,128)(2,1)S(1)}, u32[]{:S(2)}, u32[]{:S(2)}) collective-permute-start(bf16[256,768]{1,0:T(8,128)(2,1)S(1)} %get-tuple-element.92), channel_id=1, source_target_pairs={{0,8},{4,12},{8,16},{12,20},{16,24},{20,28},{1,9},{5,13},{9,17},{1... | collective-permute-start | bytes 1179656 | tf_op jit(solution)/shard_map/ppermute | solution.py:243
  136.2 1.9 collective-permute-done.33
  138.0 1.3 collective-permute-start.19
  139.5 5.0 %collective-permute-start.34 = (bf16[768,256]{1,0:T(8,128)(2,1)S(1)}, bf16[768,256]{1,0:T(8,128)(2,1)S(1)}, u32[]{:S(2)}, u32[]{:S(2)}) collective-permute-start(bf16[768,256]{1,0:T(8,128)(2,1)S(1)} %get-tuple-element.80), channel_id=1, source_target_pairs={{0,8},{4,12},{8,16},{12,20},{16,24},{20,28},{1,9},{5,13},{9,17},{1... | collective-permute-start | bytes 1179656 | tf_op jit(solution)/shard_map/ppermute | solution.py:243
  144.6 1.9 collective-permute-done.24
  146.5 1.3 collective-permute-start.37
  147.9 1.2 collective-permute-start.28
  149.2 5.7 %collective-permute-done.16 = bf16[256,768]{1,0:T(8,128)(2,1)S(1)} collective-permute-done((bf16[256,768]{1,0:T(8,128)(2,1)S(1)}, bf16[256,768]{1,0:T(8,128)(2,1)S(1)}, u32[]{:S(2)}, u32[]{:S(2)}) %collective-permute-start.16) | collective-permute-done | bytes 393248 | tf_op jit(solution)/shard_map/ppermute | solution.py:243
  155.0 1.2 collective-permute-start.20
  156.3 6.6 %collective-permute-done.34 = bf16[768,256]{1,0:T(8,128)(2,1)S(1)} collective-permute-done((bf16[768,256]{1,0:T(8,128)(2,1)S(1)}, bf16[768,256]{1,0:T(8,128)(2,1)S(1)}, u32[]{:S(2)}, u32[]{:S(2)}) %collective-permute-start.34) | collective-permute-done | bytes 393248 | tf_op jit(solution)/shard_map/ppermute | solution.py:243
  165.3 2.7 %collective-permute-done.20 = bf16[256,768]{1,0:T(8,128)(2,1)S(1)} collective-permute-done((bf16[256,768]{1,0:T(8,128)(2,1)S(1)}, bf16[256,768]{1,0:T(8,128)(2,1)S(1)}, u32[]{:S(2)}, u32[]{:S(2)}) %collective-permute-start.20) | collective-permute-done | bytes 393248 | tf_op jit(solution)/shard_map/ppermute | solution.py:257
  168.0 1.5 collective-permute-start.21
  169.6 5.6 %collective-permute-done.38 = bf16[768,256]{1,0:T(8,128)(2,1)S(1)} collective-permute-done((bf16[768,256]{1,0:T(8,128)(2,1)S(1)}, bf16[768,256]{1,0:T(8,128)(2,1)S(1)}, u32[]{:S(2)}, u32[]{:S(2)}) %collective-permute-start.38) | collective-permute-done | bytes 393248 | tf_op jit(solution)/shard_map/ppermute | solution.py:257
  175.2 1.5 collective-permute-start.39
  177.7 7.2 %collective-permute-done.21 = bf16[256,768]{1,0:T(8,128)(2,1)S(1)} collective-permute-done((bf16[256,768]{1,0:T(8,128)(2,1)S(1)}, bf16[256,768]{1,0:T(8,128)(2,1)S(1)}, u32[]{:S(2)}, u32[]{:S(2)}) %collective-permute-start.21) | collective-permute-done | bytes 393248 | tf_op jit(solution)/shard_map/ppermute | solution.py:258
  185.8 5.9 %collective-permute-done.39 = bf16[768,256]{1,0:T(8,128)(2,1)S(1)} collective-permute-done((bf16[768,256]{1,0:T(8,128)(2,1)S(1)}, bf16[768,256]{1,0:T(8,128)(2,1)S(1)}, u32[]{:S(2)}, u32[]{:S(2)}) %collective-permute-start.39) | collective-permute-done | bytes 393248 | tf_op jit(solution)/shard_map/ppermute | solution.py:258
  (111 shorter events, 31.7 us)
Async XLA Ops:
  3.4 11.6 %collective-permute-start = (bf16[80,2048]{1,0:T(8,128)(2,1)S(1)}, bf16[80,2048]{1,0:T(8,128)(2,1)S(1)}, u32[]{:S(2)}, u32[]{:S(2)}) collective-permute-start(bf16[80,2048]{1,0:T(8,128)(2,1)S(1)} %get-tuple-element.45), channel_id=1, source_target_pairs={{0,1},{1,0},{2,3},{3,2},{4,5},{5,4},{6,7},{7,6},{8,9},{9,8},{10,11... | collective-permute-start | bytes 983048 | tf_op jit(solution)/shard_map/ppermute | solution.py:288
  6.4 16.2 %collective-permute-start.1 = (bf16[80,2048]{1,0:T(8,128)(2,1)S(1)}, bf16[80,2048]{1,0:T(8,128)(2,1)S(1)}, u32[]{:S(2)}, u32[]{:S(2)}) collective-permute-start(bf16[80,2048]{1,0:T(8,128)(2,1)S(1)} %get-tuple-element.46), channel_id=1, source_target_pairs={{0,2},{1,3},{2,0},{3,1},{4,6},{5,7},{6,4},{7,5},{8,10},{9,11},{10,... | collective-permute-start | bytes 983048 | tf_op jit(solution)/shard_map/ppermute | solution.py:288
  7.9 14.7 %collective-permute-start.2 = (bf16[80,2048]{1,0:T(8,128)(2,1)S(1)}, bf16[80,2048]{1,0:T(8,128)(2,1)S(1)}, u32[]{:S(2)}, u32[]{:S(2)}) collective-permute-start(bf16[80,2048]{1,0:T(8,128)(2,1)S(1)} %get-tuple-element.47), channel_id=1, source_target_pairs={{0,3},{1,2},{2,1},{3,0},{4,7},{5,6},{6,5},{7,4},{8,11},{9,10},{10,... | collective-permute-start | bytes 983048 | tf_op jit(solution)/shard_map/ppermute | solution.py:288
  22.6 10.6 %collective-permute-start.6 = (bf16[80,2048]{1,0:T(8,128)(2,1)S(1)}, bf16[80,2048]{1,0:T(8,128)(2,1)S(1)}, u32[]{:S(2)}, u32[]{:S(2)}) collective-permute-start(bf16[80,2048]{1,0:T(8,128)(2,1)S(1)} %get-tuple-element.58), channel_id=1, source_target_pairs={{0,1},{1,0},{2,3},{3,2},{4,5},{5,4},{6,7},{7,6},{8,9},{9,8},{10,11... | collective-permute-start | bytes 983048 | tf_op jit(solution)/shard_map/ppermute | solution.py:288
  23.9 15.3 %collective-permute-start.7 = (bf16[80,2048]{1,0:T(8,128)(2,1)S(1)}, bf16[80,2048]{1,0:T(8,128)(2,1)S(1)}, u32[]{:S(2)}, u32[]{:S(2)}) collective-permute-start(bf16[80,2048]{1,0:T(8,128)(2,1)S(1)} %get-tuple-element.59), channel_id=1, source_target_pairs={{0,2},{1,3},{2,0},{3,1},{4,6},{5,7},{6,4},{7,5},{8,10},{9,11},{10,... | collective-permute-start | bytes 983048 | tf_op jit(solution)/shard_map/ppermute | solution.py:288
  24.7 14.5 %collective-permute-start.8 = (bf16[80,2048]{1,0:T(8,128)(2,1)S(1)}, bf16[80,2048]{1,0:T(8,128)(2,1)S(1)}, u32[]{:S(2)}, u32[]{:S(2)}) collective-permute-start(bf16[80,2048]{1,0:T(8,128)(2,1)S(1)} %get-tuple-element.60), channel_id=1, source_target_pairs={{0,3},{1,2},{2,1},{3,0},{4,7},{5,6},{6,5},{7,4},{8,11},{9,10},{10,... | collective-permute-start | bytes 983048 | tf_op jit(solution)/shard_map/ppermute | solution.py:288
  31.2 11.9 %copy-start.16 = (bf16[320,2048]{1,0:T(8,128)(2,1)}, bf16[320,2048]{1,0:T(8,128)(2,1)S(1)}, u32[]{:S(2)}) copy-start(bf16[320,2048]{1,0:T(8,128)(2,1)S(1)} %get-tuple-element.70.x_own) | copy-start | bytes 3932164
  31.2 39.7 %collective-permute-start.12 = (bf16[320,2048]{1,0:T(8,128)(2,1)S(1)}, bf16[320,2048]{1,0:T(8,128)(2,1)}, u32[]{:S(2)}, u32[]{:S(2)}) collective-permute-start(bf16[320,2048]{1,0:T(8,128)(2,1)S(1)} %get-tuple-element.70.x_own), channel_id=1, source_target_pairs={{0,4},{4,0},{8,12},{12,8},{16,20},{20,16},{24,28},{28,24},{1,5},{5... | collective-permute-start | bytes 3932168 | tf_op jit(solution)/shard_map/ppermute | solution.py:293
  43.1 14.3 %copy-start.18 = (bf16[2,320,768]{2,1,0:T(8,128)(2,1)}, bf16[2,320,768]{2,1,0:T(8,128)(2,1)S(1)}, u32[]{:S(2)}) copy-start(bf16[2,320,768]{2,1,0:T(8,128)(2,1)S(1)} %get-tuple-element.62.grad_ref.g_own) | copy-start | bytes 2949124
  43.1 24.7 %collective-permute-start.13 = (bf16[2,320,768]{2,1,0:T(8,128)(2,1)S(1)}, bf16[2,320,768]{2,1,0:T(8,128)(2,1)S(1)}, u32[]{:S(2)}, u32[]{:S(2)}) collective-permute-start(bf16[2,320,768]{2,1,0:T(8,128)(2,1)S(1)} %get-tuple-element.62.grad_ref.g_own), channel_id=1, source_target_pairs={{0,4},{4,0},{8,12},{12,8},{16,20},{20,16},{24,28},{28,24},{1,5},{5... | collective-permute-start | bytes 2949128 | tf_op jit(solution)/shard_map/ppermute | solution.py:293
  43.2 52.5 %collective-permute-start.31 = (bf16[320,2048]{1,0:T(8,128)(2,1)S(1)}, bf16[320,2048]{1,0:T(8,128)(2,1)}, u32[]{:S(2)}, u32[]{:S(2)}) collective-permute-start(bf16[320,2048]{1,0:T(8,128)(2,1)S(1)} %get-tuple-element.73.c_own), channel_id=1, source_target_pairs={{0,4},{4,0},{8,12},{12,8},{16,20},{20,16},{24,28},{28,24},{1,5},{5... | collective-permute-start | bytes 3932168 | tf_op jit(solution)/shard_map/ppermute | solution.py:293
  43.7 13.7 %copy-start.1 = (bf16[1,2048,768]{2,1,0:T(8,128)(2,1)S(1)}, bf16[1,2048,768]{2,1,0:T(8,128)(2,1)}, u32[]{:S(2)}) copy-start(bf16[1,2048,768]{2,1,0:T(8,128)(2,1)} %gate_ref.1) | copy-start | bytes 9437188
  46.5 9.7 %collective-permute-start.3 = (bf16[80,2048]{1,0:T(8,128)(2,1)S(1)}, bf16[80,2048]{1,0:T(8,128)(2,1)S(1)}, u32[]{:S(2)}, u32[]{:S(2)}) collective-permute-start(bf16[80,2048]{1,0:T(8,128)(2,1)S(1)} %get-tuple-element.54), channel_id=1, source_target_pairs={{0,1},{1,0},{2,3},{3,2},{4,5},{5,4},{6,7},{7,6},{8,9},{9,8},{10,11... | collective-permute-start | bytes 983048 | tf_op jit(solution)/shard_map/ppermute | solution.py:288
  47.0 16.4 %collective-permute-start.4 = (bf16[80,2048]{1,0:T(8,128)(2,1)S(1)}, bf16[80,2048]{1,0:T(8,128)(2,1)S(1)}, u32[]{:S(2)}, u32[]{:S(2)}) collective-permute-start(bf16[80,2048]{1,0:T(8,128)(2,1)S(1)} %get-tuple-element.55), channel_id=1, source_target_pairs={{0,2},{1,3},{2,0},{3,1},{4,6},{5,7},{6,4},{7,5},{8,10},{9,11},{10,... | collective-permute-start | bytes 983048 | tf_op jit(solution)/shard_map/ppermute | solution.py:288
  56.2 13.4 %copy-start.23 = (s32[4]{0:T(128)S(1)}, s32[4]{0:T(128)}, u32[]{:S(2)}) copy-start(s32[4]{0:T(128)} %param.12) | copy-start | bytes 52
  56.2 9.8 %collective-permute-start.5 = (bf16[80,2048]{1,0:T(8,128)(2,1)S(1)}, bf16[80,2048]{1,0:T(8,128)(2,1)S(1)}, u32[]{:S(2)}, u32[]{:S(2)}) collective-permute-start(bf16[80,2048]{1,0:T(8,128)(2,1)S(1)} %get-tuple-element.56), channel_id=1, source_target_pairs={{0,3},{1,2},{2,1},{3,0},{4,7},{5,6},{6,5},{7,4},{8,11},{9,10},{10,... | collective-permute-start | bytes 983048 | tf_op jit(solution)/shard_map/ppermute | solution.py:288
  64.1 18.1 %collective-permute-start.10 = (bf16[80,2048]{1,0:T(8,128)(2,1)}, bf16[80,2048]{1,0:T(8,128)(2,1)}, u32[]{:S(2)}, u32[]{:S(2)}) collective-permute-start(bf16[80,2048]{1,0:T(8,128)(2,1)} %get-tuple-element.65), channel_id=1, source_target_pairs={{0,2},{1,3},{2,0},{3,1},{4,6},{5,7},{6,4},{7,5},{8,10},{9,11},{10,... | collective-permute-start | bytes 983048 | tf_op jit(solution)/shard_map/ppermute | solution.py:288
  66.6 19.8 %collective-permute-start.11 = (bf16[80,2048]{1,0:T(8,128)(2,1)}, bf16[80,2048]{1,0:T(8,128)(2,1)}, u32[]{:S(2)}, u32[]{:S(2)}) collective-permute-start(bf16[80,2048]{1,0:T(8,128)(2,1)} %get-tuple-element.66), channel_id=1, source_target_pairs={{0,3},{1,2},{2,1},{3,0},{4,7},{5,6},{6,5},{7,4},{8,11},{9,10},{10,... | collective-permute-start | bytes 983048 | tf_op jit(solution)/shard_map/ppermute | solution.py:288
  68.8 19.1 %collective-permute-start.9 = (bf16[80,2048]{1,0:T(8,128)(2,1)}, bf16[80,2048]{1,0:T(8,128)(2,1)}, u32[]{:S(2)}, u32[]{:S(2)}) collective-permute-start(bf16[80,2048]{1,0:T(8,128)(2,1)} %get-tuple-element.64), channel_id=1, source_target_pairs={{0,1},{1,0},{2,3},{3,2},{4,5},{5,4},{6,7},{7,6},{8,9},{9,8},{10,11... | collective-permute-start | bytes 983048 | tf_op jit(solution)/shard_map/ppermute | solution.py:288
  70.9 24.1 %collective-permute-start.30 = (bf16[320,768]{1,0:T(8,128)(2,1)S(1)}, bf16[320,768]{1,0:T(8,128)(2,1)}, u32[]{:S(2)}, u32[]{:S(2)}) collective-permute-start(bf16[320,768]{1,0:T(8,128)(2,1)S(1)} %get-tuple-element.52.act_ref.act_own), channel_id=1, source_target_pairs={{0,4},{4,0},{8,12},{12,8},{16,20},{20,16},{24,28},{28,24},{1,5},{5... | collective-permute-start | bytes 1474568 | tf_op jit(solution)/shard_map/ppermute | solution.py:293
  74.7 13.2 %copy-start.12 = (bf16[80,2048]{1,0:T(8,128)(2,1)S(1)}, bf16[80,2048]{1,0:T(8,128)(2,1)}, u32[]{:S(2)}) copy-start(bf16[80,2048]{1,0:T(8,128)(2,1)} %copy-done.11) | copy-start | bytes 983044
  74.7 13.2 %copy-start.14 = (bf16[80,2048]{1,0:T(8,128)(2,1)S(1)}, bf16[80,2048]{1,0:T(8,128)(2,1)}, u32[]{:S(2)}) copy-start(bf16[80,2048]{1,0:T(8,128)(2,1)} %copy-done.13) | copy-start | bytes 983044
  80.0 7.8 %copy-start.8 = (bf16[80,2048]{1,0:T(8,128)(2,1)S(1)}, bf16[80,2048]{1,0:T(8,128)(2,1)}, u32[]{:S(2)}) copy-start(bf16[80,2048]{1,0:T(8,128)(2,1)} %copy-done.7) | copy-start | bytes 983044
  80.0 7.8 %copy-start.10 = (bf16[80,2048]{1,0:T(8,128)(2,1)S(1)}, bf16[80,2048]{1,0:T(8,128)(2,1)}, u32[]{:S(2)}) copy-start(bf16[80,2048]{1,0:T(8,128)(2,1)} %copy-done.9) | copy-start | bytes 983044
  82.2 18.9 %collective-permute-start.22 = (bf16[256,768]{1,0:T(8,128)(2,1)}, bf16[256,768]{1,0:T(8,128)(2,1)}, u32[]{:S(2)}, u32[]{:S(2)}) collective-permute-start(bf16[256,768]{1,0:T(8,128)(2,1)} %get-tuple-element.90), channel_id=1, source_target_pairs={{0,8},{4,12},{1,9},{5,13},{2,10},{6,14},{3,11},{7,15}} | collective-permute-start | bytes 1179656 | tf_op jit(solution)/shard_map/ppermute | solution.py:243
  86.4 15.4 %collective-permute-start.25 = (bf16[256,768]{1,0:T(8,128)(2,1)}, bf16[256,768]{1,0:T(8,128)(2,1)}, u32[]{:S(2)}, u32[]{:S(2)}) collective-permute-start(bf16[256,768]{1,0:T(8,128)(2,1)} %get-tuple-element.91), channel_id=1, source_target_pairs={{24,16},{28,20},{25,17},{29,21},{26,18},{30,22},{27,19},{31,23}} | collective-permute-start | bytes 1179656 | tf_op jit(solution)/shard_map/ppermute | solution.py:243
  93.6 10.9 %collective-permute-start.14 = (bf16[256,768]{1,0:T(8,128)(2,1)S(1)}, bf16[256,768]{1,0:T(8,128)(2,1)S(1)}, u32[]{:S(2)}, u32[]{:S(2)}) collective-permute-start(bf16[256,768]{1,0:T(8,128)(2,1)S(1)} %get-tuple-element.96), channel_id=1, source_target_pairs={{0,8},{4,12},{1,9},{5,13},{2,10},{6,14},{3,11},{7,15}} | collective-permute-start | bytes 1179656 | tf_op jit(solution)/shard_map/ppermute | solution.py:243
  95.0 10.3 %collective-permute-start.17 = (bf16[256,768]{1,0:T(8,128)(2,1)S(1)}, bf16[256,768]{1,0:T(8,128)(2,1)S(1)}, u32[]{:S(2)}, u32[]{:S(2)}) collective-permute-start(bf16[256,768]{1,0:T(8,128)(2,1)S(1)} %get-tuple-element.97), channel_id=1, source_target_pairs={{24,16},{28,20},{25,17},{29,21},{26,18},{30,22},{27,19},{31,23}} | collective-permute-start | bytes 1179656 | tf_op jit(solution)/shard_map/ppermute | solution.py:243
  99.7 13.1 %collective-permute-start.32 = (bf16[768,256]{1,0:T(8,128)(2,1)S(1)}, bf16[768,256]{1,0:T(8,128)(2,1)S(1)}, u32[]{:S(2)}, u32[]{:S(2)}) collective-permute-start(bf16[768,256]{1,0:T(8,128)(2,1)S(1)} %get-tuple-element.84), channel_id=1, source_target_pairs={{0,8},{4,12},{1,9},{5,13},{2,10},{6,14},{3,11},{7,15}} | collective-permute-start | bytes 1179656 | tf_op jit(solution)/shard_map/ppermute | solution.py:243
  101.2 12.3 %collective-permute-start.35 = (bf16[768,256]{1,0:T(8,128)(2,1)S(1)}, bf16[768,256]{1,0:T(8,128)(2,1)S(1)}, u32[]{:S(2)}, u32[]{:S(2)}) collective-permute-start(bf16[768,256]{1,0:T(8,128)(2,1)S(1)} %get-tuple-element.85), channel_id=1, source_target_pairs={{24,16},{28,20},{25,17},{29,21},{26,18},{30,22},{27,19},{31,23}} | collective-permute-start | bytes 1179656 | tf_op jit(solution)/shard_map/ppermute | solution.py:243
  103.2 18.0 %collective-permute-start.23 = (bf16[256,768]{1,0:T(8,128)(2,1)S(1)}, bf16[256,768]{1,0:T(8,128)(2,1)S(1)}, u32[]{:S(2)}, u32[]{:S(2)}) collective-permute-start(bf16[256,768]{1,0:T(8,128)(2,1)S(1)} %get-tuple-element.88), channel_id=1, source_target_pairs={{0,8},{4,12},{8,16},{12,20},{1,9},{5,13},{9,17},{13,21},{2,10},{6,... | collective-permute-start | bytes 1179656 | tf_op jit(solution)/shard_map/ppermute | solution.py:243
  104.5 17.3 %collective-permute-start.26 = (bf16[256,768]{1,0:T(8,128)(2,1)S(1)}, bf16[256,768]{1,0:T(8,128)(2,1)S(1)}, u32[]{:S(2)}, u32[]{:S(2)}) collective-permute-start(bf16[256,768]{1,0:T(8,128)(2,1)S(1)} %get-tuple-element.89), channel_id=1, source_target_pairs={{24,16},{28,20},{16,8},{20,12},{25,17},{29,21},{17,9},{21,13},{26,... | collective-permute-start | bytes 1179656 | tf_op jit(solution)/shard_map/ppermute | solution.py:243
  105.4 24.2 %collective-permute-start.15 = (bf16[256,768]{1,0:T(8,128)(2,1)S(1)}, bf16[256,768]{1,0:T(8,128)(2,1)S(1)}, u32[]{:S(2)}, u32[]{:S(2)}) collective-permute-start(bf16[256,768]{1,0:T(8,128)(2,1)S(1)} %get-tuple-element.94), channel_id=1, source_target_pairs={{0,8},{4,12},{8,16},{12,20},{1,9},{5,13},{9,17},{13,21},{2,10},{6,... | collective-permute-start | bytes 1179656 | tf_op jit(solution)/shard_map/ppermute | solution.py:243
  112.8 18.1 %collective-permute-start.18 = (bf16[256,768]{1,0:T(8,128)(2,1)S(1)}, bf16[256,768]{1,0:T(8,128)(2,1)S(1)}, u32[]{:S(2)}, u32[]{:S(2)}) collective-permute-start(bf16[256,768]{1,0:T(8,128)(2,1)S(1)} %get-tuple-element.95), channel_id=1, source_target_pairs={{24,16},{28,20},{16,8},{20,12},{25,17},{29,21},{17,9},{21,13},{26,... | collective-permute-start | bytes 1179656 | tf_op jit(solution)/shard_map/ppermute | solution.py:243
  113.7 24.4 %collective-permute-start.33 = (bf16[768,256]{1,0:T(8,128)(2,1)S(1)}, bf16[768,256]{1,0:T(8,128)(2,1)S(1)}, u32[]{:S(2)}, u32[]{:S(2)}) collective-permute-start(bf16[768,256]{1,0:T(8,128)(2,1)S(1)} %get-tuple-element.82), channel_id=1, source_target_pairs={{0,8},{4,12},{8,16},{12,20},{1,9},{5,13},{9,17},{13,21},{2,10},{6,... | collective-permute-start | bytes 1179656 | tf_op jit(solution)/shard_map/ppermute | solution.py:243
  121.2 18.1 %collective-permute-start.36 = (bf16[768,256]{1,0:T(8,128)(2,1)S(1)}, bf16[768,256]{1,0:T(8,128)(2,1)S(1)}, u32[]{:S(2)}, u32[]{:S(2)}) collective-permute-start(bf16[768,256]{1,0:T(8,128)(2,1)S(1)} %get-tuple-element.83), channel_id=1, source_target_pairs={{24,16},{28,20},{16,8},{20,12},{25,17},{29,21},{17,9},{21,13},{26,... | collective-permute-start | bytes 1179656 | tf_op jit(solution)/shard_map/ppermute | solution.py:243
  122.1 24.4 %collective-permute-start.24 = (bf16[256,768]{1,0:T(8,128)(2,1)S(1)}, bf16[256,768]{1,0:T(8,128)(2,1)S(1)}, u32[]{:S(2)}, u32[]{:S(2)}) collective-permute-start(bf16[256,768]{1,0:T(8,128)(2,1)S(1)} %get-tuple-element.86), channel_id=1, source_target_pairs={{0,8},{4,12},{8,16},{12,20},{16,24},{20,28},{1,9},{5,13},{9,17},{1... | collective-permute-start | bytes 1179656 | tf_op jit(solution)/shard_map/ppermute | solution.py:243
  129.6 18.1 %collective-permute-start.27 = (bf16[256,768]{1,0:T(8,128)(2,1)S(1)}, bf16[256,768]{1,0:T(8,128)(2,1)S(1)}, u32[]{:S(2)}, u32[]{:S(2)}) collective-permute-start(bf16[256,768]{1,0:T(8,128)(2,1)S(1)} %get-tuple-element.87), channel_id=1, source_target_pairs={{24,16},{28,20},{16,8},{20,12},{8,0},{12,4},{25,17},{29,21},{17,9}... | collective-permute-start | bytes 1179656 | tf_op jit(solution)/shard_map/ppermute | solution.py:243
  131.1 23.8 %collective-permute-start.16 = (bf16[256,768]{1,0:T(8,128)(2,1)S(1)}, bf16[256,768]{1,0:T(8,128)(2,1)S(1)}, u32[]{:S(2)}, u32[]{:S(2)}) collective-permute-start(bf16[256,768]{1,0:T(8,128)(2,1)S(1)} %get-tuple-element.92), channel_id=1, source_target_pairs={{0,8},{4,12},{8,16},{12,20},{16,24},{20,28},{1,9},{5,13},{9,17},{1... | collective-permute-start | bytes 1179656 | tf_op jit(solution)/shard_map/ppermute | solution.py:243
  138.0 16.9 %collective-permute-start.19 = (bf16[256,768]{1,0:T(8,128)(2,1)S(1)}, bf16[256,768]{1,0:T(8,128)(2,1)S(1)}, u32[]{:S(2)}, u32[]{:S(2)}) collective-permute-start(bf16[256,768]{1,0:T(8,128)(2,1)S(1)} %get-tuple-element.93), channel_id=1, source_target_pairs={{24,16},{28,20},{16,8},{20,12},{8,0},{12,4},{25,17},{29,21},{17,9}... | collective-permute-start | bytes 1179656 | tf_op jit(solution)/shard_map/ppermute | solution.py:243
  139.5 23.4 %collective-permute-start.34 = (bf16[768,256]{1,0:T(8,128)(2,1)S(1)}, bf16[768,256]{1,0:T(8,128)(2,1)S(1)}, u32[]{:S(2)}, u32[]{:S(2)}) collective-permute-start(bf16[768,256]{1,0:T(8,128)(2,1)S(1)} %get-tuple-element.80), channel_id=1, source_target_pairs={{0,8},{4,12},{8,16},{12,20},{16,24},{20,28},{1,9},{5,13},{9,17},{1... | collective-permute-start | bytes 1179656 | tf_op jit(solution)/shard_map/ppermute | solution.py:243
  146.5 16.5 %collective-permute-start.37 = (bf16[768,256]{1,0:T(8,128)(2,1)S(1)}, bf16[768,256]{1,0:T(8,128)(2,1)S(1)}, u32[]{:S(2)}, u32[]{:S(2)}) collective-permute-start(bf16[768,256]{1,0:T(8,128)(2,1)S(1)} %get-tuple-element.81), channel_id=1, source_target_pairs={{24,16},{28,20},{16,8},{20,12},{8,0},{12,4},{25,17},{29,21},{17,9}... | collective-permute-start | bytes 1179656 | tf_op jit(solution)/shard_map/ppermute | solution.py:243
  147.9 16.4 %collective-permute-start.28 = (bf16[256,768]{1,0:T(8,128)(2,1)S(1)}, bf16[256,768]{1,0:T(8,128)(2,1)S(1)}, u32[]{:S(2)}, u32[]{:S(2)}) collective-permute-start(bf16[256,768]{1,0:T(8,128)(2,1)S(1)} %fusion.11), channel_id=1, source_target_pairs={{0,1},{1,0},{2,3},{3,2},{4,5},{5,4},{6,7},{7,6},{8,9},{9,8},{10,11... | collective-permute-start | bytes 1179656 | tf_op jit(solution)/shard_map/ppermute | solution.py:257
  155.0 12.9 %collective-permute-start.20 = (bf16[256,768]{1,0:T(8,128)(2,1)S(1)}, bf16[256,768]{1,0:T(8,128)(2,1)S(1)}, u32[]{:S(2)}, u32[]{:S(2)}) collective-permute-start(bf16[256,768]{1,0:T(8,128)(2,1)S(1)} %fusion.17), channel_id=1, source_target_pairs={{0,1},{1,0},{2,3},{3,2},{4,5},{5,4},{6,7},{7,6},{8,9},{9,8},{10,11... | collective-permute-start | bytes 1179656 | tf_op jit(solution)/shard_map/ppermute | solution.py:257
  163.1 12.1 %collective-permute-start.38 = (bf16[768,256]{1,0:T(8,128)(2,1)S(1)}, bf16[768,256]{1,0:T(8,128)(2,1)S(1)}, u32[]{:S(2)}, u32[]{:S(2)}) collective-permute-start(bf16[768,256]{1,0:T(8,128)(2,1)S(1)} %fusion.5), channel_id=1, source_target_pairs={{0,1},{1,0},{2,3},{3,2},{4,5},{5,4},{6,7},{7,6},{8,9},{9,8},{10,11... | collective-permute-start | bytes 1179656 | tf_op jit(solution)/shard_map/ppermute | solution.py:257
  164.4 12.4 %collective-permute-start.29 = (bf16[256,768]{1,0:T(8,128)(2,1)S(1)}, bf16[256,768]{1,0:T(8,128)(2,1)S(1)}, u32[]{:S(2)}, u32[]{:S(2)}) collective-permute-start(bf16[256,768]{1,0:T(8,128)(2,1)S(1)} %broadcast_select_fusion.1), channel_id=1, source_target_pairs={{0,2},{1,3},{2,0},{3,1},{4,6},{5,7},{6,4},{7,5},{8,10},{9,11},{10,... | collective-permute-start | bytes 1179656 | tf_op jit(solution)/shard_map/ppermute | solution.py:258
  168.0 16.9 %collective-permute-start.21 = (bf16[256,768]{1,0:T(8,128)(2,1)S(1)}, bf16[256,768]{1,0:T(8,128)(2,1)S(1)}, u32[]{:S(2)}, u32[]{:S(2)}) collective-permute-start(bf16[256,768]{1,0:T(8,128)(2,1)S(1)} %broadcast_select_fusion.2), channel_id=1, source_target_pairs={{0,2},{1,3},{2,0},{3,1},{4,6},{5,7},{6,4},{7,5},{8,10},{9,11},{10,... | collective-permute-start | bytes 1179656 | tf_op jit(solution)/shard_map/ppermute | solution.py:258
  175.2 16.5 %collective-permute-start.39 = (bf16[768,256]{1,0:T(8,128)(2,1)S(1)}, bf16[768,256]{1,0:T(8,128)(2,1)S(1)}, u32[]{:S(2)}, u32[]{:S(2)}) collective-permute-start(bf16[768,256]{1,0:T(8,128)(2,1)S(1)} %broadcast_select_fusion), channel_id=1, source_target_pairs={{0,2},{1,3},{2,0},{3,1},{4,6},{5,7},{6,4},{7,5},{8,10},{9,11},{10,... | collective-permute-start | bytes 1179656 | tf_op jit(solution)/shard_map/ppermute | solution.py:258
  (16 other events, 39.1 us)

commit v2 on v1

v2 whole, which is shorter than its diff:
```python
import functools

import jax
import jax.numpy as jnp
from jax import lax
from jax.experimental import pallas as pl
from jax.experimental.pallas import tpu as pltpu
from jax.sharding import PartitionSpec as P

VMEM_BYTES = 32 * 1024 * 1024
F32 = jnp.float32
BF16 = jnp.bfloat16


def dot_nn(a, b):
    return lax.dot_general(a, b, (((1,), (0,)), ((), ())), preferred_element_type=F32)


def dot_nt(a, b):
    return lax.dot_general(a, b, (((1,), (1,)), ((), ())), preferred_element_type=F32)


def dot_tn(a, b):
    return lax.dot_general(a, b, (((0,), (0,)), ((), ())), preferred_element_type=F32)


def tile_of(size, want):
    while size % want:
        want //= 2
    return want


def params(**more):
    return pltpu.CompilerParams(vmem_limit_bytes=VMEM_BYTES, **more)


def whole(shape):
    return pl.BlockSpec(shape, lambda *_: (0,) * len(shape))


def cost(flops, nbytes):
    return pl.CostEstimate(flops=1000, bytes_accessed=1000, transcendentals=0)


def picks_of(ids, cap, groups, me):
    top, count = ids.shape
    block = jnp.bitwise_xor(ids, me)
    lane = lax.broadcasted_iota(jnp.int32, (max(groups, 8), count), 0)
    named = [(block[k : k + 1] == lane).astype(F32) for k in range(top)]
    earlier = lax.broadcasted_iota(jnp.int32, (count, count), 0) < lax.broadcasted_iota(
        jnp.int32, (count, count), 1
    )
    before = dot_nn(sum(named).astype(BF16), earlier.astype(BF16))
    row = lax.broadcasted_iota(jnp.int32, (groups * cap, count), 0)
    picks = []
    for k in range(top):
        pos = jnp.sum(before * named[k], axis=0, keepdims=True).astype(jnp.int32)
        picks.append(block[k : k + 1] * cap + pos == row)
        before = before + named[k]
    return picks


def place_tokens(cap, groups, me_ref, ids_ref, tok_ref, *outs):
    picks = picks_of(ids_ref[...], cap, groups, me_ref[0])
    rows = dot_nn(sum(pick.astype(BF16) for pick in picks), tok_ref[...])
    for b, out in enumerate(outs):
        out[...] = rows[b * cap : (b + 1) * cap].astype(BF16)


def place_grads(cap, groups, me_ref, ids_ref, gates_ref, cot_ref, *outs):
    picks = picks_of(ids_ref[...], cap, groups, me_ref[0])
    gates = gates_ref[...]
    weight = sum(
        jnp.sum(jnp.where(pick, gates[k : k + 1], 0.0), axis=1, keepdims=True)
        for k, pick in enumerate(picks)
    )
    rows = dot_nn(sum(pick.astype(BF16) for pick in picks), cot_ref[...])
    rows = (rows * weight).astype(BF16)
    for b, out in enumerate(outs):
        out[...] = rows[b * cap : (b + 1) * cap]


def forward(cap, groups, *refs):
    blocks, (gate_ref, up_ref), (x_ref, pre_ref, act_ref) = refs[:groups], refs[groups:-3], refs[-3:]

    @pl.when(pl.program_id(0) == 0)
    def _():
        x_ref[...] = jnp.concatenate([block[...] for block in blocks], axis=0)

    x = x_ref[...]
    gate_pre = dot_nn(x, gate_ref[0])
    up_pre = dot_nn(x, up_ref[0])
    pre_ref[0] = gate_pre
    pre_ref[1] = up_pre
    act_ref[...] = (gate_pre * jax.nn.sigmoid(gate_pre) * up_pre).astype(BF16)


def backward(c_ref, down_ref, pre_ref, grad_ref):
    hidden_grad = dot_nt(c_ref[...], down_ref[0])
    gate_pre, up_pre = pre_ref[0], pre_ref[1]
    s = jax.nn.sigmoid(gate_pre)
    grad_ref[0] = (hidden_grad * up_pre * s * (1.0 + gate_pre * (1.0 - s))).astype(BF16)
    grad_ref[1] = (hidden_grad * gate_pre * s).astype(BF16)


def join(*refs):
    blocks, out_ref = refs[:-1], refs[-1]
    out_ref[...] = jnp.concatenate([block[...] for block in blocks], axis=0)


def expert_rows(cap, act_ref, down_ref, *outs):
    rows = dot_nn(act_ref[...], down_ref[0])
    for b, out in enumerate(outs):
        out[...] = rows[b * cap : (b + 1) * cap].astype(BF16)


def input_rows(cap, grad_ref, gate_ref, up_ref, *outs):
    rows = dot_nt(grad_ref[0], gate_ref[0]) + dot_nt(grad_ref[1], up_ref[0])
    for b, out in enumerate(outs):
        out[...] = rows[b * cap : (b + 1) * cap].astype(BF16)


def both(own_ref, other_ref, *at):
    if at:
        return jnp.concatenate([own_ref[at[0]], other_ref[at[0]]], axis=0)
    return jnp.concatenate([own_ref[...], other_ref[...]], axis=0)


def store_at_step(outs, value):
    for n, out in enumerate(outs):

        @pl.when(pl.program_id(0) == n)
        def _(out=out):
            out[...] = value


def down_share(order_ref, act_own, act_other, c_own, c_other, *outs_and_scratch):
    *outs, turned = outs_and_scratch

    @pl.when(pl.program_id(0) == 0)
    def _():
        turned[...] = both(act_own, act_other).T

    store_at_step(outs, dot_nn(turned[...], both(c_own, c_other)).astype(BF16))


def gate_up_share(order_ref, x_own, x_other, g_own, g_other, *outs):
    half = len(outs) // 2
    turned = both(x_own, x_other).T
    store_at_step(outs[:half], dot_nn(turned, both(g_own, g_other, 0)).astype(BF16))
    store_at_step(outs[half:], dot_nn(turned, both(g_own, g_other, 1)).astype(BF16))


def add_kernel(left_ref, right_ref, out_ref):
    out_ref[...] = (left_ref[...].astype(F32) + right_ref[...].astype(F32)).astype(out_ref.dtype)


def added(name, dtype, left, right):
    return pl.pallas_call(
        add_kernel,
        out_shape=jax.ShapeDtypeStruct(left.shape, dtype),
        compiler_params=params(),
        cost_estimate=cost(0, 0),
        name=name,
    )(left, right)


def end_kernel(end_ref, alone_ref, left_ref, right_ref, out_ref):
    @pl.when(end_ref[0] == 1)
    def _():
        out_ref[...] = alone_ref[...]

    @pl.when(end_ref[0] == 0)
    def _():
        out_ref[...] = (left_ref[...].astype(F32) + right_ref[...].astype(F32)).astype(BF16)


def at_end(kernel, name, end, *parts):
    smem, vmem = pl.BlockSpec(memory_space=pltpu.SMEM), pl.BlockSpec(memory_space=pltpu.VMEM)
    return pl.pallas_call(
        kernel,
        out_shape=jax.ShapeDtypeStruct(parts[0].shape, BF16),
        in_specs=[smem] + [vmem] * len(parts),
        out_specs=vmem,
        compiler_params=params(),
        cost_estimate=cost(0, 0),
        name=name,
    )(end, *parts)


def final_kernel(end_ref, near_ref, last_ref, inner_ref, middle_ref, out_ref):
    last = last_ref[...].astype(F32)

    @pl.when(end_ref[0] == 1)
    def _():
        out_ref[...] = (near_ref[...].astype(F32) + last).astype(BF16)

    @pl.when(end_ref[0] == 0)
    def _():
        inner = inner_ref[...].astype(F32) + middle_ref[...].astype(F32)
        out_ref[...] = (inner + last).astype(BF16)


def combine(cap, groups, me_ref, ids_ref, gates_ref, cot_ref, *refs):
    outs, grads = refs[:groups], refs[groups : 2 * groups]
    mixed_ref, token_ref, dots_ref = refs[2 * groups :]
    picks = [pick.astype(BF16) for pick in picks_of(ids_ref[...], cap, groups, me_ref[0])]
    gates = gates_ref[...]
    count, width = mixed_ref.shape
    eye = lax.broadcasted_iota(jnp.int32, (count, count), 0) == lax.broadcasted_iota(
        jnp.int32, (count, count), 1
    )
    weights = [
        jnp.sum(jnp.where(eye, gates[k : k + 1], 0.0), axis=1, keepdims=True)
        for k in range(len(picks))
    ]
    tile = tile_of(width, 512)
    dots = [0.0] * len(picks)
    for start in range(0, width, tile):
        cols = slice(start, start + tile)
        rows = jnp.concatenate([ref[:, cols] for ref in outs], axis=0)
        cot = cot_ref[:, cols].astype(F32)
        mixed = 0.0
        for k, pick in enumerate(picks):
            picked = dot_tn(pick, rows)
            mixed = mixed + weights[k] * picked
            dots[k] = dots[k] + jnp.sum(cot * picked, axis=1, keepdims=True)
        mixed_ref[:, cols] = mixed.astype(BF16)
        rows = jnp.concatenate([ref[:, cols] for ref in grads], axis=0)
        token_ref[:, cols] = dot_tn(sum(picks), rows).astype(BF16)
    dots_ref[...] = jnp.concatenate(
        [jnp.sum(jnp.where(eye, dot, 0.0), axis=0, keepdims=True) for dot in dots], axis=0
    )


def after(value, *others):
    return lax.optimization_barrier((value, others))[0]


def rows_of_core(core, count, cols, own, other):
    rows = jnp.concatenate([own, other], axis=0).reshape(-1, count, 2, cols)
    return lax.dynamic_index_in_dim(rows, core, 2, keepdims=False)


def down_shares(order, cols, name, act, act_other, c_rows, c_other):
    total, ff = act.shape
    count = order.shape[0]
    block = pl.BlockSpec((total, cols), lambda n, order_ref: (0, order_ref[n]))
    return pl.pallas_call(
        down_share,
        out_shape=[jax.ShapeDtypeStruct((ff, cols), BF16)] * count,
        grid_spec=pltpu.PrefetchScalarGridSpec(
            num_scalar_prefetch=1,
            grid=(count,),
            in_specs=[whole((total, ff))] * 2 + [block] * 2,
            out_specs=[whole((ff, cols))] * count,
            scratch_shapes=[pltpu.VMEM((ff, 2 * total), BF16)],
        ),
        compiler_params=params(),
        cost_estimate=cost(4 * total * count * cols * ff, 5e6),
        name=name,
    )(order, act, act_other, c_rows, c_other)


def gate_up_shares(order, cols, name, x_rows, x_other, grads, grads_other):
    total, width = x_rows.shape
    ff = grads.shape[2]
    count = order.shape[0]
    block = pl.BlockSpec((total, cols), lambda n, order_ref: (0, order_ref[n]))
    return pl.pallas_call(
        gate_up_share,
        out_shape=[jax.ShapeDtypeStruct((cols, ff), BF16)] * (2 * count),
        grid_spec=pltpu.PrefetchScalarGridSpec(
            num_scalar_prefetch=1,
            grid=(count,),
            in_specs=[block] * 2 + [whole((2, total, ff))] * 2,
            out_specs=[whole((cols, ff))] * (2 * count),
        ),
        compiler_params=params(),
        cost_estimate=cost(8 * total * count * cols * ff, 6e6),
        name=name,
    )(order, x_rows, x_other, grads, grads_other)


def add(part, own):
    return (part.astype(F32) + own.astype(F32)).astype(BF16)


class LineSum:
    def __init__(self, share, chips, chip):
        self.share, self.chips, self.chip = share, chips, chip
        self.got = None
        self.steps = 0

    def share_at(self, index):
        index = jnp.clip(index, 0, self.chips - 1)
        return lax.dynamic_index_in_dim(self.share, index, 0, keepdims=False)

    def pairs(self, s):
        last = self.chips - 1
        up = [(i, i + 1) for i in range(s)]
        down = [(last - a, last - b) for a, b in up]
        return [[(2 * a + c, 2 * b + c) for a, b in way for c in (0, 1)] for way in (up, down)]

    def message(self, index, side):
        own = self.share_at(index)
        return own if self.got is None else add(self.got[side], own)

    def step(self):
        self.steps += 1
        s, chip, chips = self.steps, self.chip, self.chips
        up, down = self.pairs(s)
        if 2 * s < chips - 1:
            index = jnp.where(chip < s, chips - s + chip, chip - chips + s)
            sent = lax.ppermute(self.message(index, 0), "dp", up + down)
            self.got = (sent, sent)
        else:
            self.got = (
                lax.ppermute(self.message(chips - s + chip, 0), "dp", up),
                lax.ppermute(self.message(chip - chips + s, 1), "dp", down),
            )

    def total(self):
        own = self.share_at(self.chip).astype(F32)
        return (own + self.got[0].astype(F32) + self.got[1].astype(F32)).astype(BF16)


def relocated(total, turn, partner, me, groups):
    if turn is not None:
        return lax.ppermute(total, "expert", [(i, i ^ turn) for i in range(groups)]).astype(F32)[None]
    is_mate = (partner == me)[:, None, None]
    parts = jnp.where(is_mate, total[None], jnp.zeros_like(total)[None])
    parts = lax.all_to_all(parts, "expert", split_axis=0, concat_axis=0, tiled=True)
    mate = lax.dynamic_index_in_dim(partner, me, 0, keepdims=False)
    return lax.dynamic_index_in_dim(parts, mate, 0, keepdims=True).astype(F32)


def shards(tokens, cotangent, expert_ids, gate_weights, partner, w_gate, w_up, w_down):
    args = (tokens, cotangent, expert_ids.T, gate_weights.T, partner, w_gate, w_up, w_down)
    if lax.axis_size("expert") == 4:
        turns = [functools.partial(layer, turn) for turn in (1, 2, 3)]
        return lax.switch(partner[0] - 1, turns, *args)
    return layer(None, *args)


def layer(turn, tokens, cotangent, ids, gates, partner, w_gate, w_up, w_down):
    groups = lax.axis_size("expert")
    replicas = lax.axis_size("dp")
    me = lax.axis_index("expert")
    replica = lax.axis_index("dp")
    chips, chip, core = replicas // 2, replica // 2, replica % 2
    count, width = tokens.shape
    top = ids.shape[0]
    ff = w_gate.shape[2]
    cap = min(count, 5 * count * top // (4 * groups))
    total = groups * cap
    cols = width // replicas
    me_arr = me.astype(jnp.int32).reshape(1)
    smem = pl.BlockSpec(memory_space=pltpu.SMEM)
    vmem = pl.BlockSpec(memory_space=pltpu.VMEM)
    block_shape = jax.ShapeDtypeStruct((cap, width), BF16)

    def exchange(blocks):
        return [blocks[0]] + [
            lax.ppermute(blocks[b], "expert", [(i, i ^ b) for i in range(groups)])
            for b in range(1, groups)
        ]

    def swap(part):
        return lax.ppermute(part, "dp", [(i, i ^ 1) for i in range(replicas)])

    def joined(blocks, name):
        return pl.pallas_call(
            join,
            out_shape=jax.ShapeDtypeStruct((total, blocks[0].shape[1]), BF16),
            in_specs=[vmem] * groups,
            out_specs=vmem,
            compiler_params=params(),
            cost_estimate=cost(0, 4 * total * blocks[0].shape[1]),
            name=name,
        )(*blocks)

    x_blocks = pl.pallas_call(
        functools.partial(place_tokens, cap, groups),
        out_shape=[block_shape] * groups,
        in_specs=[smem, vmem, vmem],
        out_specs=[vmem] * groups,
        compiler_params=params(),
        name="place_tokens",
    )(me_arr, ids, tokens)
    c_blocks = pl.pallas_call(
        functools.partial(place_grads, cap, groups),
        out_shape=[block_shape] * groups,
        in_specs=[smem, vmem, vmem, vmem],
        out_specs=[vmem] * groups,
        compiler_params=params(),
        name="place_grads",
    )(me_arr, ids, gates, cotangent)
    x_blocks = exchange(x_blocks)
    c_blocks = exchange(c_blocks)

    tile = tile_of(ff, 256)
    x_rows, pre, act = pl.pallas_call(
        functools.partial(forward, cap, groups),
        out_shape=[
            jax.ShapeDtypeStruct((total, width), BF16),
            jax.ShapeDtypeStruct((2, total, ff), F32),
            jax.ShapeDtypeStruct((total, ff), BF16),
        ],
        grid=(ff // tile,),
        in_specs=[whole((cap, width))] * groups
        + [pl.BlockSpec((1, width, tile), lambda j: (0, 0, j))] * 2,
        out_specs=[
            whole((total, width)),
            pl.BlockSpec((2, total, tile), lambda j: (0, 0, j)),
            pl.BlockSpec((total, tile), lambda j: (0, j)),
        ],
        compiler_params=params(),
        cost_estimate=cost(4 * total * width * ff, 10e6),
        name="forward",
    )(*x_blocks, w_gate, w_up)
    act_other = swap(act)

    wide = tile_of(width, 512)

    def run_backward(c_rows):
        return pl.pallas_call(
            backward,
            out_shape=jax.ShapeDtypeStruct((2, total, ff), BF16),
            grid=(ff // tile,),
            in_specs=[
                whole((total, width)),
                pl.BlockSpec((1, tile, width), lambda j: (0, j, 0)),
                pl.BlockSpec((2, total, tile), lambda j: (0, 0, j)),
            ],
            out_specs=pl.BlockSpec((2, total, tile), lambda j: (0, 0, j)),
            compiler_params=params(),
            cost_estimate=cost(2 * total * width * ff, 10e6),
            name="backward",
        )(c_rows, w_down, pre)

    def run_expert_rows(act):
        return pl.pallas_call(
            functools.partial(expert_rows, cap),
            out_shape=[block_shape] * groups,
            grid=(width // wide,),
            in_specs=[whole((total, ff)), pl.BlockSpec((1, ff, wide), lambda j: (0, 0, j))],
            out_specs=[pl.BlockSpec((cap, wide), lambda j: (0, j))] * groups,
            compiler_params=params(),
            cost_estimate=cost(2 * total * width * ff, 5e6),
            name="expert_rows",
        )(act, w_down)

    def run_input_rows(grads):
        return pl.pallas_call(
            functools.partial(input_rows, cap),
            out_shape=[block_shape] * groups,
            grid=(width // wide,),
            in_specs=[whole((2, total, ff))] + [pl.BlockSpec((1, wide, ff), lambda j: (0, j, 0))] * 2,
            out_specs=[pl.BlockSpec((cap, wide), lambda j: (0, j))] * groups,
            compiler_params=params(),
            cost_estimate=cost(4 * total * width * ff, 9e6),
            name="input_rows",
        )(grads, w_gate, w_up)

    if turn is not None and chips == 4 and cols % 128 == 0:
        low = chip < 2
        end = ((chip == 0) | (chip == 3)).astype(jnp.int32).reshape(1)
        order = (2 * jnp.where(low, 3 - jnp.arange(4), jnp.arange(4)) + core).astype(jnp.int32)

        def swap_ends(part):
            return lax.ppermute(part, "dp", [(i, i ^ 2) for i in range(replicas)])

        def swap_middle(part):
            pairs = [(2, 4), (4, 2), (3, 5), (5, 3), (0, 1), (1, 0), (6, 7), (7, 6)]
            return lax.ppermute(part, "dp", pairs)

        def to_mate(part):
            return lax.ppermute(part, "expert", [(i, i ^ turn) for i in range(groups)])

        c_rows = joined(after(c_blocks, act), "join_grads")
        c_other, x_other = swap(c_rows), swap(x_rows)
        grads = run_backward(c_rows)
        d_a, d_b, d_c, d_d = down_shares(
            order, cols, "down_shares", act, act_other, c_rows, after(c_other, grads)
        )
        d_1, d_2 = swap_ends(d_a), swap_ends(after(d_b, d_a))
        grads_other = swap(after(grads, d_a))

        out_rows = run_expert_rows(after(act, d_a))
        out_blocks = exchange(out_rows)
        g_a, g_b, u_a, u_b = gate_up_shares(
            order[:2], cols, "gate_up_far", x_rows, x_other, grads, after(grads_other, *out_rows)
        )

        m = added("down_mid1", BF16, *after((d_1, d_a), g_a))
        d_m1, g_1 = swap_middle(m), swap_ends(after(g_a, m))
        grad_rows = run_input_rows(after(grads, m))
        grad_blocks = exchange(grad_rows)

        m = added("down_mid2", BF16, *after((d_2, d_b), *grad_rows))
        d_m2, u_1 = swap_middle(m), swap_ends(after(u_a, m))
        g_c, g_d, u_c, u_d = gate_up_shares(
            order[2:], cols, "gate_up_near", x_rows, x_other, grads, after(grads_other, m)
        )

        m = added("gate_mid1", BF16, *after((g_1, g_a), g_c))
        g_m1 = swap_middle(m)
        e = at_end(end_kernel, "down_last", end, *after((d_c, d_m1, d_d), m, *out_blocks))
        d_3 = swap_ends(e)
        m = added("up_mid1", BF16, *after((u_1, u_a), e))
        u_m1, g_2 = swap_middle(m), swap_ends(after(g_b, m))

        t = at_end(final_kernel, "down_sum", end, *after((d_d, d_3, d_c, d_m2), m, *grad_blocks))
        d_t, u_2 = to_mate(t), swap_ends(after(u_b, t))
        m = added("gate_mid2", BF16, *after((g_2, g_b), t))
        g_m2 = swap_middle(m)
        e = at_end(end_kernel, "gate_last", end, *after((g_c, g_m1, g_d), m))
        g_3 = swap_ends(e)
        m = added("up_mid2", BF16, *after((u_2, u_b), e))
        u_m2 = swap_middle(m)
        e = at_end(end_kernel, "up_last", end, *after((u_c, u_m1, u_d), m))
        u_3 = swap_ends(e)
        t = at_end(final_kernel, "gate_sum", end, *after((g_d, g_3, g_c, g_m2), e))
        g_t = to_mate(t)
        t = at_end(final_kernel, "up_sum", end, *after((u_d, u_3, u_c, u_m2), t))
        u_t = to_mate(t)
        slot_down, slot_gate, slot_up = [part.astype(F32)[None] for part in (d_t, g_t, u_t)]
    else:
        c_rows = joined(c_blocks, "join_grads")
        grads = run_backward(c_rows)
        out_blocks = exchange(run_expert_rows(act))
        grad_blocks = exchange(run_input_rows(grads))
        acts = jnp.concatenate([act, act_other], axis=0)
        both_grads = jnp.concatenate([grads, swap(grads)], axis=1)
        c_both = rows_of_core(core, chips, cols, c_rows, swap(c_rows))
        x_both = rows_of_core(core, chips, cols, x_rows, swap(x_rows))

        def dot(spec, left, right):
            return jnp.einsum(spec, left, right, preferred_element_type=F32).astype(BF16)

        lines = [
            LineSum(share, chips, chip)
            for share in (
                dot("rf,rzc->zfc", acts, c_both),
                dot("rzc,rf->zcf", x_both, both_grads[0]),
                dot("rzc,rf->zcf", x_both, both_grads[1]),
            )
        ]
        for _ in range(1, chips):
            for line in lines:
                line.step()
        slot_down, slot_gate, slot_up = [
            relocated(line.total(), turn, partner, me, groups) for line in lines
        ]

    mixed_out, token_grad, gate_grad = pl.pallas_call(
        functools.partial(combine, cap, groups),
        out_shape=[
            jax.ShapeDtypeStruct((count, width), BF16),
            jax.ShapeDtypeStruct((count, width), BF16),
            jax.ShapeDtypeStruct((top, count), F32),
        ],
        in_specs=[smem] + [vmem] * (3 + 2 * groups),
        out_specs=[vmem] * 3,
        compiler_params=params(),
        cost_estimate=cost(6 * total * width * count, 6e6),
        name="combine",
    )(me_arr, ids, gates, cotangent, *out_blocks, *grad_blocks)
    return mixed_out, token_grad, gate_grad.T, slot_gate, slot_up, slot_down


def solution(mesh):
    rows = P(("dp", "expert"), None)
    in_specs = (
        rows,
        rows,
        rows,
        rows,
        P(),
        P("expert", None, None),
        P("expert", None, None),
        P("expert", None, None),
    )
    out_specs = (
        rows,
        rows,
        rows,
        P("expert", "dp", None),
        P("expert", "dp", None),
        P("expert", None, "dp"),
    )
    return jax.shard_map(shards, mesh=mesh, in_specs=in_specs, out_specs=out_specs, check_vma=False)
```

time: 194 us -> 148 us (0.76)
  starting transfers between devices: 64.1 us -> 36.8 us
  waiting for transfers between devices: 73.4 us -> 58.6 us
  Pallas kernels: 31.4 us -> 40.4 us
  local copies, waits for them, and re-layouts: 16.2 us -> 7.22 us
  other arithmetic: 5.66 us -> 2.81 us
    ppermute x24 -> x18, starting transfers between devices: 49.6 us -> 16.6 us  [the longest x9 14.8 us: swap_ends(): return lax.ppermute(part, 'dp', [(i, i ^ 2) for i in range(replicas)])]
    unnamed x51 -> x0, local copies, waits for them, and re-layouts: 13.3 us -> none
    pallas_call x9 -> x23, Pallas kernels: 31.4 us -> 40.4 us  [the longest x2 9.14 us: gate_up_shares(): pl.pallas_call(gate_up_share, out_shape=[jax.ShapeDtypeStruct((cols, ff),...]
    ppermute x12, waiting for transfers between devices: 28.4 us -> 20.2 us  [exchange(): lax.ppermute(blocks[b], 'expert', [(i, i ^ b) for i in range(groups)])]
    cond x0 -> x60, local copies, waits for them, and re-layouts: none -> 7.15 us
    ppermute x24 -> x18, waiting for transfers between devices: 45.1 us -> 38.5 us  [the longest x9 25.4 us: swap_ends(): return lax.ppermute(part, 'dp', [(i, i ^ 2) for i in range(replicas)])]
    ppermute x12, starting transfers between devices: 13.8 us -> 19 us  [exchange(): lax.ppermute(blocks[b], 'expert', [(i, i ^ b) for i in range(groups)])]
    convert_element_type x9 -> x0, other arithmetic: 2.72 us -> none  [the longest x6 2.28 us: add(): return (part.astype(F32) + own.astype(F32)).astype(BF16)]
  transfers between devices with their start and end apart: 40 -> 34, of which waited for: 17 -> 14; matrix products, arithmetic and copies ran while one was open for 5% -> 1% of each run, Pallas kernels for 16% -> 26%
where the time goes in v2:
time: 148 us
  waiting for transfers between devices  58.6 us (40%)
  Pallas kernels  40.4 us (27%)
  starting transfers between devices  36.8 us (25%)
  local copies, waits for them, and re-layouts  7.22 us (5%)
  other arithmetic  2.81 us (2%)
    ppermute x9, waiting for transfers between devices, swap_ends(): return lax.ppermute(part, 'dp', [(i, i ^ 2) for i in range(replicas)])  25.4 us
    ppermute x12, waiting for transfers between devices, exchange(): lax.ppermute(blocks[b], 'expert', [(i, i ^ b) for i in range(groups)])  20.2 us
    ppermute x12, starting transfers between devices, exchange(): lax.ppermute(blocks[b], 'expert', [(i, i ^ b) for i in range(groups)])  19 us
    ppermute x9, starting transfers between devices, swap_ends(): return lax.ppermute(part, 'dp', [(i, i ^ 2) for i in range(replicas)])  14.8 us
    ppermute x3, waiting for transfers between devices, to_mate(): return lax.ppermute(part, 'expert', [(i, i ^ turn) for i in range(groups)])  13 us
    pallas_call x2, Pallas kernels, gate_up_shares(): pl.pallas_call(gate_up_share, out_shape=[jax.ShapeDtypeStruct((cols, ff),...  9.14 us
    cond x60, local copies, waits for them, and re-layouts  7.15 us
    pallas_call x1, Pallas kernels, layer(): pl.pallas_call(functools.partial(forward, cap, groups), out_shape=[jax.Sh...  5.8 us
  transfers between devices with their start and end apart: 34, of which 14 were waited for; matrix products, arithmetic and copies ran while one was open for 1% of the time, Pallas kernels for 26%

profile of v2, /device:TPU:0, one launch (start us, length us, event | category | flops | bytes accessed | tf_op | source)
XLA Modules:
  0.0 147.5 jit_solution(8835474298195816029)
XLA Ops:
  1.3 146.2 %conditional.1 = (bf16[128,2048]{1,0:T(8,128)(2,1)}, bf16[128,2048]{1,0:T(8,128)(2,1)}, f32[128,2]{0,1:T(2,128)}, f32[1,256,768]{2,1,0:T(8,128)}, f32[1,256,768]{2,1,0:T(8,128)}, /*index=5*/f32[1,768,256]{2,1,0:T(8,128)}) conditional(s32[]{:T(128)} %bitcast.27, (s32[2,128]{1,0:T(2,128)}, bf16[128,2048]{1,0:T(8,128)(2,1)}, ...), branch_computations={%region_0.1_spmd, %region_1.2_spmd, %region_2.3_spmd} | conditional | flops 610869 | bytes 152861680 | solution.py:342
  1.3 1.7 %place_tokens.3 = (bf16[80,2048]{1,0:T(8,128)(2,1)S(1)}, bf16[80,2048]{1,0:T(8,128)(2,1)S(1)}, bf16[80,2048]{1,0:T(8,128)(2,1)S(1)}, bf16[80,2048]{1,0:T(8,128)(2,1)S(1)}) custom-call(s32[1]{0:T(128)} %bitcast.me_ref, s32[2,128]{1,0:T(2,128)} %get-tuple-element.42.ids_ref, bf16[128,2048]{1,0:T(8,128)(2,1)} %get-tuple-element.334.tok_ref), custom_call_target="tpu_custom_call" | custom-call | tf_op jit(solution)/shard_map/cond/branch_0_fun/place_tokens/pallas_call | solution.py:383
  3.0 3.0 %collective-permute-start = (bf16[80,2048]{1,0:T(8,128)(2,1)S(1)}, bf16[80,2048]{1,0:T(8,128)(2,1)S(1)}, u32[]{:S(2)}, u32[]{:S(2)}) collective-permute-start(bf16[80,2048]{1,0:T(8,128)(2,1)S(1)} %get-tuple-element.47), channel_id=1, source_target_pairs={{0,1},{1,0},{2,3},{3,2},{4,5},{5,4},{6,7},{7,6},{8,9},{9,8},{10,11... | collective-permute-start | bytes 983048 | tf_op jit(solution)/shard_map/cond/branch_0_fun/ppermute | solution.py:365
  6.0 1.5 %collective-permute-start.1 = (bf16[80,2048]{1,0:T(8,128)(2,1)S(1)}, bf16[80,2048]{1,0:T(8,128)(2,1)S(1)}, u32[]{:S(2)}, u32[]{:S(2)}) collective-permute-start(bf16[80,2048]{1,0:T(8,128)(2,1)S(1)} %get-tuple-element.48), channel_id=1, source_target_pairs={{0,2},{1,3},{2,0},{3,1},{4,6},{5,7},{6,4},{7,5},{8,10},{9,11},{10,... | collective-permute-start | bytes 983048 | tf_op jit(solution)/shard_map/cond/branch_0_fun/ppermute | solution.py:365
  7.5 1.7 %place_grads.3 = (bf16[80,2048]{1,0:T(8,128)(2,1)S(1)}, bf16[80,2048]{1,0:T(8,128)(2,1)S(1)}, bf16[80,2048]{1,0:T(8,128)(2,1)S(1)}, bf16[80,2048]{1,0:T(8,128)(2,1)S(1)}) custom-call(s32[1]{0:T(128)} %bitcast.me_ref, s32[2,128]{1,0:T(2,128)} %get-tuple-element.42.ids_ref, f32[2,128]{1,0:T(2,128)} %get-tuple-element.43.gates_ref, ...), custom_call_target="tpu_custom_call" | custom-call | tf_op jit(solution)/shard_map/cond/branch_0_fun/place_grads/pallas_call | solution.py:391
  9.3 2.0 %collective-permute-start.4 = (bf16[80,2048]{1,0:T(8,128)(2,1)S(1)}, bf16[80,2048]{1,0:T(8,128)(2,1)S(1)}, u32[]{:S(2)}, u32[]{:S(2)}) collective-permute-start(bf16[80,2048]{1,0:T(8,128)(2,1)S(1)} %get-tuple-element.54), channel_id=1, source_target_pairs={{0,1},{1,0},{2,3},{3,2},{4,5},{5,4},{6,7},{7,6},{8,9},{9,8},{10,11... | collective-permute-start | bytes 983048 | tf_op jit(solution)/shard_map/cond/branch_0_fun/ppermute | solution.py:365
  11.3 1.5 %collective-permute-start.5 = (bf16[80,2048]{1,0:T(8,128)(2,1)S(1)}, bf16[80,2048]{1,0:T(8,128)(2,1)S(1)}, u32[]{:S(2)}, u32[]{:S(2)}) collective-permute-start(bf16[80,2048]{1,0:T(8,128)(2,1)S(1)} %get-tuple-element.55), channel_id=1, source_target_pairs={{0,2},{1,3},{2,0},{3,1},{4,6},{5,7},{6,4},{7,5},{8,10},{9,11},{10,... | collective-permute-start | bytes 983048 | tf_op jit(solution)/shard_map/cond/branch_0_fun/ppermute | solution.py:365
  12.8 1.7 %collective-permute-done.refs_1_ = bf16[80,2048]{1,0:T(8,128)(2,1)S(1)} collective-permute-done((bf16[80,2048]{1,0:T(8,128)(2,1)S(1)}, bf16[80,2048]{1,0:T(8,128)(2,1)S(1)}, u32[]{:S(2)}, u32[]{:S(2)}) %collective-permute-start) | collective-permute-done | bytes 327712 | tf_op jit(solution)/shard_map/cond/branch_0_fun/ppermute | solution.py:365
  14.5 3.0 %collective-permute-start.6 = (bf16[80,2048]{1,0:T(8,128)(2,1)S(1)}, bf16[80,2048]{1,0:T(8,128)(2,1)S(1)}, u32[]{:S(2)}, u32[]{:S(2)}) collective-permute-start(bf16[80,2048]{1,0:T(8,128)(2,1)S(1)} %get-tuple-element.56), channel_id=1, source_target_pairs={{0,3},{1,2},{2,1},{3,0},{4,7},{5,6},{6,5},{7,4},{8,11},{9,10},{10,... | collective-permute-start | bytes 983048 | tf_op jit(solution)/shard_map/cond/branch_0_fun/ppermute | solution.py:365
  17.6 6.1 %collective-permute-done.1.refs_2_ = bf16[80,2048]{1,0:T(8,128)(2,1)S(1)} collective-permute-done((bf16[80,2048]{1,0:T(8,128)(2,1)S(1)}, bf16[80,2048]{1,0:T(8,128)(2,1)S(1)}, u32[]{:S(2)}, u32[]{:S(2)}) %collective-permute-start.1) | collective-permute-done | bytes 327712 | tf_op jit(solution)/shard_map/cond/branch_0_fun/ppermute | solution.py:365
  23.7 5.8 %forward.3 = (bf16[320,2048]{1,0:T(8,128)(2,1)}, f32[2,320,768]{2,1,0:T(8,128)S(1)}, bf16[320,768]{1,0:T(8,128)(2,1)S(1)}) custom-call(bf16[80,2048]{1,0:T(8,128)(2,1)S(1)} %get-tuple-element.46.refs_0_, bf16[80,2048]{1,0:T(8,128)(2,1)S(1)} %collective-permute-done.refs_1_, bf16[80,2048]{1,0:T(8,128)(2,1)S(1)} %collective-permute-done.1.refs_2_, ...), custom_call_target="tpu_custom_call" | custom-call | flops 1000 | bytes 1000 | tf_op jit(solution)/shard_map/cond/branch_0_fun/forward/pallas_call | solution.py:403
  29.5 6.8 %collective-permute-done.5.refs_2_ = bf16[80,2048]{1,0:T(8,128)(2,1)S(1)} collective-permute-done((bf16[80,2048]{1,0:T(8,128)(2,1)S(1)}, bf16[80,2048]{1,0:T(8,128)(2,1)S(1)}, u32[]{:S(2)}, u32[]{:S(2)}) %collective-permute-start.5) | collective-permute-done | bytes 327712 | tf_op jit(solution)/shard_map/cond/branch_0_fun/ppermute | solution.py:365
  37.0 1.5 %copy-done.1 = f32[2,320,768]{2,1,0:T(8,128)S(1)} copy-done((f32[2,320,768]{2,1,0:T(8,128)S(1)}, f32[2,320,768]{2,1,0:T(8,128)}, u32[]{:S(2)}) %copy-start.1) | copy-done | bytes 1966104 | tf_op jit(solution)/shard_map/cond
  38.6 3.8 %backward.3.g_own.grad_ref = bf16[2,320,768]{2,1,0:T(8,128)(2,1)S(1)} custom-call(bf16[320,2048]{1,0:T(8,128)(2,1)S(1)} %join_grads.3.c_ref.c_own, bf16[1,768,2048]{2,1,0:T(8,128)(2,1)} %get-tuple-element.346.down_ref, f32[2,320,768]{2,1,0:T(8,128)S(1)} %copy-done.1), custom_call_target="tpu_custom_call" | custom-call | flops 1000 | bytes 1000 | tf_op jit(solution)/shard_map/cond/branch_0_fun/backward/pallas_call | solution.py:427
  43.2 1.0 copy-done.13
  44.2 4.4 %down_shares.3 = (bf16[768,256]{1,0:T(8,128)(2,1)S(1)}, bf16[768,256]{1,0:T(8,128)(2,1)S(1)}, bf16[768,256]{1,0:T(8,128)(2,1)S(1)}, bf16[768,256]{1,0:T(8,128)(2,1)S(1)}) custom-call(s32[4]{0:T(128)S(1)} %fusion.1.order_ref, bf16[320,768]{1,0:T(8,128)(2,1)S(1)} %get-tuple-element.65.act_own.act_ref, bf16[320,768]{1,0:T(8,128)(2,1)S(1)} %copy-done.13, ...), custom_call_target="tpu_custom_call" | custom-call | flops 1000 | bytes 1000 | tf_op jit(solution)/shard_map/cond/branch_0_fun/down_shares/pallas_call | solution.py:249
  49.1 1.6 %collective-permute-start.11 = (bf16[768,256]{1,0:T(8,128)(2,1)S(1)}, bf16[768,256]{1,0:T(8,128)(2,1)S(1)}, u32[]{:S(2)}, u32[]{:S(2)}) collective-permute-start(bf16[768,256]{1,0:T(8,128)(2,1)S(1)} %get-tuple-element.75.right_ref), channel_id=1, source_target_pairs={{0,8},{4,12},{8,0},{12,4},{16,24},{20,28},{24,16},{28,20},{1,9},{5... | collective-permute-start | bytes 1179656 | tf_op jit(solution)/shard_map/cond/branch_0_fun/ppermute | solution.py:472
  51.2 2.8 %expert_rows.3 = (bf16[80,2048]{1,0:T(8,128)(2,1)S(1)}, bf16[80,2048]{1,0:T(8,128)(2,1)S(1)}, bf16[80,2048]{1,0:T(8,128)(2,1)S(1)}, bf16[80,2048]{1,0:T(8,128)(2,1)}) custom-call(bf16[320,768]{1,0:T(8,128)(2,1)S(1)} %get-tuple-element.65.act_own.act_ref, bf16[1,768,2048]{2,1,0:T(8,128)(2,1)S(1)} %copy-done.78), custom_call_target="tpu_custom_call" | custom-call | flops 1000 | bytes 1000 | tf_op jit(solution)/shard_map/cond/branch_0_fun/expert_rows/pallas_call | solution.py:443
  54.0 1.3 collective-permute-start.8
  55.3 5.1 %gate_up_far.3 = (bf16[256,768]{1,0:T(8,128)(2,1)S(1)}, bf16[256,768]{1,0:T(8,128)(2,1)S(1)}, bf16[256,768]{1,0:T(8,128)(2,1)}, bf16[256,768]{1,0:T(8,128)(2,1)S(1)}) custom-call(s32[2]{0:T(128)S(1)} %get-tuple-element.350.order_ref, bf16[320,2048]{1,0:T(8,128)(2,1)} %get-tuple-element.70.x_own, bf16[320,2048]{1,0:T(8,128)(2,1)} %collective-permute-done.12.x_other, ...), custom_call_target="tpu_custom_call" | custom-call | flops 1000 | bytes 1000 | tf_op jit(solution)/shard_map/cond/branch_0_fun/gate_up_far/pallas_call | solution.py:270
  62.0 1.6 %collective-permute-start.18 = (bf16[256,768]{1,0:T(8,128)(2,1)S(1)}, bf16[256,768]{1,0:T(8,128)(2,1)S(1)}, u32[]{:S(2)}, u32[]{:S(2)}) collective-permute-start(bf16[256,768]{1,0:T(8,128)(2,1)S(1)} %get-tuple-element.93.right_ref), channel_id=1, source_target_pairs={{0,8},{4,12},{8,0},{12,4},{16,24},{20,28},{24,16},{28,20},{1,9},{5... | collective-permute-start | bytes 1179656 | tf_op jit(solution)/shard_map/cond/branch_0_fun/ppermute | solution.py:472
  63.5 1.5 %collective-permute-start.9 = (bf16[80,2048]{1,0:T(8,128)(2,1)S(1)}, bf16[80,2048]{1,0:T(8,128)(2,1)S(1)}, u32[]{:S(2)}, u32[]{:S(2)}) collective-permute-start(bf16[80,2048]{1,0:T(8,128)(2,1)S(1)} %get-tuple-element.68), channel_id=1, source_target_pairs={{0,2},{1,3},{2,0},{3,1},{4,6},{5,7},{6,4},{7,5},{8,10},{9,11},{10,... | collective-permute-start | bytes 983048 | tf_op jit(solution)/shard_map/cond/branch_0_fun/ppermute | solution.py:365
  65.1 3.6 %input_rows.3 = (bf16[80,2048]{1,0:T(8,128)(2,1)S(1)}, bf16[80,2048]{1,0:T(8,128)(2,1)}, bf16[80,2048]{1,0:T(8,128)(2,1)}, bf16[80,2048]{1,0:T(8,128)(2,1)S(1)}) custom-call(bf16[2,320,768]{2,1,0:T(8,128)(2,1)S(1)} %backward.3.g_own.grad_ref, bf16[1,2048,768]{2,1,0:T(8,128)(2,1)S(1)} %copy-done.72, bf16[1,2048,768]{2,1,0:T(8,128)(2,1)S(1)} %copy-done.75), custom_call_target="tpu_custom_call" | custom-call | flops 1000 | bytes 1000 | tf_op jit(solution)/shard_map/cond/branch_0_fun/input_rows/pallas_call | solution.py:455
  69.5 1.5 %collective-permute-start.10 = (bf16[80,2048]{1,0:T(8,128)(2,1)}, bf16[80,2048]{1,0:T(8,128)(2,1)}, u32[]{:S(2)}, u32[]{:S(2)}) collective-permute-start(bf16[80,2048]{1,0:T(8,128)(2,1)} %get-tuple-element.69), channel_id=1, source_target_pairs={{0,3},{1,2},{2,1},{3,0},{4,7},{5,6},{6,5},{7,4},{8,11},{9,10},{10,... | collective-permute-start | bytes 983048 | tf_op jit(solution)/shard_map/cond/branch_0_fun/ppermute | solution.py:365
  72.6 2.1 %collective-permute-start.20 = (bf16[256,768]{1,0:T(8,128)(2,1)}, bf16[256,768]{1,0:T(8,128)(2,1)}, u32[]{:S(2)}, u32[]{:S(2)}) collective-permute-start(bf16[256,768]{1,0:T(8,128)(2,1)} %get-tuple-element.103.right_ref), channel_id=1, source_target_pairs={{0,8},{4,12},{8,0},{12,4},{16,24},{20,28},{24,16},{28,20},{1,9},{5... | collective-permute-start | bytes 1179656 | tf_op jit(solution)/shard_map/cond/branch_0_fun/ppermute | solution.py:472
  75.5 1.0 collective-permute-start.14
  76.4 1.5 %collective-permute-done.18.left_ref = bf16[256,768]{1,0:T(8,128)(2,1)S(1)} collective-permute-done((bf16[256,768]{1,0:T(8,128)(2,1)S(1)}, bf16[256,768]{1,0:T(8,128)(2,1)S(1)}, u32[]{:S(2)}, u32[]{:S(2)}) %collective-permute-start.18) | collective-permute-done | bytes 393248 | tf_op jit(solution)/shard_map/cond/branch_0_fun/ppermute | solution.py:472
  78.7 1.5 %collective-permute-start.15 = (bf16[80,2048]{1,0:T(8,128)(2,1)}, bf16[80,2048]{1,0:T(8,128)(2,1)}, u32[]{:S(2)}, u32[]{:S(2)}) collective-permute-start(bf16[80,2048]{1,0:T(8,128)(2,1)} %get-tuple-element.79), channel_id=1, source_target_pairs={{0,2},{1,3},{2,0},{3,1},{4,6},{5,7},{6,4},{7,5},{8,10},{9,11},{10,... | collective-permute-start | bytes 983048 | tf_op jit(solution)/shard_map/cond/branch_0_fun/ppermute | solution.py:365
  80.2 4.1 %gate_up_near.3 = (bf16[256,768]{1,0:T(8,128)(2,1)S(1)}, bf16[256,768]{1,0:T(8,128)(2,1)S(1)}, bf16[256,768]{1,0:T(8,128)(2,1)S(1)}, bf16[256,768]{1,0:T(8,128)(2,1)S(1)}) custom-call(s32[2]{0:T(128)S(1)} %get-tuple-element.349.order_ref, bf16[320,2048]{1,0:T(8,128)(2,1)} %get-tuple-element.70.x_own, bf16[320,2048]{1,0:T(8,128)(2,1)} %collective-permute-done.12.x_other, ...), custom_call_target="tpu_custom_call" | custom-call | flops 1000 | bytes 1000 | tf_op jit(solution)/shard_map/cond/branch_0_fun/gate_up_near/pallas_call | solution.py:270
  85.3 1.1 down_last.3
  86.4 2.5 %collective-permute-start.23 = (bf16[768,256]{1,0:T(8,128)(2,1)S(1)}, bf16[768,256]{1,0:T(8,128)(2,1)S(1)}, u32[]{:S(2)}, u32[]{:S(2)}) collective-permute-start(bf16[768,256]{1,0:T(8,128)(2,1)S(1)} %down_last.3), channel_id=1, source_target_pairs={{0,8},{4,12},{8,0},{12,4},{16,24},{20,28},{24,16},{28,20},{1,9},{5... | collective-permute-start | bytes 1179656 | tf_op jit(solution)/shard_map/cond/branch_0_fun/ppermute | solution.py:472
  89.0 1.2 collective-permute-start.16
  90.1 1.2 up_mid1.3
  91.5 5.5 %collective-permute-done.16.refs_7_ = bf16[80,2048]{1,0:T(8,128)(2,1)S(1)} collective-permute-done((bf16[80,2048]{1,0:T(8,128)(2,1)S(1)}, bf16[80,2048]{1,0:T(8,128)(2,1)S(1)}, u32[]{:S(2)}, u32[]{:S(2)}) %collective-permute-start.16) | collective-permute-done | bytes 327712 | tf_op jit(solution)/shard_map/cond/branch_0_fun/ppermute | solution.py:365
  97.1 1.9 %collective-permute-done.23.last_ref = bf16[768,256]{1,0:T(8,128)(2,1)S(1)} collective-permute-done((bf16[768,256]{1,0:T(8,128)(2,1)S(1)}, bf16[768,256]{1,0:T(8,128)(2,1)S(1)}, u32[]{:S(2)}, u32[]{:S(2)}) %collective-permute-start.23) | collective-permute-done | bytes 393248 | tf_op jit(solution)/shard_map/cond/branch_0_fun/ppermute | solution.py:472
  99.1 2.1 %collective-permute-start.28 = (bf16[256,768]{1,0:T(8,128)(2,1)S(1)}, bf16[256,768]{1,0:T(8,128)(2,1)S(1)}, u32[]{:S(2)}, u32[]{:S(2)}) collective-permute-start(bf16[256,768]{1,0:T(8,128)(2,1)S(1)} %copy-done.19), channel_id=1, source_target_pairs={{0,8},{4,12},{8,0},{12,4},{16,24},{20,28},{24,16},{28,20},{1,9},{5... | collective-permute-start | bytes 1179656 | tf_op jit(solution)/shard_map/cond/branch_0_fun/ppermute | solution.py:472
  101.2 6.2 %collective-permute-done.22.left_ref = bf16[256,768]{1,0:T(8,128)(2,1)S(1)} collective-permute-done((bf16[256,768]{1,0:T(8,128)(2,1)S(1)}, bf16[256,768]{1,0:T(8,128)(2,1)S(1)}, u32[]{:S(2)}, u32[]{:S(2)}) %collective-permute-start.22) | collective-permute-done | bytes 393248 | tf_op jit(solution)/shard_map/cond/branch_0_fun/ppermute | solution.py:472
  107.6 2.1 %collective-permute-start.25 = (bf16[256,768]{1,0:T(8,128)(2,1)S(1)}, bf16[256,768]{1,0:T(8,128)(2,1)S(1)}, u32[]{:S(2)}, u32[]{:S(2)}) collective-permute-start(bf16[256,768]{1,0:T(8,128)(2,1)S(1)} %gate_last.3), channel_id=1, source_target_pairs={{0,8},{4,12},{8,0},{12,4},{16,24},{20,28},{24,16},{28,20},{1,9},{5... | collective-permute-start | bytes 1179656 | tf_op jit(solution)/shard_map/cond/branch_0_fun/ppermute | solution.py:472
  109.7 6.1 %collective-permute-done.28.left_ref = bf16[256,768]{1,0:T(8,128)(2,1)S(1)} collective-permute-done((bf16[256,768]{1,0:T(8,128)(2,1)S(1)}, bf16[256,768]{1,0:T(8,128)(2,1)S(1)}, u32[]{:S(2)}, u32[]{:S(2)}) %collective-permute-start.28) | collective-permute-done | bytes 393248 | tf_op jit(solution)/shard_map/cond/branch_0_fun/ppermute | solution.py:472
  116.0 2.1 %collective-permute-start.30 = (bf16[256,768]{1,0:T(8,128)(2,1)S(1)}, bf16[256,768]{1,0:T(8,128)(2,1)S(1)}, u32[]{:S(2)}, u32[]{:S(2)}) collective-permute-start(bf16[256,768]{1,0:T(8,128)(2,1)S(1)} %up_last.3), channel_id=1, source_target_pairs={{0,8},{4,12},{8,0},{12,4},{16,24},{20,28},{24,16},{28,20},{1,9},{5... | collective-permute-start | bytes 1179656 | tf_op jit(solution)/shard_map/cond/branch_0_fun/ppermute | solution.py:472
  118.7 5.5 %collective-permute-done.25.last_ref = bf16[256,768]{1,0:T(8,128)(2,1)S(1)} collective-permute-done((bf16[256,768]{1,0:T(8,128)(2,1)S(1)}, bf16[256,768]{1,0:T(8,128)(2,1)S(1)}, u32[]{:S(2)}, u32[]{:S(2)}) %collective-permute-start.25) | collective-permute-done | bytes 393248 | tf_op jit(solution)/shard_map/cond/branch_0_fun/ppermute | solution.py:472
  125.0 3.3 %combine.3 = (bf16[128,2048]{1,0:T(8,128)(2,1)}, bf16[128,2048]{1,0:T(8,128)(2,1)}, f32[2,128]{1,0:T(2,128)}) custom-call(s32[1]{0:T(128)} %bitcast.me_ref, s32[2,128]{1,0:T(2,128)S(1)} %copy-done.84, f32[2,128]{1,0:T(2,128)S(1)} %copy-done.87, bf16[128,2048]{1,0:T(8,128)(2,1)S(1)} %copy-done.81, bf16[80,2048]{1,0:T(8,128)(2,1)S(1)} %get-tuple-element.66.refs_0_, ...), custom_call_target="tpu_custom_call" | custom-call | flops 1000 | bytes 1000 | tf_op jit(solution)/shard_map/cond/branch_0_fun/combine/pallas_call | solution.py:557
  128.3 2.6 %collective-permute-done.30.last_ref = bf16[256,768]{1,0:T(8,128)(2,1)S(1)} collective-permute-done((bf16[256,768]{1,0:T(8,128)(2,1)S(1)}, bf16[256,768]{1,0:T(8,128)(2,1)S(1)}, u32[]{:S(2)}, u32[]{:S(2)}) %collective-permute-start.30) | collective-permute-done | bytes 393248 | tf_op jit(solution)/shard_map/cond/branch_0_fun/ppermute | solution.py:472
  131.7 0.9 bitcast_convert_fusion
  132.6 5.9 %collective-permute-done.29 = bf16[256,768]{1,0:T(8,128)(2,1)S(1)} collective-permute-done((bf16[256,768]{1,0:T(8,128)(2,1)S(1)}, bf16[256,768]{1,0:T(8,128)(2,1)S(1)}, u32[]{:S(2)}, u32[]{:S(2)}) %collective-permute-start.29) | collective-permute-done | bytes 393248 | tf_op jit(solution)/shard_map/cond/branch_0_fun/ppermute | solution.py:479
  138.5 0.9 bitcast_convert_fusion.2
  139.5 7.1 %collective-permute-done.32 = bf16[256,768]{1,0:T(8,128)(2,1)S(1)} collective-permute-done((bf16[256,768]{1,0:T(8,128)(2,1)S(1)}, bf16[256,768]{1,0:T(8,128)(2,1)S(1)}, u32[]{:S(2)}, u32[]{:S(2)}) %collective-permute-start.32) | collective-permute-done | bytes 393248 | tf_op jit(solution)/shard_map/cond/branch_0_fun/ppermute | solution.py:479
  146.6 0.9 bitcast_convert_fusion.1
  (109 shorter events, 11.5 us)
Async XLA Ops:
  3.0 11.5 %collective-permute-start = (bf16[80,2048]{1,0:T(8,128)(2,1)S(1)}, bf16[80,2048]{1,0:T(8,128)(2,1)S(1)}, u32[]{:S(2)}, u32[]{:S(2)}) collective-permute-start(bf16[80,2048]{1,0:T(8,128)(2,1)S(1)} %get-tuple-element.47), channel_id=1, source_target_pairs={{0,1},{1,0},{2,3},{3,2},{4,5},{5,4},{6,7},{7,6},{8,9},{9,8},{10,11... | collective-permute-start | bytes 983048 | tf_op jit(solution)/shard_map/cond/branch_0_fun/ppermute | solution.py:365
  6.0 17.7 %collective-permute-start.1 = (bf16[80,2048]{1,0:T(8,128)(2,1)S(1)}, bf16[80,2048]{1,0:T(8,128)(2,1)S(1)}, u32[]{:S(2)}, u32[]{:S(2)}) collective-permute-start(bf16[80,2048]{1,0:T(8,128)(2,1)S(1)} %get-tuple-element.48), channel_id=1, source_target_pairs={{0,2},{1,3},{2,0},{3,1},{4,6},{5,7},{6,4},{7,5},{8,10},{9,11},{10,... | collective-permute-start | bytes 983048 | tf_op jit(solution)/shard_map/cond/branch_0_fun/ppermute | solution.py:365
  7.5 16.1 %collective-permute-start.2 = (bf16[80,2048]{1,0:T(8,128)(2,1)S(1)}, bf16[80,2048]{1,0:T(8,128)(2,1)S(1)}, u32[]{:S(2)}, u32[]{:S(2)}) collective-permute-start(bf16[80,2048]{1,0:T(8,128)(2,1)S(1)} %get-tuple-element.49), channel_id=1, source_target_pairs={{0,3},{1,2},{2,1},{3,0},{4,7},{5,6},{6,5},{7,4},{8,11},{9,10},{10,... | collective-permute-start | bytes 983048 | tf_op jit(solution)/shard_map/cond/branch_0_fun/ppermute | solution.py:365
  9.3 20.2 %collective-permute-start.4 = (bf16[80,2048]{1,0:T(8,128)(2,1)S(1)}, bf16[80,2048]{1,0:T(8,128)(2,1)S(1)}, u32[]{:S(2)}, u32[]{:S(2)}) collective-permute-start(bf16[80,2048]{1,0:T(8,128)(2,1)S(1)} %get-tuple-element.54), channel_id=1, source_target_pairs={{0,1},{1,0},{2,3},{3,2},{4,5},{5,4},{6,7},{7,6},{8,9},{9,8},{10,11... | collective-permute-start | bytes 983048 | tf_op jit(solution)/shard_map/cond/branch_0_fun/ppermute | solution.py:365
  11.3 25.0 %collective-permute-start.5 = (bf16[80,2048]{1,0:T(8,128)(2,1)S(1)}, bf16[80,2048]{1,0:T(8,128)(2,1)S(1)}, u32[]{:S(2)}, u32[]{:S(2)}) collective-permute-start(bf16[80,2048]{1,0:T(8,128)(2,1)S(1)} %get-tuple-element.55), channel_id=1, source_target_pairs={{0,2},{1,3},{2,0},{3,1},{4,6},{5,7},{6,4},{7,5},{8,10},{9,11},{10,... | collective-permute-start | bytes 983048 | tf_op jit(solution)/shard_map/cond/branch_0_fun/ppermute | solution.py:365
  14.5 21.7 %collective-permute-start.6 = (bf16[80,2048]{1,0:T(8,128)(2,1)S(1)}, bf16[80,2048]{1,0:T(8,128)(2,1)S(1)}, u32[]{:S(2)}, u32[]{:S(2)}) collective-permute-start(bf16[80,2048]{1,0:T(8,128)(2,1)S(1)} %get-tuple-element.56), channel_id=1, source_target_pairs={{0,3},{1,2},{2,1},{3,0},{4,7},{5,6},{6,5},{7,4},{8,11},{9,10},{10,... | collective-permute-start | bytes 983048 | tf_op jit(solution)/shard_map/cond/branch_0_fun/ppermute | solution.py:365
  36.3 6.0 %collective-permute-start.7 = (bf16[320,2048]{1,0:T(8,128)(2,1)S(1)}, bf16[320,2048]{1,0:T(8,128)(2,1)}, u32[]{:S(2)}, u32[]{:S(2)}) collective-permute-start(bf16[320,2048]{1,0:T(8,128)(2,1)S(1)} %join_grads.3.c_ref.c_own), channel_id=1, source_target_pairs={{0,4},{4,0},{8,12},{12,8},{16,20},{20,16},{24,28},{28,24},{1,5},{5... | collective-permute-start | bytes 3932168 | tf_op jit(solution)/shard_map/cond/branch_0_fun/ppermute | solution.py:370
  36.4 6.0 %collective-permute-start.3 = (bf16[320,768]{1,0:T(8,128)(2,1)S(1)}, bf16[320,768]{1,0:T(8,128)(2,1)S(1)}, u32[]{:S(2)}, u32[]{:S(2)}) collective-permute-start(bf16[320,768]{1,0:T(8,128)(2,1)S(1)} %get-tuple-element.65.act_own.act_ref), channel_id=1, source_target_pairs={{0,4},{4,0},{8,12},{12,8},{16,20},{20,16},{24,28},{28,24},{1,5},{5... | collective-permute-start | bytes 1474568 | tf_op jit(solution)/shard_map/cond/branch_0_fun/ppermute | solution.py:370
  36.9 18.4 %collective-permute-start.12 = (bf16[320,2048]{1,0:T(8,128)(2,1)}, bf16[320,2048]{1,0:T(8,128)(2,1)}, u32[]{:S(2)}, u32[]{:S(2)}) collective-permute-start(bf16[320,2048]{1,0:T(8,128)(2,1)} %get-tuple-element.70.x_own), channel_id=1, source_target_pairs={{0,4},{4,0},{8,12},{12,8},{16,20},{20,16},{24,28},{28,24},{1,5},{5... | collective-permute-start | bytes 3932168 | tf_op jit(solution)/shard_map/cond/branch_0_fun/ppermute | solution.py:370
  38.6 12.6 %copy-start.78 = (bf16[1,768,2048]{2,1,0:T(8,128)(2,1)S(1)}, bf16[1,768,2048]{2,1,0:T(8,128)(2,1)}, u32[]{:S(2)}) copy-start(bf16[1,768,2048]{2,1,0:T(8,128)(2,1)} %get-tuple-element.346.down_ref) | copy-start | bytes 9437188 | tf_op jit(solution)/shard_map/cond
  48.6 6.7 %collective-permute-start.13 = (bf16[2,320,768]{2,1,0:T(8,128)(2,1)S(1)}, bf16[2,320,768]{2,1,0:T(8,128)(2,1)S(1)}, u32[]{:S(2)}, u32[]{:S(2)}) collective-permute-start(bf16[2,320,768]{2,1,0:T(8,128)(2,1)S(1)} %backward.3.g_own.grad_ref), channel_id=1, source_target_pairs={{0,4},{4,0},{8,12},{12,8},{16,20},{20,16},{24,28},{28,24},{1,5},{5... | collective-permute-start | bytes 2949128 | tf_op jit(solution)/shard_map/cond/branch_0_fun/ppermute | solution.py:370
  49.1 12.0 %collective-permute-start.11 = (bf16[768,256]{1,0:T(8,128)(2,1)S(1)}, bf16[768,256]{1,0:T(8,128)(2,1)S(1)}, u32[]{:S(2)}, u32[]{:S(2)}) collective-permute-start(bf16[768,256]{1,0:T(8,128)(2,1)S(1)} %get-tuple-element.75.right_ref), channel_id=1, source_target_pairs={{0,8},{4,12},{8,0},{12,4},{16,24},{20,28},{24,16},{28,20},{1,9},{5... | collective-permute-start | bytes 1179656 | tf_op jit(solution)/shard_map/cond/branch_0_fun/ppermute | solution.py:472
  50.7 18.8 %collective-permute-start.17 = (bf16[768,256]{1,0:T(8,128)(2,1)S(1)}, bf16[768,256]{1,0:T(8,128)(2,1)S(1)}, u32[]{:S(2)}, u32[]{:S(2)}) collective-permute-start(bf16[768,256]{1,0:T(8,128)(2,1)S(1)} %get-tuple-element.87.right_ref), channel_id=1, source_target_pairs={{0,8},{4,12},{8,0},{12,4},{16,24},{20,28},{24,16},{28,20},{1,9},{5... | collective-permute-start | bytes 1179656 | tf_op jit(solution)/shard_map/cond/branch_0_fun/ppermute | solution.py:472
  51.2 13.9 %copy-start.75 = (bf16[1,2048,768]{2,1,0:T(8,128)(2,1)S(1)}, bf16[1,2048,768]{2,1,0:T(8,128)(2,1)}, u32[]{:S(2)}) copy-start(bf16[1,2048,768]{2,1,0:T(8,128)(2,1)} %get-tuple-element.340.refs_5_.up_ref) | copy-start | bytes 9437188 | tf_op jit(solution)/shard_map/cond
  54.0 17.9 %collective-permute-start.8 = (bf16[80,2048]{1,0:T(8,128)(2,1)S(1)}, bf16[80,2048]{1,0:T(8,128)(2,1)S(1)}, u32[]{:S(2)}, u32[]{:S(2)}) collective-permute-start(bf16[80,2048]{1,0:T(8,128)(2,1)S(1)} %get-tuple-element.67), channel_id=1, source_target_pairs={{0,1},{1,0},{2,3},{3,2},{4,5},{5,4},{6,7},{7,6},{8,9},{9,8},{10,11... | collective-permute-start | bytes 983048 | tf_op jit(solution)/shard_map/cond/branch_0_fun/ppermute | solution.py:365
  55.3 9.8 %copy-start.72 = (bf16[1,2048,768]{2,1,0:T(8,128)(2,1)S(1)}, bf16[1,2048,768]{2,1,0:T(8,128)(2,1)}, u32[]{:S(2)}) copy-start(bf16[1,2048,768]{2,1,0:T(8,128)(2,1)} %get-tuple-element.337.refs_4_.gate_ref) | copy-start | bytes 9437188 | tf_op jit(solution)/shard_map/cond
  60.4 8.3 %copy-start.24 = (bf16[256,768]{1,0:T(8,128)(2,1)}, bf16[256,768]{1,0:T(8,128)(2,1)S(1)}, u32[]{:S(2)}) copy-start(bf16[256,768]{1,0:T(8,128)(2,1)S(1)} %get-tuple-element.110.right_ref) | copy-start | bytes 1179652 | tf_op jit(solution)/shard_map/cond
  60.4 8.3 %copy-start.36 = (bf16[256,768]{1,0:T(8,128)(2,1)}, bf16[256,768]{1,0:T(8,128)(2,1)S(1)}, u32[]{:S(2)}) copy-start(bf16[256,768]{1,0:T(8,128)(2,1)S(1)} %get-tuple-element.93.right_ref) | copy-start | bytes 1179652 | tf_op jit(solution)/shard_map/cond
  62.0 16.0 %collective-permute-start.18 = (bf16[256,768]{1,0:T(8,128)(2,1)S(1)}, bf16[256,768]{1,0:T(8,128)(2,1)S(1)}, u32[]{:S(2)}, u32[]{:S(2)}) collective-permute-start(bf16[256,768]{1,0:T(8,128)(2,1)S(1)} %get-tuple-element.93.right_ref), channel_id=1, source_target_pairs={{0,8},{4,12},{8,0},{12,4},{16,24},{20,28},{24,16},{28,20},{1,9},{5... | collective-permute-start | bytes 1179656 | tf_op jit(solution)/shard_map/cond/branch_0_fun/ppermute | solution.py:472
  63.5 11.2 %collective-permute-start.9 = (bf16[80,2048]{1,0:T(8,128)(2,1)S(1)}, bf16[80,2048]{1,0:T(8,128)(2,1)S(1)}, u32[]{:S(2)}, u32[]{:S(2)}) collective-permute-start(bf16[80,2048]{1,0:T(8,128)(2,1)S(1)} %get-tuple-element.68), channel_id=1, source_target_pairs={{0,2},{1,3},{2,0},{3,1},{4,6},{5,7},{6,4},{7,5},{8,10},{9,11},{10,... | collective-permute-start | bytes 983048 | tf_op jit(solution)/shard_map/cond/branch_0_fun/ppermute | solution.py:365
  65.1 19.5 %collective-permute-start.21 = (bf16[768,256]{1,0:T(8,128)(2,1)}, bf16[768,256]{1,0:T(8,128)(2,1)}, u32[]{:S(2)}, u32[]{:S(2)}) collective-permute-start(bf16[768,256]{1,0:T(8,128)(2,1)} %down_mid1.3), channel_id=1, source_target_pairs={{8,16},{16,8},{12,20},{20,12},{0,4},{4,0},{24,28},{28,24},{9,17},{... | collective-permute-start | bytes 1179656 | tf_op jit(solution)/shard_map/cond/branch_0_fun/ppermute | solution.py:476
  68.7 9.3 %copy-start.60 = (bf16[80,2048]{1,0:T(8,128)(2,1)}, bf16[80,2048]{1,0:T(8,128)(2,1)S(1)}, u32[]{:S(2)}) copy-start(bf16[80,2048]{1,0:T(8,128)(2,1)S(1)} %get-tuple-element.77.refs_4_) | copy-start | bytes 983044 | tf_op jit(solution)/shard_map/cond
  68.7 9.2 %copy-start.66 = (bf16[80,2048]{1,0:T(8,128)(2,1)}, bf16[80,2048]{1,0:T(8,128)(2,1)S(1)}, u32[]{:S(2)}) copy-start(bf16[80,2048]{1,0:T(8,128)(2,1)S(1)} %get-tuple-element.80) | copy-start | bytes 983044 | tf_op jit(solution)/shard_map/cond
  69.5 14.9 %collective-permute-start.10 = (bf16[80,2048]{1,0:T(8,128)(2,1)}, bf16[80,2048]{1,0:T(8,128)(2,1)}, u32[]{:S(2)}, u32[]{:S(2)}) collective-permute-start(bf16[80,2048]{1,0:T(8,128)(2,1)} %get-tuple-element.69), channel_id=1, source_target_pairs={{0,3},{1,2},{2,1},{3,0},{4,7},{5,6},{6,5},{7,4},{8,11},{9,10},{10,... | collective-permute-start | bytes 983048 | tf_op jit(solution)/shard_map/cond/branch_0_fun/ppermute | solution.py:365
  72.6 16.3 %collective-permute-start.20 = (bf16[256,768]{1,0:T(8,128)(2,1)}, bf16[256,768]{1,0:T(8,128)(2,1)}, u32[]{:S(2)}, u32[]{:S(2)}) collective-permute-start(bf16[256,768]{1,0:T(8,128)(2,1)} %get-tuple-element.103.right_ref), channel_id=1, source_target_pairs={{0,8},{4,12},{8,0},{12,4},{16,24},{20,28},{24,16},{28,20},{1,9},{5... | collective-permute-start | bytes 1179656 | tf_op jit(solution)/shard_map/cond/branch_0_fun/ppermute | solution.py:472
  75.5 15.9 %collective-permute-start.14 = (bf16[80,2048]{1,0:T(8,128)(2,1)}, bf16[80,2048]{1,0:T(8,128)(2,1)}, u32[]{:S(2)}, u32[]{:S(2)}) collective-permute-start(bf16[80,2048]{1,0:T(8,128)(2,1)} %get-tuple-element.78), channel_id=1, source_target_pairs={{0,1},{1,0},{2,3},{3,2},{4,5},{5,4},{6,7},{7,6},{8,9},{9,8},{10,11... | collective-permute-start | bytes 983048 | tf_op jit(solution)/shard_map/cond/branch_0_fun/ppermute | solution.py:365
  78.7 12.8 %collective-permute-start.15 = (bf16[80,2048]{1,0:T(8,128)(2,1)}, bf16[80,2048]{1,0:T(8,128)(2,1)}, u32[]{:S(2)}, u32[]{:S(2)}) collective-permute-start(bf16[80,2048]{1,0:T(8,128)(2,1)} %get-tuple-element.79), channel_id=1, source_target_pairs={{0,2},{1,3},{2,0},{3,1},{4,6},{5,7},{6,4},{7,5},{8,10},{9,11},{10,... | collective-permute-start | bytes 983048 | tf_op jit(solution)/shard_map/cond/branch_0_fun/ppermute | solution.py:365
  84.5 12.6 %collective-permute-start.24 = (bf16[768,256]{1,0:T(8,128)(2,1)S(1)}, bf16[768,256]{1,0:T(8,128)(2,1)S(1)}, u32[]{:S(2)}, u32[]{:S(2)}) collective-permute-start(bf16[768,256]{1,0:T(8,128)(2,1)S(1)} %copy-done.31), channel_id=1, source_target_pairs={{8,16},{16,8},{12,20},{20,12},{0,4},{4,0},{24,28},{28,24},{9,17},{... | collective-permute-start | bytes 1179656 | tf_op jit(solution)/shard_map/cond/branch_0_fun/ppermute | solution.py:476
  86.4 12.7 %copy-start.19 = (bf16[256,768]{1,0:T(8,128)(2,1)S(1)}, bf16[256,768]{1,0:T(8,128)(2,1)}, u32[]{:S(2)}) copy-start(bf16[256,768]{1,0:T(8,128)(2,1)} %copy-done.18) | copy-start | bytes 1179652 | tf_op jit(solution)/shard_map/cond
  86.4 12.6 %collective-permute-start.23 = (bf16[768,256]{1,0:T(8,128)(2,1)S(1)}, bf16[768,256]{1,0:T(8,128)(2,1)S(1)}, u32[]{:S(2)}, u32[]{:S(2)}) collective-permute-start(bf16[768,256]{1,0:T(8,128)(2,1)S(1)} %down_last.3), channel_id=1, source_target_pairs={{0,8},{4,12},{8,0},{12,4},{16,24},{20,28},{24,16},{28,20},{1,9},{5... | collective-permute-start | bytes 1179656 | tf_op jit(solution)/shard_map/cond/branch_0_fun/ppermute | solution.py:472
  89.0 8.1 %collective-permute-start.16 = (bf16[80,2048]{1,0:T(8,128)(2,1)S(1)}, bf16[80,2048]{1,0:T(8,128)(2,1)S(1)}, u32[]{:S(2)}, u32[]{:S(2)}) collective-permute-start(bf16[80,2048]{1,0:T(8,128)(2,1)S(1)} %copy-done.67), channel_id=1, source_target_pairs={{0,3},{1,2},{2,1},{3,0},{4,7},{5,6},{6,5},{7,4},{8,11},{9,10},{10,... | collective-permute-start | bytes 983048 | tf_op jit(solution)/shard_map/cond/branch_0_fun/ppermute | solution.py:365
  91.4 16.0 %collective-permute-start.22 = (bf16[256,768]{1,0:T(8,128)(2,1)S(1)}, bf16[256,768]{1,0:T(8,128)(2,1)S(1)}, u32[]{:S(2)}, u32[]{:S(2)}) collective-permute-start(bf16[256,768]{1,0:T(8,128)(2,1)S(1)} %copy-done.25), channel_id=1, source_target_pairs={{0,8},{4,12},{8,0},{12,4},{16,24},{20,28},{24,16},{28,20},{1,9},{5... | collective-permute-start | bytes 1179656 | tf_op jit(solution)/shard_map/cond/branch_0_fun/ppermute | solution.py:472
  91.5 16.0 %collective-permute-start.19 = (bf16[256,768]{1,0:T(8,128)(2,1)S(1)}, bf16[256,768]{1,0:T(8,128)(2,1)S(1)}, u32[]{:S(2)}, u32[]{:S(2)}) collective-permute-start(bf16[256,768]{1,0:T(8,128)(2,1)S(1)} %gate_mid1.3), channel_id=1, source_target_pairs={{8,16},{16,8},{12,20},{20,12},{0,4},{4,0},{24,28},{28,24},{9,17},{... | collective-permute-start | bytes 1179656 | tf_op jit(solution)/shard_map/cond/branch_0_fun/ppermute | solution.py:476
  99.1 16.7 %collective-permute-start.28 = (bf16[256,768]{1,0:T(8,128)(2,1)S(1)}, bf16[256,768]{1,0:T(8,128)(2,1)S(1)}, u32[]{:S(2)}, u32[]{:S(2)}) collective-permute-start(bf16[256,768]{1,0:T(8,128)(2,1)S(1)} %copy-done.19), channel_id=1, source_target_pairs={{0,8},{4,12},{8,0},{12,4},{16,24},{20,28},{24,16},{28,20},{1,9},{5... | collective-permute-start | bytes 1179656 | tf_op jit(solution)/shard_map/cond/branch_0_fun/ppermute | solution.py:472
  101.2 14.7 %collective-permute-start.27 = (bf16[256,768]{1,0:T(8,128)(2,1)S(1)}, bf16[256,768]{1,0:T(8,128)(2,1)S(1)}, u32[]{:S(2)}, u32[]{:S(2)}) collective-permute-start(bf16[256,768]{1,0:T(8,128)(2,1)S(1)} %up_mid1.3), channel_id=1, source_target_pairs={{8,16},{16,8},{12,20},{20,12},{0,4},{4,0},{24,28},{28,24},{9,17},{... | collective-permute-start | bytes 1179656 | tf_op jit(solution)/shard_map/cond/branch_0_fun/ppermute | solution.py:476
  107.6 16.7 %collective-permute-start.25 = (bf16[256,768]{1,0:T(8,128)(2,1)S(1)}, bf16[256,768]{1,0:T(8,128)(2,1)S(1)}, u32[]{:S(2)}, u32[]{:S(2)}) collective-permute-start(bf16[256,768]{1,0:T(8,128)(2,1)S(1)} %gate_last.3), channel_id=1, source_target_pairs={{0,8},{4,12},{8,0},{12,4},{16,24},{20,28},{24,16},{28,20},{1,9},{5... | collective-permute-start | bytes 1179656 | tf_op jit(solution)/shard_map/cond/branch_0_fun/ppermute | solution.py:472
  109.7 14.6 %collective-permute-start.26 = (bf16[256,768]{1,0:T(8,128)(2,1)S(1)}, bf16[256,768]{1,0:T(8,128)(2,1)S(1)}, u32[]{:S(2)}, u32[]{:S(2)}) collective-permute-start(bf16[256,768]{1,0:T(8,128)(2,1)S(1)} %gate_mid2.3), channel_id=1, source_target_pairs={{8,16},{16,8},{12,20},{20,12},{0,4},{4,0},{24,28},{28,24},{9,17},{... | collective-permute-start | bytes 1179656 | tf_op jit(solution)/shard_map/cond/branch_0_fun/ppermute | solution.py:476
  116.0 9.0 %copy-start.49 = (bf16[80,2048]{1,0:T(8,128)(2,1)S(1)}, bf16[80,2048]{1,0:T(8,128)(2,1)}, u32[]{:S(2)}) copy-start(bf16[80,2048]{1,0:T(8,128)(2,1)} %copy-done.48) | copy-start | bytes 983044 | tf_op jit(solution)/shard_map/cond
  116.0 9.0 %copy-start.55 = (bf16[80,2048]{1,0:T(8,128)(2,1)S(1)}, bf16[80,2048]{1,0:T(8,128)(2,1)}, u32[]{:S(2)}) copy-start(bf16[80,2048]{1,0:T(8,128)(2,1)} %copy-done.54) | copy-start | bytes 983044 | tf_op jit(solution)/shard_map/cond
  116.0 9.0 %copy-start.61 = (bf16[80,2048]{1,0:T(8,128)(2,1)S(1)}, bf16[80,2048]{1,0:T(8,128)(2,1)}, u32[]{:S(2)}) copy-start(bf16[80,2048]{1,0:T(8,128)(2,1)} %copy-done.60) | copy-start | bytes 983044 | tf_op jit(solution)/shard_map/cond
  116.0 9.0 %copy-start.81 = (bf16[128,2048]{1,0:T(8,128)(2,1)S(1)}, bf16[128,2048]{1,0:T(8,128)(2,1)}, u32[]{:S(2)}) copy-start(bf16[128,2048]{1,0:T(8,128)(2,1)} %get-tuple-element.343.cot_ref) | copy-start | bytes 1572868 | tf_op jit(solution)/shard_map/cond
  116.0 8.9 %copy-start.84 = (s32[2,128]{1,0:T(2,128)S(1)}, s32[2,128]{1,0:T(2,128)}, u32[]{:S(2)}) copy-start(s32[2,128]{1,0:T(2,128)} %get-tuple-element.42.ids_ref) | copy-start | bytes 3076 | tf_op jit(solution)/shard_map/cond
  116.0 8.9 %copy-start.87 = (f32[2,128]{1,0:T(2,128)S(1)}, f32[2,128]{1,0:T(2,128)}, u32[]{:S(2)}) copy-start(f32[2,128]{1,0:T(2,128)} %get-tuple-element.43.gates_ref) | copy-start | bytes 3076 | tf_op jit(solution)/shard_map/cond
  116.0 14.9 %collective-permute-start.30 = (bf16[256,768]{1,0:T(8,128)(2,1)S(1)}, bf16[256,768]{1,0:T(8,128)(2,1)S(1)}, u32[]{:S(2)}, u32[]{:S(2)}) collective-permute-start(bf16[256,768]{1,0:T(8,128)(2,1)S(1)} %up_last.3), channel_id=1, source_target_pairs={{0,8},{4,12},{8,0},{12,4},{16,24},{20,28},{24,16},{28,20},{1,9},{5... | collective-permute-start | bytes 1179656 | tf_op jit(solution)/shard_map/cond/branch_0_fun/ppermute | solution.py:472
  118.2 12.8 %collective-permute-start.31 = (bf16[256,768]{1,0:T(8,128)(2,1)S(1)}, bf16[256,768]{1,0:T(8,128)(2,1)S(1)}, u32[]{:S(2)}, u32[]{:S(2)}) collective-permute-start(bf16[256,768]{1,0:T(8,128)(2,1)S(1)} %up_mid2.3), channel_id=1, source_target_pairs={{8,16},{16,8},{12,20},{20,12},{0,4},{4,0},{24,28},{28,24},{9,17},{... | collective-permute-start | bytes 1179656 | tf_op jit(solution)/shard_map/cond/branch_0_fun/ppermute | solution.py:476
  118.2 13.5 %collective-permute-start.33 = (bf16[768,256]{1,0:T(8,128)(2,1)S(1)}, bf16[768,256]{1,0:T(8,128)(2,1)S(1)}, u32[]{:S(2)}, u32[]{:S(2)}) collective-permute-start(bf16[768,256]{1,0:T(8,128)(2,1)S(1)} %down_sum.3), channel_id=1, source_target_pairs={{0,1},{1,0},{2,3},{3,2},{4,5},{5,4},{6,7},{7,6},{8,9},{9,8},{10,11... | collective-permute-start | bytes 1179656 | tf_op jit(solution)/shard_map/cond/branch_0_fun/ppermute | solution.py:479
  124.4 14.2 %collective-permute-start.29 = (bf16[256,768]{1,0:T(8,128)(2,1)S(1)}, bf16[256,768]{1,0:T(8,128)(2,1)S(1)}, u32[]{:S(2)}, u32[]{:S(2)}) collective-permute-start(bf16[256,768]{1,0:T(8,128)(2,1)S(1)} %gate_sum.3), channel_id=1, source_target_pairs={{0,1},{1,0},{2,3},{3,2},{4,5},{5,4},{6,7},{7,6},{8,9},{9,8},{10,11... | collective-permute-start | bytes 1179656 | tf_op jit(solution)/shard_map/cond/branch_0_fun/ppermute | solution.py:479
  131.1 15.5 %collective-permute-start.32 = (bf16[256,768]{1,0:T(8,128)(2,1)S(1)}, bf16[256,768]{1,0:T(8,128)(2,1)S(1)}, u32[]{:S(2)}, u32[]{:S(2)}) collective-permute-start(bf16[256,768]{1,0:T(8,128)(2,1)S(1)} %up_sum.3), channel_id=1, source_target_pairs={{0,1},{1,0},{2,3},{3,2},{4,5},{5,4},{6,7},{7,6},{8,9},{9,8},{10,11... | collective-permute-start | bytes 1179656 | tf_op jit(solution)/shard_map/cond/branch_0_fun/ppermute | solution.py:479
  (16 other events, 51.0 us)

commit v3 on v2

--- a/solution.py
+++ b/solution.py
@@ -7,7 +7,7 @@
 from jax.experimental.pallas import tpu as pltpu
 from jax.sharding import PartitionSpec as P
 
-VMEM_BYTES = 32 * 1024 * 1024
+VMEM_BYTES = 48 * 1024 * 1024
 F32 = jnp.float32
 BF16 = jnp.bfloat16
 
@@ -134,21 +134,72 @@
             out[...] = value
 
 
-def down_share(order_ref, act_own, act_other, c_own, c_other, *outs_and_scratch):
-    *outs, turned = outs_and_scratch
+def turn(own_ref, other_ref, out_ref):
+    out_ref[...] = both(own_ref, other_ref).T
+
+
+def turned(name, own, other):
+    rows, width = own.shape
+    tile = tile_of(width, 256)
+    block = pl.BlockSpec((rows, tile), lambda n: (0, n))
+    return pl.pallas_call(
+        turn,
+        out_shape=jax.ShapeDtypeStruct((width, 2 * rows), BF16),
+        grid=(width // tile,),
+        in_specs=[block] * 2,
+        out_specs=pl.BlockSpec((tile, 2 * rows), lambda n: (n, 0)),
+        compiler_params=params(),
+        cost_estimate=cost(0, 0),
+        name=name,
+    )(own, other)
+
+
+def down_share(order_ref, act_ref, c_own, c_other, *outs):
+    store_at_step(outs, dot_nn(act_ref[...], both(c_own, c_other)).astype(BF16))
+
+
+def gate_up_share(count, order_ref, *refs):
+    own, other, (g_own, g_other), outs, x_turned = (
+        refs[:count],
+        refs[count : 2 * count],
+        refs[2 * count : 2 * count + 2],
+        refs[2 * count + 2 : -1],
+        refs[-1],
+    )
+    cols = own[0].shape[1]
 
     @pl.when(pl.program_id(0) == 0)
     def _():
-        turned[...] = both(act_own, act_other).T
-
-    store_at_step(outs, dot_nn(turned[...], both(c_own, c_other)).astype(BF16))
-
-
-def gate_up_share(order_ref, x_own, x_other, g_own, g_other, *outs):
-    half = len(outs) // 2
-    turned = both(x_own, x_other).T
-    store_at_step(outs[:half], dot_nn(turned, both(g_own, g_other, 0)).astype(BF16))
-    store_at_step(outs[half:], dot_nn(turned, both(g_own, g_other, 1)).astype(BF16))
+        for n in range(count):
+            x_turned[n * cols : (n + 1) * cols] = both(own[n], other[n]).T
+
+    for which in range(2):
+        share = dot_nn(x_turned[...], both(g_own, g_other, which)).astype(BF16)
+        for n in range(count):
+            outs[which * count + n][...] = share[n * cols : (n + 1) * cols]
+
+
+def slot_kernel(*refs):
+    parts, (out_ref, wide, sem) = refs[:-3], refs[-3:]
+    rows = wide.shape[0] // len(parts)
+    for n, part in enumerate(parts):
+        wide[n * rows : (n + 1) * rows] = part[...].astype(F32)
+    copy = pltpu.make_async_copy(wide, out_ref.at[0], sem)
+    copy.start()
+    copy.wait()
+
+
+def slot_of(name, *parts):
+    rows, columns = sum(part.shape[0] for part in parts), parts[0].shape[1]
+    return pl.pallas_call(
+        slot_kernel,
+        out_shape=jax.ShapeDtypeStruct((1, rows, columns), F32),
+        out_specs=pl.BlockSpec(memory_space=pltpu.HBM),
+        scratch_shapes=[pltpu.VMEM((rows, columns), F32), pltpu.SemaphoreType.DMA(())],
+        compiler_params=params(),
+        cost_estimate=cost(0, 0),
+        name=name,
+    )(*parts)
 
 
 def add_kernel(left_ref, right_ref, out_ref):
@@ -165,40 +216,56 @@
     )(left, right)
 
 
-def end_kernel(end_ref, alone_ref, left_ref, right_ref, out_ref):
-    @pl.when(end_ref[0] == 1)
-    def _():
-        out_ref[...] = alone_ref[...]
-
-    @pl.when(end_ref[0] == 0)
-    def _():
-        out_ref[...] = (left_ref[...].astype(F32) + right_ref[...].astype(F32)).astype(BF16)
-
-
-def at_end(kernel, name, end, *parts):
+def end_kernel(end_ref, alone_ref, left_ref, right_ref, *outs):
+    rows = alone_ref.shape[0] // len(outs)
+    for n, out_ref in enumerate(outs):
+        at = slice(n * rows, (n + 1) * rows)
+
+        @pl.when(end_ref[0] == 1)
+        def _(at=at, out_ref=out_ref):
+            out_ref[...] = alone_ref[at]
+
+        @pl.when(end_ref[0] == 0)
+        def _(at=at, out_ref=out_ref):
+            out_ref[...] = (left_ref[at].astype(F32) + right_ref[at].astype(F32)).astype(BF16)
+
+
+def at_end(kernel, name, outs, end, *parts):
     smem, vmem = pl.BlockSpec(memory_space=pltpu.SMEM), pl.BlockSpec(memory_space=pltpu.VMEM)
     return pl.pallas_call(
         kernel,
-        out_shape=jax.ShapeDtypeStruct(parts[0].shape, BF16),
+        out_shape=outs,
         in_specs=[smem] + [vmem] * len(parts),
-        out_specs=vmem,
+        out_specs=[vmem] * len(outs),
         compiler_params=params(),
         cost_estimate=cost(0, 0),
         name=name,
     )(end, *parts)
 
 
-def final_kernel(end_ref, near_ref, last_ref, inner_ref, middle_ref, out_ref):
+def last_share(name, pieces, end, alone, left, right):
+    rows, columns = alone.shape
+    outs = [jax.ShapeDtypeStruct((rows // pieces, columns), BF16)] * pieces
+    return at_end(end_kernel, name, outs, end, alone, left, right)
+
+
+def final_kernel(at, end_ref, last_ref, near_ref, inner_ref, middle_ref, out_ref):
     last = last_ref[...].astype(F32)
 
     @pl.when(end_ref[0] == 1)
     def _():
-        out_ref[...] = (near_ref[...].astype(F32) + last).astype(BF16)
+        out_ref[...] = (near_ref[at].astype(F32) + last).astype(BF16)
 
     @pl.when(end_ref[0] == 0)
     def _():
-        inner = inner_ref[...].astype(F32) + middle_ref[...].astype(F32)
+        inner = inner_ref[at].astype(F32) + middle_ref[...].astype(F32)
         out_ref[...] = (inner + last).astype(BF16)
+
+
+def final_sum(name, piece, end, last, near, inner, middle):
+    at = slice(piece * last.shape[0], (piece + 1) * last.shape[0])
+    outs = [jax.ShapeDtypeStruct(last.shape, BF16)]
+    return at_end(functools.partial(final_kernel, at), name, outs, end, last, near, inner, middle)[0]
 
 
 def combine(cap, groups, me_ref, ids_ref, gates_ref, cot_ref, *refs):
@@ -242,8 +309,9 @@
     return lax.dynamic_index_in_dim(rows, core, 2, keepdims=False)
 
 
-def down_shares(order, cols, name, act, act_other, c_rows, c_other):
-    total, ff = act.shape
+def down_shares(order, cols, act_turned, c_rows, c_other):
+    ff, both_rows = act_turned.shape
+    total, width = c_rows.shape
     count = order.shape[0]
     block = pl.BlockSpec((total, cols), lambda n, order_ref: (0, order_ref[n]))
     return pl.pallas_call(
@@ -252,34 +320,37 @@
         grid_spec=pltpu.PrefetchScalarGridSpec(
             num_scalar_prefetch=1,
             grid=(count,),
-            in_specs=[whole((total, ff))] * 2 + [block] * 2,
+            in_specs=[whole((ff, both_rows))] + [block] * 2,
             out_specs=[whole((ff, cols))] * count,
-            scratch_shapes=[pltpu.VMEM((ff, 2 * total), BF16)],
         ),
         compiler_params=params(),
-        cost_estimate=cost(4 * total * count * cols * ff, 5e6),
-        name=name,
-    )(order, act, act_other, c_rows, c_other)
-
-
-def gate_up_shares(order, cols, name, x_rows, x_other, grads, grads_other):
+        cost_estimate=cost(2 * total * width * ff, 5e6),
+        name="down_shares",
+    )(order, act_turned, c_rows, c_other)
+
+
+def gate_up_shares(order, cols, x_rows, x_other, grads, grads_other):
     total, width = x_rows.shape
     ff = grads.shape[2]
     count = order.shape[0]
-    block = pl.BlockSpec((total, cols), lambda n, order_ref: (0, order_ref[n]))
+    tile = tile_of(ff, 256)
+    columns = [
+        pl.BlockSpec((total, cols), lambda j, order_ref, n=n: (0, order_ref[n])) for n in range(count)
+    ]
     return pl.pallas_call(
-        gate_up_share,
+        functools.partial(gate_up_share, count),
         out_shape=[jax.ShapeDtypeStruct((cols, ff), BF16)] * (2 * count),
         grid_spec=pltpu.PrefetchScalarGridSpec(
             num_scalar_prefetch=1,
-            grid=(count,),
-            in_specs=[block] * 2 + [whole((2, total, ff))] * 2,
-            out_specs=[whole((cols, ff))] * (2 * count),
+            grid=(ff // tile,),
+            in_specs=columns * 2 + [pl.BlockSpec((2, total, tile), lambda j, _: (0, 0, j))] * 2,
+            out_specs=[pl.BlockSpec((cols, tile), lambda j, _: (0, j))] * (2 * count),
+            scratch_shapes=[pltpu.VMEM((count * cols, 2 * total), BF16)],
         ),
         compiler_params=params(),
-        cost_estimate=cost(8 * total * count * cols * ff, 6e6),
-        name=name,
-    )(order, x_rows, x_other, grads, grads_other)
+        cost_estimate=cost(4 * total * width * ff, 9e6),
+        name="gate_up_shares",
+    )(order, *[x_rows] * count, *[x_other] * count, grads, grads_other)
 
 
 def add(part, own):
@@ -463,6 +534,21 @@
             name="input_rows",
         )(grads, w_gate, w_up)
 
+    def run_combine(out_blocks, grad_blocks):
+        return pl.pallas_call(
+            functools.partial(combine, cap, groups),
+            out_shape=[
+                jax.ShapeDtypeStruct((count, width), BF16),
+                jax.ShapeDtypeStruct((count, width), BF16),
+                jax.ShapeDtypeStruct((top, count), F32),
+            ],
+            in_specs=[smem] + [vmem] * (3 + 2 * groups),
+            out_specs=[vmem] * 3,
+            compiler_params=params(),
+            cost_estimate=cost(6 * total * width * count, 6e6),
+            name="combine",
+        )(me_arr, ids, gates, cotangent, *out_blocks, *grad_blocks)
+
     if turn is not None and chips == 4 and cols % 128 == 0:
         low = chip < 2
         end = ((chip == 0) | (chip == 3)).astype(jnp.int32).reshape(1)
@@ -478,54 +564,63 @@
         def to_mate(part):
             return lax.ppermute(part, "expert", [(i, i ^ turn) for i in range(groups)])
 
+        x_other = swap(x_rows)
         c_rows = joined(after(c_blocks, act), "join_grads")
-        c_other, x_other = swap(c_rows), swap(x_rows)
-        grads = run_backward(c_rows)
-        d_a, d_b, d_c, d_d = down_shares(
-            order, cols, "down_shares", act, act_other, c_rows, after(c_other, grads)
+        c_other = swap(c_rows)
+        act_turned = turned("turn_act", act, after(act_other, c_rows))
+        grads = run_backward(after(c_rows, act_turned))
+        grads_other = swap(grads)
+        d_a, d_b, d_c, d_d = down_shares(order, cols, act_turned, c_rows, after(c_other, grads))
+        d_1 = swap_ends(d_a)
+        d_2 = swap_ends(after(d_b, d_a))
+        out_rows = run_expert_rows(after(act, d_a, grads))
+        out_blocks = exchange(after(out_rows, d_a))
+        g_a, g_b, g_c, g_d, u_a, u_b, u_c, u_d = gate_up_shares(
+            order, cols, after(x_rows, d_a, out_rows[0]), x_other, grads, grads_other
         )
-        d_1, d_2 = swap_ends(d_a), swap_ends(after(d_b, d_a))
-        grads_other = swap(after(grads, d_a))
-
-        out_rows = run_expert_rows(after(act, d_a))
-        out_blocks = exchange(out_rows)
-        g_a, g_b, u_a, u_b = gate_up_shares(
-            order[:2], cols, "gate_up_far", x_rows, x_other, grads, after(grads_other, *out_rows)
-        )
-
-        m = added("down_mid1", BF16, *after((d_1, d_a), g_a))
+        grad_rows = run_input_rows(after(grads, g_a))
+
+        m = added("down_mid1", BF16, *after((d_1, d_a), grad_rows[0]))
         d_m1, g_1 = swap_middle(m), swap_ends(after(g_a, m))
-        grad_rows = run_input_rows(after(grads, m))
-        grad_blocks = exchange(grad_rows)
-
-        m = added("down_mid2", BF16, *after((d_2, d_b), *grad_rows))
+        m = added("down_mid2", BF16, *after((d_2, d_b), m, *out_blocks))
         d_m2, u_1 = swap_middle(m), swap_ends(after(u_a, m))
-        g_c, g_d, u_c, u_d = gate_up_shares(
-            order[2:], cols, "gate_up_near", x_rows, x_other, grads, after(grads_other, m)
-        )
-
-        m = added("gate_mid1", BF16, *after((g_1, g_a), g_c))
+        grad_blocks = [grad_rows[0]]
+        for n, part in enumerate(grad_rows[1:], 1):
+            part = after(part, grad_blocks[-1], m, out_blocks)
+            grad_blocks.append(lax.ppermute(part, "expert", [(i, i ^ n) for i in range(groups)]))
+
+        m = added("gate_mid1", BF16, *after((g_1, g_a), m, grad_blocks[1]))
         g_m1 = swap_middle(m)
-        e = at_end(end_kernel, "down_last", end, *after((d_c, d_m1, d_d), m, *out_blocks))
+        (e,) = last_share("down_last", 1, end, *after((d_c, d_m1, d_d), m))
         d_3 = swap_ends(e)
-        m = added("up_mid1", BF16, *after((u_1, u_a), e))
+        m = added("up_mid1", BF16, *after((u_1, u_a), e, d_m2, *grad_blocks[1:3]))
         u_m1, g_2 = swap_middle(m), swap_ends(after(g_b, m))
 
-        t = at_end(final_kernel, "down_sum", end, *after((d_d, d_3, d_c, d_m2), m, *grad_blocks))
-        d_t, u_2 = to_mate(t), swap_ends(after(u_b, t))
-        m = added("gate_mid2", BF16, *after((g_2, g_b), t))
+        t = final_sum("down_sum", 0, end, *after((d_3, d_d, d_c, d_m2), m, *grad_blocks[1:]))
+        d_t = to_mate(t)
+        (e,) = last_share("gate_last", 1, end, *after((g_c, g_m1, g_d), t))
+        g_3 = swap_ends(e)
+        m = added("gate_mid2", BF16, *after((g_2, g_b), e))
         g_m2 = swap_middle(m)
-        e = at_end(end_kernel, "gate_last", end, *after((g_c, g_m1, g_d), m))
-        g_3 = swap_ends(e)
-        m = added("up_mid2", BF16, *after((u_2, u_b), e))
-        u_m2 = swap_middle(m)
-        e = at_end(end_kernel, "up_last", end, *after((u_c, u_m1, u_d), m))
-        u_3 = swap_ends(e)
-        t = at_end(final_kernel, "gate_sum", end, *after((g_d, g_3, g_c, g_m2), e))
-        g_t = to_mate(t)
-        t = at_end(final_kernel, "up_sum", end, *after((u_d, u_3, u_c, u_m2), t))
-        u_t = to_mate(t)
-        slot_down, slot_gate, slot_up = [part.astype(F32)[None] for part in (d_t, g_t, u_t)]
+        half = u_b.shape[0] // 2
+        u_b0, u_b1 = after((u_b[:half], u_b[half:]), m)
+        u_20, u_21 = swap_ends(u_b0), swap_ends(u_b1)
+        e0, e1 = last_share("up_last", 2, end, *after((u_c, u_m1, u_d), m))
+        t = final_sum("gate_sum", 0, end, *after((g_3, g_d, g_c, g_m2), e0, d_t))
+        g_t, u_30 = to_mate(t), swap_ends(after(e0, g_3))
+        m0 = added("up_mid20", BF16, *after((u_20, u_b0), t))
+        u_m20 = swap_middle(m0)
+        m1 = added("up_mid21", BF16, *after((u_21, u_b1), m0))
+        u_m21, u_31 = swap_middle(m1), swap_ends(after(e1, m0))
+
+        slot_down = slot_of("slot_down", *after((d_t,), m1))
+        t0 = final_sum("up_sum0", 0, end, *after((u_30, u_d, u_c, u_m20), slot_down, g_t))
+        u_t0 = to_mate(t0)
+        t1 = final_sum("up_sum1", 1, end, *after((u_31, u_d, u_c, u_m21), t0))
+        u_t1 = to_mate(t1)
+        mixed_out, token_grad, gate_grad = run_combine(*after((out_blocks, grad_blocks), t1))
+        slot_gate = slot_of("slot_gate", *after((g_t,), mixed_out))
+        slot_up = slot_of("slot_up", *after((u_t0, u_t1), slot_gate))
     else:
         c_rows = joined(c_blocks, "join_grads")
         grads = run_backward(c_rows)
@@ -553,20 +648,8 @@
         slot_down, slot_gate, slot_up = [
             relocated(line.total(), turn, partner, me, groups) for line in lines
         ]
-
-    mixed_out, token_grad, gate_grad = pl.pallas_call(
-        functools.partial(combine, cap, groups),
-        out_shape=[
-            jax.ShapeDtypeStruct((count, width), BF16),
-            jax.ShapeDtypeStruct((count, width), BF16),
-            jax.ShapeDtypeStruct((top, count), F32),
-        ],
-        in_specs=[smem] + [vmem] * (3 + 2 * groups),
-        out_specs=[vmem] * 3,
-        compiler_params=params(),
-        cost_estimate=cost(6 * total * width * count, 6e6),
-        name="combine",
-    )(me_arr, ids, gates, cotangent, *out_blocks, *grad_blocks)
+        mixed_out, token_grad, gate_grad = run_combine(out_blocks, grad_blocks)
+
     return mixed_out, token_grad, gate_grad.T, slot_gate, slot_up, slot_down
 
 

time: 148 us -> 141 us (0.953)
  waiting for transfers between devices: 58.6 us -> 49.4 us
  starting transfers between devices: 36.8 us -> 42.6 us
  other arithmetic: 2.81 us -> 0.01 us
  local copies, waits for them, and re-layouts: 7.22 us -> 4.44 us
  Pallas kernels: 40.4 us -> 42.6 us
    ppermute x3 -> x4, waiting for transfers between devices: 13 us -> 1.62 us  [to_mate(): return lax.ppermute(part, 'expert', [(i, i ^ turn) for i in range(groups)])]
    ppermute x0 -> x3, waiting for transfers between devices: none -> 8.17 us  [layer(): lax.ppermute(part, 'expert', [(i, i ^ n) for i in range(groups)])]
    ppermute x12 -> x9, starting transfers between devices: 19 us -> 14.6 us  [exchange(): lax.ppermute(blocks[b], 'expert', [(i, i ^ b) for i in range(groups)])]
    ppermute x12 -> x9, waiting for transfers between devices: 20.2 us -> 16.2 us  [exchange(): lax.ppermute(blocks[b], 'expert', [(i, i ^ b) for i in range(groups)])]
    ppermute x9 -> x11, starting transfers between devices: 14.8 us -> 18.7 us  [swap_ends(): return lax.ppermute(part, 'dp', [(i, i ^ 2) for i in range(replicas)])]
    ppermute x3 -> x4, starting transfers between devices: 1.68 us -> 5.22 us  [to_mate(): return lax.ppermute(part, 'expert', [(i, i ^ turn) for i in range(groups)])]
    ppermute x0 -> x3, starting transfers between devices: none -> 3.18 us  [layer(): lax.ppermute(part, 'expert', [(i, i ^ n) for i in range(groups)])]
    broadcast_in_dim x3 -> x0, other arithmetic: 2.8 us -> none  [layer(): part.astype(F32)[None]]
  transfers between devices with their start and end apart: 34 -> 38, of which waited for: 14 -> 16; matrix products, arithmetic and copies ran while one was open for 1% -> 0% of each run, Pallas kernels for 26% -> 28%
where the time goes in v3:
time: 141 us
  waiting for transfers between devices  49.4 us (35%)
  Pallas kernels  42.6 us (30%)
  starting transfers between devices  42.6 us (30%)
  local copies, waits for them, and re-layouts  4.44 us (3%)
  between operations  1.48 us (1%)
    ppermute x11, waiting for transfers between devices, swap_ends(): return lax.ppermute(part, 'dp', [(i, i ^ 2) for i in range(replicas)])  23.4 us
    ppermute x11, starting transfers between devices, swap_ends(): return lax.ppermute(part, 'dp', [(i, i ^ 2) for i in range(replicas)])  18.7 us
    ppermute x9, waiting for transfers between devices, exchange(): lax.ppermute(blocks[b], 'expert', [(i, i ^ b) for i in range(groups)])  16.2 us
    ppermute x9, starting transfers between devices, exchange(): lax.ppermute(blocks[b], 'expert', [(i, i ^ b) for i in range(groups)])  14.6 us
    ppermute x3, waiting for transfers between devices, layer(): lax.ppermute(part, 'expert', [(i, i ^ n) for i in range(groups)])  8.17 us
    pallas_call x1, Pallas kernels, gate_up_shares(): pl.pallas_call(functools.partial(gate_up_share, count), out_shape=[jax.Sh...  6.68 us
    ppermute x4, starting transfers between devices, to_mate(): return lax.ppermute(part, 'expert', [(i, i ^ turn) for i in range(groups)])  5.22 us
    pallas_call x1, Pallas kernels, layer(): pl.pallas_call(functools.partial(forward, cap, groups), out_shape=[jax.Sh...  5.04 us
  transfers between devices with their start and end apart: 38, of which 16 were waited for; matrix products, arithmetic and copies ran while one was open for 0% of the time, Pallas kernels for 28%

profile of v3, /device:TPU:0, one launch (start us, length us, event | category | flops | bytes accessed | tf_op | source)
XLA Modules:
  0.0 141.2 jit_solution(5300899822849001670)
XLA Ops:
  1.3 139.7 %conditional.1 = (bf16[128,2048]{1,0:T(8,128)(2,1)}, bf16[128,2048]{1,0:T(8,128)(2,1)}, f32[128,2]{0,1:T(2,128)}, f32[1,256,768]{2,1,0:T(8,128)}, f32[1,256,768]{2,1,0:T(8,128)}, /*index=5*/f32[1,768,256]{2,1,0:T(8,128)}) conditional(s32[]{:T(128)} %bitcast.9, (s32[2,128]{1,0:T(2,128)}, bf16[128,2048]{1,0:T(8,128)(2,1)}, ...), branch_computations={%region_0.1_spmd, %region_1.2_spmd, %region_2.3_spmd} | conditional | flops 26045 | bytes 145657648 | solution.py:413
  1.3 1.7 %place_tokens.3 = (bf16[80,2048]{1,0:T(8,128)(2,1)S(1)}, bf16[80,2048]{1,0:T(8,128)(2,1)S(1)}, bf16[80,2048]{1,0:T(8,128)(2,1)S(1)}, bf16[80,2048]{1,0:T(8,128)(2,1)S(1)}) custom-call(s32[1]{0:T(128)} %bitcast.me_ref, s32[2,128]{1,0:T(2,128)} %get-tuple-element.42.ids_ref, bf16[128,2048]{1,0:T(8,128)(2,1)} %get-tuple-element.424.tok_ref), custom_call_target="tpu_custom_call" | custom-call | tf_op jit(solution)/shard_map/cond/branch_0_fun/place_tokens/pallas_call | solution.py:454
  3.0 3.0 %collective-permute-start = (bf16[80,2048]{1,0:T(8,128)(2,1)S(1)}, bf16[80,2048]{1,0:T(8,128)(2,1)S(1)}, u32[]{:S(2)}, u32[]{:S(2)}) collective-permute-start(bf16[80,2048]{1,0:T(8,128)(2,1)S(1)} %get-tuple-element.47), channel_id=1, source_target_pairs={{0,1},{1,0},{2,3},{3,2},{4,5},{5,4},{6,7},{7,6},{8,9},{9,8},{10,11... | collective-permute-start | bytes 983048 | tf_op jit(solution)/shard_map/cond/branch_0_fun/ppermute | solution.py:436
  6.0 1.5 %collective-permute-start.1 = (bf16[80,2048]{1,0:T(8,128)(2,1)S(1)}, bf16[80,2048]{1,0:T(8,128)(2,1)S(1)}, u32[]{:S(2)}, u32[]{:S(2)}) collective-permute-start(bf16[80,2048]{1,0:T(8,128)(2,1)S(1)} %get-tuple-element.48), channel_id=1, source_target_pairs={{0,2},{1,3},{2,0},{3,1},{4,6},{5,7},{6,4},{7,5},{8,10},{9,11},{10,... | collective-permute-start | bytes 983048 | tf_op jit(solution)/shard_map/cond/branch_0_fun/ppermute | solution.py:436
  7.5 1.7 %place_grads.3 = (bf16[80,2048]{1,0:T(8,128)(2,1)S(1)}, bf16[80,2048]{1,0:T(8,128)(2,1)S(1)}, bf16[80,2048]{1,0:T(8,128)(2,1)S(1)}, bf16[80,2048]{1,0:T(8,128)(2,1)S(1)}) custom-call(s32[1]{0:T(128)} %bitcast.me_ref, s32[2,128]{1,0:T(2,128)} %get-tuple-element.42.ids_ref, f32[2,128]{1,0:T(2,128)} %get-tuple-element.43.gates_ref, ...), custom_call_target="tpu_custom_call" | custom-call | tf_op jit(solution)/shard_map/cond/branch_0_fun/place_grads/pallas_call | solution.py:462
  9.3 2.0 %collective-permute-start.4 = (bf16[80,2048]{1,0:T(8,128)(2,1)S(1)}, bf16[80,2048]{1,0:T(8,128)(2,1)S(1)}, u32[]{:S(2)}, u32[]{:S(2)}) collective-permute-start(bf16[80,2048]{1,0:T(8,128)(2,1)S(1)} %get-tuple-element.54), channel_id=1, source_target_pairs={{0,1},{1,0},{2,3},{3,2},{4,5},{5,4},{6,7},{7,6},{8,9},{9,8},{10,11... | collective-permute-start | bytes 983048 | tf_op jit(solution)/shard_map/cond/branch_0_fun/ppermute | solution.py:436
  11.3 1.5 %collective-permute-start.5 = (bf16[80,2048]{1,0:T(8,128)(2,1)S(1)}, bf16[80,2048]{1,0:T(8,128)(2,1)S(1)}, u32[]{:S(2)}, u32[]{:S(2)}) collective-permute-start(bf16[80,2048]{1,0:T(8,128)(2,1)S(1)} %get-tuple-element.55), channel_id=1, source_target_pairs={{0,2},{1,3},{2,0},{3,1},{4,6},{5,7},{6,4},{7,5},{8,10},{9,11},{10,... | collective-permute-start | bytes 983048 | tf_op jit(solution)/shard_map/cond/branch_0_fun/ppermute | solution.py:436
  12.8 1.7 %collective-permute-done.refs_1_ = bf16[80,2048]{1,0:T(8,128)(2,1)S(1)} collective-permute-done((bf16[80,2048]{1,0:T(8,128)(2,1)S(1)}, bf16[80,2048]{1,0:T(8,128)(2,1)S(1)}, u32[]{:S(2)}, u32[]{:S(2)}) %collective-permute-start) | collective-permute-done | bytes 327712 | tf_op jit(solution)/shard_map/cond/branch_0_fun/ppermute | solution.py:436
  14.5 3.0 %collective-permute-start.6 = (bf16[80,2048]{1,0:T(8,128)(2,1)S(1)}, bf16[80,2048]{1,0:T(8,128)(2,1)S(1)}, u32[]{:S(2)}, u32[]{:S(2)}) collective-permute-start(bf16[80,2048]{1,0:T(8,128)(2,1)S(1)} %get-tuple-element.56), channel_id=1, source_target_pairs={{0,3},{1,2},{2,1},{3,0},{4,7},{5,6},{6,5},{7,4},{8,11},{9,10},{10,... | collective-permute-start | bytes 983048 | tf_op jit(solution)/shard_map/cond/branch_0_fun/ppermute | solution.py:436
  17.6 6.1 %collective-permute-done.1.refs_2_ = bf16[80,2048]{1,0:T(8,128)(2,1)S(1)} collective-permute-done((bf16[80,2048]{1,0:T(8,128)(2,1)S(1)}, bf16[80,2048]{1,0:T(8,128)(2,1)S(1)}, u32[]{:S(2)}, u32[]{:S(2)}) %collective-permute-start.1) | collective-permute-done | bytes 327712 | tf_op jit(solution)/shard_map/cond/branch_0_fun/ppermute | solution.py:436
  23.7 5.0 %forward.3 = (bf16[320,2048]{1,0:T(8,128)(2,1)S(1)}, f32[2,320,768]{2,1,0:T(8,128)S(1)}, bf16[320,768]{1,0:T(8,128)(2,1)S(1)}) custom-call(bf16[80,2048]{1,0:T(8,128)(2,1)S(1)} %get-tuple-element.46.refs_0_, bf16[80,2048]{1,0:T(8,128)(2,1)S(1)} %collective-permute-done.refs_1_, bf16[80,2048]{1,0:T(8,128)(2,1)S(1)} %collective-permute-done.1.refs_2_, ...), custom_call_target="tpu_custom_call" | custom-call | flops 1000 | bytes 1000 | tf_op jit(solution)/shard_map/cond/branch_0_fun/forward/pallas_call | solution.py:474
  28.8 7.4 %collective-permute-done.5.refs_2_ = bf16[80,2048]{1,0:T(8,128)(2,1)S(1)} collective-permute-done((bf16[80,2048]{1,0:T(8,128)(2,1)S(1)}, bf16[80,2048]{1,0:T(8,128)(2,1)S(1)}, u32[]{:S(2)}, u32[]{:S(2)}) %collective-permute-start.5) | collective-permute-done | bytes 327712 | tf_op jit(solution)/shard_map/cond/branch_0_fun/ppermute | solution.py:436
  37.5 1.0 copy-done.3
  38.4 2.8 %backward.3.refs_8_.grad_ref = bf16[2,320,768]{2,1,0:T(8,128)(2,1)} custom-call(bf16[320,2048]{1,0:T(8,128)(2,1)S(1)} %join_grads.3.c_ref.c_own, bf16[1,768,2048]{2,1,0:T(8,128)(2,1)S(1)} %copy-done.57, f32[2,320,768]{2,1,0:T(8,128)S(1)} %get-tuple-element.64.pre_ref), custom_call_target="tpu_custom_call" | custom-call | flops 1000 | bytes 1000 | tf_op jit(solution)/shard_map/cond/branch_0_fun/backward/pallas_call | solution.py:498
  41.3 1.2 copy-done.4
  42.5 4.4 %down_shares.3 = (bf16[768,256]{1,0:T(8,128)(2,1)S(1)}, bf16[768,256]{1,0:T(8,128)(2,1)S(1)}, bf16[768,256]{1,0:T(8,128)(2,1)S(1)}, bf16[768,256]{1,0:T(8,128)(2,1)S(1)}) custom-call(s32[4]{0:T(128)S(1)} %fusion.1.order_ref, bf16[768,640]{1,0:T(8,128)(2,1)S(1)} %copy-done.4, bf16[320,2048]{1,0:T(8,128)(2,1)S(1)} %join_grads.3.c_ref.c_own, ...), custom_call_target="tpu_custom_call" | custom-call | flops 1000 | bytes 1000 | tf_op jit(solution)/shard_map/cond/branch_0_fun/down_shares/pallas_call | solution.py:317
  46.9 1.6 %collective-permute-start.14 = (bf16[768,256]{1,0:T(8,128)(2,1)S(1)}, bf16[768,256]{1,0:T(8,128)(2,1)S(1)}, u32[]{:S(2)}, u32[]{:S(2)}) collective-permute-start(bf16[768,256]{1,0:T(8,128)(2,1)S(1)} %get-tuple-element.85.right_ref), channel_id=1, source_target_pairs={{0,8},{4,12},{8,0},{12,4},{16,24},{20,28},{24,16},{28,20},{1,9},{5... | collective-permute-start | bytes 1179656 | tf_op jit(solution)/shard_map/cond/branch_0_fun/ppermute | solution.py:558
  49.0 2.1 %expert_rows.3 = (bf16[80,2048]{1,0:T(8,128)(2,1)S(1)}, bf16[80,2048]{1,0:T(8,128)(2,1)S(1)}, bf16[80,2048]{1,0:T(8,128)(2,1)S(1)}, bf16[80,2048]{1,0:T(8,128)(2,1)S(1)}) custom-call(bf16[320,768]{1,0:T(8,128)(2,1)S(1)} %get-tuple-element.67.own_ref.act_ref, bf16[1,768,2048]{2,1,0:T(8,128)(2,1)S(1)} %copy-done.58), custom_call_target="tpu_custom_call" | custom-call | flops 1000 | bytes 1000 | tf_op jit(solution)/shard_map/cond/branch_0_fun/expert_rows/pallas_call | solution.py:514
  51.8 1.3 collective-permute-start.8
  53.9 1.4 %collective-permute-start.10 = (bf16[80,2048]{1,0:T(8,128)(2,1)S(1)}, bf16[80,2048]{1,0:T(8,128)(2,1)S(1)}, u32[]{:S(2)}, u32[]{:S(2)}) collective-permute-start(bf16[80,2048]{1,0:T(8,128)(2,1)S(1)} %get-tuple-element.75), channel_id=1, source_target_pairs={{0,3},{1,2},{2,1},{3,0},{4,7},{5,6},{6,5},{7,4},{8,11},{9,10},{10,... | collective-permute-start | bytes 983048 | tf_op jit(solution)/shard_map/cond/branch_0_fun/ppermute | solution.py:436
  55.3 6.7 %gate_up_shares.3 = (bf16[256,768]{1,0:T(8,128)(2,1)}, bf16[256,768]{1,0:T(8,128)(2,1)S(1)}, bf16[256,768]{1,0:T(8,128)(2,1)S(1)}, bf16[256,768]{1,0:T(8,128)(2,...) custom-call(s32[4]{0:T(128)S(1)} %fusion.1.order_ref, ...), custom_call_target="tpu_custom_call" | custom-call | flops 1000 | bytes 1000 | tf_op jit(solution)/shard_map/cond/branch_0_fun/gate_up_shares/pallas_call | solution.py:340
  62.0 4.8 %input_rows.3 = (bf16[80,2048]{1,0:T(8,128)(2,1)S(1)}, bf16[80,2048]{1,0:T(8,128)(2,1)S(1)}, bf16[80,2048]{1,0:T(8,128)(2,1)}, bf16[80,2048]{1,0:T(8,128)(2,1)S(1)}) custom-call(bf16[2,320,768]{2,1,0:T(8,128)(2,1)} %backward.3.refs_8_.grad_ref, bf16[1,2048,768]{2,1,0:T(8,128)(2,1)S(1)} %copy-done.51, bf16[1,2048,768]{2,1,0:T(8,128)(2,1)S(1)} %copy-done.54), custom_call_target="tpu_custom_call" | custom-call | flops 1000 | bytes 1000 | tf_op jit(solution)/shard_map/cond/branch_0_fun/input_rows/pallas_call | solution.py:526
  71.1 1.6 %collective-permute-start.20 = (bf16[256,768]{1,0:T(8,128)(2,1)}, bf16[256,768]{1,0:T(8,128)(2,1)}, u32[]{:S(2)}, u32[]{:S(2)}) collective-permute-start(bf16[256,768]{1,0:T(8,128)(2,1)} %get-tuple-element.100.right_ref), channel_id=1, source_target_pairs={{0,8},{4,12},{8,0},{12,4},{16,24},{20,28},{24,16},{28,20},{1,9},{5... | collective-permute-start | bytes 1179656 | tf_op jit(solution)/shard_map/cond/branch_0_fun/ppermute | solution.py:558
  72.7 3.2 %collective-permute-start.18 = (bf16[256,768]{1,0:T(8,128)(2,1)}, bf16[256,768]{1,0:T(8,128)(2,1)}, u32[]{:S(2)}, u32[]{:S(2)}) collective-permute-start(bf16[256,768]{1,0:T(8,128)(2,1)} %get-tuple-element.105.right_ref), channel_id=1, source_target_pairs={{0,8},{4,12},{8,0},{12,4},{16,24},{20,28},{24,16},{28,20},{1,9},{5... | collective-permute-start | bytes 1179656 | tf_op jit(solution)/shard_map/cond/branch_0_fun/ppermute | solution.py:558
  75.8 2.9 %collective-permute-done.15.refs_5_ = bf16[80,2048]{1,0:T(8,128)(2,1)S(1)} collective-permute-done((bf16[80,2048]{1,0:T(8,128)(2,1)S(1)}, bf16[80,2048]{1,0:T(8,128)(2,1)S(1)}, u32[]{:S(2)}, u32[]{:S(2)}) %collective-permute-start.15) | collective-permute-done | bytes 327712 | tf_op jit(solution)/shard_map/cond/branch_0_fun/ppermute | solution.py:590
  80.3 3.2 %collective-permute-done.20.left_ref = bf16[256,768]{1,0:T(8,128)(2,1)} collective-permute-done((bf16[256,768]{1,0:T(8,128)(2,1)}, bf16[256,768]{1,0:T(8,128)(2,1)}, u32[]{:S(2)}, u32[]{:S(2)}) %collective-permute-start.20) | collective-permute-done | bytes 393248 | tf_op jit(solution)/shard_map/cond/branch_0_fun/ppermute | solution.py:558
  83.5 1.2 gate_mid1.3
  84.7 1.1 down_last.3
  85.8 1.7 %collective-permute-start.25 = (bf16[768,256]{1,0:T(8,128)(2,1)S(1)}, bf16[768,256]{1,0:T(8,128)(2,1)S(1)}, u32[]{:S(2)}, u32[]{:S(2)}) collective-permute-start(bf16[768,256]{1,0:T(8,128)(2,1)S(1)} %down_last.3), channel_id=1, source_target_pairs={{0,8},{4,12},{8,0},{12,4},{16,24},{20,28},{24,16},{28,20},{1,9},{5... | collective-permute-start | bytes 1179656 | tf_op jit(solution)/shard_map/cond/branch_0_fun/ppermute | solution.py:558
  87.5 4.4 %collective-permute-done.18.left_ref = bf16[256,768]{1,0:T(8,128)(2,1)} collective-permute-done((bf16[256,768]{1,0:T(8,128)(2,1)}, bf16[256,768]{1,0:T(8,128)(2,1)}, u32[]{:S(2)}, u32[]{:S(2)}) %collective-permute-start.18) | collective-permute-done | bytes 393248 | tf_op jit(solution)/shard_map/cond/branch_0_fun/ppermute | solution.py:558
  91.9 1.2 up_mid1.3
  93.1 2.8 %collective-permute-start.23 = (bf16[256,768]{1,0:T(8,128)(2,1)S(1)}, bf16[256,768]{1,0:T(8,128)(2,1)S(1)}, u32[]{:S(2)}, u32[]{:S(2)}) collective-permute-start(bf16[256,768]{1,0:T(8,128)(2,1)S(1)} %get-tuple-element.119.right_ref), channel_id=1, source_target_pairs={{0,8},{4,12},{8,0},{12,4},{16,24},{20,28},{24,16},{28,20},{1,9},{5... | collective-permute-start | bytes 1179656 | tf_op jit(solution)/shard_map/cond/branch_0_fun/ppermute | solution.py:558
  95.9 1.5 %collective-permute-start.17 = (bf16[80,2048]{1,0:T(8,128)(2,1)S(1)}, bf16[80,2048]{1,0:T(8,128)(2,1)S(1)}, u32[]{:S(2)}, u32[]{:S(2)}) collective-permute-start(bf16[80,2048]{1,0:T(8,128)(2,1)S(1)} %copy-done.46), channel_id=1, source_target_pairs={{0,3},{1,2},{2,1},{3,0},{4,7},{5,6},{6,5},{7,4},{8,11},{9,10},{10,... | collective-permute-start | bytes 983048 | tf_op jit(solution)/shard_map/cond/branch_0_fun/ppermute | solution.py:590
  97.4 2.8 %collective-permute-done.25.last_ref = bf16[768,256]{1,0:T(8,128)(2,1)S(1)} collective-permute-done((bf16[768,256]{1,0:T(8,128)(2,1)S(1)}, bf16[768,256]{1,0:T(8,128)(2,1)S(1)}, u32[]{:S(2)}, u32[]{:S(2)}) %collective-permute-start.25) | collective-permute-done | bytes 393248 | tf_op jit(solution)/shard_map/cond/branch_0_fun/ppermute | solution.py:558
  100.2 5.2 %collective-permute-done.17.refs_7_ = bf16[80,2048]{1,0:T(8,128)(2,1)S(1)} collective-permute-done((bf16[80,2048]{1,0:T(8,128)(2,1)S(1)}, bf16[80,2048]{1,0:T(8,128)(2,1)S(1)}, u32[]{:S(2)}, u32[]{:S(2)}) %collective-permute-start.17) | collective-permute-done | bytes 327712 | tf_op jit(solution)/shard_map/cond/branch_0_fun/ppermute | solution.py:590
  105.5 1.1 down_sum.3
  106.6 1.3 collective-permute-start.29
  108.9 3.5 %collective-permute-start.26 = (bf16[128,768]{1,0:T(8,128)(2,1)S(1)}, bf16[128,768]{1,0:T(8,128)(2,1)S(1)}, u32[]{:S(2)}, u32[]{:S(2)}) collective-permute-start(bf16[128,768]{1,0:T(8,128)(2,1)S(1)} %get-tuple-element.132.right_ref), channel_id=1, source_target_pairs={{0,8},{4,12},{8,0},{12,4},{16,24},{20,28},{24,16},{28,20},{1,9},{5... | collective-permute-start | bytes 589832 | tf_op jit(solution)/shard_map/cond/branch_0_fun/ppermute | solution.py:558
  112.4 7.3 %collective-permute-done.27.last_ref = bf16[256,768]{1,0:T(8,128)(2,1)S(1)} collective-permute-done((bf16[256,768]{1,0:T(8,128)(2,1)S(1)}, bf16[256,768]{1,0:T(8,128)(2,1)S(1)}, u32[]{:S(2)}, u32[]{:S(2)}) %collective-permute-start.27) | collective-permute-done | bytes 393248 | tf_op jit(solution)/shard_map/cond/branch_0_fun/ppermute | solution.py:558
  121.1 1.2 collective-permute-start.33
  122.3 1.6 %collective-permute-done.26.left_ref = bf16[128,768]{1,0:T(8,128)(2,1)S(1)} collective-permute-done((bf16[128,768]{1,0:T(8,128)(2,1)S(1)}, bf16[128,768]{1,0:T(8,128)(2,1)S(1)}, u32[]{:S(2)}, u32[]{:S(2)}) %collective-permute-start.26) | collective-permute-done | bytes 196640 | tf_op jit(solution)/shard_map/cond/branch_0_fun/ppermute | solution.py:558
  124.1 1.6 %collective-permute-start.30 = (bf16[128,768]{1,0:T(8,128)(2,1)S(1)}, bf16[128,768]{1,0:T(8,128)(2,1)S(1)}, u32[]{:S(2)}, u32[]{:S(2)}) collective-permute-start(bf16[128,768]{1,0:T(8,128)(2,1)S(1)} %get-tuple-element.133), channel_id=1, source_target_pairs={{0,8},{4,12},{8,0},{12,4},{16,24},{20,28},{24,16},{28,20},{1,9},{5... | collective-permute-start | bytes 589832 | tf_op jit(solution)/shard_map/cond/branch_0_fun/ppermute | solution.py:558
  126.5 0.9 slot_down.3
  127.5 2.2 %collective-permute-done.33.last_ref = bf16[128,768]{1,0:T(8,128)(2,1)S(1)} collective-permute-done((bf16[128,768]{1,0:T(8,128)(2,1)S(1)}, bf16[128,768]{1,0:T(8,128)(2,1)S(1)}, u32[]{:S(2)}, u32[]{:S(2)}) %collective-permute-start.33) | collective-permute-done | bytes 196640 | tf_op jit(solution)/shard_map/cond/branch_0_fun/ppermute | solution.py:558
  129.8 2.2 %collective-permute-start.36 = (bf16[128,768]{1,0:T(8,128)(2,1)S(1)}, bf16[128,768]{1,0:T(8,128)(2,1)S(1)}, u32[]{:S(2)}, u32[]{:S(2)}) collective-permute-start(bf16[128,768]{1,0:T(8,128)(2,1)S(1)} %up_sum0.3), channel_id=1, source_target_pairs={{0,1},{1,0},{2,3},{3,2},{4,5},{5,4},{6,7},{7,6},{8,9},{9,8},{10,11... | collective-permute-start | bytes 589832 | tf_op jit(solution)/shard_map/cond/branch_0_fun/ppermute | solution.py:565
  132.8 1.3 collective-permute-start.37
  134.1 3.1 %combine.3 = (bf16[128,2048]{1,0:T(8,128)(2,1)}, bf16[128,2048]{1,0:T(8,128)(2,1)}, f32[2,128]{1,0:T(2,128)}) custom-call(s32[1]{0:T(128)} %bitcast.me_ref, s32[2,128]{1,0:T(2,128)S(1)} %copy-done.66, f32[2,128]{1,0:T(2,128)S(1)} %copy-done.69, bf16[128,2048]{1,0:T(8,128)(2,1)S(1)} %copy-done.63, bf16[80,2048]{1,0:T(8,128)(2,1)S(1)} %copy-done.16, ...), custom_call_target="tpu_custom_call" | custom-call | flops 1000 | bytes 1000 | tf_op jit(solution)/shard_map/cond/branch_0_fun/combine/pallas_call | solution.py:538
  138.2 1.6 %collective-permute-done.37.refs_1_ = bf16[128,768]{1,0:T(8,128)(2,1)S(1)} collective-permute-done((bf16[128,768]{1,0:T(8,128)(2,1)S(1)}, bf16[128,768]{1,0:T(8,128)(2,1)S(1)}, u32[]{:S(2)}, u32[]{:S(2)}) %collective-permute-start.37) | collective-permute-done | bytes 196640 | tf_op jit(solution)/shard_map/cond/branch_0_fun/ppermute | solution.py:565
  (107 shorter events, 15.2 us)
Async XLA Ops:
  3.0 11.5 %collective-permute-start = (bf16[80,2048]{1,0:T(8,128)(2,1)S(1)}, bf16[80,2048]{1,0:T(8,128)(2,1)S(1)}, u32[]{:S(2)}, u32[]{:S(2)}) collective-permute-start(bf16[80,2048]{1,0:T(8,128)(2,1)S(1)} %get-tuple-element.47), channel_id=1, source_target_pairs={{0,1},{1,0},{2,3},{3,2},{4,5},{5,4},{6,7},{7,6},{8,9},{9,8},{10,11... | collective-permute-start | bytes 983048 | tf_op jit(solution)/shard_map/cond/branch_0_fun/ppermute | solution.py:436
  6.0 17.7 %collective-permute-start.1 = (bf16[80,2048]{1,0:T(8,128)(2,1)S(1)}, bf16[80,2048]{1,0:T(8,128)(2,1)S(1)}, u32[]{:S(2)}, u32[]{:S(2)}) collective-permute-start(bf16[80,2048]{1,0:T(8,128)(2,1)S(1)} %get-tuple-element.48), channel_id=1, source_target_pairs={{0,2},{1,3},{2,0},{3,1},{4,6},{5,7},{6,4},{7,5},{8,10},{9,11},{10,... | collective-permute-start | bytes 983048 | tf_op jit(solution)/shard_map/cond/branch_0_fun/ppermute | solution.py:436
  7.5 16.1 %collective-permute-start.2 = (bf16[80,2048]{1,0:T(8,128)(2,1)S(1)}, bf16[80,2048]{1,0:T(8,128)(2,1)S(1)}, u32[]{:S(2)}, u32[]{:S(2)}) collective-permute-start(bf16[80,2048]{1,0:T(8,128)(2,1)S(1)} %get-tuple-element.49), channel_id=1, source_target_pairs={{0,3},{1,2},{2,1},{3,0},{4,7},{5,6},{6,5},{7,4},{8,11},{9,10},{10,... | collective-permute-start | bytes 983048 | tf_op jit(solution)/shard_map/cond/branch_0_fun/ppermute | solution.py:436
  9.3 19.5 %collective-permute-start.4 = (bf16[80,2048]{1,0:T(8,128)(2,1)S(1)}, bf16[80,2048]{1,0:T(8,128)(2,1)S(1)}, u32[]{:S(2)}, u32[]{:S(2)}) collective-permute-start(bf16[80,2048]{1,0:T(8,128)(2,1)S(1)} %get-tuple-element.54), channel_id=1, source_target_pairs={{0,1},{1,0},{2,3},{3,2},{4,5},{5,4},{6,7},{7,6},{8,9},{9,8},{10,11... | collective-permute-start | bytes 983048 | tf_op jit(solution)/shard_map/cond/branch_0_fun/ppermute | solution.py:436
  11.3 25.0 %collective-permute-start.5 = (bf16[80,2048]{1,0:T(8,128)(2,1)S(1)}, bf16[80,2048]{1,0:T(8,128)(2,1)S(1)}, u32[]{:S(2)}, u32[]{:S(2)}) collective-permute-start(bf16[80,2048]{1,0:T(8,128)(2,1)S(1)} %get-tuple-element.55), channel_id=1, source_target_pairs={{0,2},{1,3},{2,0},{3,1},{4,6},{5,7},{6,4},{7,5},{8,10},{9,11},{10,... | collective-permute-start | bytes 983048 | tf_op jit(solution)/shard_map/cond/branch_0_fun/ppermute | solution.py:436
  14.5 21.7 %collective-permute-start.6 = (bf16[80,2048]{1,0:T(8,128)(2,1)S(1)}, bf16[80,2048]{1,0:T(8,128)(2,1)S(1)}, u32[]{:S(2)}, u32[]{:S(2)}) collective-permute-start(bf16[80,2048]{1,0:T(8,128)(2,1)S(1)} %get-tuple-element.56), channel_id=1, source_target_pairs={{0,3},{1,2},{2,1},{3,0},{4,7},{5,6},{6,5},{7,4},{8,11},{9,10},{10,... | collective-permute-start | bytes 983048 | tf_op jit(solution)/shard_map/cond/branch_0_fun/ppermute | solution.py:436
  28.7 7.7 %copy-start = (bf16[320,2048]{1,0:T(8,128)(2,1)}, bf16[320,2048]{1,0:T(8,128)(2,1)S(1)}, u32[]{:S(2)}) copy-start(bf16[320,2048]{1,0:T(8,128)(2,1)S(1)} %get-tuple-element.77.refs_0_.refs_1_.refs_2_.refs_3_) | copy-start | bytes 3932164 | tf_op jit(solution)/shard_map/cond
  28.7 8.2 %collective-permute-start.3 = (bf16[320,768]{1,0:T(8,128)(2,1)S(1)}, bf16[320,768]{1,0:T(8,128)(2,1)S(1)}, u32[]{:S(2)}, u32[]{:S(2)}) collective-permute-start(bf16[320,768]{1,0:T(8,128)(2,1)S(1)} %get-tuple-element.67.own_ref.act_ref), channel_id=1, source_target_pairs={{0,4},{4,0},{8,12},{12,8},{16,20},{20,16},{24,28},{28,24},{1,5},{5... | collective-permute-start | bytes 1474568 | tf_op jit(solution)/shard_map/cond/branch_0_fun/ppermute | solution.py:441
  36.3 5.0 %collective-permute-start.7 = (bf16[320,2048]{1,0:T(8,128)(2,1)S(1)}, bf16[320,2048]{1,0:T(8,128)(2,1)}, u32[]{:S(2)}, u32[]{:S(2)}) collective-permute-start(bf16[320,2048]{1,0:T(8,128)(2,1)S(1)} %join_grads.3.c_ref.c_own), channel_id=1, source_target_pairs={{0,4},{4,0},{8,12},{12,8},{16,20},{20,16},{24,28},{28,24},{1,5},{5... | collective-permute-start | bytes 3932168 | tf_op jit(solution)/shard_map/cond/branch_0_fun/ppermute | solution.py:441
  36.4 16.7 %collective-permute-start.11 = (bf16[320,2048]{1,0:T(8,128)(2,1)S(1)}, bf16[320,2048]{1,0:T(8,128)(2,1)}, u32[]{:S(2)}, u32[]{:S(2)}) collective-permute-start(bf16[320,2048]{1,0:T(8,128)(2,1)S(1)} %get-tuple-element.77.refs_0_.refs_1_.refs_2_.refs_3_), channel_id=1, source_target_pairs={{0,4},{4,0},{8,12},{12,8},{16,20},{20,16},{24,28},{28,24},{1,5},{5... | collective-permute-start | bytes 3932168 | tf_op jit(solution)/shard_map/cond/branch_0_fun/ppermute | solution.py:441
  41.2 12.7 %collective-permute-start.12 = (bf16[2,320,768]{2,1,0:T(8,128)(2,1)}, bf16[2,320,768]{2,1,0:T(8,128)(2,1)}, u32[]{:S(2)}, u32[]{:S(2)}) collective-permute-start(bf16[2,320,768]{2,1,0:T(8,128)(2,1)} %backward.3.refs_8_.grad_ref), channel_id=1, source_target_pairs={{0,4},{4,0},{8,12},{12,8},{16,20},{20,16},{24,28},{28,24},{1,5},{5... | collective-permute-start | bytes 2949128 | tf_op jit(solution)/shard_map/cond/branch_0_fun/ppermute | solution.py:441
  46.9 20.6 %collective-permute-start.14 = (bf16[768,256]{1,0:T(8,128)(2,1)S(1)}, bf16[768,256]{1,0:T(8,128)(2,1)S(1)}, u32[]{:S(2)}, u32[]{:S(2)}) collective-permute-start(bf16[768,256]{1,0:T(8,128)(2,1)S(1)} %get-tuple-element.85.right_ref), channel_id=1, source_target_pairs={{0,8},{4,12},{8,0},{12,4},{16,24},{20,28},{24,16},{28,20},{1,9},{5... | collective-permute-start | bytes 1179656 | tf_op jit(solution)/shard_map/cond/branch_0_fun/ppermute | solution.py:558
  48.6 20.8 %collective-permute-start.13 = (bf16[768,256]{1,0:T(8,128)(2,1)S(1)}, bf16[768,256]{1,0:T(8,128)(2,1)S(1)}, u32[]{:S(2)}, u32[]{:S(2)}) collective-permute-start(bf16[768,256]{1,0:T(8,128)(2,1)S(1)} %get-tuple-element.87.right_ref), channel_id=1, source_target_pairs={{0,8},{4,12},{8,0},{12,4},{16,24},{20,28},{24,16},{28,20},{1,9},{5... | collective-permute-start | bytes 1179656 | tf_op jit(solution)/shard_map/cond/branch_0_fun/ppermute | solution.py:558
  51.8 16.6 %collective-permute-start.8 = (bf16[80,2048]{1,0:T(8,128)(2,1)S(1)}, bf16[80,2048]{1,0:T(8,128)(2,1)S(1)}, u32[]{:S(2)}, u32[]{:S(2)}) collective-permute-start(bf16[80,2048]{1,0:T(8,128)(2,1)S(1)} %get-tuple-element.73), channel_id=1, source_target_pairs={{0,1},{1,0},{2,3},{3,2},{4,5},{5,4},{6,7},{7,6},{8,9},{9,8},{10,11... | collective-permute-start | bytes 983048 | tf_op jit(solution)/shard_map/cond/branch_0_fun/ppermute | solution.py:436
  53.1 15.3 %collective-permute-start.9 = (bf16[80,2048]{1,0:T(8,128)(2,1)S(1)}, bf16[80,2048]{1,0:T(8,128)(2,1)S(1)}, u32[]{:S(2)}, u32[]{:S(2)}) collective-permute-start(bf16[80,2048]{1,0:T(8,128)(2,1)S(1)} %get-tuple-element.74), channel_id=1, source_target_pairs={{0,2},{1,3},{2,0},{3,1},{4,6},{5,7},{6,4},{7,5},{8,10},{9,11},{10,... | collective-permute-start | bytes 983048 | tf_op jit(solution)/shard_map/cond/branch_0_fun/ppermute | solution.py:436
  53.9 15.5 %collective-permute-start.10 = (bf16[80,2048]{1,0:T(8,128)(2,1)S(1)}, bf16[80,2048]{1,0:T(8,128)(2,1)S(1)}, u32[]{:S(2)}, u32[]{:S(2)}) collective-permute-start(bf16[80,2048]{1,0:T(8,128)(2,1)S(1)} %get-tuple-element.75), channel_id=1, source_target_pairs={{0,3},{1,2},{2,1},{3,0},{4,7},{5,6},{6,5},{7,4},{8,11},{9,10},{10,... | collective-permute-start | bytes 983048 | tf_op jit(solution)/shard_map/cond/branch_0_fun/ppermute | solution.py:436
  55.3 6.7 %copy-start.51 = (bf16[1,2048,768]{2,1,0:T(8,128)(2,1)S(1)}, bf16[1,2048,768]{2,1,0:T(8,128)(2,1)}, u32[]{:S(2)}) copy-start(bf16[1,2048,768]{2,1,0:T(8,128)(2,1)} %get-tuple-element.427.refs_4_.gate_ref) | copy-start | bytes 9437188 | tf_op jit(solution)/shard_map/cond
  55.3 6.7 %copy-start.54 = (bf16[1,2048,768]{2,1,0:T(8,128)(2,1)S(1)}, bf16[1,2048,768]{2,1,0:T(8,128)(2,1)}, u32[]{:S(2)}) copy-start(bf16[1,2048,768]{2,1,0:T(8,128)(2,1)} %get-tuple-element.430.refs_5_.up_ref) | copy-start | bytes 9437188 | tf_op jit(solution)/shard_map/cond
  67.5 11.2 %copy-start.45 = (bf16[80,2048]{1,0:T(8,128)(2,1)}, bf16[80,2048]{1,0:T(8,128)(2,1)S(1)}, u32[]{:S(2)}) copy-start(bf16[80,2048]{1,0:T(8,128)(2,1)S(1)} %get-tuple-element.92) | copy-start | bytes 983044 | tf_op jit(solution)/shard_map/cond
  68.4 16.3 %copy-start.10 = (bf16[768,256]{1,0:T(8,128)(2,1)S(1)}, bf16[768,256]{1,0:T(8,128)(2,1)}, u32[]{:S(2)}) copy-start(bf16[768,256]{1,0:T(8,128)(2,1)} %copy-done.9) | copy-start | bytes 1179652 | tf_op jit(solution)/shard_map/cond
  70.2 8.6 %collective-permute-start.15 = (bf16[80,2048]{1,0:T(8,128)(2,1)S(1)}, bf16[80,2048]{1,0:T(8,128)(2,1)S(1)}, u32[]{:S(2)}, u32[]{:S(2)}) collective-permute-start(bf16[80,2048]{1,0:T(8,128)(2,1)S(1)} %get-tuple-element.88), channel_id=1, source_target_pairs={{0,1},{1,0},{2,3},{3,2},{4,5},{5,4},{6,7},{7,6},{8,9},{9,8},{10,11... | collective-permute-start | bytes 983048 | tf_op jit(solution)/shard_map/cond/branch_0_fun/ppermute | solution.py:590
  71.1 12.4 %collective-permute-start.20 = (bf16[256,768]{1,0:T(8,128)(2,1)}, bf16[256,768]{1,0:T(8,128)(2,1)}, u32[]{:S(2)}, u32[]{:S(2)}) collective-permute-start(bf16[256,768]{1,0:T(8,128)(2,1)} %get-tuple-element.100.right_ref), channel_id=1, source_target_pairs={{0,8},{4,12},{8,0},{12,4},{16,24},{20,28},{24,16},{28,20},{1,9},{5... | collective-permute-start | bytes 1179656 | tf_op jit(solution)/shard_map/cond/branch_0_fun/ppermute | solution.py:558
  72.7 12.0 %collective-permute-start.19 = (bf16[768,256]{1,0:T(8,128)(2,1)}, bf16[768,256]{1,0:T(8,128)(2,1)}, u32[]{:S(2)}, u32[]{:S(2)}) collective-permute-start(bf16[768,256]{1,0:T(8,128)(2,1)} %down_mid1.3), channel_id=1, source_target_pairs={{8,16},{16,8},{12,20},{20,12},{0,4},{4,0},{24,28},{28,24},{9,17},{... | collective-permute-start | bytes 1179656 | tf_op jit(solution)/shard_map/cond/branch_0_fun/ppermute | solution.py:562
  72.7 19.2 %collective-permute-start.18 = (bf16[256,768]{1,0:T(8,128)(2,1)}, bf16[256,768]{1,0:T(8,128)(2,1)}, u32[]{:S(2)}, u32[]{:S(2)}) collective-permute-start(bf16[256,768]{1,0:T(8,128)(2,1)} %get-tuple-element.105.right_ref), channel_id=1, source_target_pairs={{0,8},{4,12},{8,0},{12,4},{16,24},{20,28},{24,16},{28,20},{1,9},{5... | collective-permute-start | bytes 1179656 | tf_op jit(solution)/shard_map/cond/branch_0_fun/ppermute | solution.py:558
  75.8 16.1 %collective-permute-start.21 = (bf16[768,256]{1,0:T(8,128)(2,1)}, bf16[768,256]{1,0:T(8,128)(2,1)}, u32[]{:S(2)}, u32[]{:S(2)}) collective-permute-start(bf16[768,256]{1,0:T(8,128)(2,1)} %down_mid2.3), channel_id=1, source_target_pairs={{8,16},{16,8},{12,20},{20,12},{0,4},{4,0},{24,28},{28,24},{9,17},{... | collective-permute-start | bytes 1179656 | tf_op jit(solution)/shard_map/cond/branch_0_fun/ppermute | solution.py:562
  79.5 12.4 %collective-permute-start.16 = (bf16[80,2048]{1,0:T(8,128)(2,1)}, bf16[80,2048]{1,0:T(8,128)(2,1)}, u32[]{:S(2)}, u32[]{:S(2)}) collective-permute-start(bf16[80,2048]{1,0:T(8,128)(2,1)} %get-tuple-element.90), channel_id=1, source_target_pairs={{0,2},{1,3},{2,0},{3,1},{4,6},{5,7},{6,4},{7,5},{8,10},{9,11},{10,... | collective-permute-start | bytes 983048 | tf_op jit(solution)/shard_map/cond/branch_0_fun/ppermute | solution.py:590
  84.7 11.2 %copy-start.46 = (bf16[80,2048]{1,0:T(8,128)(2,1)S(1)}, bf16[80,2048]{1,0:T(8,128)(2,1)}, u32[]{:S(2)}) copy-start(bf16[80,2048]{1,0:T(8,128)(2,1)} %copy-done.45) | copy-start | bytes 983044 | tf_op jit(solution)/shard_map/cond
  85.8 14.4 %collective-permute-start.25 = (bf16[768,256]{1,0:T(8,128)(2,1)S(1)}, bf16[768,256]{1,0:T(8,128)(2,1)S(1)}, u32[]{:S(2)}, u32[]{:S(2)}) collective-permute-start(bf16[768,256]{1,0:T(8,128)(2,1)S(1)} %down_last.3), channel_id=1, source_target_pairs={{0,8},{4,12},{8,0},{12,4},{16,24},{20,28},{24,16},{28,20},{1,9},{5... | collective-permute-start | bytes 1179656 | tf_op jit(solution)/shard_map/cond/branch_0_fun/ppermute | solution.py:558
  87.5 20.4 %collective-permute-start.24 = (bf16[256,768]{1,0:T(8,128)(2,1)S(1)}, bf16[256,768]{1,0:T(8,128)(2,1)S(1)}, u32[]{:S(2)}, u32[]{:S(2)}) collective-permute-start(bf16[256,768]{1,0:T(8,128)(2,1)S(1)} %gate_mid1.3), channel_id=1, source_target_pairs={{8,16},{16,8},{12,20},{20,12},{0,4},{4,0},{24,28},{28,24},{9,17},{... | collective-permute-start | bytes 1179656 | tf_op jit(solution)/shard_map/cond/branch_0_fun/ppermute | solution.py:562
  93.1 15.5 %collective-permute-start.23 = (bf16[256,768]{1,0:T(8,128)(2,1)S(1)}, bf16[256,768]{1,0:T(8,128)(2,1)S(1)}, u32[]{:S(2)}, u32[]{:S(2)}) collective-permute-start(bf16[256,768]{1,0:T(8,128)(2,1)S(1)} %get-tuple-element.119.right_ref), channel_id=1, source_target_pairs={{0,8},{4,12},{8,0},{12,4},{16,24},{20,28},{24,16},{28,20},{1,9},{5... | collective-permute-start | bytes 1179656 | tf_op jit(solution)/shard_map/cond/branch_0_fun/ppermute | solution.py:558
  95.9 9.6 %collective-permute-start.17 = (bf16[80,2048]{1,0:T(8,128)(2,1)S(1)}, bf16[80,2048]{1,0:T(8,128)(2,1)S(1)}, u32[]{:S(2)}, u32[]{:S(2)}) collective-permute-start(bf16[80,2048]{1,0:T(8,128)(2,1)S(1)} %copy-done.46), channel_id=1, source_target_pairs={{0,3},{1,2},{2,1},{3,0},{4,7},{5,6},{6,5},{7,4},{8,11},{9,10},{10,... | collective-permute-start | bytes 983048 | tf_op jit(solution)/shard_map/cond/branch_0_fun/ppermute | solution.py:590
  97.4 11.5 %collective-permute-start.22 = (bf16[256,768]{1,0:T(8,128)(2,1)S(1)}, bf16[256,768]{1,0:T(8,128)(2,1)S(1)}, u32[]{:S(2)}, u32[]{:S(2)}) collective-permute-start(bf16[256,768]{1,0:T(8,128)(2,1)S(1)} %up_mid1.3), channel_id=1, source_target_pairs={{8,16},{16,8},{12,20},{20,12},{0,4},{4,0},{24,28},{28,24},{9,17},{... | collective-permute-start | bytes 1179656 | tf_op jit(solution)/shard_map/cond/branch_0_fun/ppermute | solution.py:562
  106.6 13.1 %collective-permute-start.29 = (bf16[768,256]{1,0:T(8,128)(2,1)S(1)}, bf16[768,256]{1,0:T(8,128)(2,1)S(1)}, u32[]{:S(2)}, u32[]{:S(2)}) collective-permute-start(bf16[768,256]{1,0:T(8,128)(2,1)S(1)} %down_sum.3), channel_id=1, source_target_pairs={{0,1},{1,0},{2,3},{3,2},{4,5},{5,4},{6,7},{7,6},{8,9},{9,8},{10,11... | collective-permute-start | bytes 1179656 | tf_op jit(solution)/shard_map/cond/branch_0_fun/ppermute | solution.py:565
  108.0 11.7 %collective-permute-start.27 = (bf16[256,768]{1,0:T(8,128)(2,1)S(1)}, bf16[256,768]{1,0:T(8,128)(2,1)S(1)}, u32[]{:S(2)}, u32[]{:S(2)}) collective-permute-start(bf16[256,768]{1,0:T(8,128)(2,1)S(1)} %gate_last.3), channel_id=1, source_target_pairs={{0,8},{4,12},{8,0},{12,4},{16,24},{20,28},{24,16},{28,20},{1,9},{5... | collective-permute-start | bytes 1179656 | tf_op jit(solution)/shard_map/cond/branch_0_fun/ppermute | solution.py:558
  108.8 11.0 %collective-permute-start.28 = (bf16[256,768]{1,0:T(8,128)(2,1)S(1)}, bf16[256,768]{1,0:T(8,128)(2,1)S(1)}, u32[]{:S(2)}, u32[]{:S(2)}) collective-permute-start(bf16[256,768]{1,0:T(8,128)(2,1)S(1)} %gate_mid2.3), channel_id=1, source_target_pairs={{8,16},{16,8},{12,20},{20,12},{0,4},{4,0},{24,28},{28,24},{9,17},{... | collective-permute-start | bytes 1179656 | tf_op jit(solution)/shard_map/cond/branch_0_fun/ppermute | solution.py:562
  108.9 15.0 %collective-permute-start.26 = (bf16[128,768]{1,0:T(8,128)(2,1)S(1)}, bf16[128,768]{1,0:T(8,128)(2,1)S(1)}, u32[]{:S(2)}, u32[]{:S(2)}) collective-permute-start(bf16[128,768]{1,0:T(8,128)(2,1)S(1)} %get-tuple-element.132.right_ref), channel_id=1, source_target_pairs={{0,8},{4,12},{8,0},{12,4},{16,24},{20,28},{24,16},{28,20},{1,9},{5... | collective-permute-start | bytes 589832 | tf_op jit(solution)/shard_map/cond/branch_0_fun/ppermute | solution.py:558
  119.8 9.9 %collective-permute-start.35 = (bf16[256,768]{1,0:T(8,128)(2,1)S(1)}, bf16[256,768]{1,0:T(8,128)(2,1)S(1)}, u32[]{:S(2)}, u32[]{:S(2)}) collective-permute-start(bf16[256,768]{1,0:T(8,128)(2,1)S(1)} %gate_sum.3), channel_id=1, source_target_pairs={{0,1},{1,0},{2,3},{3,2},{4,5},{5,4},{6,7},{7,6},{8,9},{9,8},{10,11... | collective-permute-start | bytes 1179656 | tf_op jit(solution)/shard_map/cond/branch_0_fun/ppermute | solution.py:565
  120.2 6.1 %collective-permute-start.31 = (bf16[128,768]{1,0:T(8,128)(2,1)S(1)}, bf16[128,768]{1,0:T(8,128)(2,1)S(1)}, u32[]{:S(2)}, u32[]{:S(2)}) collective-permute-start(bf16[128,768]{1,0:T(8,128)(2,1)S(1)} %get-tuple-element.136.right_ref), channel_id=1, source_target_pairs={{0,8},{4,12},{8,0},{12,4},{16,24},{20,28},{24,16},{28,20},{1,9},{5... | collective-permute-start | bytes 589832 | tf_op jit(solution)/shard_map/cond/branch_0_fun/ppermute | solution.py:558
  121.1 8.6 %collective-permute-start.33 = (bf16[128,768]{1,0:T(8,128)(2,1)S(1)}, bf16[128,768]{1,0:T(8,128)(2,1)S(1)}, u32[]{:S(2)}, u32[]{:S(2)}) collective-permute-start(bf16[128,768]{1,0:T(8,128)(2,1)S(1)} %get-tuple-element.137), channel_id=1, source_target_pairs={{0,8},{4,12},{8,0},{12,4},{16,24},{20,28},{24,16},{28,20},{1,9},{5... | collective-permute-start | bytes 589832 | tf_op jit(solution)/shard_map/cond/branch_0_fun/ppermute | solution.py:558
  124.0 5.7 %collective-permute-start.34 = (bf16[128,768]{1,0:T(8,128)(2,1)S(1)}, bf16[128,768]{1,0:T(8,128)(2,1)S(1)}, u32[]{:S(2)}, u32[]{:S(2)}) collective-permute-start(bf16[128,768]{1,0:T(8,128)(2,1)S(1)} %up_mid20.3), channel_id=1, source_target_pairs={{8,16},{16,8},{12,20},{20,12},{0,4},{4,0},{24,28},{28,24},{9,17},{... | collective-permute-start | bytes 589832 | tf_op jit(solution)/shard_map/cond/branch_0_fun/ppermute | solution.py:562
  124.1 8.6 %collective-permute-start.30 = (bf16[128,768]{1,0:T(8,128)(2,1)S(1)}, bf16[128,768]{1,0:T(8,128)(2,1)S(1)}, u32[]{:S(2)}, u32[]{:S(2)}) collective-permute-start(bf16[128,768]{1,0:T(8,128)(2,1)S(1)} %get-tuple-element.133), channel_id=1, source_target_pairs={{0,8},{4,12},{8,0},{12,4},{16,24},{20,28},{24,16},{28,20},{1,9},{5... | collective-permute-start | bytes 589832 | tf_op jit(solution)/shard_map/cond/branch_0_fun/ppermute | solution.py:558
  126.4 6.3 %collective-permute-start.32 = (bf16[128,768]{1,0:T(8,128)(2,1)S(1)}, bf16[128,768]{1,0:T(8,128)(2,1)S(1)}, u32[]{:S(2)}, u32[]{:S(2)}) collective-permute-start(bf16[128,768]{1,0:T(8,128)(2,1)S(1)} %up_mid21.3), channel_id=1, source_target_pairs={{8,16},{16,8},{12,20},{20,12},{0,4},{4,0},{24,28},{28,24},{9,17},{... | collective-permute-start | bytes 589832 | tf_op jit(solution)/shard_map/cond/branch_0_fun/ppermute | solution.py:562
  127.4 6.6 %copy-start.16 = (bf16[80,2048]{1,0:T(8,128)(2,1)S(1)}, bf16[80,2048]{1,0:T(8,128)(2,1)}, u32[]{:S(2)}) copy-start(bf16[80,2048]{1,0:T(8,128)(2,1)} %copy-done.15) | copy-start | bytes 983044 | tf_op jit(solution)/shard_map/cond
  127.4 6.6 %copy-start.22 = (bf16[80,2048]{1,0:T(8,128)(2,1)S(1)}, bf16[80,2048]{1,0:T(8,128)(2,1)}, u32[]{:S(2)}) copy-start(bf16[80,2048]{1,0:T(8,128)(2,1)} %copy-done.21) | copy-start | bytes 983044 | tf_op jit(solution)/shard_map/cond
  127.5 6.6 %copy-start.28 = (bf16[80,2048]{1,0:T(8,128)(2,1)S(1)}, bf16[80,2048]{1,0:T(8,128)(2,1)}, u32[]{:S(2)}) copy-start(bf16[80,2048]{1,0:T(8,128)(2,1)} %copy-done.27) | copy-start | bytes 983044 | tf_op jit(solution)/shard_map/cond
  127.5 6.6 %copy-start.34 = (bf16[80,2048]{1,0:T(8,128)(2,1)S(1)}, bf16[80,2048]{1,0:T(8,128)(2,1)}, u32[]{:S(2)}) copy-start(bf16[80,2048]{1,0:T(8,128)(2,1)} %copy-done.33) | copy-start | bytes 983044 | tf_op jit(solution)/shard_map/cond
  129.8 8.4 %collective-permute-start.36 = (bf16[128,768]{1,0:T(8,128)(2,1)S(1)}, bf16[128,768]{1,0:T(8,128)(2,1)S(1)}, u32[]{:S(2)}, u32[]{:S(2)}) collective-permute-start(bf16[128,768]{1,0:T(8,128)(2,1)S(1)} %up_sum0.3), channel_id=1, source_target_pairs={{0,1},{1,0},{2,3},{3,2},{4,5},{5,4},{6,7},{7,6},{8,9},{9,8},{10,11... | collective-permute-start | bytes 589832 | tf_op jit(solution)/shard_map/cond/branch_0_fun/ppermute | solution.py:565
  132.8 7.1 %collective-permute-start.37 = (bf16[128,768]{1,0:T(8,128)(2,1)S(1)}, bf16[128,768]{1,0:T(8,128)(2,1)S(1)}, u32[]{:S(2)}, u32[]{:S(2)}) collective-permute-start(bf16[128,768]{1,0:T(8,128)(2,1)S(1)} %up_sum1.3), channel_id=1, source_target_pairs={{0,1},{1,0},{2,3},{3,2},{4,5},{5,4},{6,7},{7,6},{8,9},{9,8},{10,11... | collective-permute-start | bytes 589832 | tf_op jit(solution)/shard_map/cond/branch_0_fun/ppermute | solution.py:565
  (14 other events, 46.2 us)

commit v4 on v3

--- a/solution.py
+++ b/solution.py
@@ -7,7 +7,7 @@
 from jax.experimental.pallas import tpu as pltpu
 from jax.sharding import PartitionSpec as P
 
-VMEM_BYTES = 48 * 1024 * 1024
+VMEM_BYTES = 47 * 1024 * 1024
 F32 = jnp.float32
 BF16 = jnp.bfloat16
 
@@ -108,22 +108,28 @@
     out_ref[...] = jnp.concatenate([block[...] for block in blocks], axis=0)
 
 
-def expert_rows(cap, act_ref, down_ref, *outs):
-    rows = dot_nn(act_ref[...], down_ref[0])
-    for b, out in enumerate(outs):
-        out[...] = rows[b * cap : (b + 1) * cap].astype(BF16)
-
-
-def input_rows(cap, grad_ref, gate_ref, up_ref, *outs):
-    rows = dot_nt(grad_ref[0], gate_ref[0]) + dot_nt(grad_ref[1], up_ref[0])
-    for b, out in enumerate(outs):
-        out[...] = rows[b * cap : (b + 1) * cap].astype(BF16)
+def result_rows(cap, act_ref, grad_ref, down_ref, gate_ref, up_ref, *outs):
+    both_rows = (
+        dot_nn(act_ref[...], down_ref[0]),
+        dot_nt(grad_ref[0], gate_ref[0]) + dot_nt(grad_ref[1], up_ref[0]),
+    )
+    for n, rows in enumerate(both_rows):
+        for b, out in enumerate(outs):
+            out[n] = rows[b * cap : (b + 1) * cap].astype(BF16)
 
 
 def both(own_ref, other_ref, *at):
     if at:
         return jnp.concatenate([own_ref[at[0]], other_ref[at[0]]], axis=0)
     return jnp.concatenate([own_ref[...], other_ref[...]], axis=0)
+
+
+def store_at_step(outs, value):
+    for n, out in enumerate(outs):
+
+        @pl.when(pl.program_id(0) == n)
+        def _(out=out):
+            out[...] = value
 
 
 def store_at_step(outs, value):
@@ -154,8 +160,14 @@
     )(own, other)
 
 
-def down_share(order_ref, act_ref, c_own, c_other, *outs):
-    store_at_step(outs, dot_nn(act_ref[...], both(c_own, c_other)).astype(BF16))
+def down_share(order_ref, act_own, act_other, c_own, c_other, *outs_and_turned):
+    *outs, act_turned = outs_and_turned
+
+    @pl.when(pl.program_id(0) == 0)
+    def _():
+        act_turned[...] = both(act_own, act_other).T
+
+    store_at_step(outs, dot_nn(act_turned[...], both(c_own, c_other)).astype(BF16))
 
 
 def gate_up_share(count, order_ref, *refs):
@@ -269,8 +281,8 @@
 
 
 def combine(cap, groups, me_ref, ids_ref, gates_ref, cot_ref, *refs):
-    outs, grads = refs[:groups], refs[groups : 2 * groups]
-    mixed_ref, token_ref, dots_ref = refs[2 * groups :]
+    results = refs[:groups]
+    mixed_ref, token_ref, dots_ref = refs[groups:]
     picks = [pick.astype(BF16) for pick in picks_of(ids_ref[...], cap, groups, me_ref[0])]
     gates = gates_ref[...]
     count, width = mixed_ref.shape
@@ -285,7 +297,7 @@
     dots = [0.0] * len(picks)
     for start in range(0, width, tile):
         cols = slice(start, start + tile)
-        rows = jnp.concatenate([ref[:, cols] for ref in outs], axis=0)
+        rows = jnp.concatenate([ref[0, :, cols] for ref in results], axis=0)
         cot = cot_ref[:, cols].astype(F32)
         mixed = 0.0
         for k, pick in enumerate(picks):
@@ -293,7 +305,7 @@
             mixed = mixed + weights[k] * picked
             dots[k] = dots[k] + jnp.sum(cot * picked, axis=1, keepdims=True)
         mixed_ref[:, cols] = mixed.astype(BF16)
-        rows = jnp.concatenate([ref[:, cols] for ref in grads], axis=0)
+        rows = jnp.concatenate([ref[1, :, cols] for ref in results], axis=0)
         token_ref[:, cols] = dot_tn(sum(picks), rows).astype(BF16)
     dots_ref[...] = jnp.concatenate(
         [jnp.sum(jnp.where(eye, dot, 0.0), axis=0, keepdims=True) for dot in dots], axis=0
@@ -309,9 +321,9 @@
     return lax.dynamic_index_in_dim(rows, core, 2, keepdims=False)
 
 
-def down_shares(order, cols, act_turned, c_rows, c_other):
-    ff, both_rows = act_turned.shape
-    total, width = c_rows.shape
+def down_shares(order, cols, act, act_other, c_rows, c_other):
+    total, ff = act.shape
+    width = c_rows.shape[1]
     count = order.shape[0]
     block = pl.BlockSpec((total, cols), lambda n, order_ref: (0, order_ref[n]))
     return pl.pallas_call(
@@ -320,13 +332,14 @@
         grid_spec=pltpu.PrefetchScalarGridSpec(
             num_scalar_prefetch=1,
             grid=(count,),
-            in_specs=[whole((ff, both_rows))] + [block] * 2,
+            in_specs=[whole((total, ff))] * 2 + [block] * 2,
             out_specs=[whole((ff, cols))] * count,
+            scratch_shapes=[pltpu.VMEM((ff, 2 * total), BF16)],
         ),
         compiler_params=params(),
         cost_estimate=cost(2 * total * width * ff, 5e6),
         name="down_shares",
-    )(order, act_turned, c_rows, c_other)
+    )(order, act, act_other, c_rows, c_other)
 
 
 def gate_up_shares(order, cols, x_rows, x_other, grads, grads_other):
@@ -510,31 +523,25 @@
             name="backward",
         )(c_rows, w_down, pre)
 
-    def run_expert_rows(act):
+    def run_result_rows(act, grads):
         return pl.pallas_call(
-            functools.partial(expert_rows, cap),
-            out_shape=[block_shape] * groups,
+            functools.partial(result_rows, cap),
+            out_shape=[jax.ShapeDtypeStruct((2, cap, width), BF16)] * groups,
             grid=(width // wide,),
-            in_specs=[whole((total, ff)), pl.BlockSpec((1, ff, wide), lambda j: (0, 0, j))],
-            out_specs=[pl.BlockSpec((cap, wide), lambda j: (0, j))] * groups,
+            in_specs=[
+                whole((total, ff)),
+                whole((2, total, ff)),
+                pl.BlockSpec((1, ff, wide), lambda j: (0, 0, j)),
+                pl.BlockSpec((1, wide, ff), lambda j: (0, j, 0)),
+                pl.BlockSpec((1, wide, ff), lambda j: (0, j, 0)),
+            ],
+            out_specs=[pl.BlockSpec((2, cap, wide), lambda j: (0, 0, j))] * groups,
             compiler_params=params(),
-            cost_estimate=cost(2 * total * width * ff, 5e6),
-            name="expert_rows",
-        )(act, w_down)
-
-    def run_input_rows(grads):
-        return pl.pallas_call(
-            functools.partial(input_rows, cap),
-            out_shape=[block_shape] * groups,
-            grid=(width // wide,),
-            in_specs=[whole((2, total, ff))] + [pl.BlockSpec((1, wide, ff), lambda j: (0, j, 0))] * 2,
-            out_specs=[pl.BlockSpec((cap, wide), lambda j: (0, j))] * groups,
-            compiler_params=params(),
-            cost_estimate=cost(4 * total * width * ff, 9e6),
-            name="input_rows",
-        )(grads, w_gate, w_up)
-
-    def run_combine(out_blocks, grad_blocks):
+            cost_estimate=cost(6 * total * width * ff, 13e6),
+            name="result_rows",
+        )(act, grads, w_down, w_gate, w_up)
+
+    def run_combine(results):
         return pl.pallas_call(
             functools.partial(combine, cap, groups),
             out_shape=[
@@ -542,12 +549,12 @@
                 jax.ShapeDtypeStruct((count, width), BF16),
                 jax.ShapeDtypeStruct((top, count), F32),
             ],
-            in_specs=[smem] + [vmem] * (3 + 2 * groups),
+            in_specs=[smem] + [vmem] * (3 + groups),
             out_specs=[vmem] * 3,
             compiler_params=params(),
             cost_estimate=cost(6 * total * width * count, 6e6),
             name="combine",
-        )(me_arr, ids, gates, cotangent, *out_blocks, *grad_blocks)
+        )(me_arr, ids, gates, cotangent, *results)
 
     if turn is not None and chips == 4 and cols % 128 == 0:
         low = chip < 2
@@ -564,43 +571,39 @@
         def to_mate(part):
             return lax.ppermute(part, "expert", [(i, i ^ turn) for i in range(groups)])
 
-        x_other = swap(x_rows)
         c_rows = joined(after(c_blocks, act), "join_grads")
         c_other = swap(c_rows)
-        act_turned = turned("turn_act", act, after(act_other, c_rows))
-        grads = run_backward(after(c_rows, act_turned))
+        grads = run_backward(after(c_rows, act_other))
+        x_other = swap(after(x_rows, grads))
         grads_other = swap(grads)
-        d_a, d_b, d_c, d_d = down_shares(order, cols, act_turned, c_rows, after(c_other, grads))
+        d_a, d_b, d_c, d_d = down_shares(order, cols, act, act_other, c_rows, after(c_other, grads))
         d_1 = swap_ends(d_a)
         d_2 = swap_ends(after(d_b, d_a))
-        out_rows = run_expert_rows(after(act, d_a, grads))
-        out_blocks = exchange(after(out_rows, d_a))
         g_a, g_b, g_c, g_d, u_a, u_b, u_c, u_d = gate_up_shares(
-            order, cols, after(x_rows, d_a, out_rows[0]), x_other, grads, grads_other
+            order, cols, after(x_rows, d_a), x_other, grads, grads_other
         )
-        grad_rows = run_input_rows(after(grads, g_a))
-
-        m = added("down_mid1", BF16, *after((d_1, d_a), grad_rows[0]))
+        rows = run_result_rows(act, after(grads, g_a))
+
+        m = added("down_mid1", BF16, *after((d_1, d_a), *rows))
         d_m1, g_1 = swap_middle(m), swap_ends(after(g_a, m))
-        m = added("down_mid2", BF16, *after((d_2, d_b), m, *out_blocks))
+        m = added("down_mid2", BF16, *after((d_2, d_b), m))
         d_m2, u_1 = swap_middle(m), swap_ends(after(u_a, m))
-        grad_blocks = [grad_rows[0]]
-        for n, part in enumerate(grad_rows[1:], 1):
-            part = after(part, grad_blocks[-1], m, out_blocks)
-            grad_blocks.append(lax.ppermute(part, "expert", [(i, i ^ n) for i in range(groups)]))
-
-        m = added("gate_mid1", BF16, *after((g_1, g_a), m, grad_blocks[1]))
+        results = [rows[0]]
+        for n, part in enumerate(rows[1:], 1):
+            part = after(part, m) if n < groups - 1 else after(part, results[-1], m)
+            results.append(lax.ppermute(part, "expert", [(i, i ^ n) for i in range(groups)]))
+
+        m = added("gate_mid1", BF16, *after((g_1, g_a), m))
         g_m1 = swap_middle(m)
         (e,) = last_share("down_last", 1, end, *after((d_c, d_m1, d_d), m))
         d_3 = swap_ends(e)
-        m = added("up_mid1", BF16, *after((u_1, u_a), e, d_m2, *grad_blocks[1:3]))
+        m = added("up_mid1", BF16, *after((u_1, u_a), e, d_m2, results[1]))
         u_m1, g_2 = swap_middle(m), swap_ends(after(g_b, m))
-
-        t = final_sum("down_sum", 0, end, *after((d_3, d_d, d_c, d_m2), m, *grad_blocks[1:]))
+        t = final_sum("down_sum", 0, end, *after((d_3, d_d, d_c, d_m2), m))
         d_t = to_mate(t)
         (e,) = last_share("gate_last", 1, end, *after((g_c, g_m1, g_d), t))
         g_3 = swap_ends(e)
-        m = added("gate_mid2", BF16, *after((g_2, g_b), e))
+        m = added("gate_mid2", BF16, *after((g_2, g_b), e, results[2]))
         g_m2 = swap_middle(m)
         half = u_b.shape[0] // 2
         u_b0, u_b1 = after((u_b[:half], u_b[half:]), m)
@@ -613,19 +616,18 @@
         m1 = added("up_mid21", BF16, *after((u_21, u_b1), m0))
         u_m21, u_31 = swap_middle(m1), swap_ends(after(e1, m0))
 
-        slot_down = slot_of("slot_down", *after((d_t,), m1))
+        mixed_out, token_grad, gate_grad = run_combine(after(results, m1))
+        slot_down = slot_of("slot_down", *after((d_t,), mixed_out))
         t0 = final_sum("up_sum0", 0, end, *after((u_30, u_d, u_c, u_m20), slot_down, g_t))
         u_t0 = to_mate(t0)
         t1 = final_sum("up_sum1", 1, end, *after((u_31, u_d, u_c, u_m21), t0))
         u_t1 = to_mate(t1)
-        mixed_out, token_grad, gate_grad = run_combine(*after((out_blocks, grad_blocks), t1))
-        slot_gate = slot_of("slot_gate", *after((g_t,), mixed_out))
+        slot_gate = slot_of("slot_gate", *after((g_t,), t1))
         slot_up = slot_of("slot_up", *after((u_t0, u_t1), slot_gate))
     else:
         c_rows = joined(c_blocks, "join_grads")
         grads = run_backward(c_rows)
-        out_blocks = exchange(run_expert_rows(act))
-        grad_blocks = exchange(run_input_rows(grads))
+        results = exchange(run_result_rows(act, grads))
         acts = jnp.concatenate([act, act_other], axis=0)
         both_grads = jnp.concatenate([grads, swap(grads)], axis=1)
         c_both = rows_of_core(core, chips, cols, c_rows, swap(c_rows))
@@ -648,7 +650,7 @@
         slot_down, slot_gate, slot_up = [
             relocated(line.total(), turn, partner, me, groups) for line in lines
         ]
-        mixed_out, token_grad, gate_grad = run_combine(out_blocks, grad_blocks)
+        mixed_out, token_grad, gate_grad = run_combine(results)
 
     return mixed_out, token_grad, gate_grad.T, slot_gate, slot_up, slot_down
 

time: 141 us -> 140 us (level)
  waiting for transfers between devices: 49.4 us -> 36.5 us
  starting transfers between devices: 42.6 us -> 52.8 us
  local copies, waits for them, and re-layouts: 4.44 us -> 6.13 us
  Pallas kernels: 42.6 us -> 41 us
    ppermute x11, starting transfers between devices: 18.7 us -> 31.3 us  [swap_ends(): return lax.ppermute(part, 'dp', [(i, i ^ 2) for i in range(replicas)])]
    ppermute x11, waiting for transfers between devices: 23.4 us -> 12 us  [swap_ends(): return lax.ppermute(part, 'dp', [(i, i ^ 2) for i in range(replicas)])]
    ppermute x3, waiting for transfers between devices: 8.17 us -> 0.01 us  [layer(): lax.ppermute(part, 'expert', [(i, i ^ n) for i in range(groups)])]
    ppermute x4, waiting for transfers between devices: 1.62 us -> 9.39 us  [to_mate(): return lax.ppermute(part, 'expert', [(i, i ^ turn) for i in range(groups)])]
    ppermute x9 -> x6, starting transfers between devices: 14.6 us -> 11.1 us  [exchange(): lax.ppermute(blocks[b], 'expert', [(i, i ^ b) for i in range(groups)])]
    cond x48 -> x44, local copies, waits for them, and re-layouts: 4.41 us -> 6.1 us
    ppermute x9 -> x6, waiting for transfers between devices: 16.2 us -> 15.1 us  [exchange(): lax.ppermute(blocks[b], 'expert', [(i, i ^ b) for i in range(groups)])]
    pallas_call x3 -> x1, Pallas kernels: 7.39 us -> 6.49 us  [run_result_rows(): pl.pallas_call(functools.partial(result_rows, cap), out_shape=[jax.ShapeD...]
  transfers between devices with their start and end apart: 38 -> 35, of which waited for: 16 -> 13; matrix products, arithmetic and copies ran while one was open for 0% -> 0% of each run, Pallas kernels for 28% -> 28%
where the time goes in v4:
time: 140 us; the launch traced here: 139 us
  starting transfers between devices  52.8 us (38%)
  Pallas kernels  41 us (29%)
  waiting for transfers between devices  36.5 us (26%)
  local copies, waits for them, and re-layouts  6.13 us (4%)
  between operations  1.48 us (1%)
    ppermute x11, starting transfers between devices, swap_ends(): return lax.ppermute(part, 'dp', [(i, i ^ 2) for i in range(replicas)])  31.3 us
    ppermute x6, waiting for transfers between devices, exchange(): lax.ppermute(blocks[b], 'expert', [(i, i ^ b) for i in range(groups)])  15.1 us
    ppermute x11, waiting for transfers between devices, swap_ends(): return lax.ppermute(part, 'dp', [(i, i ^ 2) for i in range(replicas)])  12 us
    ppermute x6, starting transfers between devices, exchange(): lax.ppermute(blocks[b], 'expert', [(i, i ^ b) for i in range(groups)])  11.1 us
    ppermute x4, waiting for transfers between devices, to_mate(): return lax.ppermute(part, 'expert', [(i, i ^ turn) for i in range(groups)])  9.39 us
    pallas_call x1, Pallas kernels, gate_up_shares(): pl.pallas_call(functools.partial(gate_up_share, count), out_shape=[jax.Sh...  6.54 us
    pallas_call x1, Pallas kernels, run_result_rows(): pl.pallas_call(functools.partial(result_rows, cap), out_shape=[jax.ShapeD...  6.49 us
    cond x44, local copies, waits for them, and re-layouts  6.1 us
  transfers between devices with their start and end apart: 35, of which 13 were waited for; matrix products, arithmetic and copies ran while one was open for 0% of the time, Pallas kernels for 28%

profile of v4, /device:TPU:0, one launch (start us, length us, event | category | flops | bytes accessed | tf_op | source)
XLA Modules:
  0.0 139.0 jit_solution(16002849963209807480)
XLA Ops:
  1.3 137.6 %conditional.1 = (bf16[128,2048]{1,0:T(8,128)(2,1)}, bf16[128,2048]{1,0:T(8,128)(2,1)}, f32[128,2]{0,1:T(2,128)}, f32[1,256,768]{2,1,0:T(8,128)}, f32[1,256,768]{2,1,0:T(8,128)}, /*index=5*/f32[1,768,256]{2,1,0:T(8,128)}) conditional(s32[]{:T(128)} %bitcast.9, (s32[2,128]{1,0:T(2,128)}, bf16[128,2048]{1,0:T(8,128)(2,1)}, ...), branch_computations={%region_0.1_spmd, %region_1.2_spmd, %region_2.3_spmd} | conditional | flops 24045 | bytes 129140488 | solution.py:426
  1.5 1.7 %place_tokens.4 = (bf16[80,2048]{1,0:T(8,128)(2,1)S(1)}, bf16[80,2048]{1,0:T(8,128)(2,1)S(1)}, bf16[80,2048]{1,0:T(8,128)(2,1)S(1)}, bf16[80,2048]{1,0:T(8,128)(2,1)S(1)}) custom-call(s32[1]{0:T(128)} %bitcast.3.me_ref, s32[2,128]{1,0:T(2,128)} %get-tuple-element.148.ids_ref, bf16[128,2048]{1,0:T(8,128)(2,1)} %get-tuple-element.386.tok_ref), custom_call_target="tpu_custom_call" | custom-call | tf_op jit(solution)/shard_map/cond/branch_1_fun/place_tokens/pallas_call | solution.py:467
  3.2 3.0 %collective-permute-start.35 = (bf16[80,2048]{1,0:T(8,128)(2,1)S(1)}, bf16[80,2048]{1,0:T(8,128)(2,1)S(1)}, u32[]{:S(2)}, u32[]{:S(2)}) collective-permute-start(bf16[80,2048]{1,0:T(8,128)(2,1)S(1)} %get-tuple-element.153), channel_id=1, source_target_pairs={{0,1},{1,0},{2,3},{3,2},{4,5},{5,4},{6,7},{7,6},{8,9},{9,8},{10,11... | collective-permute-start | bytes 983048 | tf_op jit(solution)/shard_map/cond/branch_1_fun/ppermute | solution.py:449
  6.2 1.5 %collective-permute-start.36 = (bf16[80,2048]{1,0:T(8,128)(2,1)S(1)}, bf16[80,2048]{1,0:T(8,128)(2,1)S(1)}, u32[]{:S(2)}, u32[]{:S(2)}) collective-permute-start(bf16[80,2048]{1,0:T(8,128)(2,1)S(1)} %get-tuple-element.154), channel_id=1, source_target_pairs={{0,2},{1,3},{2,0},{3,1},{4,6},{5,7},{6,4},{7,5},{8,10},{9,11},{10,... | collective-permute-start | bytes 983048 | tf_op jit(solution)/shard_map/cond/branch_1_fun/ppermute | solution.py:449
  7.7 1.7 %place_grads.4 = (bf16[80,2048]{1,0:T(8,128)(2,1)S(1)}, bf16[80,2048]{1,0:T(8,128)(2,1)S(1)}, bf16[80,2048]{1,0:T(8,128)(2,1)S(1)}, bf16[80,2048]{1,0:T(8,128)(2,1)S(1)}) custom-call(s32[1]{0:T(128)} %bitcast.3.me_ref, s32[2,128]{1,0:T(2,128)} %get-tuple-element.148.ids_ref, f32[2,128]{1,0:T(2,128)} %get-tuple-element.149.gates_ref, ...), custom_call_target="tpu_custom_call" | custom-call | tf_op jit(solution)/shard_map/cond/branch_1_fun/place_grads/pallas_call | solution.py:475
  9.5 2.0 %collective-permute-start.38 = (bf16[80,2048]{1,0:T(8,128)(2,1)S(1)}, bf16[80,2048]{1,0:T(8,128)(2,1)S(1)}, u32[]{:S(2)}, u32[]{:S(2)}) collective-permute-start(bf16[80,2048]{1,0:T(8,128)(2,1)S(1)} %get-tuple-element.160), channel_id=1, source_target_pairs={{0,1},{1,0},{2,3},{3,2},{4,5},{5,4},{6,7},{7,6},{8,9},{9,8},{10,11... | collective-permute-start | bytes 983048 | tf_op jit(solution)/shard_map/cond/branch_1_fun/ppermute | solution.py:449
  11.5 1.5 %collective-permute-start.39 = (bf16[80,2048]{1,0:T(8,128)(2,1)S(1)}, bf16[80,2048]{1,0:T(8,128)(2,1)S(1)}, u32[]{:S(2)}, u32[]{:S(2)}) collective-permute-start(bf16[80,2048]{1,0:T(8,128)(2,1)S(1)} %get-tuple-element.161), channel_id=1, source_target_pairs={{0,2},{1,3},{2,0},{3,1},{4,6},{5,7},{6,4},{7,5},{8,10},{9,11},{10,... | collective-permute-start | bytes 983048 | tf_op jit(solution)/shard_map/cond/branch_1_fun/ppermute | solution.py:449
  13.0 1.7 %collective-permute-done.35.refs_1_ = bf16[80,2048]{1,0:T(8,128)(2,1)S(1)} collective-permute-done((bf16[80,2048]{1,0:T(8,128)(2,1)S(1)}, bf16[80,2048]{1,0:T(8,128)(2,1)S(1)}, u32[]{:S(2)}, u32[]{:S(2)}) %collective-permute-start.35) | collective-permute-done | bytes 327712 | tf_op jit(solution)/shard_map/cond/branch_1_fun/ppermute | solution.py:449
  14.7 3.0 %collective-permute-start.40 = (bf16[80,2048]{1,0:T(8,128)(2,1)S(1)}, bf16[80,2048]{1,0:T(8,128)(2,1)S(1)}, u32[]{:S(2)}, u32[]{:S(2)}) collective-permute-start(bf16[80,2048]{1,0:T(8,128)(2,1)S(1)} %get-tuple-element.162), channel_id=1, source_target_pairs={{0,3},{1,2},{2,1},{3,0},{4,7},{5,6},{6,5},{7,4},{8,11},{9,10},{10,... | collective-permute-start | bytes 983048 | tf_op jit(solution)/shard_map/cond/branch_1_fun/ppermute | solution.py:449
  17.8 6.1 %collective-permute-done.36.refs_2_ = bf16[80,2048]{1,0:T(8,128)(2,1)S(1)} collective-permute-done((bf16[80,2048]{1,0:T(8,128)(2,1)S(1)}, bf16[80,2048]{1,0:T(8,128)(2,1)S(1)}, u32[]{:S(2)}, u32[]{:S(2)}) %collective-permute-start.36) | collective-permute-done | bytes 327712 | tf_op jit(solution)/shard_map/cond/branch_1_fun/ppermute | solution.py:449
  23.9 5.2 %forward.4 = (bf16[320,2048]{1,0:T(8,128)(2,1)S(1)}, f32[2,320,768]{2,1,0:T(8,128)S(1)}, bf16[320,768]{1,0:T(8,128)(2,1)S(1)}) custom-call(bf16[80,2048]{1,0:T(8,128)(2,1)S(1)} %get-tuple-element.152.refs_0_, bf16[80,2048]{1,0:T(8,128)(2,1)S(1)} %collective-permute-done.35.refs_1_, bf16[80,2048]{1,0:T(8,128)(2,1)S(1)} %collective-permute-done.36.refs_2_, ...), custom_call_target="tpu_custom_call" | custom-call | flops 1000 | bytes 1000 | tf_op jit(solution)/shard_map/cond/branch_1_fun/forward/pallas_call | solution.py:487
  29.2 7.3 %collective-permute-done.39.refs_2_ = bf16[80,2048]{1,0:T(8,128)(2,1)S(1)} collective-permute-done((bf16[80,2048]{1,0:T(8,128)(2,1)S(1)}, bf16[80,2048]{1,0:T(8,128)(2,1)S(1)}, u32[]{:S(2)}, u32[]{:S(2)}) %collective-permute-start.39) | collective-permute-done | bytes 327712 | tf_op jit(solution)/shard_map/cond/branch_1_fun/ppermute | solution.py:449
  37.4 2.8 %backward.4.refs_8_.grad_ref = bf16[2,320,768]{2,1,0:T(8,128)(2,1)} custom-call(bf16[320,2048]{1,0:T(8,128)(2,1)S(1)} %join_grads.4.c_ref.c_own, bf16[1,768,2048]{2,1,0:T(8,128)(2,1)S(1)} %copy-done.50, f32[2,320,768]{2,1,0:T(8,128)S(1)} %get-tuple-element.169.pre_ref), custom_call_target="tpu_custom_call" | custom-call | flops 1000 | bytes 1000 | tf_op jit(solution)/shard_map/cond/branch_1_fun/backward/pallas_call | solution.py:511
  40.7 1.0 copy-done.15
  41.7 4.4 %down_shares.4 = (bf16[768,256]{1,0:T(8,128)(2,1)S(1)}, bf16[768,256]{1,0:T(8,128)(2,1)S(1)}, bf16[768,256]{1,0:T(8,128)(2,1)S(1)}, bf16[768,256]{1,0:T(8,128)(2,1)S(1)}) custom-call(s32[4]{0:T(128)S(1)} %fusion.3.order_ref, bf16[320,768]{1,0:T(8,128)(2,1)S(1)} %get-tuple-element.158.act_own.act_ref, bf16[320,768]{1,0:T(8,128)(2,1)S(1)} %copy-done.15, ...), custom_call_target="tpu_custom_call" | custom-call | flops 1000 | bytes 1000 | tf_op jit(solution)/shard_map/cond/branch_1_fun/down_shares/pallas_call | solution.py:329
  46.2 1.6 %collective-permute-start.46 = (bf16[768,256]{1,0:T(8,128)(2,1)S(1)}, bf16[768,256]{1,0:T(8,128)(2,1)S(1)}, u32[]{:S(2)}, u32[]{:S(2)}) collective-permute-start(bf16[768,256]{1,0:T(8,128)(2,1)S(1)} %get-tuple-element.184.right_ref), channel_id=1, source_target_pairs={{0,8},{4,12},{8,0},{12,4},{16,24},{20,28},{24,16},{28,20},{1,9},{5... | collective-permute-start | bytes 1179656 | tf_op jit(solution)/shard_map/cond/branch_1_fun/ppermute | solution.py:565
  48.3 6.5 %gate_up_shares.4 = (bf16[256,768]{1,0:T(8,128)(2,1)S(1)}, bf16[256,768]{1,0:T(8,128)(2,1)S(1)}, bf16[256,768]{1,0:T(8,128)(2,1)S(1)}, bf16[256,768]{1,0:T(8,128...) custom-call(s32[4]{0:T(128)S(1)} %fusion.3.order_ref, ...), custom_call_target="tpu_custom_call" | custom-call | flops 1000 | bytes 1000 | tf_op jit(solution)/shard_map/cond/branch_1_fun/gate_up_shares/pallas_call | solution.py:353
  56.4 6.5 %result_rows.4 = (bf16[2,80,2048]{2,1,0:T(8,128)(2,1)S(1)}, bf16[2,80,2048]{2,1,0:T(8,128)(2,1)}, bf16[2,80,2048]{2,1,0:T(8,128)(2,1)}, bf16[2,80,2048]{2,1,0:T(8,128)(2,1)S(1)}) custom-call(bf16[320,768]{1,0:T(8,128)(2,1)S(1)} %get-tuple-element.158.act_own.act_ref, bf16[2,320,768]{2,1,0:T(8,128)(2,1)} %backward.4.refs_8_.grad_ref, ...), custom_call_target="tpu_custom_call" | custom-call | flops 1000 | bytes 1000 | tf_op jit(solution)/shard_map/cond/branch_1_fun/result_rows/pallas_call | solution.py:527
  62.9 1.0 down_mid1.4
  63.8 1.6 %collective-permute-start.52 = (bf16[256,768]{1,0:T(8,128)(2,1)S(1)}, bf16[256,768]{1,0:T(8,128)(2,1)S(1)}, u32[]{:S(2)}, u32[]{:S(2)}) collective-permute-start(bf16[256,768]{1,0:T(8,128)(2,1)S(1)} %get-tuple-element.198.right_ref), channel_id=1, source_target_pairs={{0,8},{4,12},{8,0},{12,4},{16,24},{20,28},{24,16},{28,20},{1,9},{5... | collective-permute-start | bytes 1179656 | tf_op jit(solution)/shard_map/cond/branch_1_fun/ppermute | solution.py:565
  67.0 1.3 collective-permute-start.47
  68.3 3.1 %collective-permute-start.50 = (bf16[256,768]{1,0:T(8,128)(2,1)}, bf16[256,768]{1,0:T(8,128)(2,1)}, u32[]{:S(2)}, u32[]{:S(2)}) collective-permute-start(bf16[256,768]{1,0:T(8,128)(2,1)} %get-tuple-element.203.right_ref), channel_id=1, source_target_pairs={{0,8},{4,12},{8,0},{12,4},{16,24},{20,28},{24,16},{28,20},{1,9},{5... | collective-permute-start | bytes 1179656 | tf_op jit(solution)/shard_map/cond/branch_1_fun/ppermute | solution.py:565
  71.5 4.4 %collective-permute-done.52.left_ref = bf16[256,768]{1,0:T(8,128)(2,1)S(1)} collective-permute-done((bf16[256,768]{1,0:T(8,128)(2,1)S(1)}, bf16[256,768]{1,0:T(8,128)(2,1)S(1)}, u32[]{:S(2)}, u32[]{:S(2)}) %collective-permute-start.52) | collective-permute-done | bytes 393248 | tf_op jit(solution)/shard_map/cond/branch_1_fun/ppermute | solution.py:565
  76.6 1.5 %collective-permute-start.48 = (bf16[2,80,2048]{2,1,0:T(8,128)(2,1)}, bf16[2,80,2048]{2,1,0:T(8,128)(2,1)}, u32[]{:S(2)}, u32[]{:S(2)}) collective-permute-start(bf16[2,80,2048]{2,1,0:T(8,128)(2,1)} %get-tuple-element.188), channel_id=1, source_target_pairs={{0,2},{1,3},{2,0},{3,1},{4,6},{5,7},{6,4},{7,5},{8,10},{9,11},{10,... | collective-permute-start | bytes 1966088 | tf_op jit(solution)/shard_map/cond/branch_1_fun/ppermute | solution.py:594
  78.1 1.0 copy-done.33
  79.1 1.0 copy-done.39
  80.2 1.1 down_last.4
  81.3 2.2 %collective-permute-start.56 = (bf16[768,256]{1,0:T(8,128)(2,1)S(1)}, bf16[768,256]{1,0:T(8,128)(2,1)S(1)}, u32[]{:S(2)}, u32[]{:S(2)}) collective-permute-start(bf16[768,256]{1,0:T(8,128)(2,1)S(1)} %down_last.4), channel_id=1, source_target_pairs={{0,8},{4,12},{8,0},{12,4},{16,24},{20,28},{24,16},{28,20},{1,9},{5... | collective-permute-start | bytes 1179656 | tf_op jit(solution)/shard_map/cond/branch_1_fun/ppermute | solution.py:565
  84.4 1.2 up_mid1.4
  85.6 6.4 %collective-permute-start.54 = (bf16[256,768]{1,0:T(8,128)(2,1)S(1)}, bf16[256,768]{1,0:T(8,128)(2,1)S(1)}, u32[]{:S(2)}, u32[]{:S(2)}) collective-permute-start(bf16[256,768]{1,0:T(8,128)(2,1)S(1)} %copy-done.27), channel_id=1, source_target_pairs={{0,8},{4,12},{8,0},{12,4},{16,24},{20,28},{24,16},{28,20},{1,9},{5... | collective-permute-start | bytes 1179656 | tf_op jit(solution)/shard_map/cond/branch_1_fun/ppermute | solution.py:565
  92.0 1.7 %collective-permute-start.49 = (bf16[2,80,2048]{2,1,0:T(8,128)(2,1)S(1)}, bf16[2,80,2048]{2,1,0:T(8,128)(2,1)S(1)}, u32[]{:S(2)}, u32[]{:S(2)}) collective-permute-start(bf16[2,80,2048]{2,1,0:T(8,128)(2,1)S(1)} %copy-done.45), channel_id=1, source_target_pairs={{0,3},{1,2},{2,1},{3,0},{4,7},{5,6},{6,5},{7,4},{8,11},{9,10},{10,... | collective-permute-start | bytes 1966088 | tf_op jit(solution)/shard_map/cond/branch_1_fun/ppermute | solution.py:594
  93.7 1.1 down_sum.4
  95.6 3.5 %collective-permute-start.59 = (bf16[256,768]{1,0:T(8,128)(2,1)S(1)}, bf16[256,768]{1,0:T(8,128)(2,1)S(1)}, u32[]{:S(2)}, u32[]{:S(2)}) collective-permute-start(bf16[256,768]{1,0:T(8,128)(2,1)S(1)} %gate_last.4), channel_id=1, source_target_pairs={{0,8},{4,12},{8,0},{12,4},{16,24},{20,28},{24,16},{28,20},{1,9},{5... | collective-permute-start | bytes 1179656 | tf_op jit(solution)/shard_map/cond/branch_1_fun/ppermute | solution.py:565
  99.2 2.4 %collective-permute-done.54.left_ref = bf16[256,768]{1,0:T(8,128)(2,1)S(1)} collective-permute-done((bf16[256,768]{1,0:T(8,128)(2,1)S(1)}, bf16[256,768]{1,0:T(8,128)(2,1)S(1)}, u32[]{:S(2)}, u32[]{:S(2)}) %collective-permute-start.54) | collective-permute-done | bytes 393248 | tf_op jit(solution)/shard_map/cond/branch_1_fun/ppermute | solution.py:565
  101.8 5.7 %collective-permute-start.57 = (bf16[128,768]{1,0:T(8,128)(2,1)S(1)}, bf16[128,768]{1,0:T(8,128)(2,1)S(1)}, u32[]{:S(2)}, u32[]{:S(2)}) collective-permute-start(bf16[128,768]{1,0:T(8,128)(2,1)S(1)} %get-tuple-element.231.right_ref), channel_id=1, source_target_pairs={{0,8},{4,12},{8,0},{12,4},{16,24},{20,28},{24,16},{28,20},{1,9},{5... | collective-permute-start | bytes 589832 | tf_op jit(solution)/shard_map/cond/branch_1_fun/ppermute | solution.py:565
  107.5 2.5 %collective-permute-done.59.last_ref = bf16[256,768]{1,0:T(8,128)(2,1)S(1)} collective-permute-done((bf16[256,768]{1,0:T(8,128)(2,1)S(1)}, bf16[256,768]{1,0:T(8,128)(2,1)S(1)}, u32[]{:S(2)}, u32[]{:S(2)}) %collective-permute-start.59) | collective-permute-done | bytes 393248 | tf_op jit(solution)/shard_map/cond/branch_1_fun/ppermute | solution.py:565
  110.0 2.5 %collective-permute-start.58 = (bf16[128,768]{1,0:T(8,128)(2,1)S(1)}, bf16[128,768]{1,0:T(8,128)(2,1)S(1)}, u32[]{:S(2)}, u32[]{:S(2)}) collective-permute-start(bf16[128,768]{1,0:T(8,128)(2,1)S(1)} %get-tuple-element.229.right_ref), channel_id=1, source_target_pairs={{0,8},{4,12},{8,0},{12,4},{16,24},{20,28},{24,16},{28,20},{1,9},{5... | collective-permute-start | bytes 589832 | tf_op jit(solution)/shard_map/cond/branch_1_fun/ppermute | solution.py:565
  112.4 2.4 %collective-permute-done.62.refs_0_ = bf16[768,256]{1,0:T(8,128)(2,1)S(1)} collective-permute-done((bf16[768,256]{1,0:T(8,128)(2,1)S(1)}, bf16[768,256]{1,0:T(8,128)(2,1)S(1)}, u32[]{:S(2)}, u32[]{:S(2)}) %collective-permute-start.62) | collective-permute-done | bytes 393248 | tf_op jit(solution)/shard_map/cond/branch_1_fun/ppermute | solution.py:572
  115.0 1.6 %collective-permute-start.63 = (bf16[256,768]{1,0:T(8,128)(2,1)S(1)}, bf16[256,768]{1,0:T(8,128)(2,1)S(1)}, u32[]{:S(2)}, u32[]{:S(2)}) collective-permute-start(bf16[256,768]{1,0:T(8,128)(2,1)S(1)} %gate_sum.4), channel_id=1, source_target_pairs={{0,2},{1,3},{2,0},{3,1},{4,6},{5,7},{6,4},{7,5},{8,10},{9,11},{10,... | collective-permute-start | bytes 1179656 | tf_op jit(solution)/shard_map/cond/branch_1_fun/ppermute | solution.py:572
  116.5 1.6 %collective-permute-start.66 = (bf16[128,768]{1,0:T(8,128)(2,1)S(1)}, bf16[128,768]{1,0:T(8,128)(2,1)S(1)}, u32[]{:S(2)}, u32[]{:S(2)}) collective-permute-start(bf16[128,768]{1,0:T(8,128)(2,1)S(1)} %get-tuple-element.241), channel_id=1, source_target_pairs={{0,8},{4,12},{8,0},{12,4},{16,24},{20,28},{24,16},{28,20},{1,9},{5... | collective-permute-start | bytes 589832 | tf_op jit(solution)/shard_map/cond/branch_1_fun/ppermute | solution.py:565
  118.9 2.7 %collective-permute-start.64 = (bf16[128,768]{1,0:T(8,128)(2,1)S(1)}, bf16[128,768]{1,0:T(8,128)(2,1)S(1)}, u32[]{:S(2)}, u32[]{:S(2)}) collective-permute-start(bf16[128,768]{1,0:T(8,128)(2,1)S(1)} %get-tuple-element.240), channel_id=1, source_target_pairs={{0,8},{4,12},{8,0},{12,4},{16,24},{20,28},{24,16},{28,20},{1,9},{5... | collective-permute-start | bytes 589832 | tf_op jit(solution)/shard_map/cond/branch_1_fun/ppermute | solution.py:565
  121.6 3.4 %combine.4 = (bf16[128,2048]{1,0:T(8,128)(2,1)}, bf16[128,2048]{1,0:T(8,128)(2,1)}, f32[2,128]{1,0:T(2,128)}) custom-call(s32[1]{0:T(128)} %bitcast.3.me_ref, s32[2,128]{1,0:T(2,128)S(1)} %copy-done.61, f32[2,128]{1,0:T(2,128)S(1)} %copy-done.64, bf16[128,2048]{1,0:T(8,128)(2,1)S(1)} %copy-done.58, bf16[2,80,2048]{2,1,0:T(8,128)(2,1)S(1)} %get-tuple-element.232.refs_0_, ...), custom_call_target="tpu_custom_call" | custom-call | flops 1000 | bytes 1000 | tf_op jit(solution)/shard_map/cond/branch_1_fun/combine/pallas_call | solution.py:545
  125.1 0.9 slot_down.4
  126.2 1.2 collective-permute-done.64.last_ref
  128.0 1.5 %collective-permute-start.68 = (bf16[128,768]{1,0:T(8,128)(2,1)S(1)}, bf16[128,768]{1,0:T(8,128)(2,1)S(1)}, u32[]{:S(2)}, u32[]{:S(2)}) collective-permute-start(bf16[128,768]{1,0:T(8,128)(2,1)S(1)} %up_sum0.4), channel_id=1, source_target_pairs={{0,2},{1,3},{2,0},{3,1},{4,6},{5,7},{6,4},{7,5},{8,10},{9,11},{10,... | collective-permute-start | bytes 589832 | tf_op jit(solution)/shard_map/cond/branch_1_fun/ppermute | solution.py:572
  130.5 4.9 %collective-permute-done.69.refs_1_ = bf16[128,768]{1,0:T(8,128)(2,1)S(1)} collective-permute-done((bf16[128,768]{1,0:T(8,128)(2,1)S(1)}, bf16[128,768]{1,0:T(8,128)(2,1)S(1)}, u32[]{:S(2)}, u32[]{:S(2)}) %collective-permute-start.69) | collective-permute-done | bytes 196640 | tf_op jit(solution)/shard_map/cond/branch_1_fun/ppermute | solution.py:572
  135.3 2.1 %collective-permute-done.68.refs_0_ = bf16[128,768]{1,0:T(8,128)(2,1)S(1)} collective-permute-done((bf16[128,768]{1,0:T(8,128)(2,1)S(1)}, bf16[128,768]{1,0:T(8,128)(2,1)S(1)}, u32[]{:S(2)}, u32[]{:S(2)}) %collective-permute-start.68) | collective-permute-done | bytes 196640 | tf_op jit(solution)/shard_map/cond/branch_1_fun/ppermute | solution.py:572
  137.4 0.9 slot_up.4
  (95 shorter events, 10.5 us)
Async XLA Ops:
  3.2 11.5 %collective-permute-start.35 = (bf16[80,2048]{1,0:T(8,128)(2,1)S(1)}, bf16[80,2048]{1,0:T(8,128)(2,1)S(1)}, u32[]{:S(2)}, u32[]{:S(2)}) collective-permute-start(bf16[80,2048]{1,0:T(8,128)(2,1)S(1)} %get-tuple-element.153), channel_id=1, source_target_pairs={{0,1},{1,0},{2,3},{3,2},{4,5},{5,4},{6,7},{7,6},{8,9},{9,8},{10,11... | collective-permute-start | bytes 983048 | tf_op jit(solution)/shard_map/cond/branch_1_fun/ppermute | solution.py:449
  6.2 17.7 %collective-permute-start.36 = (bf16[80,2048]{1,0:T(8,128)(2,1)S(1)}, bf16[80,2048]{1,0:T(8,128)(2,1)S(1)}, u32[]{:S(2)}, u32[]{:S(2)}) collective-permute-start(bf16[80,2048]{1,0:T(8,128)(2,1)S(1)} %get-tuple-element.154), channel_id=1, source_target_pairs={{0,2},{1,3},{2,0},{3,1},{4,6},{5,7},{6,4},{7,5},{8,10},{9,11},{10,... | collective-permute-start | bytes 983048 | tf_op jit(solution)/shard_map/cond/branch_1_fun/ppermute | solution.py:449
  7.7 16.1 %collective-permute-start.37 = (bf16[80,2048]{1,0:T(8,128)(2,1)S(1)}, bf16[80,2048]{1,0:T(8,128)(2,1)S(1)}, u32[]{:S(2)}, u32[]{:S(2)}) collective-permute-start(bf16[80,2048]{1,0:T(8,128)(2,1)S(1)} %get-tuple-element.155), channel_id=1, source_target_pairs={{0,3},{1,2},{2,1},{3,0},{4,7},{5,6},{6,5},{7,4},{8,11},{9,10},{10,... | collective-permute-start | bytes 983048 | tf_op jit(solution)/shard_map/cond/branch_1_fun/ppermute | solution.py:449
  9.5 19.7 %collective-permute-start.38 = (bf16[80,2048]{1,0:T(8,128)(2,1)S(1)}, bf16[80,2048]{1,0:T(8,128)(2,1)S(1)}, u32[]{:S(2)}, u32[]{:S(2)}) collective-permute-start(bf16[80,2048]{1,0:T(8,128)(2,1)S(1)} %get-tuple-element.160), channel_id=1, source_target_pairs={{0,1},{1,0},{2,3},{3,2},{4,5},{5,4},{6,7},{7,6},{8,9},{9,8},{10,11... | collective-permute-start | bytes 983048 | tf_op jit(solution)/shard_map/cond/branch_1_fun/ppermute | solution.py:449
  11.5 24.9 %collective-permute-start.39 = (bf16[80,2048]{1,0:T(8,128)(2,1)S(1)}, bf16[80,2048]{1,0:T(8,128)(2,1)S(1)}, u32[]{:S(2)}, u32[]{:S(2)}) collective-permute-start(bf16[80,2048]{1,0:T(8,128)(2,1)S(1)} %get-tuple-element.161), channel_id=1, source_target_pairs={{0,2},{1,3},{2,0},{3,1},{4,6},{5,7},{6,4},{7,5},{8,10},{9,11},{10,... | collective-permute-start | bytes 983048 | tf_op jit(solution)/shard_map/cond/branch_1_fun/ppermute | solution.py:449
  14.7 21.7 %collective-permute-start.40 = (bf16[80,2048]{1,0:T(8,128)(2,1)S(1)}, bf16[80,2048]{1,0:T(8,128)(2,1)S(1)}, u32[]{:S(2)}, u32[]{:S(2)}) collective-permute-start(bf16[80,2048]{1,0:T(8,128)(2,1)S(1)} %get-tuple-element.162), channel_id=1, source_target_pairs={{0,3},{1,2},{2,1},{3,0},{4,7},{5,6},{6,5},{7,4},{8,11},{9,10},{10,... | collective-permute-start | bytes 983048 | tf_op jit(solution)/shard_map/cond/branch_1_fun/ppermute | solution.py:449
  23.9 13.5 %copy-start.50 = (bf16[1,768,2048]{2,1,0:T(8,128)(2,1)S(1)}, bf16[1,768,2048]{2,1,0:T(8,128)(2,1)}, u32[]{:S(2)}) copy-start(bf16[1,768,2048]{2,1,0:T(8,128)(2,1)} %get-tuple-element.398.down_ref) | copy-start | bytes 9437188 | tf_op jit(solution)/shard_map/cond
  29.1 7.5 %collective-permute-start.41 = (bf16[320,768]{1,0:T(8,128)(2,1)S(1)}, bf16[320,768]{1,0:T(8,128)(2,1)S(1)}, u32[]{:S(2)}, u32[]{:S(2)}) collective-permute-start(bf16[320,768]{1,0:T(8,128)(2,1)S(1)} %get-tuple-element.158.act_own.act_ref), channel_id=1, source_target_pairs={{0,4},{4,0},{8,12},{12,8},{16,20},{20,16},{24,28},{28,24},{1,5},{5... | collective-permute-start | bytes 1474568 | tf_op jit(solution)/shard_map/cond/branch_1_fun/ppermute | solution.py:454
  36.5 4.2 %collective-permute-start.42 = (bf16[320,2048]{1,0:T(8,128)(2,1)S(1)}, bf16[320,2048]{1,0:T(8,128)(2,1)}, u32[]{:S(2)}, u32[]{:S(2)}) collective-permute-start(bf16[320,2048]{1,0:T(8,128)(2,1)S(1)} %join_grads.4.c_ref.c_own), channel_id=1, source_target_pairs={{0,4},{4,0},{8,12},{12,8},{16,20},{20,16},{24,28},{28,24},{1,5},{5... | collective-permute-start | bytes 3932168 | tf_op jit(solution)/shard_map/cond/branch_1_fun/ppermute | solution.py:454
  40.2 8.1 %collective-permute-start.43 = (bf16[320,2048]{1,0:T(8,128)(2,1)S(1)}, bf16[320,2048]{1,0:T(8,128)(2,1)}, u32[]{:S(2)}, u32[]{:S(2)}) collective-permute-start(bf16[320,2048]{1,0:T(8,128)(2,1)S(1)} %get-tuple-element.174.refs_0_.refs_1_.refs_2_.refs_3_), channel_id=1, source_target_pairs={{0,4},{4,0},{8,12},{12,8},{16,20},{20,16},{24,28},{28,24},{1,5},{5... | collective-permute-start | bytes 3932168 | tf_op jit(solution)/shard_map/cond/branch_1_fun/ppermute | solution.py:454
  40.7 7.6 %collective-permute-start.44 = (bf16[2,320,768]{2,1,0:T(8,128)(2,1)}, bf16[2,320,768]{2,1,0:T(8,128)(2,1)}, u32[]{:S(2)}, u32[]{:S(2)}) collective-permute-start(bf16[2,320,768]{2,1,0:T(8,128)(2,1)} %backward.4.refs_8_.grad_ref), channel_id=1, source_target_pairs={{0,4},{4,0},{8,12},{12,8},{16,20},{20,16},{24,28},{28,24},{1,5},{5... | collective-permute-start | bytes 2949128 | tf_op jit(solution)/shard_map/cond/branch_1_fun/ppermute | solution.py:454
  46.2 8.7 %copy-start.4 = (bf16[768,256]{1,0:T(8,128)(2,1)}, bf16[768,256]{1,0:T(8,128)(2,1)S(1)}, u32[]{:S(2)}) copy-start(bf16[768,256]{1,0:T(8,128)(2,1)S(1)} %get-tuple-element.209.alone_ref.inner_ref) | copy-start | bytes 1179652 | tf_op jit(solution)/shard_map/cond
  46.2 8.7 %copy-start.6 = (bf16[768,256]{1,0:T(8,128)(2,1)}, bf16[768,256]{1,0:T(8,128)(2,1)S(1)}, u32[]{:S(2)}) copy-start(bf16[768,256]{1,0:T(8,128)(2,1)S(1)} %get-tuple-element.208.right_ref.near_ref) | copy-start | bytes 1179652 | tf_op jit(solution)/shard_map/cond
  46.2 16.7 %collective-permute-start.46 = (bf16[768,256]{1,0:T(8,128)(2,1)S(1)}, bf16[768,256]{1,0:T(8,128)(2,1)S(1)}, u32[]{:S(2)}, u32[]{:S(2)}) collective-permute-start(bf16[768,256]{1,0:T(8,128)(2,1)S(1)} %get-tuple-element.184.right_ref), channel_id=1, source_target_pairs={{0,8},{4,12},{8,0},{12,4},{16,24},{20,28},{24,16},{28,20},{1,9},{5... | collective-permute-start | bytes 1179656 | tf_op jit(solution)/shard_map/cond/branch_1_fun/ppermute | solution.py:565
  47.8 18.4 %collective-permute-start.45 = (bf16[768,256]{1,0:T(8,128)(2,1)S(1)}, bf16[768,256]{1,0:T(8,128)(2,1)S(1)}, u32[]{:S(2)}, u32[]{:S(2)}) collective-permute-start(bf16[768,256]{1,0:T(8,128)(2,1)S(1)} %get-tuple-element.186.right_ref), channel_id=1, source_target_pairs={{0,8},{4,12},{8,0},{12,4},{16,24},{20,28},{24,16},{28,20},{1,9},{5... | collective-permute-start | bytes 1179656 | tf_op jit(solution)/shard_map/cond/branch_1_fun/ppermute | solution.py:565
  48.3 8.1 %copy-start.51 = (bf16[1,768,2048]{2,1,0:T(8,128)(2,1)S(1)}, bf16[1,768,2048]{2,1,0:T(8,128)(2,1)}, u32[]{:S(2)}) copy-start(bf16[1,768,2048]{2,1,0:T(8,128)(2,1)} %get-tuple-element.398.down_ref) | copy-start | bytes 9437188 | tf_op jit(solution)/shard_map/cond
  48.3 8.1 %copy-start.55 = (bf16[1,2048,768]{2,1,0:T(8,128)(2,1)S(1)}, bf16[1,2048,768]{2,1,0:T(8,128)(2,1)}, u32[]{:S(2)}) copy-start(bf16[1,2048,768]{2,1,0:T(8,128)(2,1)} %get-tuple-element.389.refs_4_.gate_ref) | copy-start | bytes 9437188 | tf_op jit(solution)/shard_map/cond
  56.4 7.5 %copy-start.32 = (bf16[256,768]{1,0:T(8,128)(2,1)}, bf16[256,768]{1,0:T(8,128)(2,1)S(1)}, u32[]{:S(2)}) copy-start(bf16[256,768]{1,0:T(8,128)(2,1)S(1)} %get-tuple-element.198.right_ref) | copy-start | bytes 1179652 | tf_op jit(solution)/shard_map/cond
  62.9 13.0 %copy-start.44 = (bf16[2,80,2048]{2,1,0:T(8,128)(2,1)}, bf16[2,80,2048]{2,1,0:T(8,128)(2,1)S(1)}, u32[]{:S(2)}) copy-start(bf16[2,80,2048]{2,1,0:T(8,128)(2,1)S(1)} %get-tuple-element.189) | copy-start | bytes 1966084 | tf_op jit(solution)/shard_map/cond
  63.8 16.4 %copy-start.5 = (bf16[768,256]{1,0:T(8,128)(2,1)S(1)}, bf16[768,256]{1,0:T(8,128)(2,1)}, u32[]{:S(2)}) copy-start(bf16[768,256]{1,0:T(8,128)(2,1)} %copy-done.4) | copy-start | bytes 1179652 | tf_op jit(solution)/shard_map/cond
  63.8 16.4 %copy-start.7 = (bf16[768,256]{1,0:T(8,128)(2,1)S(1)}, bf16[768,256]{1,0:T(8,128)(2,1)}, u32[]{:S(2)}) copy-start(bf16[768,256]{1,0:T(8,128)(2,1)} %copy-done.6) | copy-start | bytes 1179652 | tf_op jit(solution)/shard_map/cond
  63.8 12.0 %collective-permute-start.52 = (bf16[256,768]{1,0:T(8,128)(2,1)S(1)}, bf16[256,768]{1,0:T(8,128)(2,1)S(1)}, u32[]{:S(2)}, u32[]{:S(2)}) collective-permute-start(bf16[256,768]{1,0:T(8,128)(2,1)S(1)} %get-tuple-element.198.right_ref), channel_id=1, source_target_pairs={{0,8},{4,12},{8,0},{12,4},{16,24},{20,28},{24,16},{28,20},{1,9},{5... | collective-permute-start | bytes 1179656 | tf_op jit(solution)/shard_map/cond/branch_1_fun/ppermute | solution.py:565
  67.0 17.3 %collective-permute-start.47 = (bf16[2,80,2048]{2,1,0:T(8,128)(2,1)}, bf16[2,80,2048]{2,1,0:T(8,128)(2,1)}, u32[]{:S(2)}, u32[]{:S(2)}) collective-permute-start(bf16[2,80,2048]{2,1,0:T(8,128)(2,1)} %get-tuple-element.187), channel_id=1, source_target_pairs={{0,1},{1,0},{2,3},{3,2},{4,5},{5,4},{6,7},{7,6},{8,9},{9,8},{10,11... | collective-permute-start | bytes 1966088 | tf_op jit(solution)/shard_map/cond/branch_1_fun/ppermute | solution.py:594
  68.3 11.9 %collective-permute-start.51 = (bf16[768,256]{1,0:T(8,128)(2,1)}, bf16[768,256]{1,0:T(8,128)(2,1)}, u32[]{:S(2)}, u32[]{:S(2)}) collective-permute-start(bf16[768,256]{1,0:T(8,128)(2,1)} %down_mid1.4), channel_id=1, source_target_pairs={{8,16},{16,8},{12,20},{20,12},{0,4},{4,0},{24,28},{28,24},{9,17},{... | collective-permute-start | bytes 1179656 | tf_op jit(solution)/shard_map/cond/branch_1_fun/ppermute | solution.py:569
  68.3 16.0 %collective-permute-start.50 = (bf16[256,768]{1,0:T(8,128)(2,1)}, bf16[256,768]{1,0:T(8,128)(2,1)}, u32[]{:S(2)}, u32[]{:S(2)}) collective-permute-start(bf16[256,768]{1,0:T(8,128)(2,1)} %get-tuple-element.203.right_ref), channel_id=1, source_target_pairs={{0,8},{4,12},{8,0},{12,4},{16,24},{20,28},{24,16},{28,20},{1,9},{5... | collective-permute-start | bytes 1179656 | tf_op jit(solution)/shard_map/cond/branch_1_fun/ppermute | solution.py:565
  71.5 12.9 %collective-permute-start.53 = (bf16[768,256]{1,0:T(8,128)(2,1)}, bf16[768,256]{1,0:T(8,128)(2,1)}, u32[]{:S(2)}, u32[]{:S(2)}) collective-permute-start(bf16[768,256]{1,0:T(8,128)(2,1)} %down_mid2.4), channel_id=1, source_target_pairs={{8,16},{16,8},{12,20},{20,12},{0,4},{4,0},{24,28},{28,24},{9,17},{... | collective-permute-start | bytes 1179656 | tf_op jit(solution)/shard_map/cond/branch_1_fun/ppermute | solution.py:569
  76.6 15.4 %collective-permute-start.48 = (bf16[2,80,2048]{2,1,0:T(8,128)(2,1)}, bf16[2,80,2048]{2,1,0:T(8,128)(2,1)}, u32[]{:S(2)}, u32[]{:S(2)}) collective-permute-start(bf16[2,80,2048]{2,1,0:T(8,128)(2,1)} %get-tuple-element.188), channel_id=1, source_target_pairs={{0,2},{1,3},{2,0},{3,1},{4,6},{5,7},{6,4},{7,5},{8,10},{9,11},{10,... | collective-permute-start | bytes 1966088 | tf_op jit(solution)/shard_map/cond/branch_1_fun/ppermute | solution.py:594
  80.2 11.8 %copy-start.45 = (bf16[2,80,2048]{2,1,0:T(8,128)(2,1)S(1)}, bf16[2,80,2048]{2,1,0:T(8,128)(2,1)}, u32[]{:S(2)}) copy-start(bf16[2,80,2048]{2,1,0:T(8,128)(2,1)} %copy-done.44) | copy-start | bytes 1966084 | tf_op jit(solution)/shard_map/cond
  81.3 12.3 %collective-permute-start.56 = (bf16[768,256]{1,0:T(8,128)(2,1)S(1)}, bf16[768,256]{1,0:T(8,128)(2,1)S(1)}, u32[]{:S(2)}, u32[]{:S(2)}) collective-permute-start(bf16[768,256]{1,0:T(8,128)(2,1)S(1)} %down_last.4), channel_id=1, source_target_pairs={{0,8},{4,12},{8,0},{12,4},{16,24},{20,28},{24,16},{28,20},{1,9},{5... | collective-permute-start | bytes 1179656 | tf_op jit(solution)/shard_map/cond/branch_1_fun/ppermute | solution.py:565
  84.3 11.2 %collective-permute-start.55 = (bf16[256,768]{1,0:T(8,128)(2,1)S(1)}, bf16[256,768]{1,0:T(8,128)(2,1)S(1)}, u32[]{:S(2)}, u32[]{:S(2)}) collective-permute-start(bf16[256,768]{1,0:T(8,128)(2,1)S(1)} %gate_mid1.4), channel_id=1, source_target_pairs={{8,16},{16,8},{12,20},{20,12},{0,4},{4,0},{24,28},{28,24},{9,17},{... | collective-permute-start | bytes 1179656 | tf_op jit(solution)/shard_map/cond/branch_1_fun/ppermute | solution.py:569
  85.6 16.0 %collective-permute-start.54 = (bf16[256,768]{1,0:T(8,128)(2,1)S(1)}, bf16[256,768]{1,0:T(8,128)(2,1)S(1)}, u32[]{:S(2)}, u32[]{:S(2)}) collective-permute-start(bf16[256,768]{1,0:T(8,128)(2,1)S(1)} %copy-done.27), channel_id=1, source_target_pairs={{0,8},{4,12},{8,0},{12,4},{16,24},{20,28},{24,16},{28,20},{1,9},{5... | collective-permute-start | bytes 1179656 | tf_op jit(solution)/shard_map/cond/branch_1_fun/ppermute | solution.py:565
  92.0 27.0 %collective-permute-start.49 = (bf16[2,80,2048]{2,1,0:T(8,128)(2,1)S(1)}, bf16[2,80,2048]{2,1,0:T(8,128)(2,1)S(1)}, u32[]{:S(2)}, u32[]{:S(2)}) collective-permute-start(bf16[2,80,2048]{2,1,0:T(8,128)(2,1)S(1)} %copy-done.45), channel_id=1, source_target_pairs={{0,3},{1,2},{2,1},{3,0},{4,7},{5,6},{6,5},{7,4},{8,11},{9,10},{10,... | collective-permute-start | bytes 1966088 | tf_op jit(solution)/shard_map/cond/branch_1_fun/ppermute | solution.py:594
  93.7 8.1 %collective-permute-start.61 = (bf16[256,768]{1,0:T(8,128)(2,1)S(1)}, bf16[256,768]{1,0:T(8,128)(2,1)S(1)}, u32[]{:S(2)}, u32[]{:S(2)}) collective-permute-start(bf16[256,768]{1,0:T(8,128)(2,1)S(1)} %up_mid1.4), channel_id=1, source_target_pairs={{8,16},{16,8},{12,20},{20,12},{0,4},{4,0},{24,28},{28,24},{9,17},{... | collective-permute-start | bytes 1179656 | tf_op jit(solution)/shard_map/cond/branch_1_fun/ppermute | solution.py:569
  94.8 20.0 %collective-permute-start.62 = (bf16[768,256]{1,0:T(8,128)(2,1)S(1)}, bf16[768,256]{1,0:T(8,128)(2,1)S(1)}, u32[]{:S(2)}, u32[]{:S(2)}) collective-permute-start(bf16[768,256]{1,0:T(8,128)(2,1)S(1)} %down_sum.4), channel_id=1, source_target_pairs={{0,2},{1,3},{2,0},{3,1},{4,6},{5,7},{6,4},{7,5},{8,10},{9,11},{10,... | collective-permute-start | bytes 1179656 | tf_op jit(solution)/shard_map/cond/branch_1_fun/ppermute | solution.py:572
  95.6 14.3 %collective-permute-start.59 = (bf16[256,768]{1,0:T(8,128)(2,1)S(1)}, bf16[256,768]{1,0:T(8,128)(2,1)S(1)}, u32[]{:S(2)}, u32[]{:S(2)}) collective-permute-start(bf16[256,768]{1,0:T(8,128)(2,1)S(1)} %gate_last.4), channel_id=1, source_target_pairs={{0,8},{4,12},{8,0},{12,4},{16,24},{20,28},{24,16},{28,20},{1,9},{5... | collective-permute-start | bytes 1179656 | tf_op jit(solution)/shard_map/cond/branch_1_fun/ppermute | solution.py:565
  101.6 13.2 %collective-permute-start.60 = (bf16[256,768]{1,0:T(8,128)(2,1)S(1)}, bf16[256,768]{1,0:T(8,128)(2,1)S(1)}, u32[]{:S(2)}, u32[]{:S(2)}) collective-permute-start(bf16[256,768]{1,0:T(8,128)(2,1)S(1)} %gate_mid2.4), channel_id=1, source_target_pairs={{8,16},{16,8},{12,20},{20,12},{0,4},{4,0},{24,28},{28,24},{9,17},{... | collective-permute-start | bytes 1179656 | tf_op jit(solution)/shard_map/cond/branch_1_fun/ppermute | solution.py:569
  101.8 16.5 %collective-permute-start.57 = (bf16[128,768]{1,0:T(8,128)(2,1)S(1)}, bf16[128,768]{1,0:T(8,128)(2,1)S(1)}, u32[]{:S(2)}, u32[]{:S(2)}) collective-permute-start(bf16[128,768]{1,0:T(8,128)(2,1)S(1)} %get-tuple-element.231.right_ref), channel_id=1, source_target_pairs={{0,8},{4,12},{8,0},{12,4},{16,24},{20,28},{24,16},{28,20},{1,9},{5... | collective-permute-start | bytes 589832 | tf_op jit(solution)/shard_map/cond/branch_1_fun/ppermute | solution.py:565
  110.0 8.2 %collective-permute-start.58 = (bf16[128,768]{1,0:T(8,128)(2,1)S(1)}, bf16[128,768]{1,0:T(8,128)(2,1)S(1)}, u32[]{:S(2)}, u32[]{:S(2)}) collective-permute-start(bf16[128,768]{1,0:T(8,128)(2,1)S(1)} %get-tuple-element.229.right_ref), channel_id=1, source_target_pairs={{0,8},{4,12},{8,0},{12,4},{16,24},{20,28},{24,16},{28,20},{1,9},{5... | collective-permute-start | bytes 589832 | tf_op jit(solution)/shard_map/cond/branch_1_fun/ppermute | solution.py:565
  114.8 6.8 %copy-start.58 = (bf16[128,2048]{1,0:T(8,128)(2,1)S(1)}, bf16[128,2048]{1,0:T(8,128)(2,1)}, u32[]{:S(2)}) copy-start(bf16[128,2048]{1,0:T(8,128)(2,1)} %get-tuple-element.395.cot_ref) | copy-start | bytes 1572868 | tf_op jit(solution)/shard_map/cond
  114.8 6.8 %copy-start.61 = (s32[2,128]{1,0:T(2,128)S(1)}, s32[2,128]{1,0:T(2,128)}, u32[]{:S(2)}) copy-start(s32[2,128]{1,0:T(2,128)} %get-tuple-element.148.ids_ref) | copy-start | bytes 3076 | tf_op jit(solution)/shard_map/cond
  114.8 6.8 %copy-start.64 = (f32[2,128]{1,0:T(2,128)S(1)}, f32[2,128]{1,0:T(2,128)}, u32[]{:S(2)}) copy-start(f32[2,128]{1,0:T(2,128)} %get-tuple-element.149.gates_ref) | copy-start | bytes 3076 | tf_op jit(solution)/shard_map/cond
  115.0 11.2 %collective-permute-start.63 = (bf16[256,768]{1,0:T(8,128)(2,1)S(1)}, bf16[256,768]{1,0:T(8,128)(2,1)S(1)}, u32[]{:S(2)}, u32[]{:S(2)}) collective-permute-start(bf16[256,768]{1,0:T(8,128)(2,1)S(1)} %gate_sum.4), channel_id=1, source_target_pairs={{0,2},{1,3},{2,0},{3,1},{4,6},{5,7},{6,4},{7,5},{8,10},{9,11},{10,... | collective-permute-start | bytes 1179656 | tf_op jit(solution)/shard_map/cond/branch_1_fun/ppermute | solution.py:572
  116.5 9.5 %collective-permute-start.66 = (bf16[128,768]{1,0:T(8,128)(2,1)S(1)}, bf16[128,768]{1,0:T(8,128)(2,1)S(1)}, u32[]{:S(2)}, u32[]{:S(2)}) collective-permute-start(bf16[128,768]{1,0:T(8,128)(2,1)S(1)} %get-tuple-element.241), channel_id=1, source_target_pairs={{0,8},{4,12},{8,0},{12,4},{16,24},{20,28},{24,16},{28,20},{1,9},{5... | collective-permute-start | bytes 589832 | tf_op jit(solution)/shard_map/cond/branch_1_fun/ppermute | solution.py:565
  118.2 7.8 %collective-permute-start.67 = (bf16[128,768]{1,0:T(8,128)(2,1)S(1)}, bf16[128,768]{1,0:T(8,128)(2,1)S(1)}, u32[]{:S(2)}, u32[]{:S(2)}) collective-permute-start(bf16[128,768]{1,0:T(8,128)(2,1)S(1)} %up_mid20.4), channel_id=1, source_target_pairs={{8,16},{16,8},{12,20},{20,12},{0,4},{4,0},{24,28},{28,24},{9,17},{... | collective-permute-start | bytes 589832 | tf_op jit(solution)/shard_map/cond/branch_1_fun/ppermute | solution.py:569
  118.4 7.8 %collective-permute-start.65 = (bf16[128,768]{1,0:T(8,128)(2,1)S(1)}, bf16[128,768]{1,0:T(8,128)(2,1)S(1)}, u32[]{:S(2)}, u32[]{:S(2)}) collective-permute-start(bf16[128,768]{1,0:T(8,128)(2,1)S(1)} %up_mid21.4), channel_id=1, source_target_pairs={{8,16},{16,8},{12,20},{20,12},{0,4},{4,0},{24,28},{28,24},{9,17},{... | collective-permute-start | bytes 589832 | tf_op jit(solution)/shard_map/cond/branch_1_fun/ppermute | solution.py:569
  118.9 8.4 %collective-permute-start.64 = (bf16[128,768]{1,0:T(8,128)(2,1)S(1)}, bf16[128,768]{1,0:T(8,128)(2,1)S(1)}, u32[]{:S(2)}, u32[]{:S(2)}) collective-permute-start(bf16[128,768]{1,0:T(8,128)(2,1)S(1)} %get-tuple-element.240), channel_id=1, source_target_pairs={{0,8},{4,12},{8,0},{12,4},{16,24},{20,28},{24,16},{28,20},{1,9},{5... | collective-permute-start | bytes 589832 | tf_op jit(solution)/shard_map/cond/branch_1_fun/ppermute | solution.py:565
  127.4 7.9 %collective-permute-start.69 = (bf16[128,768]{1,0:T(8,128)(2,1)S(1)}, bf16[128,768]{1,0:T(8,128)(2,1)S(1)}, u32[]{:S(2)}, u32[]{:S(2)}) collective-permute-start(bf16[128,768]{1,0:T(8,128)(2,1)S(1)} %up_sum1.4), channel_id=1, source_target_pairs={{0,2},{1,3},{2,0},{3,1},{4,6},{5,7},{6,4},{7,5},{8,10},{9,11},{10,... | collective-permute-start | bytes 589832 | tf_op jit(solution)/shard_map/cond/branch_1_fun/ppermute | solution.py:572
  128.0 9.4 %collective-permute-start.68 = (bf16[128,768]{1,0:T(8,128)(2,1)S(1)}, bf16[128,768]{1,0:T(8,128)(2,1)S(1)}, u32[]{:S(2)}, u32[]{:S(2)}) collective-permute-start(bf16[128,768]{1,0:T(8,128)(2,1)S(1)} %up_sum0.4), channel_id=1, source_target_pairs={{0,2},{1,3},{2,0},{3,1},{4,6},{5,7},{6,4},{7,5},{8,10},{9,11},{10,... | collective-permute-start | bytes 589832 | tf_op jit(solution)/shard_map/cond/branch_1_fun/ppermute | solution.py:572
  (9 other events, 17.6 us)

commit v5 on v4

--- a/solution.py
+++ b/solution.py
@@ -505,7 +505,7 @@
     )(*x_blocks, w_gate, w_up)
     act_other = swap(act)
 
-    wide = tile_of(width, 512)
+    wide = tile_of(width, 1024)
 
     def run_backward(c_rows):
         return pl.pallas_call(
@@ -597,9 +597,9 @@
         g_m1 = swap_middle(m)
         (e,) = last_share("down_last", 1, end, *after((d_c, d_m1, d_d), m))
         d_3 = swap_ends(e)
-        m = added("up_mid1", BF16, *after((u_1, u_a), e, d_m2, results[1]))
+        m = added("up_mid1", BF16, *after((u_1, u_a), e, d_m2))
         u_m1, g_2 = swap_middle(m), swap_ends(after(g_b, m))
-        t = final_sum("down_sum", 0, end, *after((d_3, d_d, d_c, d_m2), m))
+        t = final_sum("down_sum", 0, end, *after((d_3, d_d, d_c, d_m2), m, results[1]))
         d_t = to_mate(t)
         (e,) = last_share("gate_last", 1, end, *after((g_c, g_m1, g_d), t))
         g_3 = swap_ends(e)

time: 140 us -> 139 us (level)
  waiting for transfers between devices: 36.5 us -> 44 us
  starting transfers between devices: 52.8 us -> 45.7 us
    ppermute x11, starting transfers between devices: 31.3 us -> 22.9 us  [swap_ends(): return lax.ppermute(part, 'dp', [(i, i ^ 2) for i in range(replicas)])]
    ppermute x3, waiting for transfers between devices: 0.01 us -> 3.37 us  [layer(): lax.ppermute(part, 'expert', [(i, i ^ n) for i in range(groups)])]
    ppermute x11, waiting for transfers between devices: 12 us -> 14.7 us  [swap_ends(): return lax.ppermute(part, 'dp', [(i, i ^ 2) for i in range(replicas)])]
    ppermute x4, starting transfers between devices: 4.46 us -> 6.13 us  [to_mate(): return lax.ppermute(part, 'expert', [(i, i ^ turn) for i in range(groups)])]
  transfers between devices with their start and end apart: 35 -> 35, of which waited for: 13 -> 13; matrix products, arithmetic and copies ran while one was open for 0% -> 0% of each run, Pallas kernels for 28% -> 27%
where the time goes in v5:
time: 139 us
  starting transfers between devices  45.7 us (33%)
  waiting for transfers between devices  44 us (32%)
  Pallas kernels  40.7 us (29%)
  local copies, waits for them, and re-layouts  6.13 us (4%)
  between operations  1.44 us (1%)
    ppermute x11, starting transfers between devices, swap_ends(): return lax.ppermute(part, 'dp', [(i, i ^ 2) for i in range(replicas)])  22.9 us
    ppermute x6, waiting for transfers between devices, exchange(): lax.ppermute(blocks[b], 'expert', [(i, i ^ b) for i in range(groups)])  15.1 us
    ppermute x11, waiting for transfers between devices, swap_ends(): return lax.ppermute(part, 'dp', [(i, i ^ 2) for i in range(replicas)])  14.7 us
    ppermute x6, starting transfers between devices, exchange(): lax.ppermute(blocks[b], 'expert', [(i, i ^ b) for i in range(groups)])  11.1 us
    ppermute x4, waiting for transfers between devices, to_mate(): return lax.ppermute(part, 'expert', [(i, i ^ turn) for i in range(groups)])  10.8 us
    pallas_call x1, Pallas kernels, gate_up_shares(): pl.pallas_call(functools.partial(gate_up_share, count), out_shape=[jax.Sh...  6.54 us
    ppermute x4, starting transfers between devices, to_mate(): return lax.ppermute(part, 'expert', [(i, i ^ turn) for i in range(groups)])  6.13 us
    cond x44, local copies, waits for them, and re-layouts  6.1 us
  transfers between devices with their start and end apart: 35, of which 13 were waited for; matrix products, arithmetic and copies ran while one was open for 0% of the time, Pallas kernels for 27%

profile of v5, /device:TPU:0, one launch (start us, length us, event | category | flops | bytes accessed | tf_op | source)
XLA Modules:
  0.0 138.6 jit_solution(13732363326069224186)
XLA Ops:
  1.3 137.1 %conditional.1 = (bf16[128,2048]{1,0:T(8,128)(2,1)}, bf16[128,2048]{1,0:T(8,128)(2,1)}, f32[128,2]{0,1:T(2,128)}, f32[1,256,768]{2,1,0:T(8,128)}, f32[1,256,768]{2,1,0:T(8,128)}, /*index=5*/f32[1,768,256]{2,1,0:T(8,128)}) conditional(s32[]{:T(128)} %bitcast.9, (s32[2,128]{1,0:T(2,128)}, bf16[128,2048]{1,0:T(8,128)(2,1)}, ...), branch_computations={%region_0.1_spmd, %region_1.2_spmd, %region_2.3_spmd} | conditional | flops 24045 | bytes 129140488 | solution.py:426
  1.5 1.7 %place_tokens.5 = (bf16[80,2048]{1,0:T(8,128)(2,1)S(1)}, bf16[80,2048]{1,0:T(8,128)(2,1)S(1)}, bf16[80,2048]{1,0:T(8,128)(2,1)S(1)}, bf16[80,2048]{1,0:T(8,128)(2,1)S(1)}) custom-call(s32[1]{0:T(128)} %bitcast.6.me_ref, s32[2,128]{1,0:T(2,128)} %get-tuple-element.254.ids_ref, bf16[128,2048]{1,0:T(8,128)(2,1)} %get-tuple-element.387.tok_ref), custom_call_target="tpu_custom_call" | custom-call | tf_op jit(solution)/shard_map/cond/branch_2_fun/place_tokens/pallas_call | solution.py:467
  3.2 3.0 %collective-permute-start.70 = (bf16[80,2048]{1,0:T(8,128)(2,1)S(1)}, bf16[80,2048]{1,0:T(8,128)(2,1)S(1)}, u32[]{:S(2)}, u32[]{:S(2)}) collective-permute-start(bf16[80,2048]{1,0:T(8,128)(2,1)S(1)} %get-tuple-element.259), channel_id=1, source_target_pairs={{0,1},{1,0},{2,3},{3,2},{4,5},{5,4},{6,7},{7,6},{8,9},{9,8},{10,11... | collective-permute-start | bytes 983048 | tf_op jit(solution)/shard_map/cond/branch_2_fun/ppermute | solution.py:449
  6.2 1.5 %collective-permute-start.71 = (bf16[80,2048]{1,0:T(8,128)(2,1)S(1)}, bf16[80,2048]{1,0:T(8,128)(2,1)S(1)}, u32[]{:S(2)}, u32[]{:S(2)}) collective-permute-start(bf16[80,2048]{1,0:T(8,128)(2,1)S(1)} %get-tuple-element.260), channel_id=1, source_target_pairs={{0,2},{1,3},{2,0},{3,1},{4,6},{5,7},{6,4},{7,5},{8,10},{9,11},{10,... | collective-permute-start | bytes 983048 | tf_op jit(solution)/shard_map/cond/branch_2_fun/ppermute | solution.py:449
  7.7 1.7 %place_grads.5 = (bf16[80,2048]{1,0:T(8,128)(2,1)S(1)}, bf16[80,2048]{1,0:T(8,128)(2,1)S(1)}, bf16[80,2048]{1,0:T(8,128)(2,1)S(1)}, bf16[80,2048]{1,0:T(8,128)(2,1)S(1)}) custom-call(s32[1]{0:T(128)} %bitcast.6.me_ref, s32[2,128]{1,0:T(2,128)} %get-tuple-element.254.ids_ref, f32[2,128]{1,0:T(2,128)} %get-tuple-element.255.gates_ref, ...), custom_call_target="tpu_custom_call" | custom-call | tf_op jit(solution)/shard_map/cond/branch_2_fun/place_grads/pallas_call | solution.py:475
  9.5 2.0 %collective-permute-start.73 = (bf16[80,2048]{1,0:T(8,128)(2,1)S(1)}, bf16[80,2048]{1,0:T(8,128)(2,1)S(1)}, u32[]{:S(2)}, u32[]{:S(2)}) collective-permute-start(bf16[80,2048]{1,0:T(8,128)(2,1)S(1)} %get-tuple-element.266), channel_id=1, source_target_pairs={{0,1},{1,0},{2,3},{3,2},{4,5},{5,4},{6,7},{7,6},{8,9},{9,8},{10,11... | collective-permute-start | bytes 983048 | tf_op jit(solution)/shard_map/cond/branch_2_fun/ppermute | solution.py:449
  11.5 1.5 %collective-permute-start.74 = (bf16[80,2048]{1,0:T(8,128)(2,1)S(1)}, bf16[80,2048]{1,0:T(8,128)(2,1)S(1)}, u32[]{:S(2)}, u32[]{:S(2)}) collective-permute-start(bf16[80,2048]{1,0:T(8,128)(2,1)S(1)} %get-tuple-element.267), channel_id=1, source_target_pairs={{0,2},{1,3},{2,0},{3,1},{4,6},{5,7},{6,4},{7,5},{8,10},{9,11},{10,... | collective-permute-start | bytes 983048 | tf_op jit(solution)/shard_map/cond/branch_2_fun/ppermute | solution.py:449
  13.0 1.7 %collective-permute-done.70.refs_1_ = bf16[80,2048]{1,0:T(8,128)(2,1)S(1)} collective-permute-done((bf16[80,2048]{1,0:T(8,128)(2,1)S(1)}, bf16[80,2048]{1,0:T(8,128)(2,1)S(1)}, u32[]{:S(2)}, u32[]{:S(2)}) %collective-permute-start.70) | collective-permute-done | bytes 327712 | tf_op jit(solution)/shard_map/cond/branch_2_fun/ppermute | solution.py:449
  14.7 3.0 %collective-permute-start.75 = (bf16[80,2048]{1,0:T(8,128)(2,1)S(1)}, bf16[80,2048]{1,0:T(8,128)(2,1)S(1)}, u32[]{:S(2)}, u32[]{:S(2)}) collective-permute-start(bf16[80,2048]{1,0:T(8,128)(2,1)S(1)} %get-tuple-element.268), channel_id=1, source_target_pairs={{0,3},{1,2},{2,1},{3,0},{4,7},{5,6},{6,5},{7,4},{8,11},{9,10},{10,... | collective-permute-start | bytes 983048 | tf_op jit(solution)/shard_map/cond/branch_2_fun/ppermute | solution.py:449
  17.8 6.1 %collective-permute-done.71.refs_2_ = bf16[80,2048]{1,0:T(8,128)(2,1)S(1)} collective-permute-done((bf16[80,2048]{1,0:T(8,128)(2,1)S(1)}, bf16[80,2048]{1,0:T(8,128)(2,1)S(1)}, u32[]{:S(2)}, u32[]{:S(2)}) %collective-permute-start.71) | collective-permute-done | bytes 327712 | tf_op jit(solution)/shard_map/cond/branch_2_fun/ppermute | solution.py:449
  23.9 5.2 %forward.5 = (bf16[320,2048]{1,0:T(8,128)(2,1)S(1)}, f32[2,320,768]{2,1,0:T(8,128)S(1)}, bf16[320,768]{1,0:T(8,128)(2,1)S(1)}) custom-call(bf16[80,2048]{1,0:T(8,128)(2,1)S(1)} %get-tuple-element.258.refs_0_, bf16[80,2048]{1,0:T(8,128)(2,1)S(1)} %collective-permute-done.70.refs_1_, bf16[80,2048]{1,0:T(8,128)(2,1)S(1)} %collective-permute-done.71.refs_2_, ...), custom_call_target="tpu_custom_call" | custom-call | flops 1000 | bytes 1000 | tf_op jit(solution)/shard_map/cond/branch_2_fun/forward/pallas_call | solution.py:487
  29.2 7.3 %collective-permute-done.74.refs_2_ = bf16[80,2048]{1,0:T(8,128)(2,1)S(1)} collective-permute-done((bf16[80,2048]{1,0:T(8,128)(2,1)S(1)}, bf16[80,2048]{1,0:T(8,128)(2,1)S(1)}, u32[]{:S(2)}, u32[]{:S(2)}) %collective-permute-start.74) | collective-permute-done | bytes 327712 | tf_op jit(solution)/shard_map/cond/branch_2_fun/ppermute | solution.py:449
  37.4 2.8 %backward.5.refs_8_.grad_ref = bf16[2,320,768]{2,1,0:T(8,128)(2,1)} custom-call(bf16[320,2048]{1,0:T(8,128)(2,1)S(1)} %join_grads.5.c_ref.c_own, bf16[1,768,2048]{2,1,0:T(8,128)(2,1)S(1)} %copy-done.52, f32[2,320,768]{2,1,0:T(8,128)S(1)} %get-tuple-element.275.pre_ref), custom_call_target="tpu_custom_call" | custom-call | flops 1000 | bytes 1000 | tf_op jit(solution)/shard_map/cond/branch_2_fun/backward/pallas_call | solution.py:511
  40.7 1.0 copy-done.17
  41.7 4.4 %down_shares.5 = (bf16[768,256]{1,0:T(8,128)(2,1)S(1)}, bf16[768,256]{1,0:T(8,128)(2,1)S(1)}, bf16[768,256]{1,0:T(8,128)(2,1)S(1)}, bf16[768,256]{1,0:T(8,128)(2,1)S(1)}) custom-call(s32[4]{0:T(128)S(1)} %fusion.5.order_ref, bf16[320,768]{1,0:T(8,128)(2,1)S(1)} %get-tuple-element.264.act_own.act_ref, bf16[320,768]{1,0:T(8,128)(2,1)S(1)} %copy-done.17, ...), custom_call_target="tpu_custom_call" | custom-call | flops 1000 | bytes 1000 | tf_op jit(solution)/shard_map/cond/branch_2_fun/down_shares/pallas_call | solution.py:329
  46.2 1.6 %collective-permute-start.81 = (bf16[768,256]{1,0:T(8,128)(2,1)S(1)}, bf16[768,256]{1,0:T(8,128)(2,1)S(1)}, u32[]{:S(2)}, u32[]{:S(2)}) collective-permute-start(bf16[768,256]{1,0:T(8,128)(2,1)S(1)} %get-tuple-element.290.right_ref), channel_id=1, source_target_pairs={{0,8},{4,12},{8,0},{12,4},{16,24},{20,28},{24,16},{28,20},{1,9},{5... | collective-permute-start | bytes 1179656 | tf_op jit(solution)/shard_map/cond/branch_2_fun/ppermute | solution.py:565
  48.3 6.5 %gate_up_shares.5 = (bf16[256,768]{1,0:T(8,128)(2,1)S(1)}, bf16[256,768]{1,0:T(8,128)(2,1)S(1)}, bf16[256,768]{1,0:T(8,128)(2,1)S(1)}, bf16[256,768]{1,0:T(8,128...) custom-call(s32[4]{0:T(128)S(1)} %fusion.5.order_ref, ...), custom_call_target="tpu_custom_call" | custom-call | flops 1000 | bytes 1000 | tf_op jit(solution)/shard_map/cond/branch_2_fun/gate_up_shares/pallas_call | solution.py:353
  56.4 6.1 %result_rows.5 = (bf16[2,80,2048]{2,1,0:T(8,128)(2,1)S(1)}, bf16[2,80,2048]{2,1,0:T(8,128)(2,1)}, bf16[2,80,2048]{2,1,0:T(8,128)(2,1)}, bf16[2,80,2048]{2,1,0:T(8,128)(2,1)S(1)}) custom-call(bf16[320,768]{1,0:T(8,128)(2,1)S(1)} %get-tuple-element.264.act_own.act_ref, bf16[2,320,768]{2,1,0:T(8,128)(2,1)} %backward.5.refs_8_.grad_ref, ...), custom_call_target="tpu_custom_call" | custom-call | flops 1000 | bytes 1000 | tf_op jit(solution)/shard_map/cond/branch_2_fun/result_rows/pallas_call | solution.py:527
  62.5 1.0 down_mid1.5
  63.5 1.6 %collective-permute-start.87 = (bf16[256,768]{1,0:T(8,128)(2,1)S(1)}, bf16[256,768]{1,0:T(8,128)(2,1)S(1)}, u32[]{:S(2)}, u32[]{:S(2)}) collective-permute-start(bf16[256,768]{1,0:T(8,128)(2,1)S(1)} %get-tuple-element.304.right_ref), channel_id=1, source_target_pairs={{0,8},{4,12},{8,0},{12,4},{16,24},{20,28},{24,16},{28,20},{1,9},{5... | collective-permute-start | bytes 1179656 | tf_op jit(solution)/shard_map/cond/branch_2_fun/ppermute | solution.py:565
  65.1 1.2 collective-permute-done.80.left_ref
  67.1 1.9 %collective-permute-start.85 = (bf16[256,768]{1,0:T(8,128)(2,1)}, bf16[256,768]{1,0:T(8,128)(2,1)}, u32[]{:S(2)}, u32[]{:S(2)}) collective-permute-start(bf16[256,768]{1,0:T(8,128)(2,1)} %get-tuple-element.309.right_ref), channel_id=1, source_target_pairs={{0,8},{4,12},{8,0},{12,4},{16,24},{20,28},{24,16},{28,20},{1,9},{5... | collective-permute-start | bytes 1179656 | tf_op jit(solution)/shard_map/cond/branch_2_fun/ppermute | solution.py:565
  69.0 1.5 %collective-permute-start.83 = (bf16[2,80,2048]{2,1,0:T(8,128)(2,1)}, bf16[2,80,2048]{2,1,0:T(8,128)(2,1)}, u32[]{:S(2)}, u32[]{:S(2)}) collective-permute-start(bf16[2,80,2048]{2,1,0:T(8,128)(2,1)} %get-tuple-element.294), channel_id=1, source_target_pairs={{0,2},{1,3},{2,0},{3,1},{4,6},{5,7},{6,4},{7,5},{8,10},{9,11},{10,... | collective-permute-start | bytes 1966088 | tf_op jit(solution)/shard_map/cond/branch_2_fun/ppermute | solution.py:594
  70.6 4.9 %collective-permute-done.87.left_ref = bf16[256,768]{1,0:T(8,128)(2,1)S(1)} collective-permute-done((bf16[256,768]{1,0:T(8,128)(2,1)S(1)}, bf16[256,768]{1,0:T(8,128)(2,1)S(1)}, u32[]{:S(2)}, u32[]{:S(2)}) %collective-permute-start.87) | collective-permute-done | bytes 393248 | tf_op jit(solution)/shard_map/cond/branch_2_fun/ppermute | solution.py:565
  76.2 1.3 collective-permute-start.82
  79.7 1.1 down_last.5
  80.8 1.7 %collective-permute-start.91 = (bf16[768,256]{1,0:T(8,128)(2,1)S(1)}, bf16[768,256]{1,0:T(8,128)(2,1)S(1)}, u32[]{:S(2)}, u32[]{:S(2)}) collective-permute-start(bf16[768,256]{1,0:T(8,128)(2,1)S(1)} %down_last.5), channel_id=1, source_target_pairs={{0,8},{4,12},{8,0},{12,4},{16,24},{20,28},{24,16},{28,20},{1,9},{5... | collective-permute-start | bytes 1179656 | tf_op jit(solution)/shard_map/cond/branch_2_fun/ppermute | solution.py:565
  82.5 1.6 %collective-permute-done.85.left_ref = bf16[256,768]{1,0:T(8,128)(2,1)} collective-permute-done((bf16[256,768]{1,0:T(8,128)(2,1)}, bf16[256,768]{1,0:T(8,128)(2,1)}, u32[]{:S(2)}, u32[]{:S(2)}) %collective-permute-start.85) | collective-permute-done | bytes 393248 | tf_op jit(solution)/shard_map/cond/branch_2_fun/ppermute | solution.py:565
  84.0 1.2 up_mid1.5
  85.2 3.2 %collective-permute-start.89 = (bf16[256,768]{1,0:T(8,128)(2,1)S(1)}, bf16[256,768]{1,0:T(8,128)(2,1)S(1)}, u32[]{:S(2)}, u32[]{:S(2)}) collective-permute-start(bf16[256,768]{1,0:T(8,128)(2,1)S(1)} %copy-done.29), channel_id=1, source_target_pairs={{0,8},{4,12},{8,0},{12,4},{16,24},{20,28},{24,16},{28,20},{1,9},{5... | collective-permute-start | bytes 1179656 | tf_op jit(solution)/shard_map/cond/branch_2_fun/ppermute | solution.py:565
  88.5 1.5 %collective-permute-start.84 = (bf16[2,80,2048]{2,1,0:T(8,128)(2,1)S(1)}, bf16[2,80,2048]{2,1,0:T(8,128)(2,1)S(1)}, u32[]{:S(2)}, u32[]{:S(2)}) collective-permute-start(bf16[2,80,2048]{2,1,0:T(8,128)(2,1)S(1)} %copy-done.47), channel_id=1, source_target_pairs={{0,3},{1,2},{2,1},{3,0},{4,7},{5,6},{6,5},{7,4},{8,11},{9,10},{10,... | collective-permute-start | bytes 1966088 | tf_op jit(solution)/shard_map/cond/branch_2_fun/ppermute | solution.py:594
  89.9 3.4 %collective-permute-done.82.refs_1_ = bf16[2,80,2048]{2,1,0:T(8,128)(2,1)} collective-permute-done((bf16[2,80,2048]{2,1,0:T(8,128)(2,1)}, bf16[2,80,2048]{2,1,0:T(8,128)(2,1)}, u32[]{:S(2)}, u32[]{:S(2)}) %collective-permute-start.82) | collective-permute-done | bytes 655392 | tf_op jit(solution)/shard_map/cond/branch_2_fun/ppermute | solution.py:594
  93.3 1.1 down_sum.5
  94.4 1.8 %collective-permute-start.97 = (bf16[768,256]{1,0:T(8,128)(2,1)S(1)}, bf16[768,256]{1,0:T(8,128)(2,1)S(1)}, u32[]{:S(2)}, u32[]{:S(2)}) collective-permute-start(bf16[768,256]{1,0:T(8,128)(2,1)S(1)} %down_sum.5), channel_id=1, source_target_pairs={{0,3},{1,2},{2,1},{3,0},{4,7},{5,6},{6,5},{7,4},{8,11},{9,10},{10,... | collective-permute-start | bytes 1179656 | tf_op jit(solution)/shard_map/cond/branch_2_fun/ppermute | solution.py:572
  96.3 2.5 %collective-permute-start.94 = (bf16[256,768]{1,0:T(8,128)(2,1)S(1)}, bf16[256,768]{1,0:T(8,128)(2,1)S(1)}, u32[]{:S(2)}, u32[]{:S(2)}) collective-permute-start(bf16[256,768]{1,0:T(8,128)(2,1)S(1)} %gate_last.5), channel_id=1, source_target_pairs={{0,8},{4,12},{8,0},{12,4},{16,24},{20,28},{24,16},{28,20},{1,9},{5... | collective-permute-start | bytes 1179656 | tf_op jit(solution)/shard_map/cond/branch_2_fun/ppermute | solution.py:565
  98.8 1.7 %collective-permute-done.89.left_ref = bf16[256,768]{1,0:T(8,128)(2,1)S(1)} collective-permute-done((bf16[256,768]{1,0:T(8,128)(2,1)S(1)}, bf16[256,768]{1,0:T(8,128)(2,1)S(1)}, u32[]{:S(2)}, u32[]{:S(2)}) %collective-permute-start.89) | collective-permute-done | bytes 393248 | tf_op jit(solution)/shard_map/cond/branch_2_fun/ppermute | solution.py:565
  100.7 3.2 %collective-permute-start.92 = (bf16[128,768]{1,0:T(8,128)(2,1)S(1)}, bf16[128,768]{1,0:T(8,128)(2,1)S(1)}, u32[]{:S(2)}, u32[]{:S(2)}) collective-permute-start(bf16[128,768]{1,0:T(8,128)(2,1)S(1)} %get-tuple-element.337.right_ref), channel_id=1, source_target_pairs={{0,8},{4,12},{8,0},{12,4},{16,24},{20,28},{24,16},{28,20},{1,9},{5... | collective-permute-start | bytes 589832 | tf_op jit(solution)/shard_map/cond/branch_2_fun/ppermute | solution.py:565
  103.9 5.0 %collective-permute-done.94.last_ref = bf16[256,768]{1,0:T(8,128)(2,1)S(1)} collective-permute-done((bf16[256,768]{1,0:T(8,128)(2,1)S(1)}, bf16[256,768]{1,0:T(8,128)(2,1)S(1)}, u32[]{:S(2)}, u32[]{:S(2)}) %collective-permute-start.94) | collective-permute-done | bytes 393248 | tf_op jit(solution)/shard_map/cond/branch_2_fun/ppermute | solution.py:565
  108.9 2.4 %collective-permute-start.93 = (bf16[128,768]{1,0:T(8,128)(2,1)S(1)}, bf16[128,768]{1,0:T(8,128)(2,1)S(1)}, u32[]{:S(2)}, u32[]{:S(2)}) collective-permute-start(bf16[128,768]{1,0:T(8,128)(2,1)S(1)} %get-tuple-element.335.right_ref), channel_id=1, source_target_pairs={{0,8},{4,12},{8,0},{12,4},{16,24},{20,28},{24,16},{28,20},{1,9},{5... | collective-permute-start | bytes 589832 | tf_op jit(solution)/shard_map/cond/branch_2_fun/ppermute | solution.py:565
  111.4 3.6 %collective-permute-done.97.refs_0_ = bf16[768,256]{1,0:T(8,128)(2,1)S(1)} collective-permute-done((bf16[768,256]{1,0:T(8,128)(2,1)S(1)}, bf16[768,256]{1,0:T(8,128)(2,1)S(1)}, u32[]{:S(2)}, u32[]{:S(2)}) %collective-permute-start.97) | collective-permute-done | bytes 393248 | tf_op jit(solution)/shard_map/cond/branch_2_fun/ppermute | solution.py:572
  115.1 1.3 collective-permute-start.98
  116.4 1.6 %collective-permute-start.101 = (bf16[128,768]{1,0:T(8,128)(2,1)S(1)}, bf16[128,768]{1,0:T(8,128)(2,1)S(1)}, u32[]{:S(2)}, u32[]{:S(2)}) collective-permute-start(bf16[128,768]{1,0:T(8,128)(2,1)S(1)} %get-tuple-element.347), channel_id=1, source_target_pairs={{0,8},{4,12},{8,0},{12,4},{16,24},{20,28},{24,16},{28,20},{1,9},{5... | collective-permute-start | bytes 589832 | tf_op jit(solution)/shard_map/cond/branch_2_fun/ppermute | solution.py:565
  118.8 2.7 %collective-permute-start.99 = (bf16[128,768]{1,0:T(8,128)(2,1)S(1)}, bf16[128,768]{1,0:T(8,128)(2,1)S(1)}, u32[]{:S(2)}, u32[]{:S(2)}) collective-permute-start(bf16[128,768]{1,0:T(8,128)(2,1)S(1)} %get-tuple-element.346), channel_id=1, source_target_pairs={{0,8},{4,12},{8,0},{12,4},{16,24},{20,28},{24,16},{28,20},{1,9},{5... | collective-permute-start | bytes 589832 | tf_op jit(solution)/shard_map/cond/branch_2_fun/ppermute | solution.py:565
  121.5 3.4 %combine.5 = (bf16[128,2048]{1,0:T(8,128)(2,1)}, bf16[128,2048]{1,0:T(8,128)(2,1)}, f32[2,128]{1,0:T(2,128)}) custom-call(s32[1]{0:T(128)} %bitcast.6.me_ref, s32[2,128]{1,0:T(2,128)S(1)} %copy-done.62, f32[2,128]{1,0:T(2,128)S(1)} %copy-done.65, bf16[128,2048]{1,0:T(8,128)(2,1)S(1)} %copy-done.59, bf16[2,80,2048]{2,1,0:T(8,128)(2,1)S(1)} %get-tuple-element.338.refs_0_, ...), custom_call_target="tpu_custom_call" | custom-call | flops 1000 | bytes 1000 | tf_op jit(solution)/shard_map/cond/branch_2_fun/combine/pallas_call | solution.py:545
  126.4 1.8 %collective-permute-start.104 = (bf16[128,768]{1,0:T(8,128)(2,1)S(1)}, bf16[128,768]{1,0:T(8,128)(2,1)S(1)}, u32[]{:S(2)}, u32[]{:S(2)}) collective-permute-start(bf16[128,768]{1,0:T(8,128)(2,1)S(1)} %up_sum1.5), channel_id=1, source_target_pairs={{0,3},{1,2},{2,1},{3,0},{4,7},{5,6},{6,5},{7,4},{8,11},{9,10},{10,... | collective-permute-start | bytes 589832 | tf_op jit(solution)/shard_map/cond/branch_2_fun/ppermute | solution.py:572
  128.1 1.2 collective-permute-start.103
  130.3 4.9 %collective-permute-done.104.refs_1_ = bf16[128,768]{1,0:T(8,128)(2,1)S(1)} collective-permute-done((bf16[128,768]{1,0:T(8,128)(2,1)S(1)}, bf16[128,768]{1,0:T(8,128)(2,1)S(1)}, u32[]{:S(2)}, u32[]{:S(2)}) %collective-permute-start.104) | collective-permute-done | bytes 196640 | tf_op jit(solution)/shard_map/cond/branch_2_fun/ppermute | solution.py:572
  135.2 2.3 %collective-permute-done.103.refs_0_ = bf16[128,768]{1,0:T(8,128)(2,1)S(1)} collective-permute-done((bf16[128,768]{1,0:T(8,128)(2,1)S(1)}, bf16[128,768]{1,0:T(8,128)(2,1)S(1)}, u32[]{:S(2)}, u32[]{:S(2)}) %collective-permute-start.103) | collective-permute-done | bytes 196640 | tf_op jit(solution)/shard_map/cond/branch_2_fun/ppermute | solution.py:572
  (95 shorter events, 11.6 us)
Async XLA Ops:
  3.2 11.5 %collective-permute-start.70 = (bf16[80,2048]{1,0:T(8,128)(2,1)S(1)}, bf16[80,2048]{1,0:T(8,128)(2,1)S(1)}, u32[]{:S(2)}, u32[]{:S(2)}) collective-permute-start(bf16[80,2048]{1,0:T(8,128)(2,1)S(1)} %get-tuple-element.259), channel_id=1, source_target_pairs={{0,1},{1,0},{2,3},{3,2},{4,5},{5,4},{6,7},{7,6},{8,9},{9,8},{10,11... | collective-permute-start | bytes 983048 | tf_op jit(solution)/shard_map/cond/branch_2_fun/ppermute | solution.py:449
  6.2 17.7 %collective-permute-start.71 = (bf16[80,2048]{1,0:T(8,128)(2,1)S(1)}, bf16[80,2048]{1,0:T(8,128)(2,1)S(1)}, u32[]{:S(2)}, u32[]{:S(2)}) collective-permute-start(bf16[80,2048]{1,0:T(8,128)(2,1)S(1)} %get-tuple-element.260), channel_id=1, source_target_pairs={{0,2},{1,3},{2,0},{3,1},{4,6},{5,7},{6,4},{7,5},{8,10},{9,11},{10,... | collective-permute-start | bytes 983048 | tf_op jit(solution)/shard_map/cond/branch_2_fun/ppermute | solution.py:449
  7.7 16.1 %collective-permute-start.72 = (bf16[80,2048]{1,0:T(8,128)(2,1)S(1)}, bf16[80,2048]{1,0:T(8,128)(2,1)S(1)}, u32[]{:S(2)}, u32[]{:S(2)}) collective-permute-start(bf16[80,2048]{1,0:T(8,128)(2,1)S(1)} %get-tuple-element.261), channel_id=1, source_target_pairs={{0,3},{1,2},{2,1},{3,0},{4,7},{5,6},{6,5},{7,4},{8,11},{9,10},{10,... | collective-permute-start | bytes 983048 | tf_op jit(solution)/shard_map/cond/branch_2_fun/ppermute | solution.py:449
  9.5 19.7 %collective-permute-start.73 = (bf16[80,2048]{1,0:T(8,128)(2,1)S(1)}, bf16[80,2048]{1,0:T(8,128)(2,1)S(1)}, u32[]{:S(2)}, u32[]{:S(2)}) collective-permute-start(bf16[80,2048]{1,0:T(8,128)(2,1)S(1)} %get-tuple-element.266), channel_id=1, source_target_pairs={{0,1},{1,0},{2,3},{3,2},{4,5},{5,4},{6,7},{7,6},{8,9},{9,8},{10,11... | collective-permute-start | bytes 983048 | tf_op jit(solution)/shard_map/cond/branch_2_fun/ppermute | solution.py:449
  11.5 24.9 %collective-permute-start.74 = (bf16[80,2048]{1,0:T(8,128)(2,1)S(1)}, bf16[80,2048]{1,0:T(8,128)(2,1)S(1)}, u32[]{:S(2)}, u32[]{:S(2)}) collective-permute-start(bf16[80,2048]{1,0:T(8,128)(2,1)S(1)} %get-tuple-element.267), channel_id=1, source_target_pairs={{0,2},{1,3},{2,0},{3,1},{4,6},{5,7},{6,4},{7,5},{8,10},{9,11},{10,... | collective-permute-start | bytes 983048 | tf_op jit(solution)/shard_map/cond/branch_2_fun/ppermute | solution.py:449
  14.7 21.7 %collective-permute-start.75 = (bf16[80,2048]{1,0:T(8,128)(2,1)S(1)}, bf16[80,2048]{1,0:T(8,128)(2,1)S(1)}, u32[]{:S(2)}, u32[]{:S(2)}) collective-permute-start(bf16[80,2048]{1,0:T(8,128)(2,1)S(1)} %get-tuple-element.268), channel_id=1, source_target_pairs={{0,3},{1,2},{2,1},{3,0},{4,7},{5,6},{6,5},{7,4},{8,11},{9,10},{10,... | collective-permute-start | bytes 983048 | tf_op jit(solution)/shard_map/cond/branch_2_fun/ppermute | solution.py:449
  23.9 13.5 %copy-start.52 = (bf16[1,768,2048]{2,1,0:T(8,128)(2,1)S(1)}, bf16[1,768,2048]{2,1,0:T(8,128)(2,1)}, u32[]{:S(2)}) copy-start(bf16[1,768,2048]{2,1,0:T(8,128)(2,1)} %get-tuple-element.399.down_ref) | copy-start | bytes 9437188 | tf_op jit(solution)/shard_map/cond
  29.1 7.5 %collective-permute-start.76 = (bf16[320,768]{1,0:T(8,128)(2,1)S(1)}, bf16[320,768]{1,0:T(8,128)(2,1)S(1)}, u32[]{:S(2)}, u32[]{:S(2)}) collective-permute-start(bf16[320,768]{1,0:T(8,128)(2,1)S(1)} %get-tuple-element.264.act_own.act_ref), channel_id=1, source_target_pairs={{0,4},{4,0},{8,12},{12,8},{16,20},{20,16},{24,28},{28,24},{1,5},{5... | collective-permute-start | bytes 1474568 | tf_op jit(solution)/shard_map/cond/branch_2_fun/ppermute | solution.py:454
  36.5 4.2 %collective-permute-start.77 = (bf16[320,2048]{1,0:T(8,128)(2,1)S(1)}, bf16[320,2048]{1,0:T(8,128)(2,1)}, u32[]{:S(2)}, u32[]{:S(2)}) collective-permute-start(bf16[320,2048]{1,0:T(8,128)(2,1)S(1)} %join_grads.5.c_ref.c_own), channel_id=1, source_target_pairs={{0,4},{4,0},{8,12},{12,8},{16,20},{20,16},{24,28},{28,24},{1,5},{5... | collective-permute-start | bytes 3932168 | tf_op jit(solution)/shard_map/cond/branch_2_fun/ppermute | solution.py:454
  40.2 8.1 %collective-permute-start.78 = (bf16[320,2048]{1,0:T(8,128)(2,1)S(1)}, bf16[320,2048]{1,0:T(8,128)(2,1)}, u32[]{:S(2)}, u32[]{:S(2)}) collective-permute-start(bf16[320,2048]{1,0:T(8,128)(2,1)S(1)} %get-tuple-element.280.refs_0_.refs_1_.refs_2_.refs_3_), channel_id=1, source_target_pairs={{0,4},{4,0},{8,12},{12,8},{16,20},{20,16},{24,28},{28,24},{1,5},{5... | collective-permute-start | bytes 3932168 | tf_op jit(solution)/shard_map/cond/branch_2_fun/ppermute | solution.py:454
  40.7 7.6 %collective-permute-start.79 = (bf16[2,320,768]{2,1,0:T(8,128)(2,1)}, bf16[2,320,768]{2,1,0:T(8,128)(2,1)}, u32[]{:S(2)}, u32[]{:S(2)}) collective-permute-start(bf16[2,320,768]{2,1,0:T(8,128)(2,1)} %backward.5.refs_8_.grad_ref), channel_id=1, source_target_pairs={{0,4},{4,0},{8,12},{12,8},{16,20},{20,16},{24,28},{28,24},{1,5},{5... | collective-permute-start | bytes 2949128 | tf_op jit(solution)/shard_map/cond/branch_2_fun/ppermute | solution.py:454
  46.2 8.7 %copy-start.8 = (bf16[768,256]{1,0:T(8,128)(2,1)}, bf16[768,256]{1,0:T(8,128)(2,1)S(1)}, u32[]{:S(2)}) copy-start(bf16[768,256]{1,0:T(8,128)(2,1)S(1)} %get-tuple-element.315.alone_ref.inner_ref) | copy-start | bytes 1179652 | tf_op jit(solution)/shard_map/cond
  46.2 8.7 %copy-start.10 = (bf16[768,256]{1,0:T(8,128)(2,1)}, bf16[768,256]{1,0:T(8,128)(2,1)S(1)}, u32[]{:S(2)}) copy-start(bf16[768,256]{1,0:T(8,128)(2,1)S(1)} %get-tuple-element.314.right_ref.near_ref) | copy-start | bytes 1179652 | tf_op jit(solution)/shard_map/cond
  46.2 16.3 %collective-permute-start.81 = (bf16[768,256]{1,0:T(8,128)(2,1)S(1)}, bf16[768,256]{1,0:T(8,128)(2,1)S(1)}, u32[]{:S(2)}, u32[]{:S(2)}) collective-permute-start(bf16[768,256]{1,0:T(8,128)(2,1)S(1)} %get-tuple-element.290.right_ref), channel_id=1, source_target_pairs={{0,8},{4,12},{8,0},{12,4},{16,24},{20,28},{24,16},{28,20},{1,9},{5... | collective-permute-start | bytes 1179656 | tf_op jit(solution)/shard_map/cond/branch_2_fun/ppermute | solution.py:565
  47.8 18.5 %collective-permute-start.80 = (bf16[768,256]{1,0:T(8,128)(2,1)S(1)}, bf16[768,256]{1,0:T(8,128)(2,1)S(1)}, u32[]{:S(2)}, u32[]{:S(2)}) collective-permute-start(bf16[768,256]{1,0:T(8,128)(2,1)S(1)} %get-tuple-element.292.right_ref), channel_id=1, source_target_pairs={{0,8},{4,12},{8,0},{12,4},{16,24},{20,28},{24,16},{28,20},{1,9},{5... | collective-permute-start | bytes 1179656 | tf_op jit(solution)/shard_map/cond/branch_2_fun/ppermute | solution.py:565
  48.3 8.1 %copy-start.53 = (bf16[1,768,2048]{2,1,0:T(8,128)(2,1)S(1)}, bf16[1,768,2048]{2,1,0:T(8,128)(2,1)}, u32[]{:S(2)}) copy-start(bf16[1,768,2048]{2,1,0:T(8,128)(2,1)} %get-tuple-element.399.down_ref) | copy-start | bytes 9437188 | tf_op jit(solution)/shard_map/cond
  48.3 8.1 %copy-start.56 = (bf16[1,2048,768]{2,1,0:T(8,128)(2,1)S(1)}, bf16[1,2048,768]{2,1,0:T(8,128)(2,1)}, u32[]{:S(2)}) copy-start(bf16[1,2048,768]{2,1,0:T(8,128)(2,1)} %get-tuple-element.390.refs_4_.gate_ref) | copy-start | bytes 9437188 | tf_op jit(solution)/shard_map/cond
  56.4 7.1 %copy-start.34 = (bf16[256,768]{1,0:T(8,128)(2,1)}, bf16[256,768]{1,0:T(8,128)(2,1)S(1)}, u32[]{:S(2)}) copy-start(bf16[256,768]{1,0:T(8,128)(2,1)S(1)} %get-tuple-element.304.right_ref) | copy-start | bytes 1179652 | tf_op jit(solution)/shard_map/cond
  62.5 13.0 %copy-start.46 = (bf16[2,80,2048]{2,1,0:T(8,128)(2,1)}, bf16[2,80,2048]{2,1,0:T(8,128)(2,1)S(1)}, u32[]{:S(2)}) copy-start(bf16[2,80,2048]{2,1,0:T(8,128)(2,1)S(1)} %get-tuple-element.295) | copy-start | bytes 1966084 | tf_op jit(solution)/shard_map/cond
  63.5 16.1 %copy-start.9 = (bf16[768,256]{1,0:T(8,128)(2,1)S(1)}, bf16[768,256]{1,0:T(8,128)(2,1)}, u32[]{:S(2)}) copy-start(bf16[768,256]{1,0:T(8,128)(2,1)} %copy-done.8) | copy-start | bytes 1179652 | tf_op jit(solution)/shard_map/cond
  63.5 16.1 %copy-start.11 = (bf16[768,256]{1,0:T(8,128)(2,1)S(1)}, bf16[768,256]{1,0:T(8,128)(2,1)}, u32[]{:S(2)}) copy-start(bf16[768,256]{1,0:T(8,128)(2,1)} %copy-done.10) | copy-start | bytes 1179652 | tf_op jit(solution)/shard_map/cond
  63.5 12.0 %collective-permute-start.87 = (bf16[256,768]{1,0:T(8,128)(2,1)S(1)}, bf16[256,768]{1,0:T(8,128)(2,1)S(1)}, u32[]{:S(2)}, u32[]{:S(2)}) collective-permute-start(bf16[256,768]{1,0:T(8,128)(2,1)S(1)} %get-tuple-element.304.right_ref), channel_id=1, source_target_pairs={{0,8},{4,12},{8,0},{12,4},{16,24},{20,28},{24,16},{28,20},{1,9},{5... | collective-permute-start | bytes 1179656 | tf_op jit(solution)/shard_map/cond/branch_2_fun/ppermute | solution.py:565
  65.1 14.5 %collective-permute-start.86 = (bf16[768,256]{1,0:T(8,128)(2,1)}, bf16[768,256]{1,0:T(8,128)(2,1)}, u32[]{:S(2)}, u32[]{:S(2)}) collective-permute-start(bf16[768,256]{1,0:T(8,128)(2,1)} %down_mid1.5), channel_id=1, source_target_pairs={{8,16},{16,8},{12,20},{20,12},{0,4},{4,0},{24,28},{28,24},{9,17},{... | collective-permute-start | bytes 1179656 | tf_op jit(solution)/shard_map/cond/branch_2_fun/ppermute | solution.py:569
  67.1 16.9 %collective-permute-start.85 = (bf16[256,768]{1,0:T(8,128)(2,1)}, bf16[256,768]{1,0:T(8,128)(2,1)}, u32[]{:S(2)}, u32[]{:S(2)}) collective-permute-start(bf16[256,768]{1,0:T(8,128)(2,1)} %get-tuple-element.309.right_ref), channel_id=1, source_target_pairs={{0,8},{4,12},{8,0},{12,4},{16,24},{20,28},{24,16},{28,20},{1,9},{5... | collective-permute-start | bytes 1179656 | tf_op jit(solution)/shard_map/cond/branch_2_fun/ppermute | solution.py:565
  69.0 15.0 %collective-permute-start.88 = (bf16[768,256]{1,0:T(8,128)(2,1)}, bf16[768,256]{1,0:T(8,128)(2,1)}, u32[]{:S(2)}, u32[]{:S(2)}) collective-permute-start(bf16[768,256]{1,0:T(8,128)(2,1)} %down_mid2.5), channel_id=1, source_target_pairs={{8,16},{16,8},{12,20},{20,12},{0,4},{4,0},{24,28},{28,24},{9,17},{... | collective-permute-start | bytes 1179656 | tf_op jit(solution)/shard_map/cond/branch_2_fun/ppermute | solution.py:569
  69.0 19.4 %collective-permute-start.83 = (bf16[2,80,2048]{2,1,0:T(8,128)(2,1)}, bf16[2,80,2048]{2,1,0:T(8,128)(2,1)}, u32[]{:S(2)}, u32[]{:S(2)}) collective-permute-start(bf16[2,80,2048]{2,1,0:T(8,128)(2,1)} %get-tuple-element.294), channel_id=1, source_target_pairs={{0,2},{1,3},{2,0},{3,1},{4,6},{5,7},{6,4},{7,5},{8,10},{9,11},{10,... | collective-permute-start | bytes 1966088 | tf_op jit(solution)/shard_map/cond/branch_2_fun/ppermute | solution.py:594
  76.2 17.1 %collective-permute-start.82 = (bf16[2,80,2048]{2,1,0:T(8,128)(2,1)}, bf16[2,80,2048]{2,1,0:T(8,128)(2,1)}, u32[]{:S(2)}, u32[]{:S(2)}) collective-permute-start(bf16[2,80,2048]{2,1,0:T(8,128)(2,1)} %get-tuple-element.293), channel_id=1, source_target_pairs={{0,1},{1,0},{2,3},{3,2},{4,5},{5,4},{6,7},{7,6},{8,9},{9,8},{10,11... | collective-permute-start | bytes 1966088 | tf_op jit(solution)/shard_map/cond/branch_2_fun/ppermute | solution.py:594
  79.6 8.8 %copy-start.47 = (bf16[2,80,2048]{2,1,0:T(8,128)(2,1)S(1)}, bf16[2,80,2048]{2,1,0:T(8,128)(2,1)}, u32[]{:S(2)}) copy-start(bf16[2,80,2048]{2,1,0:T(8,128)(2,1)} %copy-done.46) | copy-start | bytes 1966084 | tf_op jit(solution)/shard_map/cond
  80.8 12.5 %collective-permute-start.91 = (bf16[768,256]{1,0:T(8,128)(2,1)S(1)}, bf16[768,256]{1,0:T(8,128)(2,1)S(1)}, u32[]{:S(2)}, u32[]{:S(2)}) collective-permute-start(bf16[768,256]{1,0:T(8,128)(2,1)S(1)} %down_last.5), channel_id=1, source_target_pairs={{0,8},{4,12},{8,0},{12,4},{16,24},{20,28},{24,16},{28,20},{1,9},{5... | collective-permute-start | bytes 1179656 | tf_op jit(solution)/shard_map/cond/branch_2_fun/ppermute | solution.py:565
  84.0 12.3 %collective-permute-start.90 = (bf16[256,768]{1,0:T(8,128)(2,1)S(1)}, bf16[256,768]{1,0:T(8,128)(2,1)S(1)}, u32[]{:S(2)}, u32[]{:S(2)}) collective-permute-start(bf16[256,768]{1,0:T(8,128)(2,1)S(1)} %gate_mid1.5), channel_id=1, source_target_pairs={{8,16},{16,8},{12,20},{20,12},{0,4},{4,0},{24,28},{28,24},{9,17},{... | collective-permute-start | bytes 1179656 | tf_op jit(solution)/shard_map/cond/branch_2_fun/ppermute | solution.py:569
  85.2 15.3 %collective-permute-start.89 = (bf16[256,768]{1,0:T(8,128)(2,1)S(1)}, bf16[256,768]{1,0:T(8,128)(2,1)S(1)}, u32[]{:S(2)}, u32[]{:S(2)}) collective-permute-start(bf16[256,768]{1,0:T(8,128)(2,1)S(1)} %copy-done.29), channel_id=1, source_target_pairs={{0,8},{4,12},{8,0},{12,4},{16,24},{20,28},{24,16},{28,20},{1,9},{5... | collective-permute-start | bytes 1179656 | tf_op jit(solution)/shard_map/cond/branch_2_fun/ppermute | solution.py:565
  88.5 30.3 %collective-permute-start.84 = (bf16[2,80,2048]{2,1,0:T(8,128)(2,1)S(1)}, bf16[2,80,2048]{2,1,0:T(8,128)(2,1)S(1)}, u32[]{:S(2)}, u32[]{:S(2)}) collective-permute-start(bf16[2,80,2048]{2,1,0:T(8,128)(2,1)S(1)} %copy-done.47), channel_id=1, source_target_pairs={{0,3},{1,2},{2,1},{3,0},{4,7},{5,6},{6,5},{7,4},{8,11},{9,10},{10,... | collective-permute-start | bytes 1966088 | tf_op jit(solution)/shard_map/cond/branch_2_fun/ppermute | solution.py:594
  93.3 7.4 %collective-permute-start.96 = (bf16[256,768]{1,0:T(8,128)(2,1)S(1)}, bf16[256,768]{1,0:T(8,128)(2,1)S(1)}, u32[]{:S(2)}, u32[]{:S(2)}) collective-permute-start(bf16[256,768]{1,0:T(8,128)(2,1)S(1)} %up_mid1.5), channel_id=1, source_target_pairs={{8,16},{16,8},{12,20},{20,12},{0,4},{4,0},{24,28},{28,24},{9,17},{... | collective-permute-start | bytes 1179656 | tf_op jit(solution)/shard_map/cond/branch_2_fun/ppermute | solution.py:569
  94.4 20.5 %collective-permute-start.97 = (bf16[768,256]{1,0:T(8,128)(2,1)S(1)}, bf16[768,256]{1,0:T(8,128)(2,1)S(1)}, u32[]{:S(2)}, u32[]{:S(2)}) collective-permute-start(bf16[768,256]{1,0:T(8,128)(2,1)S(1)} %down_sum.5), channel_id=1, source_target_pairs={{0,3},{1,2},{2,1},{3,0},{4,7},{5,6},{6,5},{7,4},{8,11},{9,10},{10,... | collective-permute-start | bytes 1179656 | tf_op jit(solution)/shard_map/cond/branch_2_fun/ppermute | solution.py:572
  96.3 12.6 %collective-permute-start.94 = (bf16[256,768]{1,0:T(8,128)(2,1)S(1)}, bf16[256,768]{1,0:T(8,128)(2,1)S(1)}, u32[]{:S(2)}, u32[]{:S(2)}) collective-permute-start(bf16[256,768]{1,0:T(8,128)(2,1)S(1)} %gate_last.5), channel_id=1, source_target_pairs={{0,8},{4,12},{8,0},{12,4},{16,24},{20,28},{24,16},{28,20},{1,9},{5... | collective-permute-start | bytes 1179656 | tf_op jit(solution)/shard_map/cond/branch_2_fun/ppermute | solution.py:565
  100.6 14.4 %collective-permute-start.95 = (bf16[256,768]{1,0:T(8,128)(2,1)S(1)}, bf16[256,768]{1,0:T(8,128)(2,1)S(1)}, u32[]{:S(2)}, u32[]{:S(2)}) collective-permute-start(bf16[256,768]{1,0:T(8,128)(2,1)S(1)} %gate_mid2.5), channel_id=1, source_target_pairs={{8,16},{16,8},{12,20},{20,12},{0,4},{4,0},{24,28},{28,24},{9,17},{... | collective-permute-start | bytes 1179656 | tf_op jit(solution)/shard_map/cond/branch_2_fun/ppermute | solution.py:569
  100.7 17.5 %collective-permute-start.92 = (bf16[128,768]{1,0:T(8,128)(2,1)S(1)}, bf16[128,768]{1,0:T(8,128)(2,1)S(1)}, u32[]{:S(2)}, u32[]{:S(2)}) collective-permute-start(bf16[128,768]{1,0:T(8,128)(2,1)S(1)} %get-tuple-element.337.right_ref), channel_id=1, source_target_pairs={{0,8},{4,12},{8,0},{12,4},{16,24},{20,28},{24,16},{28,20},{1,9},{5... | collective-permute-start | bytes 589832 | tf_op jit(solution)/shard_map/cond/branch_2_fun/ppermute | solution.py:565
  108.9 9.1 %collective-permute-start.93 = (bf16[128,768]{1,0:T(8,128)(2,1)S(1)}, bf16[128,768]{1,0:T(8,128)(2,1)S(1)}, u32[]{:S(2)}, u32[]{:S(2)}) collective-permute-start(bf16[128,768]{1,0:T(8,128)(2,1)S(1)} %get-tuple-element.335.right_ref), channel_id=1, source_target_pairs={{0,8},{4,12},{8,0},{12,4},{16,24},{20,28},{24,16},{28,20},{1,9},{5... | collective-permute-start | bytes 589832 | tf_op jit(solution)/shard_map/cond/branch_2_fun/ppermute | solution.py:565
  115.0 6.5 %copy-start.59 = (bf16[128,2048]{1,0:T(8,128)(2,1)S(1)}, bf16[128,2048]{1,0:T(8,128)(2,1)}, u32[]{:S(2)}) copy-start(bf16[128,2048]{1,0:T(8,128)(2,1)} %get-tuple-element.396.cot_ref) | copy-start | bytes 1572868 | tf_op jit(solution)/shard_map/cond
  115.0 6.5 %copy-start.62 = (s32[2,128]{1,0:T(2,128)S(1)}, s32[2,128]{1,0:T(2,128)}, u32[]{:S(2)}) copy-start(s32[2,128]{1,0:T(2,128)} %get-tuple-element.254.ids_ref) | copy-start | bytes 3076 | tf_op jit(solution)/shard_map/cond
  115.0 6.5 %copy-start.65 = (f32[2,128]{1,0:T(2,128)S(1)}, f32[2,128]{1,0:T(2,128)}, u32[]{:S(2)}) copy-start(f32[2,128]{1,0:T(2,128)} %get-tuple-element.255.gates_ref) | copy-start | bytes 3076 | tf_op jit(solution)/shard_map/cond
  115.1 10.8 %collective-permute-start.98 = (bf16[256,768]{1,0:T(8,128)(2,1)S(1)}, bf16[256,768]{1,0:T(8,128)(2,1)S(1)}, u32[]{:S(2)}, u32[]{:S(2)}) collective-permute-start(bf16[256,768]{1,0:T(8,128)(2,1)S(1)} %gate_sum.5), channel_id=1, source_target_pairs={{0,3},{1,2},{2,1},{3,0},{4,7},{5,6},{6,5},{7,4},{8,11},{9,10},{10,... | collective-permute-start | bytes 1179656 | tf_op jit(solution)/shard_map/cond/branch_2_fun/ppermute | solution.py:572
  116.4 9.5 %collective-permute-start.101 = (bf16[128,768]{1,0:T(8,128)(2,1)S(1)}, bf16[128,768]{1,0:T(8,128)(2,1)S(1)}, u32[]{:S(2)}, u32[]{:S(2)}) collective-permute-start(bf16[128,768]{1,0:T(8,128)(2,1)S(1)} %get-tuple-element.347), channel_id=1, source_target_pairs={{0,8},{4,12},{8,0},{12,4},{16,24},{20,28},{24,16},{28,20},{1,9},{5... | collective-permute-start | bytes 589832 | tf_op jit(solution)/shard_map/cond/branch_2_fun/ppermute | solution.py:565
  118.1 7.8 %collective-permute-start.102 = (bf16[128,768]{1,0:T(8,128)(2,1)S(1)}, bf16[128,768]{1,0:T(8,128)(2,1)S(1)}, u32[]{:S(2)}, u32[]{:S(2)}) collective-permute-start(bf16[128,768]{1,0:T(8,128)(2,1)S(1)} %up_mid20.5), channel_id=1, source_target_pairs={{8,16},{16,8},{12,20},{20,12},{0,4},{4,0},{24,28},{28,24},{9,17},{... | collective-permute-start | bytes 589832 | tf_op jit(solution)/shard_map/cond/branch_2_fun/ppermute | solution.py:569
  118.3 7.7 %collective-permute-start.100 = (bf16[128,768]{1,0:T(8,128)(2,1)S(1)}, bf16[128,768]{1,0:T(8,128)(2,1)S(1)}, u32[]{:S(2)}, u32[]{:S(2)}) collective-permute-start(bf16[128,768]{1,0:T(8,128)(2,1)S(1)} %up_mid21.5), channel_id=1, source_target_pairs={{8,16},{16,8},{12,20},{20,12},{0,4},{4,0},{24,28},{28,24},{9,17},{... | collective-permute-start | bytes 589832 | tf_op jit(solution)/shard_map/cond/branch_2_fun/ppermute | solution.py:569
  118.8 7.5 %collective-permute-start.99 = (bf16[128,768]{1,0:T(8,128)(2,1)S(1)}, bf16[128,768]{1,0:T(8,128)(2,1)S(1)}, u32[]{:S(2)}, u32[]{:S(2)}) collective-permute-start(bf16[128,768]{1,0:T(8,128)(2,1)S(1)} %get-tuple-element.346), channel_id=1, source_target_pairs={{0,8},{4,12},{8,0},{12,4},{16,24},{20,28},{24,16},{28,20},{1,9},{5... | collective-permute-start | bytes 589832 | tf_op jit(solution)/shard_map/cond/branch_2_fun/ppermute | solution.py:565
  126.4 8.8 %collective-permute-start.104 = (bf16[128,768]{1,0:T(8,128)(2,1)S(1)}, bf16[128,768]{1,0:T(8,128)(2,1)S(1)}, u32[]{:S(2)}, u32[]{:S(2)}) collective-permute-start(bf16[128,768]{1,0:T(8,128)(2,1)S(1)} %up_sum1.5), channel_id=1, source_target_pairs={{0,3},{1,2},{2,1},{3,0},{4,7},{5,6},{6,5},{7,4},{8,11},{9,10},{10,... | collective-permute-start | bytes 589832 | tf_op jit(solution)/shard_map/cond/branch_2_fun/ppermute | solution.py:572
  128.1 9.3 %collective-permute-start.103 = (bf16[128,768]{1,0:T(8,128)(2,1)S(1)}, bf16[128,768]{1,0:T(8,128)(2,1)S(1)}, u32[]{:S(2)}, u32[]{:S(2)}) collective-permute-start(bf16[128,768]{1,0:T(8,128)(2,1)S(1)} %up_sum0.5), channel_id=1, source_target_pairs={{0,3},{1,2},{2,1},{3,0},{4,7},{5,6},{6,5},{7,4},{8,11},{9,10},{10,... | collective-permute-start | bytes 589832 | tf_op jit(solution)/shard_map/cond/branch_2_fun/ppermute | solution.py:572
  (9 other events, 16.0 us)

commit v6 on v5

--- a/solution.py
+++ b/solution.py
@@ -295,18 +295,21 @@
     ]
     tile = tile_of(width, 512)
     dots = [0.0] * len(picks)
+    turned_picks = jnp.concatenate([pick.astype(F32).T for pick in picks], axis=0).astype(BF16)
+    turned_sum = sum(pick.astype(F32) for pick in picks).T.astype(BF16)
     for start in range(0, width, tile):
         cols = slice(start, start + tile)
         rows = jnp.concatenate([ref[0, :, cols] for ref in results], axis=0)
         cot = cot_ref[:, cols].astype(F32)
         mixed = 0.0
-        for k, pick in enumerate(picks):
-            picked = dot_tn(pick, rows)
+        both_ranks = dot_nn(turned_picks, rows)
+        for k in range(len(picks)):
+            picked = both_ranks[k * count : (k + 1) * count]
             mixed = mixed + weights[k] * picked
             dots[k] = dots[k] + jnp.sum(cot * picked, axis=1, keepdims=True)
         mixed_ref[:, cols] = mixed.astype(BF16)
         rows = jnp.concatenate([ref[1, :, cols] for ref in results], axis=0)
-        token_ref[:, cols] = dot_tn(sum(picks), rows).astype(BF16)
+        token_ref[:, cols] = dot_nn(turned_sum, rows).astype(BF16)
     dots_ref[...] = jnp.concatenate(
         [jnp.sum(jnp.where(eye, dot, 0.0), axis=0, keepdims=True) for dot in dots], axis=0
     )

time: 139 us -> 138 us (level); the launches traced: 139 us -> 136 us
  waiting for transfers between devices: 44 us -> 40.8 us
    ppermute x4, waiting for transfers between devices: 10.8 us -> 7.74 us  [to_mate(): return lax.ppermute(part, 'expert', [(i, i ^ turn) for i in range(groups)])]
  transfers between devices with their start and end apart: 35 -> 35, of which waited for: 13 -> 13; matrix products, arithmetic and copies ran while one was open for 0% -> 0% of each run, Pallas kernels for 27% -> 28%
where the time goes in v6:
time: 138 us; the launch traced here: 136 us
  starting transfers between devices  46 us (33%)
  waiting for transfers between devices  40.8 us (30%)
  Pallas kernels  40.7 us (29%)
  local copies, waits for them, and re-layouts  6.13 us (4%)
  between operations  1.48 us (1%)
    ppermute x11, starting transfers between devices, swap_ends(): return lax.ppermute(part, 'dp', [(i, i ^ 2) for i in range(replicas)])  23.7 us
    ppermute x6, waiting for transfers between devices, exchange(): lax.ppermute(blocks[b], 'expert', [(i, i ^ b) for i in range(groups)])  15.1 us
    ppermute x11, waiting for transfers between devices, swap_ends(): return lax.ppermute(part, 'dp', [(i, i ^ 2) for i in range(replicas)])  14.5 us
    ppermute x6, starting transfers between devices, exchange(): lax.ppermute(blocks[b], 'expert', [(i, i ^ b) for i in range(groups)])  11.1 us
    ppermute x4, waiting for transfers between devices, to_mate(): return lax.ppermute(part, 'expert', [(i, i ^ turn) for i in range(groups)])  7.74 us
    pallas_call x1, Pallas kernels, gate_up_shares(): pl.pallas_call(functools.partial(gate_up_share, count), out_shape=[jax.Sh...  6.54 us
    cond x44, local copies, waits for them, and re-layouts  6.1 us
    pallas_call x1, Pallas kernels, run_result_rows(): pl.pallas_call(functools.partial(result_rows, cap), out_shape=[jax.ShapeD...  6.09 us
  transfers between devices with their start and end apart: 35, of which 13 were waited for; matrix products, arithmetic and copies ran while one was open for 0% of the time, Pallas kernels for 28%

profile of v6, /device:TPU:0, one launch (start us, length us, event | category | flops | bytes accessed | tf_op | source)
XLA Modules:
  0.0 135.8 jit_solution(17539542035602967644)
XLA Ops:
  1.3 134.3 %conditional.1 = (bf16[128,2048]{1,0:T(8,128)(2,1)}, bf16[128,2048]{1,0:T(8,128)(2,1)}, f32[128,2]{0,1:T(2,128)}, f32[1,256,768]{2,1,0:T(8,128)}, f32[1,256,768]{2,1,0:T(8,128)}, /*index=5*/f32[1,768,256]{2,1,0:T(8,128)}) conditional(s32[]{:T(128)} %bitcast.9, (s32[2,128]{1,0:T(2,128)}, bf16[128,2048]{1,0:T(8,128)(2,1)}, ...), branch_computations={%region_0.1_spmd, %region_1.2_spmd, %region_2.3_spmd} | conditional | flops 24045 | bytes 129140488 | solution.py:429
  1.3 1.7 %place_tokens.3 = (bf16[80,2048]{1,0:T(8,128)(2,1)S(1)}, bf16[80,2048]{1,0:T(8,128)(2,1)S(1)}, bf16[80,2048]{1,0:T(8,128)(2,1)S(1)}, bf16[80,2048]{1,0:T(8,128)(2,1)S(1)}) custom-call(s32[1]{0:T(128)} %bitcast.me_ref, s32[2,128]{1,0:T(2,128)} %get-tuple-element.42.ids_ref, bf16[128,2048]{1,0:T(8,128)(2,1)} %get-tuple-element.385.tok_ref), custom_call_target="tpu_custom_call" | custom-call | tf_op jit(solution)/shard_map/cond/branch_0_fun/place_tokens/pallas_call | solution.py:470
  3.0 3.0 %collective-permute-start = (bf16[80,2048]{1,0:T(8,128)(2,1)S(1)}, bf16[80,2048]{1,0:T(8,128)(2,1)S(1)}, u32[]{:S(2)}, u32[]{:S(2)}) collective-permute-start(bf16[80,2048]{1,0:T(8,128)(2,1)S(1)} %get-tuple-element.47), channel_id=1, source_target_pairs={{0,1},{1,0},{2,3},{3,2},{4,5},{5,4},{6,7},{7,6},{8,9},{9,8},{10,11... | collective-permute-start | bytes 983048 | tf_op jit(solution)/shard_map/cond/branch_0_fun/ppermute | solution.py:452
  6.0 1.5 %collective-permute-start.1 = (bf16[80,2048]{1,0:T(8,128)(2,1)S(1)}, bf16[80,2048]{1,0:T(8,128)(2,1)S(1)}, u32[]{:S(2)}, u32[]{:S(2)}) collective-permute-start(bf16[80,2048]{1,0:T(8,128)(2,1)S(1)} %get-tuple-element.48), channel_id=1, source_target_pairs={{0,2},{1,3},{2,0},{3,1},{4,6},{5,7},{6,4},{7,5},{8,10},{9,11},{10,... | collective-permute-start | bytes 983048 | tf_op jit(solution)/shard_map/cond/branch_0_fun/ppermute | solution.py:452
  7.5 1.7 %place_grads.3 = (bf16[80,2048]{1,0:T(8,128)(2,1)S(1)}, bf16[80,2048]{1,0:T(8,128)(2,1)S(1)}, bf16[80,2048]{1,0:T(8,128)(2,1)S(1)}, bf16[80,2048]{1,0:T(8,128)(2,1)S(1)}) custom-call(s32[1]{0:T(128)} %bitcast.me_ref, s32[2,128]{1,0:T(2,128)} %get-tuple-element.42.ids_ref, f32[2,128]{1,0:T(2,128)} %get-tuple-element.43.gates_ref, ...), custom_call_target="tpu_custom_call" | custom-call | tf_op jit(solution)/shard_map/cond/branch_0_fun/place_grads/pallas_call | solution.py:478
  9.3 2.0 %collective-permute-start.3 = (bf16[80,2048]{1,0:T(8,128)(2,1)S(1)}, bf16[80,2048]{1,0:T(8,128)(2,1)S(1)}, u32[]{:S(2)}, u32[]{:S(2)}) collective-permute-start(bf16[80,2048]{1,0:T(8,128)(2,1)S(1)} %get-tuple-element.54), channel_id=1, source_target_pairs={{0,1},{1,0},{2,3},{3,2},{4,5},{5,4},{6,7},{7,6},{8,9},{9,8},{10,11... | collective-permute-start | bytes 983048 | tf_op jit(solution)/shard_map/cond/branch_0_fun/ppermute | solution.py:452
  11.3 1.5 %collective-permute-start.4 = (bf16[80,2048]{1,0:T(8,128)(2,1)S(1)}, bf16[80,2048]{1,0:T(8,128)(2,1)S(1)}, u32[]{:S(2)}, u32[]{:S(2)}) collective-permute-start(bf16[80,2048]{1,0:T(8,128)(2,1)S(1)} %get-tuple-element.55), channel_id=1, source_target_pairs={{0,2},{1,3},{2,0},{3,1},{4,6},{5,7},{6,4},{7,5},{8,10},{9,11},{10,... | collective-permute-start | bytes 983048 | tf_op jit(solution)/shard_map/cond/branch_0_fun/ppermute | solution.py:452
  12.8 1.7 %collective-permute-done.refs_1_ = bf16[80,2048]{1,0:T(8,128)(2,1)S(1)} collective-permute-done((bf16[80,2048]{1,0:T(8,128)(2,1)S(1)}, bf16[80,2048]{1,0:T(8,128)(2,1)S(1)}, u32[]{:S(2)}, u32[]{:S(2)}) %collective-permute-start) | collective-permute-done | bytes 327712 | tf_op jit(solution)/shard_map/cond/branch_0_fun/ppermute | solution.py:452
  14.5 3.0 %collective-permute-start.5 = (bf16[80,2048]{1,0:T(8,128)(2,1)S(1)}, bf16[80,2048]{1,0:T(8,128)(2,1)S(1)}, u32[]{:S(2)}, u32[]{:S(2)}) collective-permute-start(bf16[80,2048]{1,0:T(8,128)(2,1)S(1)} %get-tuple-element.56), channel_id=1, source_target_pairs={{0,3},{1,2},{2,1},{3,0},{4,7},{5,6},{6,5},{7,4},{8,11},{9,10},{10,... | collective-permute-start | bytes 983048 | tf_op jit(solution)/shard_map/cond/branch_0_fun/ppermute | solution.py:452
  17.6 6.1 %collective-permute-done.1.refs_2_ = bf16[80,2048]{1,0:T(8,128)(2,1)S(1)} collective-permute-done((bf16[80,2048]{1,0:T(8,128)(2,1)S(1)}, bf16[80,2048]{1,0:T(8,128)(2,1)S(1)}, u32[]{:S(2)}, u32[]{:S(2)}) %collective-permute-start.1) | collective-permute-done | bytes 327712 | tf_op jit(solution)/shard_map/cond/branch_0_fun/ppermute | solution.py:452
  23.7 5.2 %forward.3 = (bf16[320,2048]{1,0:T(8,128)(2,1)S(1)}, f32[2,320,768]{2,1,0:T(8,128)S(1)}, bf16[320,768]{1,0:T(8,128)(2,1)S(1)}) custom-call(bf16[80,2048]{1,0:T(8,128)(2,1)S(1)} %get-tuple-element.46.refs_0_, bf16[80,2048]{1,0:T(8,128)(2,1)S(1)} %collective-permute-done.refs_1_, bf16[80,2048]{1,0:T(8,128)(2,1)S(1)} %collective-permute-done.1.refs_2_, ...), custom_call_target="tpu_custom_call" | custom-call | flops 1000 | bytes 1000 | tf_op jit(solution)/shard_map/cond/branch_0_fun/forward/pallas_call | solution.py:490
  29.0 7.3 %collective-permute-done.4.refs_2_ = bf16[80,2048]{1,0:T(8,128)(2,1)S(1)} collective-permute-done((bf16[80,2048]{1,0:T(8,128)(2,1)S(1)}, bf16[80,2048]{1,0:T(8,128)(2,1)S(1)}, u32[]{:S(2)}, u32[]{:S(2)}) %collective-permute-start.4) | collective-permute-done | bytes 327712 | tf_op jit(solution)/shard_map/cond/branch_0_fun/ppermute | solution.py:452
  37.2 2.8 %backward.3.refs_8_.grad_ref = bf16[2,320,768]{2,1,0:T(8,128)(2,1)} custom-call(bf16[320,2048]{1,0:T(8,128)(2,1)S(1)} %join_grads.3.c_ref.c_own, bf16[1,768,2048]{2,1,0:T(8,128)(2,1)S(1)} %copy-done.48, f32[2,320,768]{2,1,0:T(8,128)S(1)} %get-tuple-element.63.pre_ref), custom_call_target="tpu_custom_call" | custom-call | flops 1000 | bytes 1000 | tf_op jit(solution)/shard_map/cond/branch_0_fun/backward/pallas_call | solution.py:514
  40.5 1.0 copy-done.13
  41.5 4.4 %down_shares.3 = (bf16[768,256]{1,0:T(8,128)(2,1)S(1)}, bf16[768,256]{1,0:T(8,128)(2,1)S(1)}, bf16[768,256]{1,0:T(8,128)(2,1)S(1)}, bf16[768,256]{1,0:T(8,128)(2,1)S(1)}) custom-call(s32[4]{0:T(128)S(1)} %fusion.1.order_ref, bf16[320,768]{1,0:T(8,128)(2,1)S(1)} %get-tuple-element.52.act_own.act_ref, bf16[320,768]{1,0:T(8,128)(2,1)S(1)} %copy-done.13, ...), custom_call_target="tpu_custom_call" | custom-call | flops 1000 | bytes 1000 | tf_op jit(solution)/shard_map/cond/branch_0_fun/down_shares/pallas_call | solution.py:332
  46.0 1.6 %collective-permute-start.11 = (bf16[768,256]{1,0:T(8,128)(2,1)S(1)}, bf16[768,256]{1,0:T(8,128)(2,1)S(1)}, u32[]{:S(2)}, u32[]{:S(2)}) collective-permute-start(bf16[768,256]{1,0:T(8,128)(2,1)S(1)} %get-tuple-element.78.right_ref), channel_id=1, source_target_pairs={{0,8},{4,12},{8,0},{12,4},{16,24},{20,28},{24,16},{28,20},{1,9},{5... | collective-permute-start | bytes 1179656 | tf_op jit(solution)/shard_map/cond/branch_0_fun/ppermute | solution.py:568
  48.1 6.5 %gate_up_shares.3 = (bf16[256,768]{1,0:T(8,128)(2,1)S(1)}, bf16[256,768]{1,0:T(8,128)(2,1)S(1)}, bf16[256,768]{1,0:T(8,128)(2,1)S(1)}, bf16[256,768]{1,0:T(8,128...) custom-call(s32[4]{0:T(128)S(1)} %fusion.1.order_ref, ...), custom_call_target="tpu_custom_call" | custom-call | flops 1000 | bytes 1000 | tf_op jit(solution)/shard_map/cond/branch_0_fun/gate_up_shares/pallas_call | solution.py:356
  56.2 6.1 %result_rows.3 = (bf16[2,80,2048]{2,1,0:T(8,128)(2,1)S(1)}, bf16[2,80,2048]{2,1,0:T(8,128)(2,1)}, bf16[2,80,2048]{2,1,0:T(8,128)(2,1)}, bf16[2,80,2048]{2,1,0:T(8,128)(2,1)S(1)}) custom-call(bf16[320,768]{1,0:T(8,128)(2,1)S(1)} %get-tuple-element.52.act_own.act_ref, bf16[2,320,768]{2,1,0:T(8,128)(2,1)} %backward.3.refs_8_.grad_ref, ...), custom_call_target="tpu_custom_call" | custom-call | flops 1000 | bytes 1000 | tf_op jit(solution)/shard_map/cond/branch_0_fun/result_rows/pallas_call | solution.py:530
  62.3 1.0 down_mid1.3
  63.3 1.6 %collective-permute-start.17 = (bf16[256,768]{1,0:T(8,128)(2,1)S(1)}, bf16[256,768]{1,0:T(8,128)(2,1)S(1)}, u32[]{:S(2)}, u32[]{:S(2)}) collective-permute-start(bf16[256,768]{1,0:T(8,128)(2,1)S(1)} %get-tuple-element.92.right_ref), channel_id=1, source_target_pairs={{0,8},{4,12},{8,0},{12,4},{16,24},{20,28},{24,16},{28,20},{1,9},{5... | collective-permute-start | bytes 1179656 | tf_op jit(solution)/shard_map/cond/branch_0_fun/ppermute | solution.py:568
  64.9 1.2 collective-permute-done.10.left_ref
  66.9 1.9 %collective-permute-start.15 = (bf16[256,768]{1,0:T(8,128)(2,1)}, bf16[256,768]{1,0:T(8,128)(2,1)}, u32[]{:S(2)}, u32[]{:S(2)}) collective-permute-start(bf16[256,768]{1,0:T(8,128)(2,1)} %get-tuple-element.97.right_ref), channel_id=1, source_target_pairs={{0,8},{4,12},{8,0},{12,4},{16,24},{20,28},{24,16},{28,20},{1,9},{5... | collective-permute-start | bytes 1179656 | tf_op jit(solution)/shard_map/cond/branch_0_fun/ppermute | solution.py:568
  68.8 1.5 %collective-permute-start.13 = (bf16[2,80,2048]{2,1,0:T(8,128)(2,1)}, bf16[2,80,2048]{2,1,0:T(8,128)(2,1)}, u32[]{:S(2)}, u32[]{:S(2)}) collective-permute-start(bf16[2,80,2048]{2,1,0:T(8,128)(2,1)} %get-tuple-element.82), channel_id=1, source_target_pairs={{0,2},{1,3},{2,0},{3,1},{4,6},{5,7},{6,4},{7,5},{8,10},{9,11},{10,... | collective-permute-start | bytes 1966088 | tf_op jit(solution)/shard_map/cond/branch_0_fun/ppermute | solution.py:597
  70.4 4.9 %collective-permute-done.17.left_ref = bf16[256,768]{1,0:T(8,128)(2,1)S(1)} collective-permute-done((bf16[256,768]{1,0:T(8,128)(2,1)S(1)}, bf16[256,768]{1,0:T(8,128)(2,1)S(1)}, u32[]{:S(2)}, u32[]{:S(2)}) %collective-permute-start.17) | collective-permute-done | bytes 393248 | tf_op jit(solution)/shard_map/cond/branch_0_fun/ppermute | solution.py:568
  76.0 1.3 collective-permute-start.12
  79.4 1.1 down_last.3
  80.6 1.7 %collective-permute-start.21 = (bf16[768,256]{1,0:T(8,128)(2,1)S(1)}, bf16[768,256]{1,0:T(8,128)(2,1)S(1)}, u32[]{:S(2)}, u32[]{:S(2)}) collective-permute-start(bf16[768,256]{1,0:T(8,128)(2,1)S(1)} %down_last.3), channel_id=1, source_target_pairs={{0,8},{4,12},{8,0},{12,4},{16,24},{20,28},{24,16},{28,20},{1,9},{5... | collective-permute-start | bytes 1179656 | tf_op jit(solution)/shard_map/cond/branch_0_fun/ppermute | solution.py:568
  82.3 1.5 %collective-permute-done.15.left_ref = bf16[256,768]{1,0:T(8,128)(2,1)} collective-permute-done((bf16[256,768]{1,0:T(8,128)(2,1)}, bf16[256,768]{1,0:T(8,128)(2,1)}, u32[]{:S(2)}, u32[]{:S(2)}) %collective-permute-start.15) | collective-permute-done | bytes 393248 | tf_op jit(solution)/shard_map/cond/branch_0_fun/ppermute | solution.py:568
  83.8 1.2 up_mid1.3
  85.0 3.2 %collective-permute-start.19 = (bf16[256,768]{1,0:T(8,128)(2,1)S(1)}, bf16[256,768]{1,0:T(8,128)(2,1)S(1)}, u32[]{:S(2)}, u32[]{:S(2)}) collective-permute-start(bf16[256,768]{1,0:T(8,128)(2,1)S(1)} %copy-done.25), channel_id=1, source_target_pairs={{0,8},{4,12},{8,0},{12,4},{16,24},{20,28},{24,16},{28,20},{1,9},{5... | collective-permute-start | bytes 1179656 | tf_op jit(solution)/shard_map/cond/branch_0_fun/ppermute | solution.py:568
  88.3 1.5 %collective-permute-start.14 = (bf16[2,80,2048]{2,1,0:T(8,128)(2,1)S(1)}, bf16[2,80,2048]{2,1,0:T(8,128)(2,1)S(1)}, u32[]{:S(2)}, u32[]{:S(2)}) collective-permute-start(bf16[2,80,2048]{2,1,0:T(8,128)(2,1)S(1)} %copy-done.43), channel_id=1, source_target_pairs={{0,3},{1,2},{2,1},{3,0},{4,7},{5,6},{6,5},{7,4},{8,11},{9,10},{10,... | collective-permute-start | bytes 1966088 | tf_op jit(solution)/shard_map/cond/branch_0_fun/ppermute | solution.py:597
  89.7 3.4 %collective-permute-done.12.refs_1_ = bf16[2,80,2048]{2,1,0:T(8,128)(2,1)} collective-permute-done((bf16[2,80,2048]{2,1,0:T(8,128)(2,1)}, bf16[2,80,2048]{2,1,0:T(8,128)(2,1)}, u32[]{:S(2)}, u32[]{:S(2)}) %collective-permute-start.12) | collective-permute-done | bytes 655392 | tf_op jit(solution)/shard_map/cond/branch_0_fun/ppermute | solution.py:597
  93.1 1.1 down_sum.3
  94.2 2.1 %collective-permute-start.27 = (bf16[768,256]{1,0:T(8,128)(2,1)S(1)}, bf16[768,256]{1,0:T(8,128)(2,1)S(1)}, u32[]{:S(2)}, u32[]{:S(2)}) collective-permute-start(bf16[768,256]{1,0:T(8,128)(2,1)S(1)} %down_sum.3), channel_id=1, source_target_pairs={{0,1},{1,0},{2,3},{3,2},{4,5},{5,4},{6,7},{7,6},{8,9},{9,8},{10,11... | collective-permute-start | bytes 1179656 | tf_op jit(solution)/shard_map/cond/branch_0_fun/ppermute | solution.py:575
  96.4 2.5 %collective-permute-start.24 = (bf16[256,768]{1,0:T(8,128)(2,1)S(1)}, bf16[256,768]{1,0:T(8,128)(2,1)S(1)}, u32[]{:S(2)}, u32[]{:S(2)}) collective-permute-start(bf16[256,768]{1,0:T(8,128)(2,1)S(1)} %gate_last.3), channel_id=1, source_target_pairs={{0,8},{4,12},{8,0},{12,4},{16,24},{20,28},{24,16},{28,20},{1,9},{5... | collective-permute-start | bytes 1179656 | tf_op jit(solution)/shard_map/cond/branch_0_fun/ppermute | solution.py:568
  98.9 1.4 %collective-permute-done.19.left_ref = bf16[256,768]{1,0:T(8,128)(2,1)S(1)} collective-permute-done((bf16[256,768]{1,0:T(8,128)(2,1)S(1)}, bf16[256,768]{1,0:T(8,128)(2,1)S(1)}, u32[]{:S(2)}, u32[]{:S(2)}) %collective-permute-start.19) | collective-permute-done | bytes 393248 | tf_op jit(solution)/shard_map/cond/branch_0_fun/ppermute | solution.py:568
  100.5 3.2 %collective-permute-start.22 = (bf16[128,768]{1,0:T(8,128)(2,1)S(1)}, bf16[128,768]{1,0:T(8,128)(2,1)S(1)}, u32[]{:S(2)}, u32[]{:S(2)}) collective-permute-start(bf16[128,768]{1,0:T(8,128)(2,1)S(1)} %get-tuple-element.125.right_ref), channel_id=1, source_target_pairs={{0,8},{4,12},{8,0},{12,4},{16,24},{20,28},{24,16},{28,20},{1,9},{5... | collective-permute-start | bytes 589832 | tf_op jit(solution)/shard_map/cond/branch_0_fun/ppermute | solution.py:568
  103.7 5.1 %collective-permute-done.24.last_ref = bf16[256,768]{1,0:T(8,128)(2,1)S(1)} collective-permute-done((bf16[256,768]{1,0:T(8,128)(2,1)S(1)}, bf16[256,768]{1,0:T(8,128)(2,1)S(1)}, u32[]{:S(2)}, u32[]{:S(2)}) %collective-permute-start.24) | collective-permute-done | bytes 393248 | tf_op jit(solution)/shard_map/cond/branch_0_fun/ppermute | solution.py:568
  108.8 2.3 %collective-permute-start.23 = (bf16[128,768]{1,0:T(8,128)(2,1)S(1)}, bf16[128,768]{1,0:T(8,128)(2,1)S(1)}, u32[]{:S(2)}, u32[]{:S(2)}) collective-permute-start(bf16[128,768]{1,0:T(8,128)(2,1)S(1)} %get-tuple-element.123.right_ref), channel_id=1, source_target_pairs={{0,8},{4,12},{8,0},{12,4},{16,24},{20,28},{24,16},{28,20},{1,9},{5... | collective-permute-start | bytes 589832 | tf_op jit(solution)/shard_map/cond/branch_0_fun/ppermute | solution.py:568
  111.2 2.6 %collective-permute-done.27.refs_0_ = bf16[768,256]{1,0:T(8,128)(2,1)S(1)} collective-permute-done((bf16[768,256]{1,0:T(8,128)(2,1)S(1)}, bf16[768,256]{1,0:T(8,128)(2,1)S(1)}, u32[]{:S(2)}, u32[]{:S(2)}) %collective-permute-start.27) | collective-permute-done | bytes 393248 | tf_op jit(solution)/shard_map/cond/branch_0_fun/ppermute | solution.py:575
  114.0 1.3 collective-permute-start.28
  115.3 1.6 %collective-permute-start.31 = (bf16[128,768]{1,0:T(8,128)(2,1)S(1)}, bf16[128,768]{1,0:T(8,128)(2,1)S(1)}, u32[]{:S(2)}, u32[]{:S(2)}) collective-permute-start(bf16[128,768]{1,0:T(8,128)(2,1)S(1)} %get-tuple-element.135), channel_id=1, source_target_pairs={{0,8},{4,12},{8,0},{12,4},{16,24},{20,28},{24,16},{28,20},{1,9},{5... | collective-permute-start | bytes 589832 | tf_op jit(solution)/shard_map/cond/branch_0_fun/ppermute | solution.py:568
  118.0 3.6 %collective-permute-start.29 = (bf16[128,768]{1,0:T(8,128)(2,1)S(1)}, bf16[128,768]{1,0:T(8,128)(2,1)S(1)}, u32[]{:S(2)}, u32[]{:S(2)}) collective-permute-start(bf16[128,768]{1,0:T(8,128)(2,1)S(1)} %get-tuple-element.134), channel_id=1, source_target_pairs={{0,8},{4,12},{8,0},{12,4},{16,24},{20,28},{24,16},{28,20},{1,9},{5... | collective-permute-start | bytes 589832 | tf_op jit(solution)/shard_map/cond/branch_0_fun/ppermute | solution.py:568
  121.6 3.5 %combine.3 = (bf16[128,2048]{1,0:T(8,128)(2,1)}, bf16[128,2048]{1,0:T(8,128)(2,1)}, f32[2,128]{1,0:T(2,128)}) custom-call(s32[1]{0:T(128)} %bitcast.me_ref, s32[2,128]{1,0:T(2,128)S(1)} %copy-done.60, f32[2,128]{1,0:T(2,128)S(1)} %copy-done.63, bf16[128,2048]{1,0:T(8,128)(2,1)S(1)} %copy-done.57, bf16[2,80,2048]{2,1,0:T(8,128)(2,1)S(1)} %get-tuple-element.126.refs_0_, ...), custom_call_target="tpu_custom_call" | custom-call | flops 1000 | bytes 1000 | tf_op jit(solution)/shard_map/cond/branch_0_fun/combine/pallas_call | solution.py:548
  126.2 1.1 collective-permute-start.34
  127.3 1.0 collective-permute-start.33
  129.3 3.0 %collective-permute-done.34.refs_1_ = bf16[128,768]{1,0:T(8,128)(2,1)S(1)} collective-permute-done((bf16[128,768]{1,0:T(8,128)(2,1)S(1)}, bf16[128,768]{1,0:T(8,128)(2,1)S(1)}, u32[]{:S(2)}, u32[]{:S(2)}) %collective-permute-start.34) | collective-permute-done | bytes 196640 | tf_op jit(solution)/shard_map/cond/branch_0_fun/ppermute | solution.py:575
  132.3 2.1 %collective-permute-done.33.refs_0_ = bf16[128,768]{1,0:T(8,128)(2,1)S(1)} collective-permute-done((bf16[128,768]{1,0:T(8,128)(2,1)S(1)}, bf16[128,768]{1,0:T(8,128)(2,1)S(1)}, u32[]{:S(2)}, u32[]{:S(2)}) %collective-permute-start.33) | collective-permute-done | bytes 196640 | tf_op jit(solution)/shard_map/cond/branch_0_fun/ppermute | solution.py:575
  (95 shorter events, 11.7 us)
Async XLA Ops:
  3.0 11.5 %collective-permute-start = (bf16[80,2048]{1,0:T(8,128)(2,1)S(1)}, bf16[80,2048]{1,0:T(8,128)(2,1)S(1)}, u32[]{:S(2)}, u32[]{:S(2)}) collective-permute-start(bf16[80,2048]{1,0:T(8,128)(2,1)S(1)} %get-tuple-element.47), channel_id=1, source_target_pairs={{0,1},{1,0},{2,3},{3,2},{4,5},{5,4},{6,7},{7,6},{8,9},{9,8},{10,11... | collective-permute-start | bytes 983048 | tf_op jit(solution)/shard_map/cond/branch_0_fun/ppermute | solution.py:452
  6.0 17.7 %collective-permute-start.1 = (bf16[80,2048]{1,0:T(8,128)(2,1)S(1)}, bf16[80,2048]{1,0:T(8,128)(2,1)S(1)}, u32[]{:S(2)}, u32[]{:S(2)}) collective-permute-start(bf16[80,2048]{1,0:T(8,128)(2,1)S(1)} %get-tuple-element.48), channel_id=1, source_target_pairs={{0,2},{1,3},{2,0},{3,1},{4,6},{5,7},{6,4},{7,5},{8,10},{9,11},{10,... | collective-permute-start | bytes 983048 | tf_op jit(solution)/shard_map/cond/branch_0_fun/ppermute | solution.py:452
  7.5 16.1 %collective-permute-start.2 = (bf16[80,2048]{1,0:T(8,128)(2,1)S(1)}, bf16[80,2048]{1,0:T(8,128)(2,1)S(1)}, u32[]{:S(2)}, u32[]{:S(2)}) collective-permute-start(bf16[80,2048]{1,0:T(8,128)(2,1)S(1)} %get-tuple-element.49), channel_id=1, source_target_pairs={{0,3},{1,2},{2,1},{3,0},{4,7},{5,6},{6,5},{7,4},{8,11},{9,10},{10,... | collective-permute-start | bytes 983048 | tf_op jit(solution)/shard_map/cond/branch_0_fun/ppermute | solution.py:452
  9.3 19.7 %collective-permute-start.3 = (bf16[80,2048]{1,0:T(8,128)(2,1)S(1)}, bf16[80,2048]{1,0:T(8,128)(2,1)S(1)}, u32[]{:S(2)}, u32[]{:S(2)}) collective-permute-start(bf16[80,2048]{1,0:T(8,128)(2,1)S(1)} %get-tuple-element.54), channel_id=1, source_target_pairs={{0,1},{1,0},{2,3},{3,2},{4,5},{5,4},{6,7},{7,6},{8,9},{9,8},{10,11... | collective-permute-start | bytes 983048 | tf_op jit(solution)/shard_map/cond/branch_0_fun/ppermute | solution.py:452
  11.3 25.0 %collective-permute-start.4 = (bf16[80,2048]{1,0:T(8,128)(2,1)S(1)}, bf16[80,2048]{1,0:T(8,128)(2,1)S(1)}, u32[]{:S(2)}, u32[]{:S(2)}) collective-permute-start(bf16[80,2048]{1,0:T(8,128)(2,1)S(1)} %get-tuple-element.55), channel_id=1, source_target_pairs={{0,2},{1,3},{2,0},{3,1},{4,6},{5,7},{6,4},{7,5},{8,10},{9,11},{10,... | collective-permute-start | bytes 983048 | tf_op jit(solution)/shard_map/cond/branch_0_fun/ppermute | solution.py:452
  14.5 21.7 %collective-permute-start.5 = (bf16[80,2048]{1,0:T(8,128)(2,1)S(1)}, bf16[80,2048]{1,0:T(8,128)(2,1)S(1)}, u32[]{:S(2)}, u32[]{:S(2)}) collective-permute-start(bf16[80,2048]{1,0:T(8,128)(2,1)S(1)} %get-tuple-element.56), channel_id=1, source_target_pairs={{0,3},{1,2},{2,1},{3,0},{4,7},{5,6},{6,5},{7,4},{8,11},{9,10},{10,... | collective-permute-start | bytes 983048 | tf_op jit(solution)/shard_map/cond/branch_0_fun/ppermute | solution.py:452
  23.7 13.5 %copy-start.48 = (bf16[1,768,2048]{2,1,0:T(8,128)(2,1)S(1)}, bf16[1,768,2048]{2,1,0:T(8,128)(2,1)}, u32[]{:S(2)}) copy-start(bf16[1,768,2048]{2,1,0:T(8,128)(2,1)} %get-tuple-element.397.down_ref) | copy-start | bytes 9437188 | tf_op jit(solution)/shard_map/cond
  28.9 7.5 %collective-permute-start.6 = (bf16[320,768]{1,0:T(8,128)(2,1)S(1)}, bf16[320,768]{1,0:T(8,128)(2,1)S(1)}, u32[]{:S(2)}, u32[]{:S(2)}) collective-permute-start(bf16[320,768]{1,0:T(8,128)(2,1)S(1)} %get-tuple-element.52.act_own.act_ref), channel_id=1, source_target_pairs={{0,4},{4,0},{8,12},{12,8},{16,20},{20,16},{24,28},{28,24},{1,5},{5... | collective-permute-start | bytes 1474568 | tf_op jit(solution)/shard_map/cond/branch_0_fun/ppermute | solution.py:457
  36.3 4.2 %collective-permute-start.7 = (bf16[320,2048]{1,0:T(8,128)(2,1)S(1)}, bf16[320,2048]{1,0:T(8,128)(2,1)}, u32[]{:S(2)}, u32[]{:S(2)}) collective-permute-start(bf16[320,2048]{1,0:T(8,128)(2,1)S(1)} %join_grads.3.c_ref.c_own), channel_id=1, source_target_pairs={{0,4},{4,0},{8,12},{12,8},{16,20},{20,16},{24,28},{28,24},{1,5},{5... | collective-permute-start | bytes 3932168 | tf_op jit(solution)/shard_map/cond/branch_0_fun/ppermute | solution.py:457
  40.0 8.1 %collective-permute-start.8 = (bf16[320,2048]{1,0:T(8,128)(2,1)S(1)}, bf16[320,2048]{1,0:T(8,128)(2,1)}, u32[]{:S(2)}, u32[]{:S(2)}) collective-permute-start(bf16[320,2048]{1,0:T(8,128)(2,1)S(1)} %get-tuple-element.68.refs_0_.refs_1_.refs_2_.refs_3_), channel_id=1, source_target_pairs={{0,4},{4,0},{8,12},{12,8},{16,20},{20,16},{24,28},{28,24},{1,5},{5... | collective-permute-start | bytes 3932168 | tf_op jit(solution)/shard_map/cond/branch_0_fun/ppermute | solution.py:457
  40.5 7.6 %collective-permute-start.9 = (bf16[2,320,768]{2,1,0:T(8,128)(2,1)}, bf16[2,320,768]{2,1,0:T(8,128)(2,1)}, u32[]{:S(2)}, u32[]{:S(2)}) collective-permute-start(bf16[2,320,768]{2,1,0:T(8,128)(2,1)} %backward.3.refs_8_.grad_ref), channel_id=1, source_target_pairs={{0,4},{4,0},{8,12},{12,8},{16,20},{20,16},{24,28},{28,24},{1,5},{5... | collective-permute-start | bytes 2949128 | tf_op jit(solution)/shard_map/cond/branch_0_fun/ppermute | solution.py:457
  46.0 8.7 %copy-start = (bf16[768,256]{1,0:T(8,128)(2,1)}, bf16[768,256]{1,0:T(8,128)(2,1)S(1)}, u32[]{:S(2)}) copy-start(bf16[768,256]{1,0:T(8,128)(2,1)S(1)} %get-tuple-element.103.alone_ref.inner_ref) | copy-start | bytes 1179652 | tf_op jit(solution)/shard_map/cond
  46.0 8.7 %copy-start.2 = (bf16[768,256]{1,0:T(8,128)(2,1)}, bf16[768,256]{1,0:T(8,128)(2,1)S(1)}, u32[]{:S(2)}) copy-start(bf16[768,256]{1,0:T(8,128)(2,1)S(1)} %get-tuple-element.102.right_ref.near_ref) | copy-start | bytes 1179652 | tf_op jit(solution)/shard_map/cond
  46.0 16.3 %collective-permute-start.11 = (bf16[768,256]{1,0:T(8,128)(2,1)S(1)}, bf16[768,256]{1,0:T(8,128)(2,1)S(1)}, u32[]{:S(2)}, u32[]{:S(2)}) collective-permute-start(bf16[768,256]{1,0:T(8,128)(2,1)S(1)} %get-tuple-element.78.right_ref), channel_id=1, source_target_pairs={{0,8},{4,12},{8,0},{12,4},{16,24},{20,28},{24,16},{28,20},{1,9},{5... | collective-permute-start | bytes 1179656 | tf_op jit(solution)/shard_map/cond/branch_0_fun/ppermute | solution.py:568
  47.6 18.5 %collective-permute-start.10 = (bf16[768,256]{1,0:T(8,128)(2,1)S(1)}, bf16[768,256]{1,0:T(8,128)(2,1)S(1)}, u32[]{:S(2)}, u32[]{:S(2)}) collective-permute-start(bf16[768,256]{1,0:T(8,128)(2,1)S(1)} %get-tuple-element.80.right_ref), channel_id=1, source_target_pairs={{0,8},{4,12},{8,0},{12,4},{16,24},{20,28},{24,16},{28,20},{1,9},{5... | collective-permute-start | bytes 1179656 | tf_op jit(solution)/shard_map/cond/branch_0_fun/ppermute | solution.py:568
  48.1 8.1 %copy-start.49 = (bf16[1,768,2048]{2,1,0:T(8,128)(2,1)S(1)}, bf16[1,768,2048]{2,1,0:T(8,128)(2,1)}, u32[]{:S(2)}) copy-start(bf16[1,768,2048]{2,1,0:T(8,128)(2,1)} %get-tuple-element.397.down_ref) | copy-start | bytes 9437188 | tf_op jit(solution)/shard_map/cond
  48.1 8.1 %copy-start.54 = (bf16[1,2048,768]{2,1,0:T(8,128)(2,1)S(1)}, bf16[1,2048,768]{2,1,0:T(8,128)(2,1)}, u32[]{:S(2)}) copy-start(bf16[1,2048,768]{2,1,0:T(8,128)(2,1)} %get-tuple-element.388.refs_4_.gate_ref) | copy-start | bytes 9437188 | tf_op jit(solution)/shard_map/cond
  56.2 7.1 %copy-start.30 = (bf16[256,768]{1,0:T(8,128)(2,1)}, bf16[256,768]{1,0:T(8,128)(2,1)S(1)}, u32[]{:S(2)}) copy-start(bf16[256,768]{1,0:T(8,128)(2,1)S(1)} %get-tuple-element.92.right_ref) | copy-start | bytes 1179652 | tf_op jit(solution)/shard_map/cond
  62.3 13.0 %copy-start.42 = (bf16[2,80,2048]{2,1,0:T(8,128)(2,1)}, bf16[2,80,2048]{2,1,0:T(8,128)(2,1)S(1)}, u32[]{:S(2)}) copy-start(bf16[2,80,2048]{2,1,0:T(8,128)(2,1)S(1)} %get-tuple-element.83) | copy-start | bytes 1966084 | tf_op jit(solution)/shard_map/cond
  63.3 16.1 %copy-start.1 = (bf16[768,256]{1,0:T(8,128)(2,1)S(1)}, bf16[768,256]{1,0:T(8,128)(2,1)}, u32[]{:S(2)}) copy-start(bf16[768,256]{1,0:T(8,128)(2,1)} %copy-done) | copy-start | bytes 1179652 | tf_op jit(solution)/shard_map/cond
  63.3 16.1 %copy-start.3 = (bf16[768,256]{1,0:T(8,128)(2,1)S(1)}, bf16[768,256]{1,0:T(8,128)(2,1)}, u32[]{:S(2)}) copy-start(bf16[768,256]{1,0:T(8,128)(2,1)} %copy-done.2) | copy-start | bytes 1179652 | tf_op jit(solution)/shard_map/cond
  63.3 12.0 %collective-permute-start.17 = (bf16[256,768]{1,0:T(8,128)(2,1)S(1)}, bf16[256,768]{1,0:T(8,128)(2,1)S(1)}, u32[]{:S(2)}, u32[]{:S(2)}) collective-permute-start(bf16[256,768]{1,0:T(8,128)(2,1)S(1)} %get-tuple-element.92.right_ref), channel_id=1, source_target_pairs={{0,8},{4,12},{8,0},{12,4},{16,24},{20,28},{24,16},{28,20},{1,9},{5... | collective-permute-start | bytes 1179656 | tf_op jit(solution)/shard_map/cond/branch_0_fun/ppermute | solution.py:568
  64.9 14.5 %collective-permute-start.16 = (bf16[768,256]{1,0:T(8,128)(2,1)}, bf16[768,256]{1,0:T(8,128)(2,1)}, u32[]{:S(2)}, u32[]{:S(2)}) collective-permute-start(bf16[768,256]{1,0:T(8,128)(2,1)} %down_mid1.3), channel_id=1, source_target_pairs={{8,16},{16,8},{12,20},{20,12},{0,4},{4,0},{24,28},{28,24},{9,17},{... | collective-permute-start | bytes 1179656 | tf_op jit(solution)/shard_map/cond/branch_0_fun/ppermute | solution.py:572
  66.9 16.9 %collective-permute-start.15 = (bf16[256,768]{1,0:T(8,128)(2,1)}, bf16[256,768]{1,0:T(8,128)(2,1)}, u32[]{:S(2)}, u32[]{:S(2)}) collective-permute-start(bf16[256,768]{1,0:T(8,128)(2,1)} %get-tuple-element.97.right_ref), channel_id=1, source_target_pairs={{0,8},{4,12},{8,0},{12,4},{16,24},{20,28},{24,16},{28,20},{1,9},{5... | collective-permute-start | bytes 1179656 | tf_op jit(solution)/shard_map/cond/branch_0_fun/ppermute | solution.py:568
  68.8 15.0 %collective-permute-start.18 = (bf16[768,256]{1,0:T(8,128)(2,1)}, bf16[768,256]{1,0:T(8,128)(2,1)}, u32[]{:S(2)}, u32[]{:S(2)}) collective-permute-start(bf16[768,256]{1,0:T(8,128)(2,1)} %down_mid2.3), channel_id=1, source_target_pairs={{8,16},{16,8},{12,20},{20,12},{0,4},{4,0},{24,28},{28,24},{9,17},{... | collective-permute-start | bytes 1179656 | tf_op jit(solution)/shard_map/cond/branch_0_fun/ppermute | solution.py:572
  68.8 19.4 %collective-permute-start.13 = (bf16[2,80,2048]{2,1,0:T(8,128)(2,1)}, bf16[2,80,2048]{2,1,0:T(8,128)(2,1)}, u32[]{:S(2)}, u32[]{:S(2)}) collective-permute-start(bf16[2,80,2048]{2,1,0:T(8,128)(2,1)} %get-tuple-element.82), channel_id=1, source_target_pairs={{0,2},{1,3},{2,0},{3,1},{4,6},{5,7},{6,4},{7,5},{8,10},{9,11},{10,... | collective-permute-start | bytes 1966088 | tf_op jit(solution)/shard_map/cond/branch_0_fun/ppermute | solution.py:597
  76.0 17.1 %collective-permute-start.12 = (bf16[2,80,2048]{2,1,0:T(8,128)(2,1)}, bf16[2,80,2048]{2,1,0:T(8,128)(2,1)}, u32[]{:S(2)}, u32[]{:S(2)}) collective-permute-start(bf16[2,80,2048]{2,1,0:T(8,128)(2,1)} %get-tuple-element.81), channel_id=1, source_target_pairs={{0,1},{1,0},{2,3},{3,2},{4,5},{5,4},{6,7},{7,6},{8,9},{9,8},{10,11... | collective-permute-start | bytes 1966088 | tf_op jit(solution)/shard_map/cond/branch_0_fun/ppermute | solution.py:597
  79.4 8.8 %copy-start.43 = (bf16[2,80,2048]{2,1,0:T(8,128)(2,1)S(1)}, bf16[2,80,2048]{2,1,0:T(8,128)(2,1)}, u32[]{:S(2)}) copy-start(bf16[2,80,2048]{2,1,0:T(8,128)(2,1)} %copy-done.42) | copy-start | bytes 1966084 | tf_op jit(solution)/shard_map/cond
  80.6 12.6 %collective-permute-start.21 = (bf16[768,256]{1,0:T(8,128)(2,1)S(1)}, bf16[768,256]{1,0:T(8,128)(2,1)S(1)}, u32[]{:S(2)}, u32[]{:S(2)}) collective-permute-start(bf16[768,256]{1,0:T(8,128)(2,1)S(1)} %down_last.3), channel_id=1, source_target_pairs={{0,8},{4,12},{8,0},{12,4},{16,24},{20,28},{24,16},{28,20},{1,9},{5... | collective-permute-start | bytes 1179656 | tf_op jit(solution)/shard_map/cond/branch_0_fun/ppermute | solution.py:568
  83.8 12.5 %collective-permute-start.20 = (bf16[256,768]{1,0:T(8,128)(2,1)S(1)}, bf16[256,768]{1,0:T(8,128)(2,1)S(1)}, u32[]{:S(2)}, u32[]{:S(2)}) collective-permute-start(bf16[256,768]{1,0:T(8,128)(2,1)S(1)} %gate_mid1.3), channel_id=1, source_target_pairs={{8,16},{16,8},{12,20},{20,12},{0,4},{4,0},{24,28},{28,24},{9,17},{... | collective-permute-start | bytes 1179656 | tf_op jit(solution)/shard_map/cond/branch_0_fun/ppermute | solution.py:572
  85.0 15.2 %collective-permute-start.19 = (bf16[256,768]{1,0:T(8,128)(2,1)S(1)}, bf16[256,768]{1,0:T(8,128)(2,1)S(1)}, u32[]{:S(2)}, u32[]{:S(2)}) collective-permute-start(bf16[256,768]{1,0:T(8,128)(2,1)S(1)} %copy-done.25), channel_id=1, source_target_pairs={{0,8},{4,12},{8,0},{12,4},{16,24},{20,28},{24,16},{28,20},{1,9},{5... | collective-permute-start | bytes 1179656 | tf_op jit(solution)/shard_map/cond/branch_0_fun/ppermute | solution.py:568
  88.3 29.8 %collective-permute-start.14 = (bf16[2,80,2048]{2,1,0:T(8,128)(2,1)S(1)}, bf16[2,80,2048]{2,1,0:T(8,128)(2,1)S(1)}, u32[]{:S(2)}, u32[]{:S(2)}) collective-permute-start(bf16[2,80,2048]{2,1,0:T(8,128)(2,1)S(1)} %copy-done.43), channel_id=1, source_target_pairs={{0,3},{1,2},{2,1},{3,0},{4,7},{5,6},{6,5},{7,4},{8,11},{9,10},{10,... | collective-permute-start | bytes 1966088 | tf_op jit(solution)/shard_map/cond/branch_0_fun/ppermute | solution.py:597
  93.1 7.4 %collective-permute-start.26 = (bf16[256,768]{1,0:T(8,128)(2,1)S(1)}, bf16[256,768]{1,0:T(8,128)(2,1)S(1)}, u32[]{:S(2)}, u32[]{:S(2)}) collective-permute-start(bf16[256,768]{1,0:T(8,128)(2,1)S(1)} %up_mid1.3), channel_id=1, source_target_pairs={{8,16},{16,8},{12,20},{20,12},{0,4},{4,0},{24,28},{28,24},{9,17},{... | collective-permute-start | bytes 1179656 | tf_op jit(solution)/shard_map/cond/branch_0_fun/ppermute | solution.py:572
  94.2 19.6 %collective-permute-start.27 = (bf16[768,256]{1,0:T(8,128)(2,1)S(1)}, bf16[768,256]{1,0:T(8,128)(2,1)S(1)}, u32[]{:S(2)}, u32[]{:S(2)}) collective-permute-start(bf16[768,256]{1,0:T(8,128)(2,1)S(1)} %down_sum.3), channel_id=1, source_target_pairs={{0,1},{1,0},{2,3},{3,2},{4,5},{5,4},{6,7},{7,6},{8,9},{9,8},{10,11... | collective-permute-start | bytes 1179656 | tf_op jit(solution)/shard_map/cond/branch_0_fun/ppermute | solution.py:575
  96.4 12.5 %collective-permute-start.24 = (bf16[256,768]{1,0:T(8,128)(2,1)S(1)}, bf16[256,768]{1,0:T(8,128)(2,1)S(1)}, u32[]{:S(2)}, u32[]{:S(2)}) collective-permute-start(bf16[256,768]{1,0:T(8,128)(2,1)S(1)} %gate_last.3), channel_id=1, source_target_pairs={{0,8},{4,12},{8,0},{12,4},{16,24},{20,28},{24,16},{28,20},{1,9},{5... | collective-permute-start | bytes 1179656 | tf_op jit(solution)/shard_map/cond/branch_0_fun/ppermute | solution.py:568
  100.4 13.5 %collective-permute-start.25 = (bf16[256,768]{1,0:T(8,128)(2,1)S(1)}, bf16[256,768]{1,0:T(8,128)(2,1)S(1)}, u32[]{:S(2)}, u32[]{:S(2)}) collective-permute-start(bf16[256,768]{1,0:T(8,128)(2,1)S(1)} %gate_mid2.3), channel_id=1, source_target_pairs={{8,16},{16,8},{12,20},{20,12},{0,4},{4,0},{24,28},{28,24},{9,17},{... | collective-permute-start | bytes 1179656 | tf_op jit(solution)/shard_map/cond/branch_0_fun/ppermute | solution.py:572
  100.5 16.9 %collective-permute-start.22 = (bf16[128,768]{1,0:T(8,128)(2,1)S(1)}, bf16[128,768]{1,0:T(8,128)(2,1)S(1)}, u32[]{:S(2)}, u32[]{:S(2)}) collective-permute-start(bf16[128,768]{1,0:T(8,128)(2,1)S(1)} %get-tuple-element.125.right_ref), channel_id=1, source_target_pairs={{0,8},{4,12},{8,0},{12,4},{16,24},{20,28},{24,16},{28,20},{1,9},{5... | collective-permute-start | bytes 589832 | tf_op jit(solution)/shard_map/cond/branch_0_fun/ppermute | solution.py:568
  108.8 8.4 %collective-permute-start.23 = (bf16[128,768]{1,0:T(8,128)(2,1)S(1)}, bf16[128,768]{1,0:T(8,128)(2,1)S(1)}, u32[]{:S(2)}, u32[]{:S(2)}) collective-permute-start(bf16[128,768]{1,0:T(8,128)(2,1)S(1)} %get-tuple-element.123.right_ref), channel_id=1, source_target_pairs={{0,8},{4,12},{8,0},{12,4},{16,24},{20,28},{24,16},{28,20},{1,9},{5... | collective-permute-start | bytes 589832 | tf_op jit(solution)/shard_map/cond/branch_0_fun/ppermute | solution.py:568
  113.8 7.8 %copy-start.57 = (bf16[128,2048]{1,0:T(8,128)(2,1)S(1)}, bf16[128,2048]{1,0:T(8,128)(2,1)}, u32[]{:S(2)}) copy-start(bf16[128,2048]{1,0:T(8,128)(2,1)} %get-tuple-element.394.cot_ref) | copy-start | bytes 1572868 | tf_op jit(solution)/shard_map/cond
  113.8 7.8 %copy-start.60 = (s32[2,128]{1,0:T(2,128)S(1)}, s32[2,128]{1,0:T(2,128)}, u32[]{:S(2)}) copy-start(s32[2,128]{1,0:T(2,128)} %get-tuple-element.42.ids_ref) | copy-start | bytes 3076 | tf_op jit(solution)/shard_map/cond
  113.8 7.8 %copy-start.63 = (f32[2,128]{1,0:T(2,128)S(1)}, f32[2,128]{1,0:T(2,128)}, u32[]{:S(2)}) copy-start(f32[2,128]{1,0:T(2,128)} %get-tuple-element.43.gates_ref) | copy-start | bytes 3076 | tf_op jit(solution)/shard_map/cond
  114.0 12.1 %collective-permute-start.28 = (bf16[256,768]{1,0:T(8,128)(2,1)S(1)}, bf16[256,768]{1,0:T(8,128)(2,1)S(1)}, u32[]{:S(2)}, u32[]{:S(2)}) collective-permute-start(bf16[256,768]{1,0:T(8,128)(2,1)S(1)} %gate_sum.3), channel_id=1, source_target_pairs={{0,1},{1,0},{2,3},{3,2},{4,5},{5,4},{6,7},{7,6},{8,9},{9,8},{10,11... | collective-permute-start | bytes 1179656 | tf_op jit(solution)/shard_map/cond/branch_0_fun/ppermute | solution.py:575
  115.3 10.7 %collective-permute-start.31 = (bf16[128,768]{1,0:T(8,128)(2,1)S(1)}, bf16[128,768]{1,0:T(8,128)(2,1)S(1)}, u32[]{:S(2)}, u32[]{:S(2)}) collective-permute-start(bf16[128,768]{1,0:T(8,128)(2,1)S(1)} %get-tuple-element.135), channel_id=1, source_target_pairs={{0,8},{4,12},{8,0},{12,4},{16,24},{20,28},{24,16},{28,20},{1,9},{5... | collective-permute-start | bytes 589832 | tf_op jit(solution)/shard_map/cond/branch_0_fun/ppermute | solution.py:568
  117.3 8.7 %collective-permute-start.32 = (bf16[128,768]{1,0:T(8,128)(2,1)S(1)}, bf16[128,768]{1,0:T(8,128)(2,1)S(1)}, u32[]{:S(2)}, u32[]{:S(2)}) collective-permute-start(bf16[128,768]{1,0:T(8,128)(2,1)S(1)} %up_mid20.3), channel_id=1, source_target_pairs={{8,16},{16,8},{12,20},{20,12},{0,4},{4,0},{24,28},{28,24},{9,17},{... | collective-permute-start | bytes 589832 | tf_op jit(solution)/shard_map/cond/branch_0_fun/ppermute | solution.py:572
  117.5 8.7 %collective-permute-start.30 = (bf16[128,768]{1,0:T(8,128)(2,1)S(1)}, bf16[128,768]{1,0:T(8,128)(2,1)S(1)}, u32[]{:S(2)}, u32[]{:S(2)}) collective-permute-start(bf16[128,768]{1,0:T(8,128)(2,1)S(1)} %up_mid21.3), channel_id=1, source_target_pairs={{8,16},{16,8},{12,20},{20,12},{0,4},{4,0},{24,28},{28,24},{9,17},{... | collective-permute-start | bytes 589832 | tf_op jit(solution)/shard_map/cond/branch_0_fun/ppermute | solution.py:572
  118.0 8.1 %collective-permute-start.29 = (bf16[128,768]{1,0:T(8,128)(2,1)S(1)}, bf16[128,768]{1,0:T(8,128)(2,1)S(1)}, u32[]{:S(2)}, u32[]{:S(2)}) collective-permute-start(bf16[128,768]{1,0:T(8,128)(2,1)S(1)} %get-tuple-element.134), channel_id=1, source_target_pairs={{0,8},{4,12},{8,0},{12,4},{16,24},{20,28},{24,16},{28,20},{1,9},{5... | collective-permute-start | bytes 589832 | tf_op jit(solution)/shard_map/cond/branch_0_fun/ppermute | solution.py:568
  126.2 6.0 %collective-permute-start.34 = (bf16[128,768]{1,0:T(8,128)(2,1)S(1)}, bf16[128,768]{1,0:T(8,128)(2,1)S(1)}, u32[]{:S(2)}, u32[]{:S(2)}) collective-permute-start(bf16[128,768]{1,0:T(8,128)(2,1)S(1)} %up_sum1.3), channel_id=1, source_target_pairs={{0,1},{1,0},{2,3},{3,2},{4,5},{5,4},{6,7},{7,6},{8,9},{9,8},{10,11... | collective-permute-start | bytes 589832 | tf_op jit(solution)/shard_map/cond/branch_0_fun/ppermute | solution.py:575
  127.3 7.1 %collective-permute-start.33 = (bf16[128,768]{1,0:T(8,128)(2,1)S(1)}, bf16[128,768]{1,0:T(8,128)(2,1)S(1)}, u32[]{:S(2)}, u32[]{:S(2)}) collective-permute-start(bf16[128,768]{1,0:T(8,128)(2,1)S(1)} %up_sum0.3), channel_id=1, source_target_pairs={{0,1},{1,0},{2,3},{3,2},{4,5},{5,4},{6,7},{7,6},{8,9},{9,8},{10,11... | collective-permute-start | bytes 589832 | tf_op jit(solution)/shard_map/cond/branch_0_fun/ppermute | solution.py:575
  (9 other events, 15.8 us)
